TPU v7x, 32 devices: a whole 2x2x4 slice. The times are simulated.
32 devices in a mesh: aa: 4 (over x, core), ba: 8 (over z, y).
Axes of the slice: x: 2, y: 2, z: 4, core: 2. Of those that a mesh axis runs over, the one named last changes fastest.
Arguments:
- tokens: bfloat16 [32768, 2048], P(('aa', 'ba')), may hold values from -42 to 42
- grad_out: bfloat16 [32768, 1024], P(('aa', 'ba')), may hold values from -6 to 6
- master_weight: float32 [2048, 1024], P(('aa', 'ba')), may hold values from -0.003 to 0.003
- first_moment: float32 [2048, 1024], P(('aa', 'ba')), may hold values from -0.6 to 0.6
- second_moment: float32 [2048, 1024], P(('aa', 'ba')), may hold values from 0.02 to 0.2
- next_tokens: bfloat16 [32768, 2048], P(('aa', 'ba')), may hold values from -72 to 72
Outputs:
- new_first: float32 [2048, 1024], P(('aa', 'ba'))
- new_second: float32 [2048, 1024], P(('aa', 'ba'))
- next_hidden: bfloat16 [32768, 512], P(('aa', 'ba'))
All inputs are finite; a program needn't handle non-finite values.
Results may differ from a plain program's by a relative error of at most 0.0064.
Values may be sent and summed in bfloat16 or wider, within the bound.
No kernel may reach another device: no remote copies, remote signals or barrier semaphores. Data moves between devices by JAX's collectives and lax.ppermute only.
A program may use at most 64 MiB of HBM per device.

v0:
```python
import math

import jax
import jax.numpy as jnp
from jax import lax
from jax.sharding import PartitionSpec as P

D = 2048
FF = 512
QB = 128


def encode_blocks(matrix):
    height, width = matrix.shape
    blocks = matrix.reshape(height, width // QB, QB)
    largest = jnp.max(jnp.abs(blocks), axis=2)
    scales = ((largest + 1e-06) / 448.0).astype(jnp.bfloat16)
    codes = (blocks / scales.astype(jnp.float32)[:, :, None]).astype(jnp.bfloat16)
    return (codes, scales)


def decoded_sum(codes, scales):
    values = codes.astype(jnp.float32) * scales.astype(jnp.float32)[:, :, :, None]
    summed = jnp.sum(values, axis=0)
    return summed.reshape(summed.shape[0], summed.shape[1] * summed.shape[2])


def reduce_tensor(tokens, cotangent):
    groups_outer = lax.axis_size("aa")
    groups_inner = lax.axis_size("ba")
    local_grad = lax.dot_general(
        tokens, cotangent, (((0,), (0,)), ((), ())), preferred_element_type=jnp.float32
    )
    height = local_grad.shape[0]
    codes, scales = encode_blocks(local_grad)
    codes = codes.reshape(groups_outer, height // groups_outer, codes.shape[1], codes.shape[2])
    scales = scales.reshape(groups_outer, height // groups_outer, scales.shape[1])
    codes, scales = (
        lax.all_to_all(codes, "aa", split_axis=0, concat_axis=0, tiled=True),
        lax.all_to_all(scales, "aa", split_axis=0, concat_axis=0, tiled=True),
    )
    partial_value = decoded_sum(codes, scales)
    rows_part = partial_value.shape[0]
    codes, scales = encode_blocks(partial_value)
    codes = codes.reshape(groups_inner, rows_part // groups_inner, codes.shape[1], codes.shape[2])
    scales = scales.reshape(groups_inner, rows_part // groups_inner, scales.shape[1])
    codes, scales = (
        lax.all_to_all(codes, "ba", split_axis=0, concat_axis=0, tiled=True),
        lax.all_to_all(scales, "ba", split_axis=0, concat_axis=0, tiled=True),
    )
    return decoded_sum(codes, scales)


def shards(tokens, grad_out, master_weight, first_moment, second_moment, next_tokens):
    half_width = grad_out.shape[1] // 2
    gate_grad = reduce_tensor(tokens, grad_out[:, :half_width])
    up_grad = reduce_tensor(tokens, grad_out[:, half_width:])
    gate_sq, up_sq = lax.psum(
        (jnp.sum(gate_grad * gate_grad), jnp.sum(up_grad * up_grad)), ("aa", "ba")
    )
    limit = math.sqrt(D * FF)
    gate_factor = jnp.minimum(1.0, limit / jnp.sqrt(gate_sq + 1e-06))
    up_factor = jnp.minimum(1.0, limit / jnp.sqrt(up_sq + 1e-06))
    clipped = jnp.concatenate([gate_grad * gate_factor, up_grad * up_factor], axis=1)
    new_first = 0.9 * first_moment + 0.1 * clipped
    new_second = 0.95 * second_moment + 0.05 * clipped * clipped
    corr_first = 1.0 - 0.9**10
    corr_second = 1.0 - 0.95**10
    updated = master_weight * (1.0 - 0.003 * 0.1) - 0.003 * (new_first / corr_first) / (
        jnp.sqrt(new_second / corr_second) + 1e-08
    )
    low_weight = updated.astype(jnp.bfloat16)
    block_rows = lax.all_gather(low_weight, "ba", axis=0, tiled=True)
    projected = jnp.dot(
        next_tokens,
        lax.all_gather(block_rows, "aa", axis=0, tiled=True),
        preferred_element_type=jnp.float32,
    )
    next_hidden = (jax.nn.silu(projected[:, :half_width]) * projected[:, half_width:]).astype(
        jnp.bfloat16
    )
    return (new_first, new_second, next_hidden)


def solution(mesh):
    in_specs = (
        P(("aa", "ba"), None),
        P(("aa", "ba"), None),
        P(("aa", "ba"), None),
        P(("aa", "ba"), None),
        P(("aa", "ba"), None),
        P(("aa", "ba"), None),
    )
    out_specs = (P(("aa", "ba"), None), P(("aa", "ba"), None), P(("aa", "ba"), None))
    return jax.shard_map(shards, mesh=mesh, in_specs=in_specs, out_specs=out_specs, check_vma=False)
```

profile of v0, /device:TPU:0, one launch (start us, length us, event | category | flops | bytes accessed | tf_op | source)
XLA Modules:
  0.0 289.0 jit_solution(3694090916546793513)
XLA Ops:
  7.2 7.0 %bitcast_reduce_fusion = (f32[2048,4]{0,1:T(4,128)S(1)}, f32[2048,512]{0,1:T(8,128)}) fusion(bf16[1024,2048]{1,0:T(8,128)(2,1)} %param.6, bf16[1024,1024]{1,0:T(8,128)(2,1)} %param.7), kind=kOutput, calls=%fused_computation | convolution fusion | flops 2149572608 | bytes 9469952 | tf_op jit(solution)/shard_map/dot_general | solution.py:31
  14.2 0.6 multiply_convert_fusion
  14.8 4.2 %all-to-all-start.5 = ((bf16[4,512,4]{1,2,0:T(4,128)(2,1)}), bf16[4,512,4]{1,2,0:T(4,128)(2,1)S(1)}, u32[]{:S(2)}, u32[]{:S(2)}) async-start(bf16[4,512,4]{1,2,0:T(4,128)(2,1)} %bitcast.4), calls=%async_computation.5 | async-start | bytes 32768 | tf_op jit(solution)/shard_map/all_to_all | solution.py:40
  19.0 6.5 %bitcast_reduce_fusion.1 = (f32[2048,4]{0,1:T(4,128)S(1)}, f32[2048,512]{0,1:T(8,128)}) fusion(bf16[1024,2048]{1,0:T(8,128)(2,1)} %param.6, bf16[1024,1024]{1,0:T(8,128)(2,1)S(1)} %copy-done.4), kind=kOutput, calls=%fused_computation.1 | convolution fusion | flops 2149572608 | bytes 9469952 | tf_op jit(solution)/shard_map/dot_general | solution.py:31
  25.6 0.6 multiply_convert_fusion.1
  26.2 0.7 convert_element_type.132
  26.9 6.0 %reshape.97 = f32[4,512,4,128]{1,0,3,2:T(4,128)} reshape(f32[2048,512]{0,1:T(8,128)} %get-tuple-element.26) | data formatting | bytes 8388608 | tf_op jit(solution)/shard_map/reshape | solution.py:15
  32.9 3.3 %all-to-all-start.1 = ((bf16[4,512,4]{1,2,0:T(4,128)(2,1)}), bf16[4,512,4]{1,2,0:T(4,128)(2,1)S(1)}, u32[]{:S(2)}, u32[]{:S(2)}) async-start(bf16[4,512,4]{1,2,0:T(4,128)(2,1)} %bitcast.1), calls=%async_computation.1 | async-start | bytes 32768 | tf_op jit(solution)/shard_map/all_to_all | solution.py:40
  36.2 4.8 %fusion = bf16[4,512,4,128]{1,3,2,0:T(8,128)(2,1)} fusion(f32[4,512,4,128]{1,0,3,2:T(4,128)} %reshape.97, f32[4,512,4]{1,2,0:T(4,128)S(1)} %convert_element_type.132), kind=kLoop, calls=%fused_computation.3 | loop fusion | flops 2097152 | bytes 6324224 | tf_op jit(solution)/shard_map/convert_element_type | solution.py:18
  41.0 3.6 %all-to-all-start.4 = ((bf16[4,512,4,128]{1,3,2,0:T(8,128)(2,1)}), bf16[4,512,4,128]{1,3,2,0:T(8,128)(2,1)S(1)}, u32[]{:S(2)}, u32[]{:S(2)}) async-start(bf16[4,512,4,128]{1,3,2,0:T(8,128)(2,1)} %fusion), calls=%async_computation.4 | async-start | bytes 4194304 | tf_op jit(solution)/shard_map/all_to_all | solution.py:39
  44.6 0.7 convert_element_type.120
  45.3 6.0 %reshape.96 = f32[4,512,4,128]{1,0,3,2:T(4,128)} reshape(f32[2048,512]{0,1:T(8,128)} %get-tuple-element.24) | data formatting | bytes 8388608 | tf_op jit(solution)/shard_map/reshape | solution.py:15
  51.3 4.8 %fusion.1 = bf16[4,512,4,128]{1,3,2,0:T(8,128)(2,1)} fusion(f32[4,512,4,128]{1,0,3,2:T(4,128)} %reshape.96, f32[4,512,4]{1,2,0:T(4,128)S(1)} %convert_element_type.120), kind=kLoop, calls=%fused_computation.5 | loop fusion | flops 2097152 | bytes 6324224 | tf_op jit(solution)/shard_map/convert_element_type | solution.py:18
  56.1 14.1 %all-to-all-done.4 = bf16[4,512,4,128]{1,3,2,0:T(8,128)(2,1)S(1)} async-done(((bf16[4,512,4,128]{1,3,2,0:T(8,128)(2,1)}), bf16[4,512,4,128]{1,3,2,0:T(8,128)(2,1)S(1)}, u32[]{:S(2)}, u32[]{:S(2)}) %all-to-all-start.4) | async-done | bytes 2097184 | tf_op jit(solution)/shard_map/all_to_all | solution.py:39
  70.3 4.4 %all-to-all-start = ((bf16[4,512,4,128]{1,3,2,0:T(8,128)(2,1)}), bf16[4,512,4,128]{1,3,2,0:T(8,128)(2,1)}, u32[]{:S(2)}, u32[]{:S(2)}) async-start(bf16[4,512,4,128]{1,3,2,0:T(8,128)(2,1)} %fusion.1), calls=%async_computation | async-start | bytes 4194304 | tf_op jit(solution)/shard_map/all_to_all | solution.py:39
  74.8 2.1 multiply_reduce_fusion
  76.9 0.1 abs_reduce_fusion
  77.0 0.1 convert_element_type.137
  77.1 0.7 reshape.100
  77.8 22.7 %all-to-all-done = bf16[4,512,4,128]{1,3,2,0:T(8,128)(2,1)} async-done(((bf16[4,512,4,128]{1,3,2,0:T(8,128)(2,1)}), bf16[4,512,4,128]{1,3,2,0:T(8,128)(2,1)}, u32[]{:S(2)}, u32[]{:S(2)}) %all-to-all-start) | async-done | bytes 2097184 | tf_op jit(solution)/shard_map/all_to_all | solution.py:39
  100.5 6.3 %all-to-all-start.7 = ((bf16[8,2,128]{2,1,0:T(2,128)(2,1)}), bf16[8,2,128]{2,1,0:T(2,128)(2,1)S(1)}, u32[]{:S(2)}, u32[]{:S(2)}) async-start(bf16[8,2,128]{2,1,0:T(2,128)(2,1)} %reshape.100), calls=%async_computation.7 | async-start | bytes 8192 | tf_op jit(solution)/shard_map/all_to_all | solution.py:49
  106.8 2.1 multiply_reduce_fusion.1
  108.9 0.1 abs_reduce_fusion.1
  109.0 0.3 copy.52
  109.5 0.7 reshape.98
  110.2 3.0 %all-to-all-done.7 = bf16[8,2,128]{2,1,0:T(2,128)(2,1)S(1)} async-done(((bf16[8,2,128]{2,1,0:T(2,128)(2,1)}), bf16[8,2,128]{2,1,0:T(2,128)(2,1)S(1)}, u32[]{:S(2)}, u32[]{:S(2)}) %all-to-all-start.7) | async-done | bytes 4128 | tf_op jit(solution)/shard_map/all_to_all | solution.py:49
  113.2 3.5 %all-to-all-start.3 = ((bf16[8,2,128]{2,1,0:T(2,128)(2,1)}), bf16[8,2,128]{2,1,0:T(2,128)(2,1)S(1)}, u32[]{:S(2)}, u32[]{:S(2)}) async-start(bf16[8,2,128]{2,1,0:T(2,128)(2,1)} %reshape.98), calls=%async_computation.3 | async-start | bytes 8192 | tf_op jit(solution)/shard_map/all_to_all | solution.py:49
  116.7 0.3 divide_convert_fusion
  117.0 0.8 copy.53
  117.9 5.0 %all-to-all-done.3 = bf16[8,2,128]{2,1,0:T(2,128)(2,1)S(1)} async-done(((bf16[8,2,128]{2,1,0:T(2,128)(2,1)}), bf16[8,2,128]{2,1,0:T(2,128)(2,1)S(1)}, u32[]{:S(2)}, u32[]{:S(2)}) %all-to-all-start.3) | async-done | bytes 4128 | tf_op jit(solution)/shard_map/all_to_all | solution.py:49
  122.8 3.5 %all-to-all-start.6 = ((bf16[8,64,4,128]{3,1,2,0:T(8,128)(2,1)}), bf16[8,64,4,128]{3,1,2,0:T(8,128)(2,1)S(1)}, u32[]{:S(2)}, u32[]{:S(2)}) async-start(bf16[8,64,4,128]{3,1,2,0:T(8,128)(2,1)} %copy.53), calls=%async_computation.6 | async-start | bytes 1048576 | tf_op jit(solution)/shard_map/all_to_all | solution.py:48
  126.4 0.3 copy.45
  126.7 0.3 divide_convert_fusion.1
  127.1 0.8 copy.46
  127.9 10.7 %all-to-all-done.6 = bf16[8,64,4,128]{3,1,2,0:T(8,128)(2,1)S(1)} async-done(((bf16[8,64,4,128]{3,1,2,0:T(8,128)(2,1)}), bf16[8,64,4,128]{3,1,2,0:T(8,128)(2,1)S(1)}, u32[]{:S(2)}, u32[]{:S(2)}) %all-to-all-start.6) | async-done | bytes 524320 | tf_op jit(solution)/shard_map/all_to_all | solution.py:48
  138.6 3.6 %all-to-all-start.2 = ((bf16[8,64,4,128]{3,1,2,0:T(8,128)(2,1)}), bf16[8,64,4,128]{3,1,2,0:T(8,128)(2,1)S(1)}, u32[]{:S(2)}, u32[]{:S(2)}) async-start(bf16[8,64,4,128]{3,1,2,0:T(8,128)(2,1)} %copy.46), calls=%async_computation.2 | async-start | bytes 1048576 | tf_op jit(solution)/shard_map/all_to_all | solution.py:48
  142.4 0.3 multiply_reduce_fusion.2
  142.8 0.6 multiply_reduce_fusion.4
  143.4 12.1 %all-to-all-done.2 = bf16[8,64,4,128]{3,1,2,0:T(8,128)(2,1)S(1)} async-done(((bf16[8,64,4,128]{3,1,2,0:T(8,128)(2,1)}), bf16[8,64,4,128]{3,1,2,0:T(8,128)(2,1)S(1)}, u32[]{:S(2)}, u32[]{:S(2)}) %all-to-all-start.2) | async-done | bytes 524320 | tf_op jit(solution)/shard_map/all_to_all | solution.py:48
  155.5 0.3 multiply_reduce_fusion.3
  155.8 0.6 multiply_reduce_fusion.5
  156.4 38.7 %all-reduce = (f32[]{:T(128)}, f32[]{:T(128)}) all-reduce(f32[]{:T(128)} %multiply_reduce_fusion.5, f32[]{:T(128)} %multiply_reduce_fusion.4), channel_id=1, replica_groups=mesh['aa'=4,'ba'=8] {'aa','ba'}, use_global_device_ids=true, to_apply=%region_5.0 | all-reduce | flops 2 | bytes 16 | tf_op jit(solution)/shard_map/psum | solution.py:58
  196.6 0.9 subtract_convert_fusion
  197.6 40.2 %all-gather.3.cloned.1.call-done = bf16[512,1024]{1,0:T(8,128)(2,1)} async-done(((bf16[64,1024]{1,0:T(8,128)(2,1)}), bf16[512,1024]{1,0:T(8,128)(2,1)}) %all-gather.3.cloned.1.call-update) | async-done | bytes 1048592 | tf_op jit(solution)/shard_map/all_gather | solution.py:73
  237.8 34.8 %all-gather.5.cloned.1.call-done = bf16[2048,1024]{1,0:T(8,128)(2,1)} async-done(((bf16[512,1024]{1,0:T(8,128)(2,1)}), bf16[2048,1024]{1,0:T(8,128)(2,1)}) %all-gather.5.cloned.1.call-update) | async-done | bytes 4194320 | tf_op jit(solution)/shard_map/all_gather | solution.py:76
  272.6 7.6 %convolution_bitcast_fusion = f32[1024,1024]{0,1:T(8,128)S(1)} fusion(bf16[2048,1024]{1,0:T(8,128)(2,1)} %all-gather.5.cloned.1.call-done, bf16[1024,2048]{1,0:T(8,128)(2,1)} %param.11), kind=kOutput, calls=%fused_computation.8 | convolution fusion | flops 4294967296 | bytes 12582912 | tf_op jit(solution)/shard_map/dot_general | solution.py:74
  280.2 0.6 fusion.2
  280.9 1.3 copy.57
  (31 shorter events, 0.5 us)
Async XLA Ops:
  7.2 11.9 %copy-start.4 = (bf16[1024,1024]{1,0:T(8,128)(2,1)S(1)}, bf16[1024,1024]{1,0:T(8,128)(2,1)}, u32[]{:S(2)}) copy-start(bf16[1024,1024]{1,0:T(8,128)(2,1)} %param.7) | copy-start | bytes 6291460
  14.8 18.1 %all-to-all-start.5 = ((bf16[4,512,4]{1,2,0:T(4,128)(2,1)}), bf16[4,512,4]{1,2,0:T(4,128)(2,1)S(1)}, u32[]{:S(2)}, u32[]{:S(2)}) async-start(bf16[4,512,4]{1,2,0:T(4,128)(2,1)} %bitcast.4), calls=%async_computation.5 | async-start | bytes 32768 | tf_op jit(solution)/shard_map/all_to_all | solution.py:40
  32.9 8.1 %all-to-all-start.1 = ((bf16[4,512,4]{1,2,0:T(4,128)(2,1)}), bf16[4,512,4]{1,2,0:T(4,128)(2,1)S(1)}, u32[]{:S(2)}, u32[]{:S(2)}) async-start(bf16[4,512,4]{1,2,0:T(4,128)(2,1)} %bitcast.1), calls=%async_computation.1 | async-start | bytes 32768 | tf_op jit(solution)/shard_map/all_to_all | solution.py:40
  41.0 29.3 %all-to-all-start.4 = ((bf16[4,512,4,128]{1,3,2,0:T(8,128)(2,1)}), bf16[4,512,4,128]{1,3,2,0:T(8,128)(2,1)S(1)}, u32[]{:S(2)}, u32[]{:S(2)}) async-start(bf16[4,512,4,128]{1,3,2,0:T(8,128)(2,1)} %fusion), calls=%async_computation.4 | async-start | bytes 4194304 | tf_op jit(solution)/shard_map/all_to_all | solution.py:39
  70.3 4.5 %copy-start = (bf16[4,512,4,128]{1,3,2,0:T(8,128)(2,1)}, bf16[4,512,4,128]{1,3,2,0:T(8,128)(2,1)S(1)}, u32[]{:S(2)}) copy-start(bf16[4,512,4,128]{1,3,2,0:T(8,128)(2,1)S(1)} %all-to-all-done.4) | copy-start | bytes 6291460
  70.3 30.2 %all-to-all-start = ((bf16[4,512,4,128]{1,3,2,0:T(8,128)(2,1)}), bf16[4,512,4,128]{1,3,2,0:T(8,128)(2,1)}, u32[]{:S(2)}, u32[]{:S(2)}) async-start(bf16[4,512,4,128]{1,3,2,0:T(8,128)(2,1)} %fusion.1), calls=%async_computation | async-start | bytes 4194304 | tf_op jit(solution)/shard_map/all_to_all | solution.py:39
  100.5 12.7 %all-to-all-start.7 = ((bf16[8,2,128]{2,1,0:T(2,128)(2,1)}), bf16[8,2,128]{2,1,0:T(2,128)(2,1)S(1)}, u32[]{:S(2)}, u32[]{:S(2)}) async-start(bf16[8,2,128]{2,1,0:T(2,128)(2,1)} %reshape.100), calls=%async_computation.7 | async-start | bytes 8192 | tf_op jit(solution)/shard_map/all_to_all | solution.py:49
  113.2 9.6 %all-to-all-start.3 = ((bf16[8,2,128]{2,1,0:T(2,128)(2,1)}), bf16[8,2,128]{2,1,0:T(2,128)(2,1)S(1)}, u32[]{:S(2)}, u32[]{:S(2)}) async-start(bf16[8,2,128]{2,1,0:T(2,128)(2,1)} %reshape.98), calls=%async_computation.3 | async-start | bytes 8192 | tf_op jit(solution)/shard_map/all_to_all | solution.py:49
  122.8 15.7 %all-to-all-start.6 = ((bf16[8,64,4,128]{3,1,2,0:T(8,128)(2,1)}), bf16[8,64,4,128]{3,1,2,0:T(8,128)(2,1)S(1)}, u32[]{:S(2)}, u32[]{:S(2)}) async-start(bf16[8,64,4,128]{3,1,2,0:T(8,128)(2,1)} %copy.53), calls=%async_computation.6 | async-start | bytes 1048576 | tf_op jit(solution)/shard_map/all_to_all | solution.py:48
  126.3 70.2 %copy-start.1 = (f32[64,1024]{1,0:T(8,128)S(1)}, f32[64,1024]{1,0:T(8,128)}, u32[]{:S(2)}) copy-start(f32[64,1024]{1,0:T(8,128)} %param.8) | copy-start | bytes 786436
  126.3 70.2 %copy-start.2 = (f32[64,1024]{1,0:T(8,128)S(1)}, f32[64,1024]{1,0:T(8,128)}, u32[]{:S(2)}) copy-start(f32[64,1024]{1,0:T(8,128)} %param.10) | copy-start | bytes 786436
  126.3 70.2 %copy-start.3 = (f32[64,1024]{1,0:T(8,128)S(1)}, f32[64,1024]{1,0:T(8,128)}, u32[]{:S(2)}) copy-start(f32[64,1024]{1,0:T(8,128)} %param.9) | copy-start | bytes 786436
  138.6 16.9 %all-to-all-start.2 = ((bf16[8,64,4,128]{3,1,2,0:T(8,128)(2,1)}), bf16[8,64,4,128]{3,1,2,0:T(8,128)(2,1)S(1)}, u32[]{:S(2)}, u32[]{:S(2)}) async-start(bf16[8,64,4,128]{3,1,2,0:T(8,128)(2,1)} %copy.46), calls=%async_computation.2 | async-start | bytes 1048576 | tf_op jit(solution)/shard_map/all_to_all | solution.py:48
  142.2 95.6 %all-gather.3.cloned.1.call-start = ((), (), s32[]{:S(2)}) async-start(), calls=%async_computation.8 | async-start | bytes 1179648 | tf_op jit(solution)/shard_map/all_gather | solution.py:73
  197.6 75.1 %all-gather.5.cloned.1.call-start = ((), (), s32[]{:S(2)}) async-start(), calls=%async_computation.9 | async-start | bytes 5242880 | tf_op jit(solution)/shard_map/all_gather | solution.py:76
Sparse Core Ops, SparseCore 0:
  197.7 40.0 all-gather.2
  239.3 33.2 all-gather.4
where the time goes:
time: 290 us; the launch traced here: 289 us
  waiting for transfers between devices  143 us (49%)
  blocking collectives  38.7 us (13%)
  starting transfers between devices  32.6 us (11%)
  matrix products  21.2 us (7%)
  other arithmetic  21 us (7%)
  local copies, waits for them, and re-layouts  17.4 us (6%)
  between operations  15.6 us (5%)
    all_gather x1, waiting for transfers between devices, shards(): block_rows = lax.all_gather(low_weight, 'ba', axis=0, tiled=True)  40.2 us
    psum x1, blocking collectives, shards(): lax.psum((jnp.sum(gate_grad * gate_grad), jnp.sum(up_grad * up_grad)), ('...  38.7 us
    all_to_all x2, waiting for transfers between devices, reduce_tensor(): lax.all_to_all(codes, 'aa', split_axis=0, concat_axis=0, tiled=True)  36.8 us
    all_gather x1, waiting for transfers between devices, shards(): lax.all_gather(block_rows, 'aa', axis=0, tiled=True)  34.8 us
    all_to_all x2, waiting for transfers between devices, reduce_tensor(): lax.all_to_all(codes, 'ba', split_axis=0, concat_axis=0, tiled=True)  22.7 us
    dot_general x2, matrix products, reduce_tensor(): lax.dot_general(tokens, cotangent, (((0,), (0,)), ((), ())), preferred_el...  13.6 us
    reshape x2, local copies, waits for them, and re-layouts, encode_blocks(): blocks = matrix.reshape(height, width // QB, QB)  12 us
    convert_element_type x4, other arithmetic, encode_blocks(): (blocks / scales.astype(jnp.float32)[:, :, None]).astype(jnp.bfloat16)  10.3 us
  transfers between devices with their start and end apart: 10, of which 8 were waited for; matrix products, arithmetic and copies ran while one was open for 14% of the time, Pallas kernels for 0%

commit v1 on v0

v1 whole, which is shorter than its diff:
```python
import functools
import math

import jax
import jax.numpy as jnp
from jax import lax
from jax.experimental import pallas as pl
from jax.experimental.pallas import tpu as pltpu
from jax.sharding import PartitionSpec as P

D = 2048
FF = 512
AXES = ("aa", "ba")
BF16 = jnp.bfloat16
F32 = jnp.float32
VMEM_LIMIT = 40 * 1024 * 1024


class Grid:
    def __init__(self):
        outer, inner = lax.axis_size("aa"), lax.axis_size("ba")
        self.c = 2
        self.x = outer // 2
        self.y = 1
        while self.y * self.y * 4 <= inner:
            self.y *= 2
        self.z = inner // self.y
        a, b = lax.axis_index("aa"), lax.axis_index("ba")
        self.at = {"x": a // self.c, "c": a % self.c, "z": b // self.y, "y": b % self.y}
        self.size = {"x": self.x, "c": self.c, "z": self.z, "y": self.y}

    def other(self, axis, step):
        return (self.at[axis] + step) % self.size[axis]

    def send(self, value, axis, step):
        pairs = []
        for x in range(self.x):
            for c in range(self.c):
                for z in range(self.z):
                    for y in range(self.y):
                        here = {"x": x, "c": c, "z": z, "y": y}
                        there = dict(here)
                        there[axis] = (here[axis] + step) % self.size[axis]
                        pairs.append((self.index(here), self.index(there)))
        return lax.ppermute(value, AXES, pairs)

    def index(self, at):
        return ((at["x"] * self.c + at["c"]) * self.z + at["z"]) * self.y + at["y"]


def pick(value, axis, index):
    return lax.dynamic_index_in_dim(value, index, axis, keepdims=False)


def grad_kernel(core_ref, tokens_ref, cot_ref, out_ref):
    out_ref[...] = lax.dot_general(
        tokens_ref[...], cot_ref[...], (((0,), (0,)), ((), ())), preferred_element_type=F32
    ).astype(out_ref.dtype)


def grad_rows(grid, tokens, cot, core, section, dtype):
    count, depth = tokens.shape
    width = cot.shape[1] // 2
    rows = depth // (grid.x * grid.c)
    tile = min(rows, 256)
    tiles = rows // tile
    return pl.pallas_call(
        grad_kernel,
        out_shape=jax.ShapeDtypeStruct((grid.x * rows, width), dtype),
        grid_spec=pltpu.PrefetchScalarGridSpec(
            num_scalar_prefetch=1,
            grid=(grid.x, tiles),
            in_specs=[
                pl.BlockSpec((count, tile), lambda x, t, core: (0, (x * 2 + core[0]) * tiles + t)),
                pl.BlockSpec((count, width), lambda x, t, core: (0, section)),
            ],
            out_specs=pl.BlockSpec((tile, width), lambda x, t, core: (x * tiles + t, 0)),
        ),
        compiler_params=pltpu.CompilerParams(vmem_limit_bytes=VMEM_LIMIT),
        cost_estimate=pl.CostEstimate(
            flops=2 * count * grid.x * rows * width,
            bytes_accessed=count * grid.x * rows * 2 + count * width * 2 + grid.x * rows * width * 4,
            transcendentals=0,
        ),
    )(core.reshape(1).astype(jnp.int32), tokens, cot)


def reduce_axis(grid, own, received, axis, dim):
    def part(step):
        index = grid.other(axis, step)
        total = pick(own, dim, index).astype(F32)
        for value in received:
            total = total + pick(value, dim, index).astype(F32)
        return total

    arriving = [grid.send(part(step).astype(BF16), axis, step) for step in range(1, grid.size[axis])]
    return part(0), arriving


def gather_axis(grid, value, axis):
    return [value] + [grid.send(value, axis, step) for step in range(1, grid.size[axis])]


def shards(tokens, grad_out, master_weight, first_moment, second_moment, next_tokens):
    grid = Grid()
    core = grid.at["c"]
    half = grad_out.shape[1] // 2
    rows = master_weight.shape[0]
    lead = (grid.x, grid.z, grid.y, rows, half)

    sent = [grad_rows(grid, tokens, grad_out, 1 - core, s, BF16) for s in (0, 1)]
    came = [grid.send(value, "c", 1) for value in sent]
    kept = [grad_rows(grid, tokens, grad_out, core, s, F32) for s in (0, 1)]
    kept = [value.reshape(lead) for value in kept]
    came = [[value.reshape(lead)] for value in came]
    gate, gate_in = reduce_axis(grid, kept[0], came[0], "x", 0)
    up, up_in = reduce_axis(grid, kept[1], came[1], "y", 2)
    gate, gate_in = reduce_axis(grid, gate, gate_in, "y", 1)
    up, up_in = reduce_axis(grid, up, up_in, "x", 0)

    both = jnp.concatenate([gate, up], axis=2)
    both_in = [jnp.concatenate(pair, axis=2) for pair in zip(gate_in, up_in)] if len(gate_in) == len(up_in) else None
    if both_in is None:
        gate = gate + sum(v.astype(F32) for v in gate_in)
        up = up + sum(v.astype(F32) for v in up_in)
        both, both_in = jnp.concatenate([gate, up], axis=2), []
    grad, grad_in = reduce_axis(grid, both, both_in, "z", 0)
    for value in grad_in:
        grad = grad + value.astype(F32)

    squares = grad * grad
    sums = jnp.stack([jnp.sum(squares[:, :half]), jnp.sum(squares[:, half:])])
    sums = jnp.broadcast_to(sums[:, None], (2, 128))
    for axis in ("c", "x", "y", "z"):
        size, step = grid.size[axis], 1
        while step < size:
            sums = sums + grid.send(sums, axis, step)
            step *= 2
    factors = jnp.minimum(1.0, math.sqrt(D * FF) / jnp.sqrt(sums[:, 0] + 1e-06))
    clipped = jnp.concatenate([grad[:, :half] * factors[0], grad[:, half:] * factors[1]], axis=1)
    new_first = 0.9 * first_moment + 0.1 * clipped
    new_second = 0.95 * second_moment + 0.05 * clipped * clipped
    corr_first = 1.0 - 0.9**10
    corr_second = 1.0 - 0.95**10
    updated = master_weight * (1.0 - 0.003 * 0.1) - 0.003 * (new_first / corr_first) / (
        jnp.sqrt(new_second / corr_second) + 1e-08
    )
    low_weight = updated.astype(BF16)

    pieces = gather_axis(grid, low_weight, "z")
    gate = jnp.stack([p[:, :half] for p in pieces])
    up = jnp.stack([p[:, half:] for p in pieces])
    gate = jnp.stack(gather_axis(grid, gate, "y"))
    up = jnp.stack(gather_axis(grid, up, "x"))
    gates = gather_axis(grid, gate, "x")
    ups = gather_axis(grid, up, "y")
    own = (gates, ups)
    other = tuple([grid.send(v, "c", 1) for v in vs] for vs in own)
    partial = project(grid, next_tokens, own, core, None)
    next_hidden = project(grid, next_tokens, other, 1 - core, partial)
    return new_first, new_second, next_hidden


def project_body(sizes, finish, at_ref, *refs):
    nx, ny, nz, rows = sizes
    refs = list(refs)
    tokens = [refs.pop(0) for _ in range(nx)]
    gates = [refs.pop(0) for _ in range(nx)]
    ups = [refs.pop(0) for _ in range(ny)]
    before = [refs.pop(0) for _ in range(2)] if finish else None
    outs = [refs.pop(0) for _ in range(1 if finish else 2)]
    gate_w, up_w = refs
    at_x, at_y, at_z = at_ref[1], at_ref[2], at_ref[3]
    block = nz * ny * rows

    @pl.when(pl.program_id(0) == 0)
    def _():
        for kx in range(nx):
            x = lax.rem(at_x + nx - kx, nx)
            for ky in range(ny):
                y = lax.rem(at_y + ny - ky, ny)
                for kz in range(nz):
                    z = lax.rem(at_z + nz - kz, nz)
                    start = pl.multiple_of((z * ny + y) * rows, rows)
                    gate_w[x, pl.ds(start, rows), :] = gates[kx][ky, kz].astype(gate_w.dtype)
                    up_w[x, pl.ds(start, rows), :] = ups[ky][kx, kz].astype(up_w.dtype)

    gate = before[0][...] if finish else None
    up = before[1][...] if finish else None
    for x in range(nx):
        for_gate = jnp.dot(tokens[x][...], gate_w[x].astype(BF16), preferred_element_type=F32)
        for_up = jnp.dot(tokens[x][...], up_w[x].astype(BF16), preferred_element_type=F32)
        gate = for_gate if gate is None else gate + for_gate
        up = for_up if up is None else up + for_up
    if finish:
        outs[0][...] = (gate / (1.0 + jnp.exp(-gate)) * up).astype(outs[0].dtype)
    else:
        outs[0][...] = gate
        outs[1][...] = up


def project(grid, tokens, pieces, core, before):
    gates, ups = pieces
    count, depth = tokens.shape
    rows, half = gates[0].shape[-2:]
    block = depth // (grid.x * grid.c)
    tile = min(count, 256)
    finish = before is not None
    held = BF16 if rows % 16 == 0 else F32
    at = jnp.stack([core, grid.at["x"], grid.at["y"], grid.at["z"]]).astype(jnp.int32)
    token_specs = [
        pl.BlockSpec((tile, block), lambda t, at, x=x: (t, x * 2 + at[0])) for x in range(grid.x)
    ]
    whole = pl.BlockSpec(memory_space=pltpu.VMEM)
    tiled = pl.BlockSpec((tile, half), lambda t, at: (t, 0))
    wide = jax.ShapeDtypeStruct((count, half), F32)
    low = jax.ShapeDtypeStruct((count, half), BF16)
    return pl.pallas_call(
        functools.partial(project_body, (grid.x, grid.y, grid.z, rows), finish),
        out_shape=low if finish else (wide, wide),
        grid_spec=pltpu.PrefetchScalarGridSpec(
            num_scalar_prefetch=1,
            grid=(count // tile,),
            in_specs=token_specs + [whole] * (grid.x + grid.y) + ([tiled, tiled] if finish else []),
            out_specs=tiled if finish else [tiled, tiled],
            scratch_shapes=[pltpu.VMEM((grid.x, block, half), held)] * 2,
        ),
        compiler_params=pltpu.CompilerParams(vmem_limit_bytes=VMEM_LIMIT),
        cost_estimate=pl.CostEstimate(
            flops=2 * count * depth * half, bytes_accessed=count * depth + 2 * depth * half, transcendentals=0
        ),
    )(at, *([tokens] * grid.x), *gates, *ups, *(before if finish else ()))


def solution(mesh):
    spec = P(AXES, None)
    return jax.shard_map(shards, mesh=mesh, in_specs=(spec,) * 6, out_specs=(spec,) * 3, check_vma=False)
```

time: 290 us -> 124 us (0.43)
  waiting for transfers between devices: 143 us -> 55.1 us
  blocking collectives: 38.7 us -> 0 us
  matrix products: 21.2 us -> 0 us
  Pallas kernels: 0 us -> 18.7 us
  between operations: 15.6 us -> 1.04 us
  local copies, waits for them, and re-layouts: 17.4 us -> 8.01 us
  starting transfers between devices: 32.6 us -> 25.7 us
  other arithmetic: 21 us -> 15.4 us
    all_gather x2 -> x0, waiting for transfers between devices: 75 us -> none  [the longest x1 40.2 us: shards(): block_rows = lax.all_gather(low_weight, 'ba', axis=0, tiled=True)]
    all_to_all x8 -> x0, waiting for transfers between devices: 67.5 us -> none  [the longest x2 36.8 us: reduce_tensor(): lax.all_to_all(codes, 'aa', split_axis=0, concat_axis=0, tiled=True)]
    ppermute x0 -> x25, waiting for transfers between devices: none -> 55.1 us  [send(): return lax.ppermute(value, AXES, pairs)]
    psum x1 -> x0, blocking collectives: 38.7 us -> none  [shards(): lax.psum((jnp.sum(gate_grad * gate_grad), jnp.sum(up_grad * up_grad)), ('...]
    all_to_all x8 -> x0, starting transfers between devices: 32.5 us -> none  [the longest x2 9.8 us: reduce_tensor(): lax.all_to_all(scales, 'ba', split_axis=0, concat_axis=0, tiled=True)]
    ppermute x0 -> x25, starting transfers between devices: none -> 25.7 us  [send(): return lax.ppermute(value, AXES, pairs)]
    dot_general x3 -> x0, matrix products: 21.2 us -> none  [the longest x2 13.6 us: reduce_tensor(): lax.dot_general(tokens, cotangent, (((0,), (0,)), ((), ())), preferred_el...]
    pallas_call x0 -> x6, Pallas kernels: none -> 18.7 us  [the longest x4 10.2 us: grad_rows(): pl.pallas_call(grad_kernel, out_shape=jax.ShapeDtypeStruct((grid.x * rows...]
  transfers between devices with their start and end apart: 10 -> 25, of which waited for: 8 -> 16; matrix products, arithmetic and copies ran while one was open for 14% -> 9% of each run, Pallas kernels for 0% -> 9%
where the time goes in v1:
time: 124 us
  waiting for transfers between devices  55.1 us (44%)
  starting transfers between devices  25.7 us (21%)
  Pallas kernels  18.7 us (15%)
  other arithmetic  15.4 us (12%)
  local copies, waits for them, and re-layouts  8.01 us (6%)
    ppermute x25, waiting for transfers between devices, send(): return lax.ppermute(value, AXES, pairs)  55.1 us
    ppermute x25, starting transfers between devices, send(): return lax.ppermute(value, AXES, pairs)  25.7 us
    pallas_call x4, Pallas kernels, grad_rows(): pl.pallas_call(grad_kernel, out_shape=jax.ShapeDtypeStruct((grid.x * rows...  10.2 us
    pallas_call x2, Pallas kernels, project(): pl.pallas_call(functools.partial(project_body, (grid.x, grid.y, grid.z, r...  8.57 us
    unnamed x23, local copies, waits for them, and re-layouts  7.35 us
    convert_element_type x3, other arithmetic, reduce_axis(): part(step).astype(BF16)  4.59 us
    add x3, other arithmetic, part(): total = total + pick(value, dim, index).astype(F32)  3.61 us
  transfers between devices with their start and end apart: 25, of which 16 were waited for; matrix products, arithmetic and copies ran while one was open for 9% of the time, Pallas kernels for 9%

profile of v1, /device:TPU:0, one launch (start us, length us, event | category | flops | bytes accessed | tf_op | source)
XLA Modules:
  0.0 123.9 jit_solution(3314967348996420370)
XLA Ops:
  0.7 2.2 %copy-done.1 = bf16[1024,2048]{1,0:T(8,128)(2,1)S(1)} copy-done((bf16[1024,2048]{1,0:T(8,128)(2,1)S(1)}, bf16[1024,2048]{1,0:T(8,128)(2,1)}, u32[]{:S(2)}) %copy-start.1) | copy-done | bytes 4194328
  2.8 1.6 %copy-done.3 = bf16[1024,1024]{1,0:T(8,128)(2,1)S(1)} copy-done((bf16[1024,1024]{1,0:T(8,128)(2,1)S(1)}, bf16[1024,1024]{1,0:T(8,128)(2,1)}, u32[]{:S(2)}) %copy-start.3) | copy-done | bytes 2097176
  4.4 3.2 %shard_map.86 = bf16[1024,512]{1,0:T(8,128)(2,1)} custom-call(s32[1]{0:T(128)} %bitcast.2.core_ref, bf16[1024,2048]{1,0:T(8,128)(2,1)S(1)} %copy-done.1, bf16[1024,1024]{1,0:T(8,128)(2,1)S(1)} %copy-done.3), custom_call_target="tpu_custom_call" | custom-call | flops 1073741824 | bytes 5242880 | tf_op jit(solution)/shard_map/pallas_call | solution.py:67
  8.0 2.4 %shard_map.88 = bf16[1024,512]{1,0:T(8,128)(2,1)S(1)} custom-call(s32[1]{0:T(128)} %bitcast.2.core_ref, bf16[1024,2048]{1,0:T(8,128)(2,1)S(1)} %copy-done.1, bf16[1024,1024]{1,0:T(8,128)(2,1)S(1)} %copy-done.3), custom_call_target="tpu_custom_call" | custom-call | flops 1073741824 | bytes 5242880 | tf_op jit(solution)/shard_map/pallas_call | solution.py:67
  10.6 2.2 %copy-done.2 = bf16[1024,2048]{1,0:T(8,128)(2,1)S(1)} copy-done((bf16[1024,2048]{1,0:T(8,128)(2,1)S(1)}, bf16[1024,2048]{1,0:T(8,128)(2,1)}, u32[]{:S(2)}) %copy-start.2) | copy-done | bytes 4194328
  12.7 2.3 %shard_map.85 = f32[1024,512]{1,0:T(8,128)S(1)} custom-call(s32[1]{0:T(128)} %bitcast.core_ref, bf16[1024,2048]{1,0:T(8,128)(2,1)S(1)} %copy-done.2, bf16[1024,1024]{1,0:T(8,128)(2,1)S(1)} %copy-done.4), custom_call_target="tpu_custom_call" | custom-call | flops 1073741824 | bytes 5242880 | tf_op jit(solution)/shard_map/pallas_call | solution.py:67
  15.1 2.3 %constant_dynamic-slice_fusion.1 = (f32[1,4,2,64,512]{4,3,2,1,0:T(8,128)S(1)}, f32[1,4,2,64,512]{4,3,2,1,0:T(8,128)}) fusion(f32[2,4,2,64,512]{4,3,2,1,0:T(8,128)S(1)} %bitcast.90, s32[]{:T(128)S(6)} %select_n.116, bf16[2,4,2,64,512]{4,3,2,1,0:T(8,128)(2,1)} %bitcast.3, s32[]{:T(128)S(6)} %select_n.111), kind=kLoop, calls=%fused_computation.66 | loop fusion | flops 524288 | bytes 4718600 | tf_op jit(solution)/shard_map/jit(dynamic_index_in_dim)/dynamic_slice | solution.py:52
  17.4 2.0 %fusion.2 = bf16[4,2,64,512]{3,2,0,1:T(8,128)(2,1)} fusion(f32[1,4,2,64,512]{4,3,2,1,0:T(8,128)S(1)} %get-tuple-element.14, bf16[2,4,2,64,512]{4,3,2,1,0:T(8,128)(2,1)} %bitcast.3, s32[]{:T(128)S(6)} %select_n.116), kind=kLoop, calls=%fused_computation.14 | loop fusion | flops 786432 | bytes 2097156 | tf_op jit(solution)/shard_map/convert_element_type | solution.py:96
  19.4 2.9 %collective-permute-start.1 = (bf16[4,2,64,512]{3,2,0,1:T(8,128)(2,1)}, bf16[4,2,64,512]{3,2,0,1:T(8,128)(2,1)}, u32[]{:S(2)}, u32[]{:S(2)}) collective-permute-start(bf16[4,2,64,512]{3,2,0,1:T(8,128)(2,1)} %fusion.2), channel_id=1, source_target_pairs={{0,16},{1,17},{2,18},{3,19},{4,20},{5,21},{6,22},{7,23},{8,24},{9,... | collective-permute-start | bytes 1572872 | tf_op jit(solution)/shard_map/ppermute | solution.py:45
  22.3 2.3 %shard_map.87 = f32[1024,512]{1,0:T(8,128)S(1)} custom-call(s32[1]{0:T(128)} %bitcast.core_ref, bf16[1024,2048]{1,0:T(8,128)(2,1)S(1)} %copy-done.2, bf16[1024,1024]{1,0:T(8,128)(2,1)S(1)} %copy-done.4), custom_call_target="tpu_custom_call" | custom-call | flops 1073741824 | bytes 5242880 | tf_op jit(solution)/shard_map/pallas_call | solution.py:67
  24.7 1.3 %copy-done.5 = f32[1024,512]{1,0:T(8,128)} copy-done((f32[1024,512]{1,0:T(8,128)}, f32[1024,512]{1,0:T(8,128)S(1)}, u32[]{:S(2)}) %copy-start.5) | copy-done | bytes 2097176
  26.0 2.5 %fusion.3 = bf16[2,4,64,512]{3,2,1,0:T(8,128)(2,1)} fusion(f32[2,4,2,64,512]{4,3,2,1,0:T(8,128)} %bitcast.91, s32[]{:T(128)S(6)} %select_n.118, bf16[2,4,2,64,512]{4,3,2,1,0:T(8,128)(2,1)} %bitcast.8), kind=kLoop, calls=%fused_computation.15 | loop fusion | flops 786432 | bytes 2097156 | tf_op jit(solution)/shard_map/convert_element_type | solution.py:96
  28.5 1.5 %collective-permute-start.3 = (bf16[2,4,64,512]{3,2,1,0:T(8,128)(2,1)}, bf16[2,4,64,512]{3,2,1,0:T(8,128)(2,1)}, u32[]{:S(2)}, u32[]{:S(2)}) collective-permute-start(bf16[2,4,64,512]{3,2,1,0:T(8,128)(2,1)} %fusion.3), channel_id=1, source_target_pairs={{0,1},{1,0},{2,3},{3,2},{4,5},{5,4},{6,7},{7,6},{8,9},{9,8},{10,11... | collective-permute-start | bytes 1572872 | tf_op jit(solution)/shard_map/ppermute | solution.py:45
  30.0 1.2 convert_add_fusion
  31.3 3.6 %collective-permute-done.1 = bf16[4,2,64,512]{3,2,0,1:T(8,128)(2,1)} collective-permute-done((bf16[4,2,64,512]{3,2,0,1:T(8,128)(2,1)}, bf16[4,2,64,512]{3,2,0,1:T(8,128)(2,1)}, u32[]{:S(2)}, u32[]{:S(2)}) %collective-permute-start.1) | collective-permute-done | bytes 524320 | tf_op jit(solution)/shard_map/ppermute | solution.py:45
  34.8 1.2 fusion.7
  36.0 1.8 %collective-permute-start.4 = (bf16[4,64,512]{2,1,0:T(8,128)(2,1)S(1)}, bf16[4,64,512]{2,1,0:T(8,128)(2,1)S(1)}, u32[]{:S(2)}, u32[]{:S(2)}) collective-permute-start(bf16[4,64,512]{2,1,0:T(8,128)(2,1)S(1)} %get-tuple-element.20), channel_id=1, source_target_pairs={{0,1},{1,0},{2,3},{3,2},{4,5},{5,4},{6,7},{7,6},{8,9},{9,8},{10,11... | collective-permute-start | bytes 786440 | tf_op jit(solution)/shard_map/ppermute | solution.py:45
  37.9 5.8 %collective-permute-done.3 = bf16[2,4,64,512]{3,2,1,0:T(8,128)(2,1)} collective-permute-done((bf16[2,4,64,512]{3,2,1,0:T(8,128)(2,1)}, bf16[2,4,64,512]{3,2,1,0:T(8,128)(2,1)}, u32[]{:S(2)}, u32[]{:S(2)}) %collective-permute-start.3) | collective-permute-done | bytes 524320 | tf_op jit(solution)/shard_map/ppermute | solution.py:45
  43.6 1.2 fusion.6
  45.0 3.0 %collective-permute-done.4 = bf16[4,64,512]{2,1,0:T(8,128)(2,1)S(1)} collective-permute-done((bf16[4,64,512]{2,1,0:T(8,128)(2,1)S(1)}, bf16[4,64,512]{2,1,0:T(8,128)(2,1)S(1)}, u32[]{:S(2)}, u32[]{:S(2)}) %collective-permute-start.4) | collective-permute-done | bytes 262176 | tf_op jit(solution)/shard_map/ppermute | solution.py:45
  48.0 3.3 %collective-permute-done.5 = bf16[4,64,512]{2,1,0:T(8,128)(2,1)S(1)} collective-permute-done((bf16[4,64,512]{2,1,0:T(8,128)(2,1)S(1)}, bf16[4,64,512]{2,1,0:T(8,128)(2,1)S(1)}, u32[]{:S(2)}, u32[]{:S(2)}) %collective-permute-start.5) | collective-permute-done | bytes 262176 | tf_op jit(solution)/shard_map/ppermute | solution.py:45
  51.4 1.6 %collective-permute-start.6 = (bf16[64,1024]{1,0:T(8,128)(2,1)S(1)}, bf16[64,1024]{1,0:T(8,128)(2,1)S(1)}, u32[]{:S(2)}, u32[]{:S(2)}) collective-permute-start(bf16[64,1024]{1,0:T(8,128)(2,1)S(1)} %get-tuple-element.16), channel_id=1, source_target_pairs={{0,2},{1,3},{2,4},{3,5},{4,6},{5,7},{6,0},{7,1},{8,10},{9,11},{10,... | collective-permute-start | bytes 393224 | tf_op jit(solution)/shard_map/ppermute | solution.py:45
  53.1 2.6 %collective-permute-start.7 = (bf16[64,1024]{1,0:T(8,128)(2,1)S(1)}, bf16[64,1024]{1,0:T(8,128)(2,1)S(1)}, u32[]{:S(2)}, u32[]{:S(2)}) collective-permute-start(bf16[64,1024]{1,0:T(8,128)(2,1)S(1)} %get-tuple-element.18), channel_id=1, source_target_pairs={{0,4},{1,5},{2,6},{3,7},{4,0},{5,1},{6,2},{7,3},{8,12},{9,13},{10,... | collective-permute-start | bytes 393224 | tf_op jit(solution)/shard_map/ppermute | solution.py:45
  55.7 1.4 %collective-permute-start.8 = (bf16[64,1024]{1,0:T(8,128)(2,1)S(1)}, bf16[64,1024]{1,0:T(8,128)(2,1)S(1)}, u32[]{:S(2)}, u32[]{:S(2)}) collective-permute-start(bf16[64,1024]{1,0:T(8,128)(2,1)S(1)} %get-tuple-element.17), channel_id=1, source_target_pairs={{0,6},{1,7},{2,0},{3,1},{4,2},{5,3},{6,4},{7,5},{8,14},{9,15},{10,... | collective-permute-start | bytes 393224 | tf_op jit(solution)/shard_map/ppermute | solution.py:45
  57.0 1.6 %collective-permute-done.6 = bf16[64,1024]{1,0:T(8,128)(2,1)S(1)} collective-permute-done((bf16[64,1024]{1,0:T(8,128)(2,1)S(1)}, bf16[64,1024]{1,0:T(8,128)(2,1)S(1)}, u32[]{:S(2)}, u32[]{:S(2)}) %collective-permute-start.6) | collective-permute-done | bytes 131104 | tf_op jit(solution)/shard_map/ppermute | solution.py:45
  58.6 4.1 %collective-permute-done.7 = bf16[64,1024]{1,0:T(8,128)(2,1)S(1)} collective-permute-done((bf16[64,1024]{1,0:T(8,128)(2,1)S(1)}, bf16[64,1024]{1,0:T(8,128)(2,1)S(1)}, u32[]{:S(2)}, u32[]{:S(2)}) %collective-permute-start.7) | collective-permute-done | bytes 131104 | tf_op jit(solution)/shard_map/ppermute | solution.py:45
  63.4 1.4 %pad_maximum_fusion.5 = f32[2]{0:T(128)S(1)} fusion(f32[1]{0:T(128)} %bitcast.21, f32[1]{0:T(128)} %bitcast.20), kind=kLoop, calls=%fused_computation.70 | loop fusion | flops 2 | bytes 16 | tf_op jit(solution)/shard_map/stack | solution.py:132
  64.8 1.1 collective-permute-done.9
  66.7 2.9 %collective-permute-done.10 = f32[2,128]{1,0:T(2,128)S(1)} collective-permute-done((f32[2,128]{1,0:T(2,128)S(1)}, f32[2,128]{1,0:T(2,128)S(1)}, u32[]{:S(2)}, u32[]{:S(2)}) %collective-permute-start.10) | collective-permute-done | bytes 1056 | tf_op jit(solution)/shard_map/ppermute | solution.py:45
  69.7 1.5 %collective-permute-start.11 = (f32[2,128]{1,0:T(2,128)S(1)}, f32[2,128]{1,0:T(2,128)S(1)}, u32[]{:S(2)}, u32[]{:S(2)}) collective-permute-start(f32[2,128]{1,0:T(2,128)S(1)} %fusion.35), channel_id=1, source_target_pairs={{0,1},{1,0},{2,3},{3,2},{4,5},{5,4},{6,7},{7,6},{8,9},{9,8},{10,11... | collective-permute-start | bytes 3080 | tf_op jit(solution)/shard_map/ppermute | solution.py:45
  71.2 2.0 %collective-permute-done.11 = f32[2,128]{1,0:T(2,128)S(1)} collective-permute-done((f32[2,128]{1,0:T(2,128)S(1)}, f32[2,128]{1,0:T(2,128)S(1)}, u32[]{:S(2)}, u32[]{:S(2)}) %collective-permute-start.11) | collective-permute-done | bytes 1056 | tf_op jit(solution)/shard_map/ppermute | solution.py:45
  73.2 2.0 %collective-permute-start.12 = (f32[2,128]{1,0:T(2,128)S(1)}, f32[2,128]{1,0:T(2,128)S(1)}, u32[]{:S(2)}, u32[]{:S(2)}) collective-permute-start(f32[2,128]{1,0:T(2,128)S(1)} %add.241), channel_id=1, source_target_pairs={{0,2},{1,3},{2,4},{3,5},{4,6},{5,7},{6,0},{7,1},{8,10},{9,11},{10,... | collective-permute-start | bytes 3080 | tf_op jit(solution)/shard_map/ppermute | solution.py:45
  75.2 3.4 %collective-permute-done.12 = f32[2,128]{1,0:T(2,128)S(1)} collective-permute-done((f32[2,128]{1,0:T(2,128)S(1)}, f32[2,128]{1,0:T(2,128)S(1)}, u32[]{:S(2)}, u32[]{:S(2)}) %collective-permute-start.12) | collective-permute-done | bytes 1056 | tf_op jit(solution)/shard_map/ppermute | solution.py:45
  78.6 4.5 %collective-permute-done.13 = f32[2,128]{1,0:T(2,128)S(1)} collective-permute-done((f32[2,128]{1,0:T(2,128)S(1)}, f32[2,128]{1,0:T(2,128)S(1)}, u32[]{:S(2)}, u32[]{:S(2)}) %collective-permute-start.13) | collective-permute-done | bytes 1056 | tf_op jit(solution)/shard_map/ppermute | solution.py:45
  83.6 1.3 %slice_multiply_fusion.1 = (f32[64,512]{1,0:T(8,128)S(1)}, f32[64,512]{1,0:T(8,128)S(1)}) fusion(f32[64,1024]{1,0:T(8,128)S(1)} %get-tuple-element.13, f32[]{:T(128)} %bitcast.22, f32[]{:T(128)} %bitcast.23), kind=kLoop, calls=%fused_computation.53 | loop fusion | flops 65536 | bytes 524296 | tf_op jit(solution)/shard_map/mul | solution.py:140
  85.0 1.0 subtract_convert_fusion
  86.1 1.6 %collective-permute-start.15 = (bf16[64,1024]{1,0:T(8,128)(2,1)S(1)}, bf16[64,1024]{1,0:T(8,128)(2,1)S(1)}, u32[]{:S(2)}, u32[]{:S(2)}) collective-permute-start(bf16[64,1024]{1,0:T(8,128)(2,1)S(1)} %get-tuple-element.9), channel_id=1, source_target_pairs={{0,4},{1,5},{2,6},{3,7},{4,0},{5,1},{6,2},{7,3},{8,12},{9,13},{10,... | collective-permute-start | bytes 393224 | tf_op jit(solution)/shard_map/ppermute | solution.py:45
  87.7 2.1 %collective-permute-start.16 = (bf16[64,1024]{1,0:T(8,128)(2,1)S(1)}, bf16[64,1024]{1,0:T(8,128)(2,1)S(1)}, u32[]{:S(2)}, u32[]{:S(2)}) collective-permute-start(bf16[64,1024]{1,0:T(8,128)(2,1)S(1)} %get-tuple-element.9), channel_id=1, source_target_pairs={{0,6},{1,7},{2,0},{3,1},{4,2},{5,3},{6,4},{7,5},{8,14},{9,15},{10,... | collective-permute-start | bytes 393224 | tf_op jit(solution)/shard_map/ppermute | solution.py:45
  89.8 3.1 %collective-permute-done.14 = bf16[64,1024]{1,0:T(8,128)(2,1)S(1)} collective-permute-done((bf16[64,1024]{1,0:T(8,128)(2,1)S(1)}, bf16[64,1024]{1,0:T(8,128)(2,1)S(1)}, u32[]{:S(2)}, u32[]{:S(2)}) %collective-permute-start.14) | collective-permute-done | bytes 131104 | tf_op jit(solution)/shard_map/ppermute | solution.py:45
  92.9 2.0 %collective-permute-done.15 = bf16[64,1024]{1,0:T(8,128)(2,1)S(1)} collective-permute-done((bf16[64,1024]{1,0:T(8,128)(2,1)S(1)}, bf16[64,1024]{1,0:T(8,128)(2,1)S(1)}, u32[]{:S(2)}, u32[]{:S(2)}) %collective-permute-start.15) | collective-permute-done | bytes 131104 | tf_op jit(solution)/shard_map/ppermute | solution.py:45
  95.0 0.8 collective-permute-start.21
  95.8 1.4 %collective-permute-start.17 = (bf16[4,64,512]{2,1,0:T(8,128)(2,1)S(1)}, bf16[4,64,512]{2,1,0:T(8,128)(2,1)S(1)}, u32[]{:S(2)}, u32[]{:S(2)}) collective-permute-start(bf16[4,64,512]{2,1,0:T(8,128)(2,1)S(1)} %get-tuple-element.26), channel_id=1, source_target_pairs={{0,1},{1,0},{2,3},{3,2},{4,5},{5,4},{6,7},{7,6},{8,9},{9,8},{10,11... | collective-permute-start | bytes 786440 | tf_op jit(solution)/shard_map/ppermute | solution.py:45
  97.2 6.8 %collective-permute-done.21 = bf16[4,64,512]{2,1,0:T(8,128)(2,1)S(1)} collective-permute-done((bf16[4,64,512]{2,1,0:T(8,128)(2,1)S(1)}, bf16[4,64,512]{2,1,0:T(8,128)(2,1)S(1)}, u32[]{:S(2)}, u32[]{:S(2)}) %collective-permute-start.21) | collective-permute-done | bytes 262176 | tf_op jit(solution)/shard_map/ppermute | solution.py:45
  104.0 1.8 %collective-permute-start.23 = (bf16[2,4,64,512]{3,2,1,0:T(8,128)(2,1)S(1)}, bf16[2,4,64,512]{3,2,1,0:T(8,128)(2,1)S(1)}, u32[]{:S(2)}, u32[]{:S(2)}) collective-permute-start(bf16[2,4,64,512]{3,2,1,0:T(8,128)(2,1)S(1)} %pad_maximum_fusion.1.refs_4_), channel_id=1, source_target_pairs={{0,1},{1,0},{2,3},{3,2},{4,5},{5,4},{6,7},{7,6},{8,9},{9,8},{10,11... | collective-permute-start | bytes 1572872 | tf_op jit(solution)/shard_map/ppermute | solution.py:45
  107.1 6.2 %collective-permute-done.23.refs_5_ = bf16[2,4,64,512]{3,2,1,0:T(8,128)(2,1)S(1)} collective-permute-done((bf16[2,4,64,512]{3,2,1,0:T(8,128)(2,1)S(1)}, bf16[2,4,64,512]{3,2,1,0:T(8,128)(2,1)S(1)}, u32[]{:S(2)}, u32[]{:S(2)}) %collective-permute-start.23) | collective-permute-done | bytes 524320 | tf_op jit(solution)/shard_map/ppermute | solution.py:45
  113.3 1.9 %collective-permute-done.19.refs_3_ = bf16[2,4,64,512]{3,2,1,0:T(8,128)(2,1)S(1)} collective-permute-done((bf16[2,4,64,512]{3,2,1,0:T(8,128)(2,1)S(1)}, bf16[2,4,64,512]{3,2,1,0:T(8,128)(2,1)S(1)}, u32[]{:S(2)}, u32[]{:S(2)}) %collective-permute-start.19) | collective-permute-done | bytes 524320 | tf_op jit(solution)/shard_map/ppermute | solution.py:45
  115.3 3.8 %shard_map.89 = (f32[1024,512]{1,0:T(8,128)S(1)}, f32[1024,512]{1,0:T(8,128)S(1)}) custom-call(s32[4]{0:T(128)S(1)} %add_add_fusion.1.at_ref, bf16[1024,2048]{1,0:T(8,128)(2,1)S(1)} %copy-done, bf16[1024,2048]{1,0:T(8,128)(2,1)S(1)} %copy-done, bf16[2,4,64,512]{3,2,1,0:T(8,128)(2,1)S(1)} %pad_maximum_fusion.refs_2_, ...), custom_call_target="tpu_custom_call" | custom-call | flops 2147483648 | bytes 4194304 | tf_op jit(solution)/shard_map/pallas_call | solution.py:218
  119.2 4.7 %shard_map.90 = bf16[1024,512]{1,0:T(8,128)(2,1)} custom-call(s32[4]{0:T(128)S(1)} %add_add_fusion.at_ref, bf16[1024,2048]{1,0:T(8,128)(2,1)S(1)} %copy-done, bf16[1024,2048]{1,0:T(8,128)(2,1)S(1)} %copy-done, bf16[2,4,64,512]{3,2,1,0:T(8,128)(2,1)S(1)} %collective-permute-done.18.refs_2_, bf16[2,4,64,512]{3,2,1,0:T(8,128)(2,1)S(1)} %collective-permute-done.20.refs_3_, ...), custom_call_target="tpu_custom_call" | custom-call | flops 2147483648 | bytes 4194304 | tf_op jit(solution)/shard_map/pallas_call | solution.py:218
  (62 shorter events, 4.8 us)
Async XLA Ops:
  0.6 2.2 %copy-start.1 = (bf16[1024,2048]{1,0:T(8,128)(2,1)S(1)}, bf16[1024,2048]{1,0:T(8,128)(2,1)}, u32[]{:S(2)}) copy-start(bf16[1024,2048]{1,0:T(8,128)(2,1)} %tokens_ref.7) | copy-start | bytes 12582916
  2.8 1.6 %copy-start.3 = (bf16[1024,1024]{1,0:T(8,128)(2,1)S(1)}, bf16[1024,1024]{1,0:T(8,128)(2,1)}, u32[]{:S(2)}) copy-start(bf16[1024,1024]{1,0:T(8,128)(2,1)} %cot_ref.7) | copy-start | bytes 6291460
  7.6 2.9 %copy-start.4 = (bf16[1024,1024]{1,0:T(8,128)(2,1)S(1)}, bf16[1024,1024]{1,0:T(8,128)(2,1)}, u32[]{:S(2)}) copy-start(bf16[1024,1024]{1,0:T(8,128)(2,1)} %cot_ref.7) | copy-start | bytes 6291460
  7.6 7.5 %collective-permute-start = (bf16[1024,512]{1,0:T(8,128)(2,1)}, bf16[1024,512]{1,0:T(8,128)(2,1)}, u32[]{:S(2)}, u32[]{:S(2)}) collective-permute-start(bf16[1024,512]{1,0:T(8,128)(2,1)} %shard_map.86), channel_id=1, source_target_pairs={{0,8},{1,9},{2,10},{3,11},{4,12},{5,13},{6,14},{7,15},{8,0},{9,1},... | collective-permute-start | bytes 3145736 | tf_op jit(solution)/shard_map/ppermute | solution.py:45
  10.4 15.6 %collective-permute-start.2 = (bf16[1024,512]{1,0:T(8,128)(2,1)S(1)}, bf16[1024,512]{1,0:T(8,128)(2,1)}, u32[]{:S(2)}, u32[]{:S(2)}) collective-permute-start(bf16[1024,512]{1,0:T(8,128)(2,1)S(1)} %shard_map.88), channel_id=1, source_target_pairs={{0,8},{1,9},{2,10},{3,11},{4,12},{5,13},{6,14},{7,15},{8,0},{9,1},... | collective-permute-start | bytes 3145736 | tf_op jit(solution)/shard_map/ppermute | solution.py:45
  10.6 2.2 %copy-start.2 = (bf16[1024,2048]{1,0:T(8,128)(2,1)S(1)}, bf16[1024,2048]{1,0:T(8,128)(2,1)}, u32[]{:S(2)}) copy-start(bf16[1024,2048]{1,0:T(8,128)(2,1)} %tokens_ref.7) | copy-start | bytes 12582916
  19.4 15.4 %collective-permute-start.1 = (bf16[4,2,64,512]{3,2,0,1:T(8,128)(2,1)}, bf16[4,2,64,512]{3,2,0,1:T(8,128)(2,1)}, u32[]{:S(2)}, u32[]{:S(2)}) collective-permute-start(bf16[4,2,64,512]{3,2,0,1:T(8,128)(2,1)} %fusion.2), channel_id=1, source_target_pairs={{0,16},{1,17},{2,18},{3,19},{4,20},{5,21},{6,22},{7,23},{8,24},{9,... | collective-permute-start | bytes 1572872 | tf_op jit(solution)/shard_map/ppermute | solution.py:45
  24.7 1.3 %copy-start.5 = (f32[1024,512]{1,0:T(8,128)}, f32[1024,512]{1,0:T(8,128)S(1)}, u32[]{:S(2)}) copy-start(f32[1024,512]{1,0:T(8,128)S(1)} %shard_map.87) | copy-start | bytes 6291460
  26.0 4.0 %copy-start.6 = (f32[1024,512]{1,0:T(8,128)S(1)}, f32[1024,512]{1,0:T(8,128)}, u32[]{:S(2)}) copy-start(f32[1024,512]{1,0:T(8,128)} %copy-done.5) | copy-start | bytes 6291460
  26.0 8.8 %copy-start.7 = (f32[1,4,2,64,512]{4,3,2,1,0:T(8,128)S(1)}, f32[1,4,2,64,512]{4,3,2,1,0:T(8,128)}, u32[]{:S(2)}) copy-start(f32[1,4,2,64,512]{4,3,2,1,0:T(8,128)} %get-tuple-element.15) | copy-start | bytes 3145732
  28.5 15.1 %collective-permute-start.3 = (bf16[2,4,64,512]{3,2,1,0:T(8,128)(2,1)}, bf16[2,4,64,512]{3,2,1,0:T(8,128)(2,1)}, u32[]{:S(2)}, u32[]{:S(2)}) collective-permute-start(bf16[2,4,64,512]{3,2,1,0:T(8,128)(2,1)} %fusion.3), channel_id=1, source_target_pairs={{0,1},{1,0},{2,3},{3,2},{4,5},{5,4},{6,7},{7,6},{8,9},{9,8},{10,11... | collective-permute-start | bytes 1572872 | tf_op jit(solution)/shard_map/ppermute | solution.py:45
  36.0 11.9 %collective-permute-start.4 = (bf16[4,64,512]{2,1,0:T(8,128)(2,1)S(1)}, bf16[4,64,512]{2,1,0:T(8,128)(2,1)S(1)}, u32[]{:S(2)}, u32[]{:S(2)}) collective-permute-start(bf16[4,64,512]{2,1,0:T(8,128)(2,1)S(1)} %get-tuple-element.20), channel_id=1, source_target_pairs={{0,1},{1,0},{2,3},{3,2},{4,5},{5,4},{6,7},{7,6},{8,9},{9,8},{10,11... | collective-permute-start | bytes 786440 | tf_op jit(solution)/shard_map/ppermute | solution.py:45
  44.8 6.4 %collective-permute-start.5 = (bf16[4,64,512]{2,1,0:T(8,128)(2,1)S(1)}, bf16[4,64,512]{2,1,0:T(8,128)(2,1)S(1)}, u32[]{:S(2)}, u32[]{:S(2)}) collective-permute-start(bf16[4,64,512]{2,1,0:T(8,128)(2,1)S(1)} %get-tuple-element.22), channel_id=1, source_target_pairs={{0,16},{1,17},{2,18},{3,19},{4,20},{5,21},{6,22},{7,23},{8,24},{9,... | collective-permute-start | bytes 786440 | tf_op jit(solution)/shard_map/ppermute | solution.py:45
  51.3 33.6 %copy-start.8 = (f32[64,1024]{1,0:T(8,128)S(1)}, f32[64,1024]{1,0:T(8,128)}, u32[]{:S(2)}) copy-start(f32[64,1024]{1,0:T(8,128)} %param.8) | copy-start | bytes 786436
  51.3 33.6 %copy-start.9 = (f32[64,1024]{1,0:T(8,128)S(1)}, f32[64,1024]{1,0:T(8,128)}, u32[]{:S(2)}) copy-start(f32[64,1024]{1,0:T(8,128)} %param.10) | copy-start | bytes 786436
  51.3 33.6 %copy-start.10 = (f32[64,1024]{1,0:T(8,128)S(1)}, f32[64,1024]{1,0:T(8,128)}, u32[]{:S(2)}) copy-start(f32[64,1024]{1,0:T(8,128)} %param.9) | copy-start | bytes 786436
  51.4 7.1 %collective-permute-start.6 = (bf16[64,1024]{1,0:T(8,128)(2,1)S(1)}, bf16[64,1024]{1,0:T(8,128)(2,1)S(1)}, u32[]{:S(2)}, u32[]{:S(2)}) collective-permute-start(bf16[64,1024]{1,0:T(8,128)(2,1)S(1)} %get-tuple-element.16), channel_id=1, source_target_pairs={{0,2},{1,3},{2,4},{3,5},{4,6},{5,7},{6,0},{7,1},{8,10},{9,11},{10,... | collective-permute-start | bytes 393224 | tf_op jit(solution)/shard_map/ppermute | solution.py:45
  53.1 9.6 %collective-permute-start.7 = (bf16[64,1024]{1,0:T(8,128)(2,1)S(1)}, bf16[64,1024]{1,0:T(8,128)(2,1)S(1)}, u32[]{:S(2)}, u32[]{:S(2)}) collective-permute-start(bf16[64,1024]{1,0:T(8,128)(2,1)S(1)} %get-tuple-element.18), channel_id=1, source_target_pairs={{0,4},{1,5},{2,6},{3,7},{4,0},{5,1},{6,2},{7,3},{8,12},{9,13},{10,... | collective-permute-start | bytes 393224 | tf_op jit(solution)/shard_map/ppermute | solution.py:45
  55.7 7.0 %collective-permute-start.8 = (bf16[64,1024]{1,0:T(8,128)(2,1)S(1)}, bf16[64,1024]{1,0:T(8,128)(2,1)S(1)}, u32[]{:S(2)}, u32[]{:S(2)}) collective-permute-start(bf16[64,1024]{1,0:T(8,128)(2,1)S(1)} %get-tuple-element.17), channel_id=1, source_target_pairs={{0,6},{1,7},{2,0},{3,1},{4,2},{5,3},{6,4},{7,5},{8,14},{9,15},{10,... | collective-permute-start | bytes 393224 | tf_op jit(solution)/shard_map/ppermute | solution.py:45
  64.8 1.1 collective-permute-start.9
  66.0 3.6 %collective-permute-start.10 = (f32[2,128]{1,0:T(2,128)S(1)}, f32[2,128]{1,0:T(2,128)S(1)}, u32[]{:S(2)}, u32[]{:S(2)}) collective-permute-start(f32[2,128]{1,0:T(2,128)S(1)} %broadcast_add_fusion), channel_id=1, source_target_pairs={{0,16},{1,17},{2,18},{3,19},{4,20},{5,21},{6,22},{7,23},{8,24},{9,... | collective-permute-start | bytes 3080 | tf_op jit(solution)/shard_map/ppermute | solution.py:45
  69.7 3.6 %collective-permute-start.11 = (f32[2,128]{1,0:T(2,128)S(1)}, f32[2,128]{1,0:T(2,128)S(1)}, u32[]{:S(2)}, u32[]{:S(2)}) collective-permute-start(f32[2,128]{1,0:T(2,128)S(1)} %fusion.35), channel_id=1, source_target_pairs={{0,1},{1,0},{2,3},{3,2},{4,5},{5,4},{6,7},{7,6},{8,9},{9,8},{10,11... | collective-permute-start | bytes 3080 | tf_op jit(solution)/shard_map/ppermute | solution.py:45
  73.2 5.4 %collective-permute-start.12 = (f32[2,128]{1,0:T(2,128)S(1)}, f32[2,128]{1,0:T(2,128)S(1)}, u32[]{:S(2)}, u32[]{:S(2)}) collective-permute-start(f32[2,128]{1,0:T(2,128)S(1)} %add.241), channel_id=1, source_target_pairs={{0,2},{1,3},{2,4},{3,5},{4,6},{5,7},{6,0},{7,1},{8,10},{9,11},{10,... | collective-permute-start | bytes 3080 | tf_op jit(solution)/shard_map/ppermute | solution.py:45
  78.6 4.5 %collective-permute-start.13 = (f32[2,128]{1,0:T(2,128)S(1)}, f32[2,128]{1,0:T(2,128)S(1)}, u32[]{:S(2)}, u32[]{:S(2)}) collective-permute-start(f32[2,128]{1,0:T(2,128)S(1)} %add.242), channel_id=1, source_target_pairs={{0,4},{1,5},{2,6},{3,7},{4,0},{5,1},{6,2},{7,3},{8,12},{9,13},{10,... | collective-permute-start | bytes 3080 | tf_op jit(solution)/shard_map/ppermute | solution.py:45
  85.9 7.0 %collective-permute-start.14 = (bf16[64,1024]{1,0:T(8,128)(2,1)S(1)}, bf16[64,1024]{1,0:T(8,128)(2,1)S(1)}, u32[]{:S(2)}, u32[]{:S(2)}) collective-permute-start(bf16[64,1024]{1,0:T(8,128)(2,1)S(1)} %get-tuple-element.9), channel_id=1, source_target_pairs={{0,2},{1,3},{2,4},{3,5},{4,6},{5,7},{6,0},{7,1},{8,10},{9,11},{10,... | collective-permute-start | bytes 393224 | tf_op jit(solution)/shard_map/ppermute | solution.py:45
  86.1 8.8 %collective-permute-start.15 = (bf16[64,1024]{1,0:T(8,128)(2,1)S(1)}, bf16[64,1024]{1,0:T(8,128)(2,1)S(1)}, u32[]{:S(2)}, u32[]{:S(2)}) collective-permute-start(bf16[64,1024]{1,0:T(8,128)(2,1)S(1)} %get-tuple-element.9), channel_id=1, source_target_pairs={{0,4},{1,5},{2,6},{3,7},{4,0},{5,1},{6,2},{7,3},{8,12},{9,13},{10,... | collective-permute-start | bytes 393224 | tf_op jit(solution)/shard_map/ppermute | solution.py:45
  87.7 7.2 %collective-permute-start.16 = (bf16[64,1024]{1,0:T(8,128)(2,1)S(1)}, bf16[64,1024]{1,0:T(8,128)(2,1)S(1)}, u32[]{:S(2)}, u32[]{:S(2)}) collective-permute-start(bf16[64,1024]{1,0:T(8,128)(2,1)S(1)} %get-tuple-element.9), channel_id=1, source_target_pairs={{0,6},{1,7},{2,0},{3,1},{4,2},{5,3},{6,4},{7,5},{8,14},{9,15},{10,... | collective-permute-start | bytes 393224 | tf_op jit(solution)/shard_map/ppermute | solution.py:45
  92.9 22.4 %copy-start = (bf16[1024,2048]{1,0:T(8,128)(2,1)S(1)}, bf16[1024,2048]{1,0:T(8,128)(2,1)}, u32[]{:S(2)}) copy-start(bf16[1024,2048]{1,0:T(8,128)(2,1)} %refs_1_.3) | copy-start | bytes 12582916
  95.0 9.0 %collective-permute-start.21 = (bf16[4,64,512]{2,1,0:T(8,128)(2,1)S(1)}, bf16[4,64,512]{2,1,0:T(8,128)(2,1)S(1)}, u32[]{:S(2)}, u32[]{:S(2)}) collective-permute-start(bf16[4,64,512]{2,1,0:T(8,128)(2,1)S(1)} %get-tuple-element.24), channel_id=1, source_target_pairs={{0,16},{1,17},{2,18},{3,19},{4,20},{5,21},{6,22},{7,23},{8,24},{9,... | collective-permute-start | bytes 786440 | tf_op jit(solution)/shard_map/ppermute | solution.py:45
  95.8 10.0 %collective-permute-start.17 = (bf16[4,64,512]{2,1,0:T(8,128)(2,1)S(1)}, bf16[4,64,512]{2,1,0:T(8,128)(2,1)S(1)}, u32[]{:S(2)}, u32[]{:S(2)}) collective-permute-start(bf16[4,64,512]{2,1,0:T(8,128)(2,1)S(1)} %get-tuple-element.26), channel_id=1, source_target_pairs={{0,1},{1,0},{2,3},{3,2},{4,5},{5,4},{6,7},{7,6},{8,9},{9,8},{10,11... | collective-permute-start | bytes 786440 | tf_op jit(solution)/shard_map/ppermute | solution.py:45
  104.0 9.2 %collective-permute-start.23 = (bf16[2,4,64,512]{3,2,1,0:T(8,128)(2,1)S(1)}, bf16[2,4,64,512]{3,2,1,0:T(8,128)(2,1)S(1)}, u32[]{:S(2)}, u32[]{:S(2)}) collective-permute-start(bf16[2,4,64,512]{3,2,1,0:T(8,128)(2,1)S(1)} %pad_maximum_fusion.1.refs_4_), channel_id=1, source_target_pairs={{0,1},{1,0},{2,3},{3,2},{4,5},{5,4},{6,7},{7,6},{8,9},{9,8},{10,11... | collective-permute-start | bytes 1572872 | tf_op jit(solution)/shard_map/ppermute | solution.py:45
  105.9 9.2 %collective-permute-start.19 = (bf16[2,4,64,512]{3,2,1,0:T(8,128)(2,1)S(1)}, bf16[2,4,64,512]{3,2,1,0:T(8,128)(2,1)S(1)}, u32[]{:S(2)}, u32[]{:S(2)}) collective-permute-start(bf16[2,4,64,512]{3,2,1,0:T(8,128)(2,1)S(1)} %pad_maximum_fusion.refs_2_), channel_id=1, source_target_pairs={{0,16},{1,17},{2,18},{3,19},{4,20},{5,21},{6,22},{7,23},{8,24},{9,... | collective-permute-start | bytes 1572872 | tf_op jit(solution)/shard_map/ppermute | solution.py:45
  106.6 12.6 %collective-permute-start.22 = (bf16[2,4,64,512]{3,2,1,0:T(8,128)(2,1)S(1)}, bf16[2,4,64,512]{3,2,1,0:T(8,128)(2,1)S(1)}, u32[]{:S(2)}, u32[]{:S(2)}) collective-permute-start(bf16[2,4,64,512]{3,2,1,0:T(8,128)(2,1)S(1)} %pad_maximum_fusion.1.refs_4_), channel_id=1, source_target_pairs={{0,8},{1,9},{2,10},{3,11},{4,12},{5,13},{6,14},{7,15},{8,0},{9,1},... | collective-permute-start | bytes 1572872 | tf_op jit(solution)/shard_map/ppermute | solution.py:45
  106.6 12.6 %collective-permute-start.18 = (bf16[2,4,64,512]{3,2,1,0:T(8,128)(2,1)S(1)}, bf16[2,4,64,512]{3,2,1,0:T(8,128)(2,1)S(1)}, u32[]{:S(2)}, u32[]{:S(2)}) collective-permute-start(bf16[2,4,64,512]{3,2,1,0:T(8,128)(2,1)S(1)} %pad_maximum_fusion.refs_2_), channel_id=1, source_target_pairs={{0,8},{1,9},{2,10},{3,11},{4,12},{5,13},{6,14},{7,15},{8,0},{9,1},... | collective-permute-start | bytes 1572872 | tf_op jit(solution)/shard_map/ppermute | solution.py:45
  113.3 5.9 %collective-permute-start.24 = (bf16[2,4,64,512]{3,2,1,0:T(8,128)(2,1)S(1)}, bf16[2,4,64,512]{3,2,1,0:T(8,128)(2,1)S(1)}, u32[]{:S(2)}, u32[]{:S(2)}) collective-permute-start(bf16[2,4,64,512]{3,2,1,0:T(8,128)(2,1)S(1)} %collective-permute-done.23.refs_5_), channel_id=1, source_target_pairs={{0,8},{1,9},{2,10},{3,11},{4,12},{5,13},{6,14},{7,15},{8,0},{9,1},... | collective-permute-start | bytes 1572872 | tf_op jit(solution)/shard_map/ppermute | solution.py:45
  115.1 4.0 %collective-permute-start.20 = (bf16[2,4,64,512]{3,2,1,0:T(8,128)(2,1)S(1)}, bf16[2,4,64,512]{3,2,1,0:T(8,128)(2,1)S(1)}, u32[]{:S(2)}, u32[]{:S(2)}) collective-permute-start(bf16[2,4,64,512]{3,2,1,0:T(8,128)(2,1)S(1)} %collective-permute-done.19.refs_3_), channel_id=1, source_target_pairs={{0,8},{1,9},{2,10},{3,11},{4,12},{5,13},{6,14},{7,15},{8,0},{9,1},... | collective-permute-start | bytes 1572872 | tf_op jit(solution)/shard_map/ppermute | solution.py:45

commit v2 on v0

v2 whole, which is shorter than its diff:
```python
import functools
import math

import jax
import jax.numpy as jnp
from jax import lax
from jax.experimental import pallas as pl
from jax.experimental.pallas import tpu as pltpu
from jax.sharding import PartitionSpec as P

D = 2048
FF = 512
AXES = ("aa", "ba")
BF16 = jnp.bfloat16
F32 = jnp.float32
LARGE = 60 * 1024 * 1024
SMALL = 24 * 1024 * 1024


class Grid:
    def __init__(self):
        outer, inner = lax.axis_size("aa"), lax.axis_size("ba")
        y = 1
        while y * y * 4 <= inner:
            y *= 2
        self.size = {"x": outer // 2, "c": 2, "z": inner // y, "y": y}

    def here(self, axis, step=0):
        a, b = lax.axis_index("aa"), lax.axis_index("ba")
        inner = self.size["c"] if axis in "xc" else self.size["y"]
        index = a if axis in "xc" else b
        at = lax.div(index, inner) if axis in "xz" else lax.rem(index, inner)
        return lax.rem(at + step % self.size[axis], self.size[axis]) if step else at

    def send(self, value, **steps):
        pairs = []
        for x in range(self.size["x"]):
            for c in range(self.size["c"]):
                for z in range(self.size["z"]):
                    for y in range(self.size["y"]):
                        here = {"x": x, "c": c, "z": z, "y": y}
                        there = {k: (v + steps.get(k, 0)) % self.size[k] for k, v in here.items()}
                        pairs.append((self.index(here), self.index(there)))
        return lax.ppermute(value, AXES, pairs)

    def index(self, at):
        return ((at["x"] * self.size["c"] + at["c"]) * self.size["z"] + at["z"]) * self.size["y"] + at["y"]


def pick(value, axis, index):
    return lax.dynamic_index_in_dim(value, index, axis, keepdims=False)


def kernel_params(flops, moved, limit=LARGE):
    return dict(
        compiler_params=pltpu.CompilerParams(vmem_limit_bytes=limit),
        cost_estimate=pl.CostEstimate(flops=flops, bytes_accessed=moved, transcendentals=0),
    )


def grad_kernel(tokens_ref, cot_ref, *out_refs):
    value = lax.dot_general(
        tokens_ref[...], cot_ref[...], (((0,), (0,)), ((), ())), preferred_element_type=F32
    )
    width = out_refs[0].shape[1]
    for k, ref in enumerate(out_refs):
        ref[...] = value[:, k * width : (k + 1) * width].astype(ref.dtype)


def grad_rows(grid, tokens, cot, step, dtype):
    count, depth = tokens.shape
    width = cot.shape[1] // 2
    n = grid.size["x"]
    rows = depth // (n * 2)
    shape = jax.ShapeDtypeStruct((n * rows, width), dtype)
    spec = pl.BlockSpec((rows, width), lambda x: (x, 0))
    return pl.pallas_call(
        grad_kernel,
        out_shape=[shape, shape],
        grid=(n,),
        in_specs=[
            pl.BlockSpec((count, rows), lambda x: (0, x * 2 + grid.here("c", step))),
            pl.BlockSpec((count, 2 * width), lambda x: (0, 0)),
        ],
        out_specs=[spec, spec],
        **kernel_params(
            4 * count * n * rows * width, count * n * rows * 2 + count * width * 4 + n * rows * width * 4
        ),
    )(tokens, cot)


DIM = {"x": 0, "y": 2}


def scatter_xy(grid, kept, came, order):
    one_axis, two_axis = order
    n_one, n_two = grid.size[one_axis], grid.size[two_axis]

    def pair_sum(step):
        at = grid.here(one_axis, step)
        return pick(kept, DIM[one_axis], at) + pick(came, DIM[one_axis], at).astype(F32)

    arriving = [grid.send(pair_sum(one).astype(BF16), **{one_axis: one}) for one in range(1, n_one)]
    yield
    own = pair_sum(0)
    for value in arriving:
        own = own + value.astype(F32)
    dim = 1 if two_axis == "y" else 0
    arriving = [
        grid.send(pick(own, dim, grid.here(two_axis, two)).astype(BF16), **{two_axis: two}) for two in range(1, n_two)
    ]
    yield
    total = pick(own, dim, grid.here(two_axis))
    for value in arriving:
        total = total + value.astype(F32)
    yield total


def scatter_z(grid, totals):
    whole = jnp.concatenate(totals, axis=2)
    arriving = [
        grid.send(pick(whole, 0, grid.here("z", k)).astype(BF16), z=k) for k in range(1, grid.size["z"])
    ]
    yield
    total = pick(whole, 0, grid.here("z"))
    for value in arriving:
        total = total + value.astype(F32)
    yield total


def sum_everywhere(grid, value):
    value = value + grid.send(value, c=1)
    plane = [(kx, ky) for kx in range(grid.size["x"]) for ky in range(grid.size["y"]) if kx + ky]
    value = sum([grid.send(value, x=kx, y=ky) for kx, ky in plane], value)
    return sum([grid.send(value, z=k) for k in range(1, grid.size["z"])], value)


def moments(clipped, first, second):
    return 0.9 * first + 0.1 * clipped, 0.95 * second + 0.05 * clipped * clipped


def clip_factor(square):
    return jnp.minimum(1.0, math.sqrt(D * FF) / jnp.sqrt(square + 1e-06))


def adam(clipped, weight, first, second):
    new_first, new_second = moments(clipped, first, second)
    corr_first = 1.0 - 0.9**10
    corr_second = 1.0 - 0.95**10
    updated = weight * (1.0 - 0.003 * 0.1) - 0.003 * (new_first / corr_first) / (
        jnp.sqrt(new_second / corr_second) + 1e-08
    )
    return updated.astype(BF16)


def gather_z(grid, low, parts):
    pieces = [low] + [grid.send(low, z=k) for k in range(1, grid.size["z"])]
    width = low.shape[1] // parts
    return [jnp.stack([p[:, s * width : (s + 1) * width] for p in pieces]) for s in range(parts)]


def gather_xy(grid, value, order):
    one_axis, two_axis = order
    pieces = [value] + [grid.send(value, **{two_axis: two}) for two in range(1, grid.size[two_axis])]
    value = jnp.stack(pieces)
    return [value] + [grid.send(value, **{one_axis: one}) for one in range(1, grid.size[one_axis])]


def project_kernel(grid, orders, rows, finish, tokens, *refs):
    refs = list(refs)
    size = grid.size
    pieces = [[[refs.pop(0) for _ in range(size[order[0]])] for order in orders] for _ in range(2)]
    gate = refs.pop(0) if finish else None
    out, held = refs
    width = out.shape[1] // len(orders)

    @pl.when(pl.program_id(0) == 0)
    def _():
        for kc in range(2):
            for kx in range(size["x"]):
                for ky in range(size["y"]):
                    for kz in range(size["z"]):
                        at = grid.here("x", -kx) * 2 + grid.here("c", kc)
                        at = (at * size["z"] + grid.here("z", -kz)) * size["y"] + grid.here("y", -ky)
                        start = pl.multiple_of(at * rows, rows)
                        for s, order in enumerate(orders):
                            one, two = (kx, ky) if order == "xy" else (ky, kx)
                            held[pl.ds(start, rows), s * width : (s + 1) * width] = pieces[kc][s][one][
                                two, kz
                            ].astype(held.dtype)

    value = jnp.dot(tokens[...], held[...].astype(BF16), preferred_element_type=F32)
    if finish:
        before = gate[...]
        value = before / (1.0 + jnp.exp(-before)) * value
    out[...] = value.astype(out.dtype)


def project(grid, tokens, pieces, orders, gate=None):
    count, depth = tokens.shape
    rows, width = pieces[0][0][0].shape[-2:]
    width *= len(orders)
    tile = min(count, 256)
    held = BF16 if rows % 16 == 0 else F32
    flat = [piece for core in pieces for part in core for piece in part]
    tiled = pl.BlockSpec((tile, width), lambda t: (t, 0))
    finish = gate is not None
    return pl.pallas_call(
        functools.partial(project_kernel, grid, orders, rows, finish),
        out_shape=jax.ShapeDtypeStruct((count, width), BF16 if finish else F32),
        grid=(count // tile,),
        in_specs=[pl.BlockSpec((tile, depth), lambda t: (t, 0))]
        + [pl.BlockSpec(memory_space=pltpu.VMEM)] * len(flat)
        + ([tiled] if finish else []),
        out_specs=tiled,
        scratch_shapes=[pltpu.VMEM((depth, width), held)],
        **kernel_params(2 * count * depth * width, count * depth * 2 + count * width * 8, SMALL),
    )(tokens, *flat, *([gate] if finish else []))


def shards(tokens, grad_out, master_weight, first_moment, second_moment, next_tokens):
    grid = Grid()
    half = grad_out.shape[1] // 2
    rows = master_weight.shape[0]
    lead = (grid.size["x"], grid.size["z"], grid.size["y"], rows, half)
    orders = ("xy", "yx")
    width = half // len(orders)

    sent = grad_rows(grid, tokens, grad_out, 1, BF16)
    came = [grid.send(value, c=1).reshape(lead) for value in sent]
    kept = [value.reshape(lead) for value in grad_rows(grid, tokens, grad_out, 0, F32)]

    def section(s):
        columns = slice(s * half, (s + 1) * half)
        ways = []
        for k, order in enumerate(orders):
            cut = slice(k * width, (k + 1) * width)
            ways.append(scatter_xy(grid, kept[s][..., cut], came[s][..., cut], order))
        for way in ways:
            next(way)
        yield
        for way in ways:
            next(way)
        yield
        way = scatter_z(grid, [next(way) for way in ways])
        next(way)
        yield
        grad = next(way)
        column_sums = sum_everywhere(grid, jnp.sum(grad * grad, axis=0).reshape(-1, 128))
        yield
        clipped = grad * clip_factor(jnp.sum(column_sums))
        state = [value[:, columns] for value in (master_weight, first_moment, second_moment)]
        low = adam(clipped, *state)
        low, clipped = lax.optimization_barrier((low, clipped))
        new = moments(clipped, *state[1:])
        values = gather_z(grid, low, len(orders))
        yield
        own = [gather_xy(grid, value, order) for value, order in zip(values, orders)]
        yield
        other = [[grid.send(piece, c=1) for piece in part] for part in own]
        yield new, (own, other)

    results = [None, None]
    ways = [section(0), section(1)]
    for step in range(7):
        for s in (0, 1):
            results[s] = next(ways[s])
    gate = project(grid, next_tokens, results[0][1], orders)
    next_hidden = project(grid, next_tokens, results[1][1], orders, gate)
    new_first, new_second = (jnp.concatenate([results[0][0][k], results[1][0][k]], axis=1) for k in (0, 1))
    return new_first, new_second, next_hidden


def solution(mesh):
    spec = P(AXES, None)
    return jax.shard_map(shards, mesh=mesh, in_specs=(spec,) * 6, out_specs=(spec,) * 3, check_vma=False)
```

time: 290 us -> 112 us (0.39)
  waiting for transfers between devices: 143 us -> 22.1 us
  blocking collectives: 38.7 us -> 0 us
  starting transfers between devices: 32.6 us -> 58.2 us
  matrix products: 21.2 us -> 0 us
  Pallas kernels: 0 us -> 17.7 us
  other arithmetic: 21 us -> 3.43 us
  between operations: 15.6 us -> 2.49 us
  local copies, waits for them, and re-layouts: 17.4 us -> 7.53 us
    all_gather x2 -> x0, waiting for transfers between devices: 75 us -> none  [the longest x1 40.2 us: shards(): block_rows = lax.all_gather(low_weight, 'ba', axis=0, tiled=True)]
    all_to_all x8 -> x0, waiting for transfers between devices: 67.5 us -> none  [the longest x2 36.8 us: reduce_tensor(): lax.all_to_all(codes, 'aa', split_axis=0, concat_axis=0, tiled=True)]
    ppermute x0 -> x52, starting transfers between devices: none -> 58.2 us  [send(): return lax.ppermute(value, AXES, pairs)]
    psum x1 -> x0, blocking collectives: 38.7 us -> none  [shards(): lax.psum((jnp.sum(gate_grad * gate_grad), jnp.sum(up_grad * up_grad)), ('...]
    all_to_all x8 -> x0, starting transfers between devices: 32.5 us -> none  [the longest x2 9.8 us: reduce_tensor(): lax.all_to_all(scales, 'ba', split_axis=0, concat_axis=0, tiled=True)]
    ppermute x0 -> x52, waiting for transfers between devices: none -> 22.1 us  [send(): return lax.ppermute(value, AXES, pairs)]
    dot_general x3 -> x0, matrix products: 21.2 us -> none  [the longest x2 13.6 us: reduce_tensor(): lax.dot_general(tokens, cotangent, (((0,), (0,)), ((), ())), preferred_el...]
    pallas_call x0 -> x4, Pallas kernels: none -> 17.7 us  [the longest x2 10.9 us: grad_rows(): pl.pallas_call(grad_kernel, out_shape=[shape, shape], grid=(n,), in_specs...]
  transfers between devices with their start and end apart: 10 -> 52, of which waited for: 8 -> 13; matrix products, arithmetic and copies ran while one was open for 14% -> 8% of each run, Pallas kernels for 0% -> 8%
where the time goes in v2:
time: 112 us
  starting transfers between devices  58.2 us (52%)
  waiting for transfers between devices  22.1 us (20%)
  Pallas kernels  17.7 us (16%)
  local copies, waits for them, and re-layouts  7.53 us (7%)
  other arithmetic  3.43 us (3%)
  between operations  2.49 us (2%)
    ppermute x52, starting transfers between devices, send(): return lax.ppermute(value, AXES, pairs)  58.2 us
    ppermute x52, waiting for transfers between devices, send(): return lax.ppermute(value, AXES, pairs)  22.1 us
    pallas_call x2, Pallas kernels, grad_rows(): pl.pallas_call(grad_kernel, out_shape=[shape, shape], grid=(n,), in_specs...  10.9 us
    pallas_call x2, Pallas kernels, project(): pl.pallas_call(functools.partial(project_kernel, grid, orders, rows, fini...  6.86 us
    slice x4, local copies, waits for them, and re-layouts, section(): ways.append(scatter_xy(grid, kept[s][..., cut], came[s][..., cut], order))  5.6 us
  transfers between devices with their start and end apart: 52, of which 13 were waited for; matrix products, arithmetic and copies ran while one was open for 8% of the time, Pallas kernels for 8%

profile of v2, /device:TPU:0, one launch (start us, length us, event | category | flops | bytes accessed | tf_op | source)
XLA Modules:
  0.0 111.5 jit_solution(3769719142051595336)
XLA Ops:
  0.6 5.4 %shard_map.86 = (bf16[1024,512]{1,0:T(8,128)(2,1)}, bf16[1024,512]{1,0:T(8,128)(2,1)}) custom-call(bf16[1024,2048]{1,0:T(8,128)(2,1)} %tokens_ref.3, bf16[1024,1024]{1,0:T(8,128)(2,1)} %cot_ref.3), custom_call_target="tpu_custom_call" | custom-call | flops 2147483648 | bytes 6291456 | tf_op jit(solution)/shard_map/pallas_call | solution.py:77
  6.5 5.5 %shard_map.85 = (f32[1024,512]{1,0:T(8,128)}, f32[1024,512]{1,0:T(8,128)}) custom-call(bf16[1024,2048]{1,0:T(8,128)(2,1)} %tokens_ref.3, bf16[1024,1024]{1,0:T(8,128)(2,1)} %cot_ref.3), custom_call_target="tpu_custom_call" | custom-call | flops 2147483648 | bytes 6291456 | tf_op jit(solution)/shard_map/pallas_call | solution.py:77
  12.0 1.9 %fusion.71 = (f32[2,4,2,64,256]{4,3,2,1,0:T(8,128)S(1)}, f32[2,4,2,64,256]{4,3,2,1,0:T(8,128)S(1)}) fusion(f32[2,4,2,64,512]{4,3,2,1,0:T(8,128)} %bitcast.159), kind=kLoop, calls=%fused_computation.155 | loop fusion | bytes 4194304 | tf_op jit(solution)/shard_map/slice | solution.py:238
  14.2 1.2 %fusion.70 = (f32[2,4,2,64,256]{4,3,2,1,0:T(8,128)}, f32[2,4,2,64,256]{4,3,2,1,0:T(8,128)S(1)}) fusion(f32[2,4,2,64,512]{4,3,2,1,0:T(8,128)S(1)} %bitcast.158), kind=kLoop, calls=%fused_computation.154 | loop fusion | bytes 4194304 | tf_op jit(solution)/shard_map/slice | solution.py:238
  15.5 1.1 %copy-done.1 = f32[2,4,2,64,256]{4,3,2,1,0:T(8,128)S(1)} copy-done((f32[2,4,2,64,256]{4,3,2,1,0:T(8,128)S(1)}, f32[2,4,2,64,256]{4,3,2,1,0:T(8,128)}, u32[]{:S(2)}) %copy-start.1) | copy-done | bytes 1048600
  16.8 1.3 %fusion.73 = (bf16[2,4,2,64,256]{4,3,2,1,0:T(8,128)(2,1)S(1)}, bf16[2,4,2,64,256]{4,3,2,1,0:T(8,128)(2,1)S(1)}) fusion(bf16[2,4,2,64,512]{4,3,2,1,0:T(8,128)(2,1)} %bitcast.16), kind=kLoop, calls=%fused_computation.157 | loop fusion | bytes 2097152 | tf_op jit(solution)/shard_map/slice | solution.py:238
  18.2 3.0 %collective-permute-start.16 = (bf16[4,2,64,256]{3,2,0,1:T(8,128)(2,1)S(1)}, bf16[4,2,64,256]{3,2,0,1:T(8,128)(2,1)S(1)}, u32[]{:S(2)}, u32[]{:S(2)}) collective-permute-start(bf16[4,2,64,256]{3,2,0,1:T(8,128)(2,1)S(1)} %fusion.13), channel_id=1, source_target_pairs={{0,16},{1,17},{2,18},{3,19},{4,20},{5,21},{6,22},{7,23},{8,24},{9,... | collective-permute-start | bytes 786440 | tf_op jit(solution)/shard_map/ppermute | solution.py:44
  21.3 1.6 %collective-permute-start.18 = (bf16[2,4,64,256]{3,2,1,0:T(8,128)(2,1)S(1)}, bf16[2,4,64,256]{3,2,1,0:T(8,128)(2,1)S(1)}, u32[]{:S(2)}, u32[]{:S(2)}) collective-permute-start(bf16[2,4,64,256]{3,2,1,0:T(8,128)(2,1)S(1)} %fusion.15), channel_id=1, source_target_pairs={{0,1},{1,0},{2,3},{3,2},{4,5},{5,4},{6,7},{7,6},{8,9},{9,8},{10,11... | collective-permute-start | bytes 786440 | tf_op jit(solution)/shard_map/ppermute | solution.py:44
  22.8 1.3 %fusion.72 = (bf16[2,4,2,64,256]{4,3,2,1,0:T(8,128)(2,1)S(1)}, bf16[2,4,2,64,256]{4,3,2,1,0:T(8,128)(2,1)S(1)}) fusion(bf16[2,4,2,64,512]{4,3,2,1,0:T(8,128)(2,1)} %bitcast.1), kind=kLoop, calls=%fused_computation.156 | loop fusion | bytes 2097152 | tf_op jit(solution)/shard_map/slice | solution.py:238
  25.0 3.3 %collective-permute-done.16 = bf16[4,2,64,256]{3,2,0,1:T(8,128)(2,1)S(1)} collective-permute-done((bf16[4,2,64,256]{3,2,0,1:T(8,128)(2,1)S(1)}, bf16[4,2,64,256]{3,2,0,1:T(8,128)(2,1)S(1)}, u32[]{:S(2)}, u32[]{:S(2)}) %collective-permute-start.16) | collective-permute-done | bytes 262176 | tf_op jit(solution)/shard_map/ppermute | solution.py:44
  28.4 2.1 %collective-permute-start.17 = (bf16[4,64,256]{2,1,0:T(8,128)(2,1)S(1)}, bf16[4,64,256]{2,1,0:T(8,128)(2,1)S(1)}, u32[]{:S(2)}, u32[]{:S(2)}) collective-permute-start(bf16[4,64,256]{2,1,0:T(8,128)(2,1)S(1)} %fusion.32), channel_id=1, source_target_pairs={{0,1},{1,0},{2,3},{3,2},{4,5},{5,4},{6,7},{7,6},{8,9},{9,8},{10,11... | collective-permute-start | bytes 393224 | tf_op jit(solution)/shard_map/ppermute | solution.py:44
  30.7 1.6 %collective-permute-start.19 = (bf16[4,64,256]{2,1,0:T(8,128)(2,1)S(1)}, bf16[4,64,256]{2,1,0:T(8,128)(2,1)S(1)}, u32[]{:S(2)}, u32[]{:S(2)}) collective-permute-start(bf16[4,64,256]{2,1,0:T(8,128)(2,1)S(1)} %fusion.33), channel_id=1, source_target_pairs={{0,16},{1,17},{2,18},{3,19},{4,20},{5,21},{6,22},{7,23},{8,24},{9,... | collective-permute-start | bytes 393224 | tf_op jit(solution)/shard_map/ppermute | solution.py:44
  32.2 1.7 %collective-permute-done.1 = bf16[4,2,64,256]{3,2,0,1:T(8,128)(2,1)S(1)} collective-permute-done((bf16[4,2,64,256]{3,2,0,1:T(8,128)(2,1)S(1)}, bf16[4,2,64,256]{3,2,0,1:T(8,128)(2,1)S(1)}, u32[]{:S(2)}, u32[]{:S(2)}) %collective-permute-start.1) | collective-permute-done | bytes 262176 | tf_op jit(solution)/shard_map/ppermute | solution.py:44
  34.0 2.1 %collective-permute-start.2 = (bf16[4,64,256]{2,1,0:T(8,128)(2,1)S(1)}, bf16[4,64,256]{2,1,0:T(8,128)(2,1)S(1)}, u32[]{:S(2)}, u32[]{:S(2)}) collective-permute-start(bf16[4,64,256]{2,1,0:T(8,128)(2,1)S(1)} %fusion.30), channel_id=1, source_target_pairs={{0,1},{1,0},{2,3},{3,2},{4,5},{5,4},{6,7},{7,6},{8,9},{9,8},{10,11... | collective-permute-start | bytes 393224 | tf_op jit(solution)/shard_map/ppermute | solution.py:44
  36.3 1.6 %collective-permute-start.4 = (bf16[4,64,256]{2,1,0:T(8,128)(2,1)S(1)}, bf16[4,64,256]{2,1,0:T(8,128)(2,1)S(1)}, u32[]{:S(2)}, u32[]{:S(2)}) collective-permute-start(bf16[4,64,256]{2,1,0:T(8,128)(2,1)S(1)} %fusion.31), channel_id=1, source_target_pairs={{0,16},{1,17},{2,18},{3,19},{4,20},{5,21},{6,22},{7,23},{8,24},{9,... | collective-permute-start | bytes 393224 | tf_op jit(solution)/shard_map/ppermute | solution.py:44
  37.9 1.1 collective-permute-done.17
  39.1 1.6 %collective-permute-start.20 = (bf16[64,512]{1,0:T(8,128)(2,1)S(1)}, bf16[64,512]{1,0:T(8,128)(2,1)S(1)}, u32[]{:S(2)}, u32[]{:S(2)}) collective-permute-start(bf16[64,512]{1,0:T(8,128)(2,1)S(1)} %get-tuple-element.46), channel_id=1, source_target_pairs={{0,2},{1,3},{2,4},{3,5},{4,6},{5,7},{6,0},{7,1},{8,10},{9,11},{10,... | collective-permute-start | bytes 196616 | tf_op jit(solution)/shard_map/ppermute | solution.py:44
  40.7 2.6 %collective-permute-start.21 = (bf16[64,512]{1,0:T(8,128)(2,1)S(1)}, bf16[64,512]{1,0:T(8,128)(2,1)S(1)}, u32[]{:S(2)}, u32[]{:S(2)}) collective-permute-start(bf16[64,512]{1,0:T(8,128)(2,1)S(1)} %get-tuple-element.47), channel_id=1, source_target_pairs={{0,4},{1,5},{2,6},{3,7},{4,0},{5,1},{6,2},{7,3},{8,12},{9,13},{10,... | collective-permute-start | bytes 196616 | tf_op jit(solution)/shard_map/ppermute | solution.py:44
  43.3 1.3 %collective-permute-start.22 = (bf16[64,512]{1,0:T(8,128)(2,1)S(1)}, bf16[64,512]{1,0:T(8,128)(2,1)S(1)}, u32[]{:S(2)}, u32[]{:S(2)}) collective-permute-start(bf16[64,512]{1,0:T(8,128)(2,1)S(1)} %get-tuple-element.48), channel_id=1, source_target_pairs={{0,6},{1,7},{2,0},{3,1},{4,2},{5,3},{6,4},{7,5},{8,14},{9,15},{10,... | collective-permute-start | bytes 196616 | tf_op jit(solution)/shard_map/ppermute | solution.py:44
  45.9 2.8 %collective-permute-start.7 = (bf16[64,512]{1,0:T(8,128)(2,1)S(1)}, bf16[64,512]{1,0:T(8,128)(2,1)S(1)}, u32[]{:S(2)}, u32[]{:S(2)}) collective-permute-start(bf16[64,512]{1,0:T(8,128)(2,1)S(1)} %get-tuple-element.43), channel_id=1, source_target_pairs={{0,6},{1,7},{2,0},{3,1},{4,2},{5,3},{6,4},{7,5},{8,14},{9,15},{10,... | collective-permute-start | bytes 196616 | tf_op jit(solution)/shard_map/ppermute | solution.py:44
  48.8 2.2 %collective-permute-done.5 = bf16[64,512]{1,0:T(8,128)(2,1)S(1)} collective-permute-done((bf16[64,512]{1,0:T(8,128)(2,1)S(1)}, bf16[64,512]{1,0:T(8,128)(2,1)S(1)}, u32[]{:S(2)}, u32[]{:S(2)}) %collective-permute-start.5) | collective-permute-done | bytes 65568 | tf_op jit(solution)/shard_map/ppermute | solution.py:44
  51.0 1.2 %collective-permute-done.6 = bf16[64,512]{1,0:T(8,128)(2,1)S(1)} collective-permute-done((bf16[64,512]{1,0:T(8,128)(2,1)S(1)}, bf16[64,512]{1,0:T(8,128)(2,1)S(1)}, u32[]{:S(2)}, u32[]{:S(2)}) %collective-permute-start.6) | collective-permute-done | bytes 65568 | tf_op jit(solution)/shard_map/ppermute | solution.py:44
  52.4 1.6 %collective-permute-start.24 = (f32[4,128]{1,0:T(4,128)S(1)}, f32[4,128]{1,0:T(4,128)S(1)}, u32[]{:S(2)}, u32[]{:S(2)}) collective-permute-start(f32[4,128]{1,0:T(4,128)S(1)} %bitcast_add_fusion.8), channel_id=1, source_target_pairs={{0,1},{1,0},{2,3},{3,2},{4,5},{5,4},{6,7},{7,6},{8,9},{9,8},{10,11... | collective-permute-start | bytes 6152 | tf_op jit(solution)/shard_map/ppermute | solution.py:44
  54.4 1.5 %collective-permute-start.26 = (f32[4,128]{1,0:T(4,128)S(1)}, f32[4,128]{1,0:T(4,128)S(1)}, u32[]{:S(2)}, u32[]{:S(2)}) collective-permute-start(f32[4,128]{1,0:T(4,128)S(1)} %bitcast_add_fusion.8), channel_id=1, source_target_pairs={{0,17},{1,16},{2,19},{3,18},{4,21},{5,20},{6,23},{7,22},{8,25},{9,... | collective-permute-start | bytes 6152 | tf_op jit(solution)/shard_map/ppermute | solution.py:44
  56.4 2.5 %collective-permute-start.11 = (f32[4,128]{1,0:T(4,128)S(1)}, f32[4,128]{1,0:T(4,128)S(1)}, u32[]{:S(2)}, u32[]{:S(2)}) collective-permute-start(f32[4,128]{1,0:T(4,128)S(1)} %bitcast_add_fusion.9), channel_id=1, source_target_pairs={{0,17},{1,16},{2,19},{3,18},{4,21},{5,20},{6,23},{7,22},{8,25},{9,... | collective-permute-start | bytes 6152 | tf_op jit(solution)/shard_map/ppermute | solution.py:44
  59.5 1.3 %collective-permute-start.27 = (f32[4,128]{1,0:T(4,128)S(1)}, f32[4,128]{1,0:T(4,128)S(1)}, u32[]{:S(2)}, u32[]{:S(2)}) collective-permute-start(f32[4,128]{1,0:T(4,128)S(1)} %add_add_fusion), channel_id=1, source_target_pairs={{0,2},{1,3},{2,4},{3,5},{4,6},{5,7},{6,0},{7,1},{8,10},{9,11},{10,... | collective-permute-start | bytes 6152 | tf_op jit(solution)/shard_map/ppermute | solution.py:44
  60.8 1.9 %collective-permute-start.28 = (f32[4,128]{1,0:T(4,128)S(1)}, f32[4,128]{1,0:T(4,128)S(1)}, u32[]{:S(2)}, u32[]{:S(2)}) collective-permute-start(f32[4,128]{1,0:T(4,128)S(1)} %add_add_fusion), channel_id=1, source_target_pairs={{0,4},{1,5},{2,6},{3,7},{4,0},{5,1},{6,2},{7,3},{8,12},{9,13},{10,... | collective-permute-start | bytes 6152 | tf_op jit(solution)/shard_map/ppermute | solution.py:44
  63.4 1.4 %collective-permute-start.12 = (f32[4,128]{1,0:T(4,128)S(1)}, f32[4,128]{1,0:T(4,128)S(1)}, u32[]{:S(2)}, u32[]{:S(2)}) collective-permute-start(f32[4,128]{1,0:T(4,128)S(1)} %add_add_fusion.1), channel_id=1, source_target_pairs={{0,2},{1,3},{2,4},{3,5},{4,6},{5,7},{6,0},{7,1},{8,10},{9,11},{10,... | collective-permute-start | bytes 6152 | tf_op jit(solution)/shard_map/ppermute | solution.py:44
  64.8 1.0 collective-permute-start.13
  65.8 2.6 %collective-permute-start.14 = (f32[4,128]{1,0:T(4,128)S(1)}, f32[4,128]{1,0:T(4,128)S(1)}, u32[]{:S(2)}, u32[]{:S(2)}) collective-permute-start(f32[4,128]{1,0:T(4,128)S(1)} %add_add_fusion.1), channel_id=1, source_target_pairs={{0,6},{1,7},{2,0},{3,1},{4,2},{5,3},{6,4},{7,5},{8,14},{9,15},{10,... | collective-permute-start | bytes 6152 | tf_op jit(solution)/shard_map/ppermute | solution.py:44
  71.3 1.7 %collective-permute-start.41 = (bf16[64,512]{1,0:T(8,128)(2,1)S(1)}, bf16[64,512]{1,0:T(8,128)(2,1)S(1)}, u32[]{:S(2)}, u32[]{:S(2)}) collective-permute-start(bf16[64,512]{1,0:T(8,128)(2,1)S(1)} %get-tuple-element.18), channel_id=1, source_target_pairs={{0,2},{1,3},{2,4},{3,5},{4,6},{5,7},{6,0},{7,1},{8,10},{9,11},{10,... | collective-permute-start | bytes 196616 | tf_op jit(solution)/shard_map/ppermute | solution.py:44
  73.0 2.9 %collective-permute-start.42 = (bf16[64,512]{1,0:T(8,128)(2,1)S(1)}, bf16[64,512]{1,0:T(8,128)(2,1)S(1)}, u32[]{:S(2)}, u32[]{:S(2)}) collective-permute-start(bf16[64,512]{1,0:T(8,128)(2,1)S(1)} %get-tuple-element.18), channel_id=1, source_target_pairs={{0,4},{1,5},{2,6},{3,7},{4,0},{5,1},{6,2},{7,3},{8,12},{9,13},{10,... | collective-permute-start | bytes 196616 | tf_op jit(solution)/shard_map/ppermute | solution.py:44
  76.0 2.0 %collective-permute-start.30 = (bf16[64,512]{1,0:T(8,128)(2,1)S(1)}, bf16[64,512]{1,0:T(8,128)(2,1)S(1)}, u32[]{:S(2)}, u32[]{:S(2)}) collective-permute-start(bf16[64,512]{1,0:T(8,128)(2,1)S(1)} %get-tuple-element.17), channel_id=1, source_target_pairs={{0,2},{1,3},{2,4},{3,5},{4,6},{5,7},{6,0},{7,1},{8,10},{9,11},{10,... | collective-permute-start | bytes 196616 | tf_op jit(solution)/shard_map/ppermute | solution.py:44
  78.3 2.2 %collective-permute-start.32 = (bf16[64,512]{1,0:T(8,128)(2,1)S(1)}, bf16[64,512]{1,0:T(8,128)(2,1)S(1)}, u32[]{:S(2)}, u32[]{:S(2)}) collective-permute-start(bf16[64,512]{1,0:T(8,128)(2,1)S(1)} %get-tuple-element.17), channel_id=1, source_target_pairs={{0,6},{1,7},{2,0},{3,1},{4,2},{5,3},{6,4},{7,5},{8,14},{9,15},{10,... | collective-permute-start | bytes 196616 | tf_op jit(solution)/shard_map/ppermute | solution.py:44
  80.9 1.0 collective-permute-start.46
  82.0 1.1 collective-permute-start.44
  83.8 1.0 collective-permute-start.35
  84.9 1.1 %collective-permute-done.46 = bf16[4,64,256]{2,1,0:T(8,128)(2,1)S(1)} collective-permute-done((bf16[4,64,256]{2,1,0:T(8,128)(2,1)S(1)}, bf16[4,64,256]{2,1,0:T(8,128)(2,1)S(1)}, u32[]{:S(2)}, u32[]{:S(2)}) %collective-permute-start.46) | collective-permute-done | bytes 131104 | tf_op jit(solution)/shard_map/ppermute | solution.py:44
  86.0 1.6 %collective-permute-start.47 = (bf16[2,4,64,256]{3,2,1,0:T(8,128)(2,1)S(1)}, bf16[2,4,64,256]{3,2,1,0:T(8,128)(2,1)S(1)}, u32[]{:S(2)}, u32[]{:S(2)}) collective-permute-start(bf16[2,4,64,256]{3,2,1,0:T(8,128)(2,1)S(1)} %pad_maximum_fusion.5.refs_2_), channel_id=1, source_target_pairs={{0,1},{1,0},{2,3},{3,2},{4,5},{5,4},{6,7},{7,6},{8,9},{9,8},{10,11... | collective-permute-start | bytes 786440 | tf_op jit(solution)/shard_map/ppermute | solution.py:44
  88.0 1.1 %collective-permute-start.45 = (bf16[2,4,64,256]{3,2,1,0:T(8,128)(2,1)S(1)}, bf16[2,4,64,256]{3,2,1,0:T(8,128)(2,1)S(1)}, u32[]{:S(2)}, u32[]{:S(2)}) collective-permute-start(bf16[2,4,64,256]{3,2,1,0:T(8,128)(2,1)S(1)} %pad_maximum_fusion.4.refs_0_), channel_id=1, source_target_pairs={{0,16},{1,17},{2,18},{3,19},{4,20},{5,21},{6,22},{7,23},{8,24},{9,... | collective-permute-start | bytes 786440 | tf_op jit(solution)/shard_map/ppermute | solution.py:44
  89.2 1.6 %collective-permute-start.33 = (bf16[4,64,256]{2,1,0:T(8,128)(2,1)S(1)}, bf16[4,64,256]{2,1,0:T(8,128)(2,1)S(1)}, u32[]{:S(2)}, u32[]{:S(2)}) collective-permute-start(bf16[4,64,256]{2,1,0:T(8,128)(2,1)S(1)} %get-tuple-element.64), channel_id=1, source_target_pairs={{0,1},{1,0},{2,3},{3,2},{4,5},{5,4},{6,7},{7,6},{8,9},{9,8},{10,11... | collective-permute-start | bytes 393224 | tf_op jit(solution)/shard_map/ppermute | solution.py:44
  90.8 4.4 %collective-permute-done.33 = bf16[4,64,256]{2,1,0:T(8,128)(2,1)S(1)} collective-permute-done((bf16[4,64,256]{2,1,0:T(8,128)(2,1)S(1)}, bf16[4,64,256]{2,1,0:T(8,128)(2,1)S(1)}, u32[]{:S(2)}, u32[]{:S(2)}) %collective-permute-start.33) | collective-permute-done | bytes 131104 | tf_op jit(solution)/shard_map/ppermute | solution.py:44
  95.3 1.5 %collective-permute-start.36 = (bf16[2,4,64,256]{3,2,1,0:T(8,128)(2,1)S(1)}, bf16[2,4,64,256]{3,2,1,0:T(8,128)(2,1)S(1)}, u32[]{:S(2)}, u32[]{:S(2)}) collective-permute-start(bf16[2,4,64,256]{3,2,1,0:T(8,128)(2,1)S(1)} %pad_maximum_fusion.3.refs_2_), channel_id=1, source_target_pairs={{0,1},{1,0},{2,3},{3,2},{4,5},{5,4},{6,7},{7,6},{8,9},{9,8},{10,11... | collective-permute-start | bytes 786440 | tf_op jit(solution)/shard_map/ppermute | solution.py:44
  98.1 4.2 %collective-permute-done.36.refs_3_ = bf16[2,4,64,256]{3,2,1,0:T(8,128)(2,1)S(1)} collective-permute-done((bf16[2,4,64,256]{3,2,1,0:T(8,128)(2,1)S(1)}, bf16[2,4,64,256]{3,2,1,0:T(8,128)(2,1)S(1)}, u32[]{:S(2)}, u32[]{:S(2)}) %collective-permute-start.36) | collective-permute-done | bytes 262176 | tf_op jit(solution)/shard_map/ppermute | solution.py:44
  102.2 1.0 collective-permute-done.34.refs_1_
  103.8 0.8 pad_maximum_fusion
  104.6 3.0 %shard_map.87.refs_8_ = f32[1024,512]{1,0:T(8,128)S(1)} custom-call(bf16[1024,2048]{1,0:T(8,128)(2,1)S(1)} %copy-done, bf16[2,4,64,256]{3,2,1,0:T(8,128)(2,1)S(1)} %pad_maximum_fusion.4.refs_0_, bf16[2,4,64,256]{3,2,1,0:T(8,128)(2,1)S(1)} %collective-permute-done.45.refs_1_, bf16[2,4,64,256]{3,2,1,0:T(8,128)(2,1)S(1)} %pad_maximum_fusion.5.refs_2_, ...), custom_call_target="tpu_custom_call" | custom-call | flops 2147483648 | bytes 8388608 | tf_op jit(solution)/shard_map/pallas_call | solution.py:208
  107.7 3.9 %shard_map.88 = bf16[1024,512]{1,0:T(8,128)(2,1)} custom-call(bf16[1024,2048]{1,0:T(8,128)(2,1)S(1)} %copy-done, bf16[2,4,64,256]{3,2,1,0:T(8,128)(2,1)S(1)} %pad_maximum_fusion.2.refs_0_, bf16[2,4,64,256]{3,2,1,0:T(8,128)(2,1)S(1)} %collective-permute-done.34.refs_1_, bf16[2,4,64,256]{3,2,1,0:T(8,128)(2,1)S(1)} %pad_maximum_fusion.3.refs_2_, ...), custom_call_target="tpu_custom_call" | custom-call | flops 2147483648 | bytes 8388608 | tf_op jit(solution)/shard_map/pallas_call | solution.py:208
  (125 shorter events, 11.5 us)
Async XLA Ops:
  6.0 10.8 %collective-permute-start.15 = (bf16[1024,512]{1,0:T(8,128)(2,1)}, bf16[1024,512]{1,0:T(8,128)(2,1)}, u32[]{:S(2)}, u32[]{:S(2)}) collective-permute-start(bf16[1024,512]{1,0:T(8,128)(2,1)} %get-tuple-element.15), channel_id=1, source_target_pairs={{0,8},{1,9},{2,10},{3,11},{4,12},{5,13},{6,14},{7,15},{8,0},{9,1},... | collective-permute-start | bytes 3145736 | tf_op jit(solution)/shard_map/ppermute | solution.py:44
  6.5 16.4 %collective-permute-start = (bf16[1024,512]{1,0:T(8,128)(2,1)}, bf16[1024,512]{1,0:T(8,128)(2,1)}, u32[]{:S(2)}, u32[]{:S(2)}) collective-permute-start(bf16[1024,512]{1,0:T(8,128)(2,1)} %get-tuple-element.12), channel_id=1, source_target_pairs={{0,8},{1,9},{2,10},{3,11},{4,12},{5,13},{6,14},{7,15},{8,0},{9,1},... | collective-permute-start | bytes 3145736 | tf_op jit(solution)/shard_map/ppermute | solution.py:44
  18.2 10.1 %collective-permute-start.16 = (bf16[4,2,64,256]{3,2,0,1:T(8,128)(2,1)S(1)}, bf16[4,2,64,256]{3,2,0,1:T(8,128)(2,1)S(1)}, u32[]{:S(2)}, u32[]{:S(2)}) collective-permute-start(bf16[4,2,64,256]{3,2,0,1:T(8,128)(2,1)S(1)} %fusion.13), channel_id=1, source_target_pairs={{0,16},{1,17},{2,18},{3,19},{4,20},{5,21},{6,22},{7,23},{8,24},{9,... | collective-permute-start | bytes 786440 | tf_op jit(solution)/shard_map/ppermute | solution.py:44
  21.3 9.3 %collective-permute-start.18 = (bf16[2,4,64,256]{3,2,1,0:T(8,128)(2,1)S(1)}, bf16[2,4,64,256]{3,2,1,0:T(8,128)(2,1)S(1)}, u32[]{:S(2)}, u32[]{:S(2)}) collective-permute-start(bf16[2,4,64,256]{3,2,1,0:T(8,128)(2,1)S(1)} %fusion.15), channel_id=1, source_target_pairs={{0,1},{1,0},{2,3},{3,2},{4,5},{5,4},{6,7},{7,6},{8,9},{9,8},{10,11... | collective-permute-start | bytes 786440 | tf_op jit(solution)/shard_map/ppermute | solution.py:44
  24.2 9.7 %collective-permute-start.1 = (bf16[4,2,64,256]{3,2,0,1:T(8,128)(2,1)S(1)}, bf16[4,2,64,256]{3,2,0,1:T(8,128)(2,1)S(1)}, u32[]{:S(2)}, u32[]{:S(2)}) collective-permute-start(bf16[4,2,64,256]{3,2,0,1:T(8,128)(2,1)S(1)} %fusion.12), channel_id=1, source_target_pairs={{0,16},{1,17},{2,18},{3,19},{4,20},{5,21},{6,22},{7,23},{8,24},{9,... | collective-permute-start | bytes 786440 | tf_op jit(solution)/shard_map/ppermute | solution.py:44
  24.9 11.3 %collective-permute-start.3 = (bf16[2,4,64,256]{3,2,1,0:T(8,128)(2,1)S(1)}, bf16[2,4,64,256]{3,2,1,0:T(8,128)(2,1)S(1)}, u32[]{:S(2)}, u32[]{:S(2)}) collective-permute-start(bf16[2,4,64,256]{3,2,1,0:T(8,128)(2,1)S(1)} %fusion.14), channel_id=1, source_target_pairs={{0,1},{1,0},{2,3},{3,2},{4,5},{5,4},{6,7},{7,6},{8,9},{9,8},{10,11... | collective-permute-start | bytes 786440 | tf_op jit(solution)/shard_map/ppermute | solution.py:44
  28.4 10.5 %collective-permute-start.17 = (bf16[4,64,256]{2,1,0:T(8,128)(2,1)S(1)}, bf16[4,64,256]{2,1,0:T(8,128)(2,1)S(1)}, u32[]{:S(2)}, u32[]{:S(2)}) collective-permute-start(bf16[4,64,256]{2,1,0:T(8,128)(2,1)S(1)} %fusion.32), channel_id=1, source_target_pairs={{0,1},{1,0},{2,3},{3,2},{4,5},{5,4},{6,7},{7,6},{8,9},{9,8},{10,11... | collective-permute-start | bytes 393224 | tf_op jit(solution)/shard_map/ppermute | solution.py:44
  30.7 8.3 %collective-permute-start.19 = (bf16[4,64,256]{2,1,0:T(8,128)(2,1)S(1)}, bf16[4,64,256]{2,1,0:T(8,128)(2,1)S(1)}, u32[]{:S(2)}, u32[]{:S(2)}) collective-permute-start(bf16[4,64,256]{2,1,0:T(8,128)(2,1)S(1)} %fusion.33), channel_id=1, source_target_pairs={{0,16},{1,17},{2,18},{3,19},{4,20},{5,21},{6,22},{7,23},{8,24},{9,... | collective-permute-start | bytes 393224 | tf_op jit(solution)/shard_map/ppermute | solution.py:44
  34.0 10.6 %collective-permute-start.2 = (bf16[4,64,256]{2,1,0:T(8,128)(2,1)S(1)}, bf16[4,64,256]{2,1,0:T(8,128)(2,1)S(1)}, u32[]{:S(2)}, u32[]{:S(2)}) collective-permute-start(bf16[4,64,256]{2,1,0:T(8,128)(2,1)S(1)} %fusion.30), channel_id=1, source_target_pairs={{0,1},{1,0},{2,3},{3,2},{4,5},{5,4},{6,7},{7,6},{8,9},{9,8},{10,11... | collective-permute-start | bytes 393224 | tf_op jit(solution)/shard_map/ppermute | solution.py:44
  36.3 8.4 %collective-permute-start.4 = (bf16[4,64,256]{2,1,0:T(8,128)(2,1)S(1)}, bf16[4,64,256]{2,1,0:T(8,128)(2,1)S(1)}, u32[]{:S(2)}, u32[]{:S(2)}) collective-permute-start(bf16[4,64,256]{2,1,0:T(8,128)(2,1)S(1)} %fusion.31), channel_id=1, source_target_pairs={{0,16},{1,17},{2,18},{3,19},{4,20},{5,21},{6,22},{7,23},{8,24},{9,... | collective-permute-start | bytes 393224 | tf_op jit(solution)/shard_map/ppermute | solution.py:44
  39.1 6.8 %collective-permute-start.20 = (bf16[64,512]{1,0:T(8,128)(2,1)S(1)}, bf16[64,512]{1,0:T(8,128)(2,1)S(1)}, u32[]{:S(2)}, u32[]{:S(2)}) collective-permute-start(bf16[64,512]{1,0:T(8,128)(2,1)S(1)} %get-tuple-element.46), channel_id=1, source_target_pairs={{0,2},{1,3},{2,4},{3,5},{4,6},{5,7},{6,0},{7,1},{8,10},{9,11},{10,... | collective-permute-start | bytes 196616 | tf_op jit(solution)/shard_map/ppermute | solution.py:44
  40.7 7.9 %collective-permute-start.21 = (bf16[64,512]{1,0:T(8,128)(2,1)S(1)}, bf16[64,512]{1,0:T(8,128)(2,1)S(1)}, u32[]{:S(2)}, u32[]{:S(2)}) collective-permute-start(bf16[64,512]{1,0:T(8,128)(2,1)S(1)} %get-tuple-element.47), channel_id=1, source_target_pairs={{0,4},{1,5},{2,6},{3,7},{4,0},{5,1},{6,2},{7,3},{8,12},{9,13},{10,... | collective-permute-start | bytes 196616 | tf_op jit(solution)/shard_map/ppermute | solution.py:44
  43.3 5.3 %collective-permute-start.22 = (bf16[64,512]{1,0:T(8,128)(2,1)S(1)}, bf16[64,512]{1,0:T(8,128)(2,1)S(1)}, u32[]{:S(2)}, u32[]{:S(2)}) collective-permute-start(bf16[64,512]{1,0:T(8,128)(2,1)S(1)} %get-tuple-element.48), channel_id=1, source_target_pairs={{0,6},{1,7},{2,0},{3,1},{4,2},{5,3},{6,4},{7,5},{8,14},{9,15},{10,... | collective-permute-start | bytes 196616 | tf_op jit(solution)/shard_map/ppermute | solution.py:44
  44.8 6.2 %collective-permute-start.5 = (bf16[64,512]{1,0:T(8,128)(2,1)S(1)}, bf16[64,512]{1,0:T(8,128)(2,1)S(1)}, u32[]{:S(2)}, u32[]{:S(2)}) collective-permute-start(bf16[64,512]{1,0:T(8,128)(2,1)S(1)} %get-tuple-element.41), channel_id=1, source_target_pairs={{0,2},{1,3},{2,4},{3,5},{4,6},{5,7},{6,0},{7,1},{8,10},{9,11},{10,... | collective-permute-start | bytes 196616 | tf_op jit(solution)/shard_map/ppermute | solution.py:44
  45.5 6.7 %collective-permute-start.6 = (bf16[64,512]{1,0:T(8,128)(2,1)S(1)}, bf16[64,512]{1,0:T(8,128)(2,1)S(1)}, u32[]{:S(2)}, u32[]{:S(2)}) collective-permute-start(bf16[64,512]{1,0:T(8,128)(2,1)S(1)} %get-tuple-element.42), channel_id=1, source_target_pairs={{0,4},{1,5},{2,6},{3,7},{4,0},{5,1},{6,2},{7,3},{8,12},{9,13},{10,... | collective-permute-start | bytes 196616 | tf_op jit(solution)/shard_map/ppermute | solution.py:44
  45.9 6.4 %collective-permute-start.7 = (bf16[64,512]{1,0:T(8,128)(2,1)S(1)}, bf16[64,512]{1,0:T(8,128)(2,1)S(1)}, u32[]{:S(2)}, u32[]{:S(2)}) collective-permute-start(bf16[64,512]{1,0:T(8,128)(2,1)S(1)} %get-tuple-element.43), channel_id=1, source_target_pairs={{0,6},{1,7},{2,0},{3,1},{4,2},{5,3},{6,4},{7,5},{8,14},{9,15},{10,... | collective-permute-start | bytes 196616 | tf_op jit(solution)/shard_map/ppermute | solution.py:44
  52.4 6.5 %collective-permute-start.24 = (f32[4,128]{1,0:T(4,128)S(1)}, f32[4,128]{1,0:T(4,128)S(1)}, u32[]{:S(2)}, u32[]{:S(2)}) collective-permute-start(f32[4,128]{1,0:T(4,128)S(1)} %bitcast_add_fusion.8), channel_id=1, source_target_pairs={{0,1},{1,0},{2,3},{3,2},{4,5},{5,4},{6,7},{7,6},{8,9},{9,8},{10,11... | collective-permute-start | bytes 6152 | tf_op jit(solution)/shard_map/ppermute | solution.py:44
  54.0 5.5 %collective-permute-start.25 = (f32[4,128]{1,0:T(4,128)S(1)}, f32[4,128]{1,0:T(4,128)S(1)}, u32[]{:S(2)}, u32[]{:S(2)}) collective-permute-start(f32[4,128]{1,0:T(4,128)S(1)} %bitcast_add_fusion.8), channel_id=1, source_target_pairs={{0,16},{1,17},{2,18},{3,19},{4,20},{5,21},{6,22},{7,23},{8,24},{9,... | collective-permute-start | bytes 6152 | tf_op jit(solution)/shard_map/ppermute | solution.py:44
  54.4 5.0 %collective-permute-start.26 = (f32[4,128]{1,0:T(4,128)S(1)}, f32[4,128]{1,0:T(4,128)S(1)}, u32[]{:S(2)}, u32[]{:S(2)}) collective-permute-start(f32[4,128]{1,0:T(4,128)S(1)} %bitcast_add_fusion.8), channel_id=1, source_target_pairs={{0,17},{1,16},{2,19},{3,18},{4,21},{5,20},{6,23},{7,22},{8,25},{9,... | collective-permute-start | bytes 6152 | tf_op jit(solution)/shard_map/ppermute | solution.py:44
  56.0 6.7 %collective-permute-start.10 = (f32[4,128]{1,0:T(4,128)S(1)}, f32[4,128]{1,0:T(4,128)S(1)}, u32[]{:S(2)}, u32[]{:S(2)}) collective-permute-start(f32[4,128]{1,0:T(4,128)S(1)} %bitcast_add_fusion.9), channel_id=1, source_target_pairs={{0,16},{1,17},{2,18},{3,19},{4,20},{5,21},{6,22},{7,23},{8,24},{9,... | collective-permute-start | bytes 6152 | tf_op jit(solution)/shard_map/ppermute | solution.py:44
  56.4 6.9 %collective-permute-start.11 = (f32[4,128]{1,0:T(4,128)S(1)}, f32[4,128]{1,0:T(4,128)S(1)}, u32[]{:S(2)}, u32[]{:S(2)}) collective-permute-start(f32[4,128]{1,0:T(4,128)S(1)} %bitcast_add_fusion.9), channel_id=1, source_target_pairs={{0,17},{1,16},{2,19},{3,18},{4,21},{5,20},{6,23},{7,22},{8,25},{9,... | collective-permute-start | bytes 6152 | tf_op jit(solution)/shard_map/ppermute | solution.py:44
  59.0 4.4 %collective-permute-start.9 = (f32[4,128]{1,0:T(4,128)S(1)}, f32[4,128]{1,0:T(4,128)S(1)}, u32[]{:S(2)}, u32[]{:S(2)}) collective-permute-start(f32[4,128]{1,0:T(4,128)S(1)} %bitcast_add_fusion.9), channel_id=1, source_target_pairs={{0,1},{1,0},{2,3},{3,2},{4,5},{5,4},{6,7},{7,6},{8,9},{9,8},{10,11... | collective-permute-start | bytes 6152 | tf_op jit(solution)/shard_map/ppermute | solution.py:44
  59.5 6.3 %collective-permute-start.27 = (f32[4,128]{1,0:T(4,128)S(1)}, f32[4,128]{1,0:T(4,128)S(1)}, u32[]{:S(2)}, u32[]{:S(2)}) collective-permute-start(f32[4,128]{1,0:T(4,128)S(1)} %add_add_fusion), channel_id=1, source_target_pairs={{0,2},{1,3},{2,4},{3,5},{4,6},{5,7},{6,0},{7,1},{8,10},{9,11},{10,... | collective-permute-start | bytes 6152 | tf_op jit(solution)/shard_map/ppermute | solution.py:44
  60.8 7.6 %collective-permute-start.28 = (f32[4,128]{1,0:T(4,128)S(1)}, f32[4,128]{1,0:T(4,128)S(1)}, u32[]{:S(2)}, u32[]{:S(2)}) collective-permute-start(f32[4,128]{1,0:T(4,128)S(1)} %add_add_fusion), channel_id=1, source_target_pairs={{0,4},{1,5},{2,6},{3,7},{4,0},{5,1},{6,2},{7,3},{8,12},{9,13},{10,... | collective-permute-start | bytes 6152 | tf_op jit(solution)/shard_map/ppermute | solution.py:44
  62.7 5.7 %collective-permute-start.29 = (f32[4,128]{1,0:T(4,128)S(1)}, f32[4,128]{1,0:T(4,128)S(1)}, u32[]{:S(2)}, u32[]{:S(2)}) collective-permute-start(f32[4,128]{1,0:T(4,128)S(1)} %add_add_fusion), channel_id=1, source_target_pairs={{0,6},{1,7},{2,0},{3,1},{4,2},{5,3},{6,4},{7,5},{8,14},{9,15},{10,... | collective-permute-start | bytes 6152 | tf_op jit(solution)/shard_map/ppermute | solution.py:44
  63.4 6.3 %collective-permute-start.12 = (f32[4,128]{1,0:T(4,128)S(1)}, f32[4,128]{1,0:T(4,128)S(1)}, u32[]{:S(2)}, u32[]{:S(2)}) collective-permute-start(f32[4,128]{1,0:T(4,128)S(1)} %add_add_fusion.1), channel_id=1, source_target_pairs={{0,2},{1,3},{2,4},{3,5},{4,6},{5,7},{6,0},{7,1},{8,10},{9,11},{10,... | collective-permute-start | bytes 6152 | tf_op jit(solution)/shard_map/ppermute | solution.py:44
  64.8 4.9 %collective-permute-start.13 = (f32[4,128]{1,0:T(4,128)S(1)}, f32[4,128]{1,0:T(4,128)S(1)}, u32[]{:S(2)}, u32[]{:S(2)}) collective-permute-start(f32[4,128]{1,0:T(4,128)S(1)} %add_add_fusion.1), channel_id=1, source_target_pairs={{0,4},{1,5},{2,6},{3,7},{4,0},{5,1},{6,2},{7,3},{8,12},{9,13},{10,... | collective-permute-start | bytes 6152 | tf_op jit(solution)/shard_map/ppermute | solution.py:44
  71.3 7.0 %collective-permute-start.41 = (bf16[64,512]{1,0:T(8,128)(2,1)S(1)}, bf16[64,512]{1,0:T(8,128)(2,1)S(1)}, u32[]{:S(2)}, u32[]{:S(2)}) collective-permute-start(bf16[64,512]{1,0:T(8,128)(2,1)S(1)} %get-tuple-element.18), channel_id=1, source_target_pairs={{0,2},{1,3},{2,4},{3,5},{4,6},{5,7},{6,0},{7,1},{8,10},{9,11},{10,... | collective-permute-start | bytes 196616 | tf_op jit(solution)/shard_map/ppermute | solution.py:44
  73.0 7.5 %collective-permute-start.42 = (bf16[64,512]{1,0:T(8,128)(2,1)S(1)}, bf16[64,512]{1,0:T(8,128)(2,1)S(1)}, u32[]{:S(2)}, u32[]{:S(2)}) collective-permute-start(bf16[64,512]{1,0:T(8,128)(2,1)S(1)} %get-tuple-element.18), channel_id=1, source_target_pairs={{0,4},{1,5},{2,6},{3,7},{4,0},{5,1},{6,2},{7,3},{8,12},{9,13},{10,... | collective-permute-start | bytes 196616 | tf_op jit(solution)/shard_map/ppermute | solution.py:44
  75.9 5.0 %collective-permute-start.43 = (bf16[64,512]{1,0:T(8,128)(2,1)S(1)}, bf16[64,512]{1,0:T(8,128)(2,1)S(1)}, u32[]{:S(2)}, u32[]{:S(2)}) collective-permute-start(bf16[64,512]{1,0:T(8,128)(2,1)S(1)} %get-tuple-element.18), channel_id=1, source_target_pairs={{0,6},{1,7},{2,0},{3,1},{4,2},{5,3},{6,4},{7,5},{8,14},{9,15},{10,... | collective-permute-start | bytes 196616 | tf_op jit(solution)/shard_map/ppermute | solution.py:44
  76.0 7.1 %collective-permute-start.30 = (bf16[64,512]{1,0:T(8,128)(2,1)S(1)}, bf16[64,512]{1,0:T(8,128)(2,1)S(1)}, u32[]{:S(2)}, u32[]{:S(2)}) collective-permute-start(bf16[64,512]{1,0:T(8,128)(2,1)S(1)} %get-tuple-element.17), channel_id=1, source_target_pairs={{0,2},{1,3},{2,4},{3,5},{4,6},{5,7},{6,0},{7,1},{8,10},{9,11},{10,... | collective-permute-start | bytes 196616 | tf_op jit(solution)/shard_map/ppermute | solution.py:44
  78.0 5.8 %collective-permute-start.31 = (bf16[64,512]{1,0:T(8,128)(2,1)S(1)}, bf16[64,512]{1,0:T(8,128)(2,1)S(1)}, u32[]{:S(2)}, u32[]{:S(2)}) collective-permute-start(bf16[64,512]{1,0:T(8,128)(2,1)S(1)} %get-tuple-element.17), channel_id=1, source_target_pairs={{0,4},{1,5},{2,6},{3,7},{4,0},{5,1},{6,2},{7,3},{8,12},{9,13},{10,... | collective-permute-start | bytes 196616 | tf_op jit(solution)/shard_map/ppermute | solution.py:44
  78.3 5.5 %collective-permute-start.32 = (bf16[64,512]{1,0:T(8,128)(2,1)S(1)}, bf16[64,512]{1,0:T(8,128)(2,1)S(1)}, u32[]{:S(2)}, u32[]{:S(2)}) collective-permute-start(bf16[64,512]{1,0:T(8,128)(2,1)S(1)} %get-tuple-element.17), channel_id=1, source_target_pairs={{0,6},{1,7},{2,0},{3,1},{4,2},{5,3},{6,4},{7,5},{8,14},{9,15},{10,... | collective-permute-start | bytes 196616 | tf_op jit(solution)/shard_map/ppermute | solution.py:44
  80.9 5.0 %collective-permute-start.46 = (bf16[4,64,256]{2,1,0:T(8,128)(2,1)S(1)}, bf16[4,64,256]{2,1,0:T(8,128)(2,1)S(1)}, u32[]{:S(2)}, u32[]{:S(2)}) collective-permute-start(bf16[4,64,256]{2,1,0:T(8,128)(2,1)S(1)} %get-tuple-element.58), channel_id=1, source_target_pairs={{0,16},{1,17},{2,18},{3,19},{4,20},{5,21},{6,22},{7,23},{8,24},{9,... | collective-permute-start | bytes 393224 | tf_op jit(solution)/shard_map/ppermute | solution.py:44
  82.0 6.0 %collective-permute-start.44 = (bf16[4,64,256]{2,1,0:T(8,128)(2,1)S(1)}, bf16[4,64,256]{2,1,0:T(8,128)(2,1)S(1)}, u32[]{:S(2)}, u32[]{:S(2)}) collective-permute-start(bf16[4,64,256]{2,1,0:T(8,128)(2,1)S(1)} %get-tuple-element.60), channel_id=1, source_target_pairs={{0,1},{1,0},{2,3},{3,2},{4,5},{5,4},{6,7},{7,6},{8,9},{9,8},{10,11... | collective-permute-start | bytes 393224 | tf_op jit(solution)/shard_map/ppermute | solution.py:44
  83.8 6.9 %collective-permute-start.35 = (bf16[4,64,256]{2,1,0:T(8,128)(2,1)S(1)}, bf16[4,64,256]{2,1,0:T(8,128)(2,1)S(1)}, u32[]{:S(2)}, u32[]{:S(2)}) collective-permute-start(bf16[4,64,256]{2,1,0:T(8,128)(2,1)S(1)} %get-tuple-element.62), channel_id=1, source_target_pairs={{0,16},{1,17},{2,18},{3,19},{4,20},{5,21},{6,22},{7,23},{8,24},{9,... | collective-permute-start | bytes 393224 | tf_op jit(solution)/shard_map/ppermute | solution.py:44
  86.0 10.8 %collective-permute-start.47 = (bf16[2,4,64,256]{3,2,1,0:T(8,128)(2,1)S(1)}, bf16[2,4,64,256]{3,2,1,0:T(8,128)(2,1)S(1)}, u32[]{:S(2)}, u32[]{:S(2)}) collective-permute-start(bf16[2,4,64,256]{3,2,1,0:T(8,128)(2,1)S(1)} %pad_maximum_fusion.5.refs_2_), channel_id=1, source_target_pairs={{0,1},{1,0},{2,3},{3,2},{4,5},{5,4},{6,7},{7,6},{8,9},{9,8},{10,11... | collective-permute-start | bytes 786440 | tf_op jit(solution)/shard_map/ppermute | solution.py:44
  87.6 9.7 %collective-permute-start.50 = (bf16[2,4,64,256]{3,2,1,0:T(8,128)(2,1)S(1)}, bf16[2,4,64,256]{3,2,1,0:T(8,128)(2,1)S(1)}, u32[]{:S(2)}, u32[]{:S(2)}) collective-permute-start(bf16[2,4,64,256]{3,2,1,0:T(8,128)(2,1)S(1)} %pad_maximum_fusion.5.refs_2_), channel_id=1, source_target_pairs={{0,8},{1,9},{2,10},{3,11},{4,12},{5,13},{6,14},{7,15},{8,0},{9,1},... | collective-permute-start | bytes 786440 | tf_op jit(solution)/shard_map/ppermute | solution.py:44
  88.0 9.3 %collective-permute-start.45 = (bf16[2,4,64,256]{3,2,1,0:T(8,128)(2,1)S(1)}, bf16[2,4,64,256]{3,2,1,0:T(8,128)(2,1)S(1)}, u32[]{:S(2)}, u32[]{:S(2)}) collective-permute-start(bf16[2,4,64,256]{3,2,1,0:T(8,128)(2,1)S(1)} %pad_maximum_fusion.4.refs_0_), channel_id=1, source_target_pairs={{0,16},{1,17},{2,18},{3,19},{4,20},{5,21},{6,22},{7,23},{8,24},{9,... | collective-permute-start | bytes 786440 | tf_op jit(solution)/shard_map/ppermute | solution.py:44
  89.2 6.1 %collective-permute-start.33 = (bf16[4,64,256]{2,1,0:T(8,128)(2,1)S(1)}, bf16[4,64,256]{2,1,0:T(8,128)(2,1)S(1)}, u32[]{:S(2)}, u32[]{:S(2)}) collective-permute-start(bf16[4,64,256]{2,1,0:T(8,128)(2,1)S(1)} %get-tuple-element.64), channel_id=1, source_target_pairs={{0,1},{1,0},{2,3},{3,2},{4,5},{5,4},{6,7},{7,6},{8,9},{9,8},{10,11... | collective-permute-start | bytes 393224 | tf_op jit(solution)/shard_map/ppermute | solution.py:44
  90.8 7.2 %collective-permute-start.48 = (bf16[2,4,64,256]{3,2,1,0:T(8,128)(2,1)S(1)}, bf16[2,4,64,256]{3,2,1,0:T(8,128)(2,1)S(1)}, u32[]{:S(2)}, u32[]{:S(2)}) collective-permute-start(bf16[2,4,64,256]{3,2,1,0:T(8,128)(2,1)S(1)} %pad_maximum_fusion.4.refs_0_), channel_id=1, source_target_pairs={{0,8},{1,9},{2,10},{3,11},{4,12},{5,13},{6,14},{7,15},{8,0},{9,1},... | collective-permute-start | bytes 786440 | tf_op jit(solution)/shard_map/ppermute | solution.py:44
  95.3 7.0 %collective-permute-start.36 = (bf16[2,4,64,256]{3,2,1,0:T(8,128)(2,1)S(1)}, bf16[2,4,64,256]{3,2,1,0:T(8,128)(2,1)S(1)}, u32[]{:S(2)}, u32[]{:S(2)}) collective-permute-start(bf16[2,4,64,256]{3,2,1,0:T(8,128)(2,1)S(1)} %pad_maximum_fusion.3.refs_2_), channel_id=1, source_target_pairs={{0,1},{1,0},{2,3},{3,2},{4,5},{5,4},{6,7},{7,6},{8,9},{9,8},{10,11... | collective-permute-start | bytes 786440 | tf_op jit(solution)/shard_map/ppermute | solution.py:44
  96.8 6.4 %collective-permute-start.34 = (bf16[2,4,64,256]{3,2,1,0:T(8,128)(2,1)S(1)}, bf16[2,4,64,256]{3,2,1,0:T(8,128)(2,1)S(1)}, u32[]{:S(2)}, u32[]{:S(2)}) collective-permute-start(bf16[2,4,64,256]{3,2,1,0:T(8,128)(2,1)S(1)} %pad_maximum_fusion.2.refs_0_), channel_id=1, source_target_pairs={{0,16},{1,17},{2,18},{3,19},{4,20},{5,21},{6,22},{7,23},{8,24},{9,... | collective-permute-start | bytes 786440 | tf_op jit(solution)/shard_map/ppermute | solution.py:44
  97.3 5.9 %collective-permute-start.51 = (bf16[2,4,64,256]{3,2,1,0:T(8,128)(2,1)S(1)}, bf16[2,4,64,256]{3,2,1,0:T(8,128)(2,1)S(1)}, u32[]{:S(2)}, u32[]{:S(2)}) collective-permute-start(bf16[2,4,64,256]{3,2,1,0:T(8,128)(2,1)S(1)} %collective-permute-done.47.refs_3_), channel_id=1, source_target_pairs={{0,8},{1,9},{2,10},{3,11},{4,12},{5,13},{6,14},{7,15},{8,0},{9,1},... | collective-permute-start | bytes 786440 | tf_op jit(solution)/shard_map/ppermute | solution.py:44
  97.3 7.3 %collective-permute-start.49 = (bf16[2,4,64,256]{3,2,1,0:T(8,128)(2,1)S(1)}, bf16[2,4,64,256]{3,2,1,0:T(8,128)(2,1)S(1)}, u32[]{:S(2)}, u32[]{:S(2)}) collective-permute-start(bf16[2,4,64,256]{3,2,1,0:T(8,128)(2,1)S(1)} %collective-permute-done.45.refs_1_), channel_id=1, source_target_pairs={{0,8},{1,9},{2,10},{3,11},{4,12},{5,13},{6,14},{7,15},{8,0},{9,1},... | collective-permute-start | bytes 786440 | tf_op jit(solution)/shard_map/ppermute | solution.py:44
  97.9 9.7 %collective-permute-start.39 = (bf16[2,4,64,256]{3,2,1,0:T(8,128)(2,1)S(1)}, bf16[2,4,64,256]{3,2,1,0:T(8,128)(2,1)S(1)}, u32[]{:S(2)}, u32[]{:S(2)}) collective-permute-start(bf16[2,4,64,256]{3,2,1,0:T(8,128)(2,1)S(1)} %pad_maximum_fusion.3.refs_2_), channel_id=1, source_target_pairs={{0,8},{1,9},{2,10},{3,11},{4,12},{5,13},{6,14},{7,15},{8,0},{9,1},... | collective-permute-start | bytes 786440 | tf_op jit(solution)/shard_map/ppermute | solution.py:44
  102.2 5.4 %collective-permute-start.37 = (bf16[2,4,64,256]{3,2,1,0:T(8,128)(2,1)S(1)}, bf16[2,4,64,256]{3,2,1,0:T(8,128)(2,1)S(1)}, u32[]{:S(2)}, u32[]{:S(2)}) collective-permute-start(bf16[2,4,64,256]{3,2,1,0:T(8,128)(2,1)S(1)} %pad_maximum_fusion.2.refs_0_), channel_id=1, source_target_pairs={{0,8},{1,9},{2,10},{3,11},{4,12},{5,13},{6,14},{7,15},{8,0},{9,1},... | collective-permute-start | bytes 786440 | tf_op jit(solution)/shard_map/ppermute | solution.py:44
  103.3 4.4 %collective-permute-start.38 = (bf16[2,4,64,256]{3,2,1,0:T(8,128)(2,1)S(1)}, bf16[2,4,64,256]{3,2,1,0:T(8,128)(2,1)S(1)}, u32[]{:S(2)}, u32[]{:S(2)}) collective-permute-start(bf16[2,4,64,256]{3,2,1,0:T(8,128)(2,1)S(1)} %collective-permute-done.34.refs_1_), channel_id=1, source_target_pairs={{0,8},{1,9},{2,10},{3,11},{4,12},{5,13},{6,14},{7,15},{8,0},{9,1},... | collective-permute-start | bytes 786440 | tf_op jit(solution)/shard_map/ppermute | solution.py:44
  (10 other events, 131.5 us)

commit v3 on v2

--- a/solution.py
+++ b/solution.py
@@ -58,58 +58,123 @@
     )
 
 
-def grad_kernel(tokens_ref, cot_ref, *out_refs):
-    value = lax.dot_general(
-        tokens_ref[...], cot_ref[...], (((0,), (0,)), ((), ())), preferred_element_type=F32
-    )
-    width = out_refs[0].shape[1]
-    for k, ref in enumerate(out_refs):
-        ref[...] = value[:, k * width : (k + 1) * width].astype(ref.dtype)
-
-
-def grad_rows(grid, tokens, cot, step, dtype):
+def column_block(grid, x, step, rows):
+    return pl.ds(pl.multiple_of((x * 2 + grid.here("c", step)) * rows, rows), rows)
+
+
+def product(block, cot):
+    return lax.dot_general(block, cot, (((0,), (0,)), ((), ())), preferred_element_type=F32)
+
+
+def sent_kernel(grid, tokens_ref, cot_ref, *refs):
+    outs, (tokens, cot, sems) = refs[:-3], refs[-3:]
+    n, _, rows = tokens.shape
+    width = outs[0].shape[1]
+    copies = [pltpu.make_async_copy(cot_ref, cot, sems.at[n])]
+    for x in range(n):
+        block = tokens_ref.at[:, column_block(grid, x, 1, rows)]
+        copies.append(pltpu.make_async_copy(block, tokens.at[x], sems.at[x]))
+    for copy in copies:
+        copy.start()
+    copies[0].wait()
+    for x in range(n):
+        copies[1 + x].wait()
+        value = product(tokens[x], cot[...])
+        for k, ref in enumerate(outs):
+            ref[pl.ds(x * rows, rows), :] = value[:, k * width : (k + 1) * width].astype(ref.dtype)
+
+
+def sent_rows(grid, tokens, cot, parts):
     count, depth = tokens.shape
-    width = cot.shape[1] // 2
+    width = cot.shape[1] // parts
     n = grid.size["x"]
     rows = depth // (n * 2)
-    shape = jax.ShapeDtypeStruct((n * rows, width), dtype)
-    spec = pl.BlockSpec((rows, width), lambda x: (x, 0))
     return pl.pallas_call(
-        grad_kernel,
-        out_shape=[shape, shape],
-        grid=(n,),
-        in_specs=[
-            pl.BlockSpec((count, rows), lambda x: (0, x * 2 + grid.here("c", step))),
-            pl.BlockSpec((count, 2 * width), lambda x: (0, 0)),
+        functools.partial(sent_kernel, grid),
+        out_shape=[jax.ShapeDtypeStruct((n * rows, width), BF16)] * parts,
+        in_specs=[pl.BlockSpec(memory_space=pltpu.HBM)] * 2,
+        out_specs=[pl.BlockSpec(memory_space=pltpu.VMEM)] * parts,
+        scratch_shapes=[
+            pltpu.VMEM((n, count, rows), BF16),
+            pltpu.VMEM(cot.shape, BF16),
+            pltpu.SemaphoreType.DMA((n + 1,)),
         ],
-        out_specs=[spec, spec],
-        **kernel_params(
-            4 * count * n * rows * width, count * n * rows * 2 + count * width * 4 + n * rows * width * 4
-        ),
-    )(tokens, cot)
-
-
-DIM = {"x": 0, "y": 2}
-
-
-def scatter_xy(grid, kept, came, order):
+        **kernel_params(2 * count * n * rows * cot.shape[1], count * n * rows * 2 + cot.size * 2, SMALL),
+    )(*(pltpu.with_memory_space_constraint(v, pltpu.HBM) for v in (tokens, cot)))
+
+
+def kept_kernel(grid, orders, block_rows, tokens, cot, *refs):
+    refs = list(refs)
+    came = [refs.pop(0) for _ in orders]
+    outs = [[refs.pop(0) for _ in range(grid.size[order[0]])] for order in orders]
+    arrived, buffer, sems = refs
+    nx, ny, nz = (grid.size[axis] for axis in "xyz")
+    rows, width = buffer.shape
+    copies = [pltpu.make_async_copy(ref, arrived.at[k], sems.at[k]) for k, ref in enumerate(came)]
+    for copy in copies:
+        copy.start()
+    for kx in range(nx):
+        x = grid.here("x", kx)
+        value = product(tokens[:, column_block(grid, x, 0, rows)], cot[...])
+        for k, order in enumerate(orders):
+            if kx == 0:
+                copies[k].wait()
+            here = pl.ds(pl.multiple_of(x * rows, rows), rows)
+            part = value[:, k * width : (k + 1) * width] + arrived[k, here, :].astype(F32)
+            if order == "xy":
+                outs[k][kx][...] = part.astype(outs[k][kx].dtype)
+                continue
+            buffer[...] = part
+            for ky in range(ny):
+                for z in range(nz):
+                    start = pl.multiple_of((z * ny + grid.here("y", ky)) * block_rows, block_rows)
+                    outs[k][ky][x, z] = buffer[pl.ds(start, block_rows), :].astype(outs[k][ky].dtype)
+
+
+def kept_rows(grid, tokens, cot, came, orders):
+    count, depth = tokens.shape
+    width = cot.shape[1] // len(orders)
+    nx, ny, nz = (grid.size[axis] for axis in "xyz")
+    rows = depth // (nx * 2)
+    block_rows = rows // (nz * ny)
+    shapes = {"xy": (rows, width), "yx": (nx, nz, block_rows, width)}
+    out_shape = [
+        jax.ShapeDtypeStruct(shapes[order], BF16 if k else F32)
+        for order in orders
+        for k in range(grid.size[order[0]])
+    ]
+    whole = pl.BlockSpec(memory_space=pltpu.VMEM)
+    outs = pl.pallas_call(
+        functools.partial(kept_kernel, grid, orders, block_rows),
+        out_shape=out_shape,
+        in_specs=[whole] * 2 + [pl.BlockSpec(memory_space=pl.ANY)] * len(came),
+        out_specs=[whole] * len(out_shape),
+        scratch_shapes=[
+            pltpu.VMEM((len(orders), nx * rows, width), BF16),
+            pltpu.VMEM((rows, width), F32),
+            pltpu.SemaphoreType.DMA((len(orders),)),
+        ],
+        **kernel_params(2 * count * nx * rows * cot.shape[1], count * nx * rows * 2 + cot.size * 2, SMALL),
+    )(tokens, cot, *came)
+    outs = iter(outs)
+    result = []
+    for order in orders:
+        values = [next(outs) for _ in range(grid.size[order[0]])]
+        result.append([v.reshape(nz, ny, block_rows, width) if order == "xy" else v for v in values])
+    return result
+
+
+def scatter_xy(grid, sums, order):
     one_axis, two_axis = order
     n_one, n_two = grid.size[one_axis], grid.size[two_axis]
-
-    def pair_sum(step):
-        at = grid.here(one_axis, step)
-        return pick(kept, DIM[one_axis], at) + pick(came, DIM[one_axis], at).astype(F32)
-
-    arriving = [grid.send(pair_sum(one).astype(BF16), **{one_axis: one}) for one in range(1, n_one)]
-    yield
-    own = pair_sum(0)
+    arriving = yield [(sums[one], {one_axis: one}) for one in range(1, n_one)]
+    own = sums[0]
     for value in arriving:
         own = own + value.astype(F32)
     dim = 1 if two_axis == "y" else 0
-    arriving = [
-        grid.send(pick(own, dim, grid.here(two_axis, two)).astype(BF16), **{two_axis: two}) for two in range(1, n_two)
+    arriving = yield [
+        (pick(own, dim, grid.here(two_axis, two)).astype(BF16), {two_axis: two}) for two in range(1, n_two)
     ]
-    yield
     total = pick(own, dim, grid.here(two_axis))
     for value in arriving:
         total = total + value.astype(F32)
@@ -118,10 +183,9 @@
 
 def scatter_z(grid, totals):
     whole = jnp.concatenate(totals, axis=2)
-    arriving = [
-        grid.send(pick(whole, 0, grid.here("z", k)).astype(BF16), z=k) for k in range(1, grid.size["z"])
+    arriving = yield [
+        (pick(whole, 0, grid.here("z", k)).astype(BF16), {"z": k}) for k in range(1, grid.size["z"])
     ]
-    yield
     total = pick(whole, 0, grid.here("z"))
     for value in arriving:
         total = total + value.astype(F32)
@@ -154,16 +218,25 @@
 
 
 def gather_z(grid, low, parts):
-    pieces = [low] + [grid.send(low, z=k) for k in range(1, grid.size["z"])]
+    pieces = yield [(low, {"z": k}) for k in range(1, grid.size["z"])]
     width = low.shape[1] // parts
-    return [jnp.stack([p[:, s * width : (s + 1) * width] for p in pieces]) for s in range(parts)]
+    yield [jnp.stack([p[:, s * width : (s + 1) * width] for p in [low] + pieces]) for s in range(parts)]
 
 
 def gather_xy(grid, value, order):
     one_axis, two_axis = order
-    pieces = [value] + [grid.send(value, **{two_axis: two}) for two in range(1, grid.size[two_axis])]
-    value = jnp.stack(pieces)
-    return [value] + [grid.send(value, **{one_axis: one}) for one in range(1, grid.size[one_axis])]
+    pieces = yield [(value, {two_axis: two}) for two in range(1, grid.size[two_axis])]
+    value = jnp.stack([value] + pieces)
+    pieces = yield [(value, {one_axis: one}) for one in range(1, grid.size[one_axis])]
+    yield [value] + pieces
+
+
+def stage(grid, wanted, after=()):
+    values = [value for sends in wanted for value, _ in sends]
+    if after:
+        values, _ = lax.optimization_barrier((values, tuple(after)))
+    flat = iter(values)
+    return [[grid.send(next(flat), **steps) for _, steps in sends] for sends in wanted], values
 
 
 def project_kernel(grid, orders, rows, finish, tokens, *refs):
@@ -221,53 +294,65 @@
 def shards(tokens, grad_out, master_weight, first_moment, second_moment, next_tokens):
     grid = Grid()
     half = grad_out.shape[1] // 2
-    rows = master_weight.shape[0]
-    lead = (grid.size["x"], grid.size["z"], grid.size["y"], rows, half)
     orders = ("xy", "yx")
-    width = half // len(orders)
-
-    sent = grad_rows(grid, tokens, grad_out, 1, BF16)
-    came = [grid.send(value, c=1).reshape(lead) for value in sent]
-    kept = [value.reshape(lead) for value in grad_rows(grid, tokens, grad_out, 0, F32)]
+
+    came = [grid.send(value, c=1) for value in sent_rows(grid, tokens, grad_out, 2 * len(orders))]
+    sums = kept_rows(grid, tokens, grad_out, came, 2 * orders)
 
     def section(s):
         columns = slice(s * half, (s + 1) * half)
-        ways = []
-        for k, order in enumerate(orders):
-            cut = slice(k * width, (k + 1) * width)
-            ways.append(scatter_xy(grid, kept[s][..., cut], came[s][..., cut], order))
-        for way in ways:
-            next(way)
-        yield
-        for way in ways:
-            next(way)
-        yield
-        way = scatter_z(grid, [next(way) for way in ways])
-        next(way)
-        yield
-        grad = next(way)
-        column_sums = sum_everywhere(grid, jnp.sum(grad * grad, axis=0).reshape(-1, 128))
-        yield
-        clipped = grad * clip_factor(jnp.sum(column_sums))
+        first = s * len(orders)
+        ways = [scatter_xy(grid, sums[first + k], order) for k, order in enumerate(orders)]
+        wanted = [next(way) for way in ways]
+        for _ in range(2):
+            came_in, values = stage(grid, wanted, (yield))
+            yield values
+            wanted = [way.send(got) for way, got in zip(ways, came_in)]
+        way = scatter_z(grid, wanted)
+        (came_in,), values = stage(grid, [next(way)], (yield))
+        yield values
+        grad = way.send(came_in)
+        square = yield jnp.sum(grad * grad, axis=0).reshape(-1, 128)
+        clipped = grad * clip_factor(square)
         state = [value[:, columns] for value in (master_weight, first_moment, second_moment)]
         low = adam(clipped, *state)
         low, clipped = lax.optimization_barrier((low, clipped))
         new = moments(clipped, *state[1:])
-        values = gather_z(grid, low, len(orders))
+        way = gather_z(grid, low, len(orders))
         yield
-        own = [gather_xy(grid, value, order) for value, order in zip(values, orders)]
-        yield
-        other = [[grid.send(piece, c=1) for piece in part] for part in own]
-        yield new, (own, other)
-
-    results = [None, None]
+        (came_in,), values = stage(grid, [next(way)], (yield))
+        yield values
+        ways = [gather_xy(grid, value, order) for value, order in zip(way.send(came_in), orders)]
+        wanted = [next(way) for way in ways]
+        for _ in range(2):
+            came_in, values = stage(grid, wanted, (yield))
+            yield values
+            wanted = [way.send(got) for way, got in zip(ways, came_in)]
+        own = wanted
+        early = [[grid.send(part[0], c=1)] for part in own]
+        after = yield new
+        last, _ = stage(grid, [[(piece, {"c": 1}) for piece in part[1:]] for part in own], after)
+        other = [a + b for a, b in zip(early, last)]
+        yield own, other
+
     ways = [section(0), section(1)]
-    for step in range(7):
-        for s in (0, 1):
-            results[s] = next(ways[s])
-    gate = project(grid, next_tokens, results[0][1], orders)
-    next_hidden = project(grid, next_tokens, results[1][1], orders, gate)
-    new_first, new_second = (jnp.concatenate([results[0][0][k], results[1][0][k]], axis=1) for k in (0, 1))
+
+    def run(stages):
+        for _ in range(stages):
+            for way in ways:
+                next(way)
+                way.send(())
+
+    run(3)
+    squares = [next(way) for way in ways]
+    squares = sum_everywhere(grid, jnp.stack(squares))
+    for s in (0, 1):
+        ways[s].send(jnp.sum(squares[s]))
+    run(3)
+    news = [next(way) for way in ways]
+    gate = project(grid, next_tokens, ways[0].send([]), orders)
+    next_hidden = project(grid, next_tokens, ways[1].send([gate]), orders, gate)
+    new_first, new_second = (jnp.concatenate([news[0][k], news[1][k]], axis=1) for k in (0, 1))
     return new_first, new_second, next_hidden
 
 

time: 112 us -> 106 us (0.946)
  waiting for transfers between devices: 22.1 us -> 38.2 us
  starting transfers between devices: 58.2 us -> 47.6 us
  local copies, waits for them, and re-layouts: 7.53 us -> 0.21 us
  Pallas kernels: 17.7 us -> 14.8 us
    ppermute x52 -> x47, waiting for transfers between devices: 22.1 us -> 38.2 us  [send(): return lax.ppermute(value, AXES, pairs)]
    ppermute x52 -> x47, starting transfers between devices: 58.2 us -> 47.6 us  [send(): return lax.ppermute(value, AXES, pairs)]
    slice x4 -> x0, local copies, waits for them, and re-layouts: 5.6 us -> none  [section(): ways.append(scatter_xy(grid, kept[s][..., cut], came[s][..., cut], order))]
    pallas_call x2, Pallas kernels: 10.9 us -> 7.96 us  [the longest x1 4.59 us: sent_rows(): pl.pallas_call(functools.partial(sent_kernel, grid), out_shape=[jax.Shape...]
    unnamed x12, local copies, waits for them, and re-layouts: 1.51 us -> 0.03 us
  transfers between devices with their start and end apart: 52 -> 47, of which waited for: 13 -> 28; matrix products, arithmetic and copies ran while one was open for 8% -> 2% of each run, Pallas kernels for 8% -> 3%
where the time goes in v3:
time: 106 us
  starting transfers between devices  47.6 us (45%)
  waiting for transfers between devices  38.2 us (36%)
  Pallas kernels  14.8 us (14%)
  other arithmetic  2.48 us (2%)
  between operations  2.39 us (2%)
    ppermute x47, starting transfers between devices, send(): return lax.ppermute(value, AXES, pairs)  47.6 us
    ppermute x47, waiting for transfers between devices, send(): return lax.ppermute(value, AXES, pairs)  38.2 us
    pallas_call x2, Pallas kernels, project(): pl.pallas_call(functools.partial(project_kernel, grid, orders, rows, fini...  6.81 us
    pallas_call x1, Pallas kernels, sent_rows(): pl.pallas_call(functools.partial(sent_kernel, grid), out_shape=[jax.Shape...  4.59 us
    pallas_call x1, Pallas kernels, kept_rows(): pl.pallas_call(functools.partial(kept_kernel, grid, orders, block_rows),...  3.37 us
  transfers between devices with their start and end apart: 47, of which 28 were waited for; matrix products, arithmetic and copies ran while one was open for 2% of the time, Pallas kernels for 3%

profile of v3, /device:TPU:0, one launch (start us, length us, event | category | flops | bytes accessed | tf_op | source)
XLA Modules:
  0.0 105.6 jit_solution(8691006976542562128)
XLA Ops:
  0.6 4.6 %shard_map.85 = (bf16[1024,256]{1,0:T(8,128)(2,1)S(1)}, bf16[1024,256]{1,0:T(8,128)(2,1)S(1)}, bf16[1024,256]{1,0:T(8,128)(2,1)S(1)}, bf16[1024,256]{1,0:T(8,128)(2,1)S(1)}) custom-call(bf16[1024,2048]{1,0:T(8,128)(2,1)} %tokens.3, bf16[1024,1024]{1,0:T(8,128)(2,1)} %cot.1), custom_call_target="tpu_custom_call" | custom-call | flops 2147483648 | bytes 4194304 | tf_op jit(solution)/shard_map/pallas_call | solution.py:92
  6.4 0.9 collective-permute-done.refs_0_
  7.3 0.7 collective-permute-done.1.refs_1_
  8.1 0.7 collective-permute-done.2.refs_2_
  8.8 0.7 collective-permute-done.3.refs_3_
  9.6 3.4 %shard_map.86 = (f32[512,256]{1,0:T(8,128)S(1)}, bf16[512,256]{1,0:T(8,128)(2,1)S(1)}, f32[2,4,64,256]{3,2,1,0:T(8,128)S(1)}, bf16[2,4,64,256]{3,2,1,0:T(8,128)(...) custom-call(bf16[1024,2048]{1,0:T(8,128)(2,1)S(1)} %copy-done.1, ...), custom_call_target="tpu_custom_call" | custom-call | flops 2147483648 | bytes 4194304 | tf_op jit(solution)/shard_map/pallas_call | solution.py:147
  13.0 2.9 %collective-permute-start.11 = (bf16[4,2,64,256]{3,2,0,1:T(8,128)(2,1)S(1)}, bf16[4,2,64,256]{3,2,0,1:T(8,128)(2,1)S(1)}, u32[]{:S(2)}, u32[]{:S(2)}) collective-permute-start(bf16[4,2,64,256]{3,2,0,1:T(8,128)(2,1)S(1)} %copy.15), channel_id=1, source_target_pairs={{0,16},{1,17},{2,18},{3,19},{4,20},{5,21},{6,22},{7,23},{8,24},{9,... | collective-permute-start | bytes 786440 | tf_op jit(solution)/shard_map/ppermute | solution.py:44
  15.9 1.5 %collective-permute-start.13 = (bf16[2,4,64,256]{3,2,1,0:T(8,128)(2,1)S(1)}, bf16[2,4,64,256]{3,2,1,0:T(8,128)(2,1)S(1)}, u32[]{:S(2)}, u32[]{:S(2)}) collective-permute-start(bf16[2,4,64,256]{3,2,1,0:T(8,128)(2,1)S(1)} %get-tuple-element.32), channel_id=1, source_target_pairs={{0,1},{1,0},{2,3},{3,2},{4,5},{5,4},{6,7},{7,6},{8,9},{9,8},{10,11... | collective-permute-start | bytes 786440 | tf_op jit(solution)/shard_map/ppermute | solution.py:44
  18.1 4.8 %collective-permute-done.11 = bf16[4,2,64,256]{3,2,0,1:T(8,128)(2,1)S(1)} collective-permute-done((bf16[4,2,64,256]{3,2,0,1:T(8,128)(2,1)S(1)}, bf16[4,2,64,256]{3,2,0,1:T(8,128)(2,1)S(1)}, u32[]{:S(2)}, u32[]{:S(2)}) %collective-permute-start.11) | collective-permute-done | bytes 262176 | tf_op jit(solution)/shard_map/ppermute | solution.py:44
  23.1 2.2 %collective-permute-start.12 = (bf16[4,64,256]{2,1,0:T(8,128)(2,1)S(1)}, bf16[4,64,256]{2,1,0:T(8,128)(2,1)S(1)}, u32[]{:S(2)}, u32[]{:S(2)}) collective-permute-start(bf16[4,64,256]{2,1,0:T(8,128)(2,1)S(1)} %fusion.16), channel_id=1, source_target_pairs={{0,1},{1,0},{2,3},{3,2},{4,5},{5,4},{6,7},{7,6},{8,9},{9,8},{10,11... | collective-permute-start | bytes 393224 | tf_op jit(solution)/shard_map/ppermute | solution.py:44
  25.3 1.6 %collective-permute-start.14 = (bf16[4,64,256]{2,1,0:T(8,128)(2,1)S(1)}, bf16[4,64,256]{2,1,0:T(8,128)(2,1)S(1)}, u32[]{:S(2)}, u32[]{:S(2)}) collective-permute-start(bf16[4,64,256]{2,1,0:T(8,128)(2,1)S(1)} %fusion.17), channel_id=1, source_target_pairs={{0,16},{1,17},{2,18},{3,19},{4,20},{5,21},{6,22},{7,23},{8,24},{9,... | collective-permute-start | bytes 393224 | tf_op jit(solution)/shard_map/ppermute | solution.py:44
  26.9 1.7 %collective-permute-done.4 = bf16[4,2,64,256]{3,2,0,1:T(8,128)(2,1)S(1)} collective-permute-done((bf16[4,2,64,256]{3,2,0,1:T(8,128)(2,1)S(1)}, bf16[4,2,64,256]{3,2,0,1:T(8,128)(2,1)S(1)}, u32[]{:S(2)}, u32[]{:S(2)}) %collective-permute-start.4) | collective-permute-done | bytes 262176 | tf_op jit(solution)/shard_map/ppermute | solution.py:44
  28.7 2.2 %collective-permute-start.5 = (bf16[4,64,256]{2,1,0:T(8,128)(2,1)S(1)}, bf16[4,64,256]{2,1,0:T(8,128)(2,1)S(1)}, u32[]{:S(2)}, u32[]{:S(2)}) collective-permute-start(bf16[4,64,256]{2,1,0:T(8,128)(2,1)S(1)} %fusion.14), channel_id=1, source_target_pairs={{0,1},{1,0},{2,3},{3,2},{4,5},{5,4},{6,7},{7,6},{8,9},{9,8},{10,11... | collective-permute-start | bytes 393224 | tf_op jit(solution)/shard_map/ppermute | solution.py:44
  31.0 1.6 %collective-permute-start.7 = (bf16[4,64,256]{2,1,0:T(8,128)(2,1)S(1)}, bf16[4,64,256]{2,1,0:T(8,128)(2,1)S(1)}, u32[]{:S(2)}, u32[]{:S(2)}) collective-permute-start(bf16[4,64,256]{2,1,0:T(8,128)(2,1)S(1)} %fusion.15), channel_id=1, source_target_pairs={{0,16},{1,17},{2,18},{3,19},{4,20},{5,21},{6,22},{7,23},{8,24},{9,... | collective-permute-start | bytes 393224 | tf_op jit(solution)/shard_map/ppermute | solution.py:44
  32.5 1.0 collective-permute-done.12
  33.6 1.6 %collective-permute-start.15 = (bf16[64,512]{1,0:T(8,128)(2,1)S(1)}, bf16[64,512]{1,0:T(8,128)(2,1)S(1)}, u32[]{:S(2)}, u32[]{:S(2)}) collective-permute-start(bf16[64,512]{1,0:T(8,128)(2,1)S(1)} %get-tuple-element.54), channel_id=1, source_target_pairs={{0,2},{1,3},{2,4},{3,5},{4,6},{5,7},{6,0},{7,1},{8,10},{9,11},{10,... | collective-permute-start | bytes 196616 | tf_op jit(solution)/shard_map/ppermute | solution.py:44
  35.2 2.6 %collective-permute-start.16 = (bf16[64,512]{1,0:T(8,128)(2,1)S(1)}, bf16[64,512]{1,0:T(8,128)(2,1)S(1)}, u32[]{:S(2)}, u32[]{:S(2)}) collective-permute-start(bf16[64,512]{1,0:T(8,128)(2,1)S(1)} %get-tuple-element.55), channel_id=1, source_target_pairs={{0,4},{1,5},{2,6},{3,7},{4,0},{5,1},{6,2},{7,3},{8,12},{9,13},{10,... | collective-permute-start | bytes 196616 | tf_op jit(solution)/shard_map/ppermute | solution.py:44
  37.8 1.3 %collective-permute-start.17 = (bf16[64,512]{1,0:T(8,128)(2,1)S(1)}, bf16[64,512]{1,0:T(8,128)(2,1)S(1)}, u32[]{:S(2)}, u32[]{:S(2)}) collective-permute-start(bf16[64,512]{1,0:T(8,128)(2,1)S(1)} %get-tuple-element.56), channel_id=1, source_target_pairs={{0,6},{1,7},{2,0},{3,1},{4,2},{5,3},{6,4},{7,5},{8,14},{9,15},{10,... | collective-permute-start | bytes 196616 | tf_op jit(solution)/shard_map/ppermute | solution.py:44
  39.8 1.6 %collective-permute-start.8 = (bf16[64,512]{1,0:T(8,128)(2,1)S(1)}, bf16[64,512]{1,0:T(8,128)(2,1)S(1)}, u32[]{:S(2)}, u32[]{:S(2)}) collective-permute-start(bf16[64,512]{1,0:T(8,128)(2,1)S(1)} %get-tuple-element.51), channel_id=1, source_target_pairs={{0,2},{1,3},{2,4},{3,5},{4,6},{5,7},{6,0},{7,1},{8,10},{9,11},{10,... | collective-permute-start | bytes 196616 | tf_op jit(solution)/shard_map/ppermute | solution.py:44
  42.3 1.4 %collective-permute-done.17 = bf16[64,512]{1,0:T(8,128)(2,1)S(1)} collective-permute-done((bf16[64,512]{1,0:T(8,128)(2,1)S(1)}, bf16[64,512]{1,0:T(8,128)(2,1)S(1)}, u32[]{:S(2)}, u32[]{:S(2)}) %collective-permute-start.17) | collective-permute-done | bytes 65568 | tf_op jit(solution)/shard_map/ppermute | solution.py:44
  43.8 0.8 collective-permute-done.10
  44.6 1.4 %collective-permute-done.8 = bf16[64,512]{1,0:T(8,128)(2,1)S(1)} collective-permute-done((bf16[64,512]{1,0:T(8,128)(2,1)S(1)}, bf16[64,512]{1,0:T(8,128)(2,1)S(1)}, u32[]{:S(2)}, u32[]{:S(2)}) %collective-permute-start.8) | collective-permute-done | bytes 65568 | tf_op jit(solution)/shard_map/ppermute | solution.py:44
  46.0 1.5 %collective-permute-done.9 = bf16[64,512]{1,0:T(8,128)(2,1)S(1)} collective-permute-done((bf16[64,512]{1,0:T(8,128)(2,1)S(1)}, bf16[64,512]{1,0:T(8,128)(2,1)S(1)}, u32[]{:S(2)}, u32[]{:S(2)}) %collective-permute-start.9) | collective-permute-done | bytes 65568 | tf_op jit(solution)/shard_map/ppermute | solution.py:44
  47.7 1.2 %collective-permute-done.18 = f32[2,4,128]{2,1,0:T(4,128)S(1)} collective-permute-done((f32[2,4,128]{2,1,0:T(4,128)S(1)}, f32[2,4,128]{2,1,0:T(4,128)S(1)}, u32[]{:S(2)}, u32[]{:S(2)}) %collective-permute-start.18) | collective-permute-done | bytes 4128 | tf_op jit(solution)/shard_map/ppermute | solution.py:44
  48.8 1.5 %collective-permute-start.19 = (f32[2,4,128]{2,1,0:T(4,128)S(1)}, f32[2,4,128]{2,1,0:T(4,128)S(1)}, u32[]{:S(2)}, u32[]{:S(2)}) collective-permute-start(f32[2,4,128]{2,1,0:T(4,128)S(1)} %fusion.48), channel_id=1, source_target_pairs={{0,1},{1,0},{2,3},{3,2},{4,5},{5,4},{6,7},{7,6},{8,9},{9,8},{10,11... | collective-permute-start | bytes 12296 | tf_op jit(solution)/shard_map/ppermute | solution.py:44
  50.7 1.6 %collective-permute-start.21 = (f32[2,4,128]{2,1,0:T(4,128)S(1)}, f32[2,4,128]{2,1,0:T(4,128)S(1)}, u32[]{:S(2)}, u32[]{:S(2)}) collective-permute-start(f32[2,4,128]{2,1,0:T(4,128)S(1)} %fusion.48), channel_id=1, source_target_pairs={{0,17},{1,16},{2,19},{3,18},{4,21},{5,20},{6,23},{7,22},{8,25},{9,... | collective-permute-start | bytes 12296 | tf_op jit(solution)/shard_map/ppermute | solution.py:44
  52.4 1.5 %collective-permute-done.20 = f32[2,4,128]{2,1,0:T(4,128)S(1)} collective-permute-done((f32[2,4,128]{2,1,0:T(4,128)S(1)}, f32[2,4,128]{2,1,0:T(4,128)S(1)}, u32[]{:S(2)}, u32[]{:S(2)}) %collective-permute-start.20) | collective-permute-done | bytes 4128 | tf_op jit(solution)/shard_map/ppermute | solution.py:44
  54.0 1.3 %collective-permute-done.21 = f32[2,4,128]{2,1,0:T(4,128)S(1)} collective-permute-done((f32[2,4,128]{2,1,0:T(4,128)S(1)}, f32[2,4,128]{2,1,0:T(4,128)S(1)}, u32[]{:S(2)}, u32[]{:S(2)}) %collective-permute-start.21) | collective-permute-done | bytes 4128 | tf_op jit(solution)/shard_map/ppermute | solution.py:44
  55.2 2.4 %collective-permute-start.24 = (f32[2,4,128]{2,1,0:T(4,128)S(1)}, f32[2,4,128]{2,1,0:T(4,128)S(1)}, u32[]{:S(2)}, u32[]{:S(2)}) collective-permute-start(f32[2,4,128]{2,1,0:T(4,128)S(1)} %add_add_fusion.1), channel_id=1, source_target_pairs={{0,6},{1,7},{2,0},{3,1},{4,2},{5,3},{6,4},{7,5},{8,14},{9,15},{10,... | collective-permute-start | bytes 12296 | tf_op jit(solution)/shard_map/ppermute | solution.py:44
  59.0 3.2 %collective-permute-done.23 = f32[2,4,128]{2,1,0:T(4,128)S(1)} collective-permute-done((f32[2,4,128]{2,1,0:T(4,128)S(1)}, f32[2,4,128]{2,1,0:T(4,128)S(1)}, u32[]{:S(2)}, u32[]{:S(2)}) %collective-permute-start.23) | collective-permute-done | bytes 4128 | tf_op jit(solution)/shard_map/ppermute | solution.py:44
  62.2 0.9 collective-permute-done.22
  65.4 1.2 %collective-permute-start.34 = (bf16[64,512]{1,0:T(8,128)(2,1)S(1)}, bf16[64,512]{1,0:T(8,128)(2,1)S(1)}, u32[]{:S(2)}, u32[]{:S(2)}) collective-permute-start(bf16[64,512]{1,0:T(8,128)(2,1)S(1)} %get-tuple-element.36), channel_id=1, source_target_pairs={{0,4},{1,5},{2,6},{3,7},{4,0},{5,1},{6,2},{7,3},{8,12},{9,13},{10,... | collective-permute-start | bytes 196616 | tf_op jit(solution)/shard_map/ppermute | solution.py:44
  66.6 2.8 %collective-permute-start.35 = (bf16[64,512]{1,0:T(8,128)(2,1)S(1)}, bf16[64,512]{1,0:T(8,128)(2,1)S(1)}, u32[]{:S(2)}, u32[]{:S(2)}) collective-permute-start(bf16[64,512]{1,0:T(8,128)(2,1)S(1)} %get-tuple-element.36), channel_id=1, source_target_pairs={{0,6},{1,7},{2,0},{3,1},{4,2},{5,3},{6,4},{7,5},{8,14},{9,15},{10,... | collective-permute-start | bytes 196616 | tf_op jit(solution)/shard_map/ppermute | solution.py:44
  69.8 1.5 %collective-permute-start.26 = (bf16[64,512]{1,0:T(8,128)(2,1)S(1)}, bf16[64,512]{1,0:T(8,128)(2,1)S(1)}, u32[]{:S(2)}, u32[]{:S(2)}) collective-permute-start(bf16[64,512]{1,0:T(8,128)(2,1)S(1)} %get-tuple-element.35), channel_id=1, source_target_pairs={{0,4},{1,5},{2,6},{3,7},{4,0},{5,1},{6,2},{7,3},{8,12},{9,13},{10,... | collective-permute-start | bytes 196616 | tf_op jit(solution)/shard_map/ppermute | solution.py:44
  71.3 0.9 collective-permute-done.33
  72.2 2.0 %collective-permute-start.27 = (bf16[64,512]{1,0:T(8,128)(2,1)S(1)}, bf16[64,512]{1,0:T(8,128)(2,1)S(1)}, u32[]{:S(2)}, u32[]{:S(2)}) collective-permute-start(bf16[64,512]{1,0:T(8,128)(2,1)S(1)} %get-tuple-element.35), channel_id=1, source_target_pairs={{0,6},{1,7},{2,0},{3,1},{4,2},{5,3},{6,4},{7,5},{8,14},{9,15},{10,... | collective-permute-start | bytes 196616 | tf_op jit(solution)/shard_map/ppermute | solution.py:44
  74.3 1.6 %collective-permute-start.38 = (bf16[4,64,256]{2,1,0:T(8,128)(2,1)S(1)}, bf16[4,64,256]{2,1,0:T(8,128)(2,1)S(1)}, u32[]{:S(2)}, u32[]{:S(2)}) collective-permute-start(bf16[4,64,256]{2,1,0:T(8,128)(2,1)S(1)} %get-tuple-element.64), channel_id=1, source_target_pairs={{0,16},{1,17},{2,18},{3,19},{4,20},{5,21},{6,22},{7,23},{8,24},{9,... | collective-permute-start | bytes 393224 | tf_op jit(solution)/shard_map/ppermute | solution.py:44
  77.2 3.5 %collective-permute-done.38 = bf16[4,64,256]{2,1,0:T(8,128)(2,1)S(1)} collective-permute-done((bf16[4,64,256]{2,1,0:T(8,128)(2,1)S(1)}, bf16[4,64,256]{2,1,0:T(8,128)(2,1)S(1)}, u32[]{:S(2)}, u32[]{:S(2)}) %collective-permute-start.38) | collective-permute-done | bytes 131104 | tf_op jit(solution)/shard_map/ppermute | solution.py:44
  81.3 1.6 %collective-permute-start.37 = (bf16[2,4,64,256]{3,2,1,0:T(8,128)(2,1)S(1)}, bf16[2,4,64,256]{3,2,1,0:T(8,128)(2,1)S(1)}, u32[]{:S(2)}, u32[]{:S(2)}) collective-permute-start(bf16[2,4,64,256]{3,2,1,0:T(8,128)(2,1)S(1)} %pad_maximum_fusion.4.refs_0_), channel_id=1, source_target_pairs={{0,16},{1,17},{2,18},{3,19},{4,20},{5,21},{6,22},{7,23},{8,24},{9,... | collective-permute-start | bytes 786440 | tf_op jit(solution)/shard_map/ppermute | solution.py:44
  83.6 1.6 %collective-permute-start.28 = (bf16[4,64,256]{2,1,0:T(8,128)(2,1)S(1)}, bf16[4,64,256]{2,1,0:T(8,128)(2,1)S(1)}, u32[]{:S(2)}, u32[]{:S(2)}) collective-permute-start(bf16[4,64,256]{2,1,0:T(8,128)(2,1)S(1)} %get-tuple-element.70), channel_id=1, source_target_pairs={{0,1},{1,0},{2,3},{3,2},{4,5},{5,4},{6,7},{7,6},{8,9},{9,8},{10,11... | collective-permute-start | bytes 393224 | tf_op jit(solution)/shard_map/ppermute | solution.py:44
  85.2 4.0 %collective-permute-done.30 = bf16[4,64,256]{2,1,0:T(8,128)(2,1)S(1)} collective-permute-done((bf16[4,64,256]{2,1,0:T(8,128)(2,1)S(1)}, bf16[4,64,256]{2,1,0:T(8,128)(2,1)S(1)}, u32[]{:S(2)}, u32[]{:S(2)}) %collective-permute-start.30) | collective-permute-done | bytes 131104 | tf_op jit(solution)/shard_map/ppermute | solution.py:44
  90.0 1.4 %collective-permute-start.31 = (bf16[2,4,64,256]{3,2,1,0:T(8,128)(2,1)S(1)}, bf16[2,4,64,256]{3,2,1,0:T(8,128)(2,1)S(1)}, u32[]{:S(2)}, u32[]{:S(2)}) collective-permute-start(bf16[2,4,64,256]{3,2,1,0:T(8,128)(2,1)S(1)} %pad_maximum_fusion.3.refs_2_), channel_id=1, source_target_pairs={{0,1},{1,0},{2,3},{3,2},{4,5},{5,4},{6,7},{7,6},{8,9},{9,8},{10,11... | collective-permute-start | bytes 786440 | tf_op jit(solution)/shard_map/ppermute | solution.py:44
  91.5 1.6 %collective-permute-start.29 = (bf16[2,4,64,256]{3,2,1,0:T(8,128)(2,1)S(1)}, bf16[2,4,64,256]{3,2,1,0:T(8,128)(2,1)S(1)}, u32[]{:S(2)}, u32[]{:S(2)}) collective-permute-start(bf16[2,4,64,256]{3,2,1,0:T(8,128)(2,1)S(1)} %pad_maximum_fusion.2.refs_0_), channel_id=1, source_target_pairs={{0,16},{1,17},{2,18},{3,19},{4,20},{5,21},{6,22},{7,23},{8,24},{9,... | collective-permute-start | bytes 786440 | tf_op jit(solution)/shard_map/ppermute | solution.py:44
  93.6 3.0 %shard_map.87.refs_8_ = f32[1024,512]{1,0:T(8,128)S(1)} custom-call(bf16[1024,2048]{1,0:T(8,128)(2,1)S(1)} %copy-done, bf16[2,4,64,256]{3,2,1,0:T(8,128)(2,1)S(1)} %pad_maximum_fusion.4.refs_0_, bf16[2,4,64,256]{3,2,1,0:T(8,128)(2,1)S(1)} %collective-permute-done.37.refs_1_, bf16[2,4,64,256]{3,2,1,0:T(8,128)(2,1)S(1)} %pad_maximum_fusion.5.refs_2_, ...), custom_call_target="tpu_custom_call" | custom-call | flops 2147483648 | bytes 8388608 | tf_op jit(solution)/shard_map/pallas_call | solution.py:281
  96.6 1.9 %collective-permute-done.31.refs_3_ = bf16[2,4,64,256]{3,2,1,0:T(8,128)(2,1)S(1)} collective-permute-done((bf16[2,4,64,256]{3,2,1,0:T(8,128)(2,1)S(1)}, bf16[2,4,64,256]{3,2,1,0:T(8,128)(2,1)S(1)}, u32[]{:S(2)}, u32[]{:S(2)}) %collective-permute-start.31) | collective-permute-done | bytes 262176 | tf_op jit(solution)/shard_map/ppermute | solution.py:44
  98.5 1.4 %collective-permute-done.29.refs_1_ = bf16[2,4,64,256]{3,2,1,0:T(8,128)(2,1)S(1)} collective-permute-done((bf16[2,4,64,256]{3,2,1,0:T(8,128)(2,1)S(1)}, bf16[2,4,64,256]{3,2,1,0:T(8,128)(2,1)S(1)}, u32[]{:S(2)}, u32[]{:S(2)}) %collective-permute-start.29) | collective-permute-done | bytes 262176 | tf_op jit(solution)/shard_map/ppermute | solution.py:44
  100.5 0.8 pad_maximum_fusion
  101.8 3.8 %shard_map.88 = bf16[1024,512]{1,0:T(8,128)(2,1)} custom-call(bf16[1024,2048]{1,0:T(8,128)(2,1)S(1)} %copy-done, bf16[2,4,64,256]{3,2,1,0:T(8,128)(2,1)S(1)} %pad_maximum_fusion.2.refs_0_, bf16[2,4,64,256]{3,2,1,0:T(8,128)(2,1)S(1)} %collective-permute-done.29.refs_1_, bf16[2,4,64,256]{3,2,1,0:T(8,128)(2,1)S(1)} %pad_maximum_fusion.3.refs_2_, ...), custom_call_target="tpu_custom_call" | custom-call | flops 2147483648 | bytes 8388608 | tf_op jit(solution)/shard_map/pallas_call | solution.py:281
  (104 shorter events, 12.1 us)
Async XLA Ops:
  5.2 2.1 %collective-permute-start = (bf16[1024,256]{1,0:T(8,128)(2,1)S(1)}, bf16[1024,256]{1,0:T(8,128)(2,1)S(1)}, u32[]{:S(2)}, u32[]{:S(2)}) collective-permute-start(bf16[1024,256]{1,0:T(8,128)(2,1)S(1)} %get-tuple-element.21), channel_id=1, source_target_pairs={{0,8},{1,9},{2,10},{3,11},{4,12},{5,13},{6,14},{7,15},{8,0},{9,1},... | collective-permute-start | bytes 1572872 | tf_op jit(solution)/shard_map/ppermute | solution.py:44
  5.8 2.3 %collective-permute-start.1 = (bf16[1024,256]{1,0:T(8,128)(2,1)S(1)}, bf16[1024,256]{1,0:T(8,128)(2,1)S(1)}, u32[]{:S(2)}, u32[]{:S(2)}) collective-permute-start(bf16[1024,256]{1,0:T(8,128)(2,1)S(1)} %get-tuple-element.22), channel_id=1, source_target_pairs={{0,8},{1,9},{2,10},{3,11},{4,12},{5,13},{6,14},{7,15},{8,0},{9,1},... | collective-permute-start | bytes 1572872 | tf_op jit(solution)/shard_map/ppermute | solution.py:44
  5.8 3.0 %collective-permute-start.2 = (bf16[1024,256]{1,0:T(8,128)(2,1)S(1)}, bf16[1024,256]{1,0:T(8,128)(2,1)S(1)}, u32[]{:S(2)}, u32[]{:S(2)}) collective-permute-start(bf16[1024,256]{1,0:T(8,128)(2,1)S(1)} %get-tuple-element.23), channel_id=1, source_target_pairs={{0,8},{1,9},{2,10},{3,11},{4,12},{5,13},{6,14},{7,15},{8,0},{9,1},... | collective-permute-start | bytes 1572872 | tf_op jit(solution)/shard_map/ppermute | solution.py:44
  6.3 3.3 %collective-permute-start.3 = (bf16[1024,256]{1,0:T(8,128)(2,1)S(1)}, bf16[1024,256]{1,0:T(8,128)(2,1)S(1)}, u32[]{:S(2)}, u32[]{:S(2)}) collective-permute-start(bf16[1024,256]{1,0:T(8,128)(2,1)S(1)} %get-tuple-element.24), channel_id=1, source_target_pairs={{0,8},{1,9},{2,10},{3,11},{4,12},{5,13},{6,14},{7,15},{8,0},{9,1},... | collective-permute-start | bytes 1572872 | tf_op jit(solution)/shard_map/ppermute | solution.py:44
  13.0 10.0 %collective-permute-start.11 = (bf16[4,2,64,256]{3,2,0,1:T(8,128)(2,1)S(1)}, bf16[4,2,64,256]{3,2,0,1:T(8,128)(2,1)S(1)}, u32[]{:S(2)}, u32[]{:S(2)}) collective-permute-start(bf16[4,2,64,256]{3,2,0,1:T(8,128)(2,1)S(1)} %copy.15), channel_id=1, source_target_pairs={{0,16},{1,17},{2,18},{3,19},{4,20},{5,21},{6,22},{7,23},{8,24},{9,... | collective-permute-start | bytes 786440 | tf_op jit(solution)/shard_map/ppermute | solution.py:44
  15.9 9.3 %collective-permute-start.13 = (bf16[2,4,64,256]{3,2,1,0:T(8,128)(2,1)S(1)}, bf16[2,4,64,256]{3,2,1,0:T(8,128)(2,1)S(1)}, u32[]{:S(2)}, u32[]{:S(2)}) collective-permute-start(bf16[2,4,64,256]{3,2,1,0:T(8,128)(2,1)S(1)} %get-tuple-element.32), channel_id=1, source_target_pairs={{0,1},{1,0},{2,3},{3,2},{4,5},{5,4},{6,7},{7,6},{8,9},{9,8},{10,11... | collective-permute-start | bytes 786440 | tf_op jit(solution)/shard_map/ppermute | solution.py:44
  17.4 11.2 %collective-permute-start.4 = (bf16[4,2,64,256]{3,2,0,1:T(8,128)(2,1)S(1)}, bf16[4,2,64,256]{3,2,0,1:T(8,128)(2,1)S(1)}, u32[]{:S(2)}, u32[]{:S(2)}) collective-permute-start(bf16[4,2,64,256]{3,2,0,1:T(8,128)(2,1)S(1)} %copy.13), channel_id=1, source_target_pairs={{0,16},{1,17},{2,18},{3,19},{4,20},{5,21},{6,22},{7,23},{8,24},{9,... | collective-permute-start | bytes 786440 | tf_op jit(solution)/shard_map/ppermute | solution.py:44
  18.0 12.9 %collective-permute-start.6 = (bf16[2,4,64,256]{3,2,1,0:T(8,128)(2,1)S(1)}, bf16[2,4,64,256]{3,2,1,0:T(8,128)(2,1)S(1)}, u32[]{:S(2)}, u32[]{:S(2)}) collective-permute-start(bf16[2,4,64,256]{3,2,1,0:T(8,128)(2,1)S(1)} %get-tuple-element.28), channel_id=1, source_target_pairs={{0,1},{1,0},{2,3},{3,2},{4,5},{5,4},{6,7},{7,6},{8,9},{9,8},{10,11... | collective-permute-start | bytes 786440 | tf_op jit(solution)/shard_map/ppermute | solution.py:44
  23.1 10.4 %collective-permute-start.12 = (bf16[4,64,256]{2,1,0:T(8,128)(2,1)S(1)}, bf16[4,64,256]{2,1,0:T(8,128)(2,1)S(1)}, u32[]{:S(2)}, u32[]{:S(2)}) collective-permute-start(bf16[4,64,256]{2,1,0:T(8,128)(2,1)S(1)} %fusion.16), channel_id=1, source_target_pairs={{0,1},{1,0},{2,3},{3,2},{4,5},{5,4},{6,7},{7,6},{8,9},{9,8},{10,11... | collective-permute-start | bytes 393224 | tf_op jit(solution)/shard_map/ppermute | solution.py:44
  25.3 8.2 %collective-permute-start.14 = (bf16[4,64,256]{2,1,0:T(8,128)(2,1)S(1)}, bf16[4,64,256]{2,1,0:T(8,128)(2,1)S(1)}, u32[]{:S(2)}, u32[]{:S(2)}) collective-permute-start(bf16[4,64,256]{2,1,0:T(8,128)(2,1)S(1)} %fusion.17), channel_id=1, source_target_pairs={{0,16},{1,17},{2,18},{3,19},{4,20},{5,21},{6,22},{7,23},{8,24},{9,... | collective-permute-start | bytes 393224 | tf_op jit(solution)/shard_map/ppermute | solution.py:44
  28.7 36.4 %copy-start.3 = (f32[64,1024]{1,0:T(8,128)S(1)}, f32[64,1024]{1,0:T(8,128)}, u32[]{:S(2)}) copy-start(f32[64,1024]{1,0:T(8,128)} %param.9) | copy-start | bytes 786436
  28.7 10.5 %collective-permute-start.5 = (bf16[4,64,256]{2,1,0:T(8,128)(2,1)S(1)}, bf16[4,64,256]{2,1,0:T(8,128)(2,1)S(1)}, u32[]{:S(2)}, u32[]{:S(2)}) collective-permute-start(bf16[4,64,256]{2,1,0:T(8,128)(2,1)S(1)} %fusion.14), channel_id=1, source_target_pairs={{0,1},{1,0},{2,3},{3,2},{4,5},{5,4},{6,7},{7,6},{8,9},{9,8},{10,11... | collective-permute-start | bytes 393224 | tf_op jit(solution)/shard_map/ppermute | solution.py:44
  31.0 8.2 %collective-permute-start.7 = (bf16[4,64,256]{2,1,0:T(8,128)(2,1)S(1)}, bf16[4,64,256]{2,1,0:T(8,128)(2,1)S(1)}, u32[]{:S(2)}, u32[]{:S(2)}) collective-permute-start(bf16[4,64,256]{2,1,0:T(8,128)(2,1)S(1)} %fusion.15), channel_id=1, source_target_pairs={{0,16},{1,17},{2,18},{3,19},{4,20},{5,21},{6,22},{7,23},{8,24},{9,... | collective-permute-start | bytes 393224 | tf_op jit(solution)/shard_map/ppermute | solution.py:44
  33.6 7.8 %collective-permute-start.15 = (bf16[64,512]{1,0:T(8,128)(2,1)S(1)}, bf16[64,512]{1,0:T(8,128)(2,1)S(1)}, u32[]{:S(2)}, u32[]{:S(2)}) collective-permute-start(bf16[64,512]{1,0:T(8,128)(2,1)S(1)} %get-tuple-element.54), channel_id=1, source_target_pairs={{0,2},{1,3},{2,4},{3,5},{4,6},{5,7},{6,0},{7,1},{8,10},{9,11},{10,... | collective-permute-start | bytes 196616 | tf_op jit(solution)/shard_map/ppermute | solution.py:44
  35.2 7.1 %collective-permute-start.16 = (bf16[64,512]{1,0:T(8,128)(2,1)S(1)}, bf16[64,512]{1,0:T(8,128)(2,1)S(1)}, u32[]{:S(2)}, u32[]{:S(2)}) collective-permute-start(bf16[64,512]{1,0:T(8,128)(2,1)S(1)} %get-tuple-element.55), channel_id=1, source_target_pairs={{0,4},{1,5},{2,6},{3,7},{4,0},{5,1},{6,2},{7,3},{8,12},{9,13},{10,... | collective-permute-start | bytes 196616 | tf_op jit(solution)/shard_map/ppermute | solution.py:44
  37.8 5.9 %collective-permute-start.17 = (bf16[64,512]{1,0:T(8,128)(2,1)S(1)}, bf16[64,512]{1,0:T(8,128)(2,1)S(1)}, u32[]{:S(2)}, u32[]{:S(2)}) collective-permute-start(bf16[64,512]{1,0:T(8,128)(2,1)S(1)} %get-tuple-element.56), channel_id=1, source_target_pairs={{0,6},{1,7},{2,0},{3,1},{4,2},{5,3},{6,4},{7,5},{8,14},{9,15},{10,... | collective-permute-start | bytes 196616 | tf_op jit(solution)/shard_map/ppermute | solution.py:44
  39.3 5.3 %collective-permute-start.10 = (bf16[64,512]{1,0:T(8,128)(2,1)S(1)}, bf16[64,512]{1,0:T(8,128)(2,1)S(1)}, u32[]{:S(2)}, u32[]{:S(2)}) collective-permute-start(bf16[64,512]{1,0:T(8,128)(2,1)S(1)} %get-tuple-element.53), channel_id=1, source_target_pairs={{0,6},{1,7},{2,0},{3,1},{4,2},{5,3},{6,4},{7,5},{8,14},{9,15},{10,... | collective-permute-start | bytes 196616 | tf_op jit(solution)/shard_map/ppermute | solution.py:44
  39.8 6.2 %collective-permute-start.8 = (bf16[64,512]{1,0:T(8,128)(2,1)S(1)}, bf16[64,512]{1,0:T(8,128)(2,1)S(1)}, u32[]{:S(2)}, u32[]{:S(2)}) collective-permute-start(bf16[64,512]{1,0:T(8,128)(2,1)S(1)} %get-tuple-element.51), channel_id=1, source_target_pairs={{0,2},{1,3},{2,4},{3,5},{4,6},{5,7},{6,0},{7,1},{8,10},{9,11},{10,... | collective-permute-start | bytes 196616 | tf_op jit(solution)/shard_map/ppermute | solution.py:44
  41.4 6.1 %collective-permute-start.9 = (bf16[64,512]{1,0:T(8,128)(2,1)S(1)}, bf16[64,512]{1,0:T(8,128)(2,1)S(1)}, u32[]{:S(2)}, u32[]{:S(2)}) collective-permute-start(bf16[64,512]{1,0:T(8,128)(2,1)S(1)} %get-tuple-element.52), channel_id=1, source_target_pairs={{0,4},{1,5},{2,6},{3,7},{4,0},{5,1},{6,2},{7,3},{8,12},{9,13},{10,... | collective-permute-start | bytes 196616 | tf_op jit(solution)/shard_map/ppermute | solution.py:44
  47.6 1.2 %collective-permute-start.18 = (f32[2,4,128]{2,1,0:T(4,128)S(1)}, f32[2,4,128]{2,1,0:T(4,128)S(1)}, u32[]{:S(2)}, u32[]{:S(2)}) collective-permute-start(f32[2,4,128]{2,1,0:T(4,128)S(1)} %pad_maximum_fusion.10), channel_id=1, source_target_pairs={{0,8},{1,9},{2,10},{3,11},{4,12},{5,13},{6,14},{7,15},{8,0},{9,1},... | collective-permute-start | bytes 12296 | tf_op jit(solution)/shard_map/ppermute | solution.py:44
  48.8 3.6 %collective-permute-start.19 = (f32[2,4,128]{2,1,0:T(4,128)S(1)}, f32[2,4,128]{2,1,0:T(4,128)S(1)}, u32[]{:S(2)}, u32[]{:S(2)}) collective-permute-start(f32[2,4,128]{2,1,0:T(4,128)S(1)} %fusion.48), channel_id=1, source_target_pairs={{0,1},{1,0},{2,3},{3,2},{4,5},{5,4},{6,7},{7,6},{8,9},{9,8},{10,11... | collective-permute-start | bytes 12296 | tf_op jit(solution)/shard_map/ppermute | solution.py:44
  50.3 3.6 %collective-permute-start.20 = (f32[2,4,128]{2,1,0:T(4,128)S(1)}, f32[2,4,128]{2,1,0:T(4,128)S(1)}, u32[]{:S(2)}, u32[]{:S(2)}) collective-permute-start(f32[2,4,128]{2,1,0:T(4,128)S(1)} %fusion.48), channel_id=1, source_target_pairs={{0,16},{1,17},{2,18},{3,19},{4,20},{5,21},{6,22},{7,23},{8,24},{9,... | collective-permute-start | bytes 12296 | tf_op jit(solution)/shard_map/ppermute | solution.py:44
  50.7 4.5 %collective-permute-start.21 = (f32[2,4,128]{2,1,0:T(4,128)S(1)}, f32[2,4,128]{2,1,0:T(4,128)S(1)}, u32[]{:S(2)}, u32[]{:S(2)}) collective-permute-start(f32[2,4,128]{2,1,0:T(4,128)S(1)} %fusion.48), channel_id=1, source_target_pairs={{0,17},{1,16},{2,19},{3,18},{4,21},{5,20},{6,23},{7,22},{8,25},{9,... | collective-permute-start | bytes 12296 | tf_op jit(solution)/shard_map/ppermute | solution.py:44
  55.2 3.8 %collective-permute-start.24 = (f32[2,4,128]{2,1,0:T(4,128)S(1)}, f32[2,4,128]{2,1,0:T(4,128)S(1)}, u32[]{:S(2)}, u32[]{:S(2)}) collective-permute-start(f32[2,4,128]{2,1,0:T(4,128)S(1)} %add_add_fusion.1), channel_id=1, source_target_pairs={{0,6},{1,7},{2,0},{3,1},{4,2},{5,3},{6,4},{7,5},{8,14},{9,15},{10,... | collective-permute-start | bytes 12296 | tf_op jit(solution)/shard_map/ppermute | solution.py:44
  57.7 4.5 %collective-permute-start.23 = (f32[2,4,128]{2,1,0:T(4,128)S(1)}, f32[2,4,128]{2,1,0:T(4,128)S(1)}, u32[]{:S(2)}, u32[]{:S(2)}) collective-permute-start(f32[2,4,128]{2,1,0:T(4,128)S(1)} %add_add_fusion.1), channel_id=1, source_target_pairs={{0,4},{1,5},{2,6},{3,7},{4,0},{5,1},{6,2},{7,3},{8,12},{9,13},{10,... | collective-permute-start | bytes 12296 | tf_op jit(solution)/shard_map/ppermute | solution.py:44
  57.7 5.4 %collective-permute-start.22 = (f32[2,4,128]{2,1,0:T(4,128)S(1)}, f32[2,4,128]{2,1,0:T(4,128)S(1)}, u32[]{:S(2)}, u32[]{:S(2)}) collective-permute-start(f32[2,4,128]{2,1,0:T(4,128)S(1)} %add_add_fusion.1), channel_id=1, source_target_pairs={{0,2},{1,3},{2,4},{3,5},{4,6},{5,7},{6,0},{7,1},{8,10},{9,11},{10,... | collective-permute-start | bytes 12296 | tf_op jit(solution)/shard_map/ppermute | solution.py:44
  65.3 6.9 %collective-permute-start.33 = (bf16[64,512]{1,0:T(8,128)(2,1)S(1)}, bf16[64,512]{1,0:T(8,128)(2,1)S(1)}, u32[]{:S(2)}, u32[]{:S(2)}) collective-permute-start(bf16[64,512]{1,0:T(8,128)(2,1)S(1)} %get-tuple-element.36), channel_id=1, source_target_pairs={{0,2},{1,3},{2,4},{3,5},{4,6},{5,7},{6,0},{7,1},{8,10},{9,11},{10,... | collective-permute-start | bytes 196616 | tf_op jit(solution)/shard_map/ppermute | solution.py:44
  65.4 8.8 %collective-permute-start.34 = (bf16[64,512]{1,0:T(8,128)(2,1)S(1)}, bf16[64,512]{1,0:T(8,128)(2,1)S(1)}, u32[]{:S(2)}, u32[]{:S(2)}) collective-permute-start(bf16[64,512]{1,0:T(8,128)(2,1)S(1)} %get-tuple-element.36), channel_id=1, source_target_pairs={{0,4},{1,5},{2,6},{3,7},{4,0},{5,1},{6,2},{7,3},{8,12},{9,13},{10,... | collective-permute-start | bytes 196616 | tf_op jit(solution)/shard_map/ppermute | solution.py:44
  66.6 7.7 %collective-permute-start.35 = (bf16[64,512]{1,0:T(8,128)(2,1)S(1)}, bf16[64,512]{1,0:T(8,128)(2,1)S(1)}, u32[]{:S(2)}, u32[]{:S(2)}) collective-permute-start(bf16[64,512]{1,0:T(8,128)(2,1)S(1)} %get-tuple-element.36), channel_id=1, source_target_pairs={{0,6},{1,7},{2,0},{3,1},{4,2},{5,3},{6,4},{7,5},{8,14},{9,15},{10,... | collective-permute-start | bytes 196616 | tf_op jit(solution)/shard_map/ppermute | solution.py:44
  69.4 7.1 %collective-permute-start.25 = (bf16[64,512]{1,0:T(8,128)(2,1)S(1)}, bf16[64,512]{1,0:T(8,128)(2,1)S(1)}, u32[]{:S(2)}, u32[]{:S(2)}) collective-permute-start(bf16[64,512]{1,0:T(8,128)(2,1)S(1)} %get-tuple-element.35), channel_id=1, source_target_pairs={{0,2},{1,3},{2,4},{3,5},{4,6},{5,7},{6,0},{7,1},{8,10},{9,11},{10,... | collective-permute-start | bytes 196616 | tf_op jit(solution)/shard_map/ppermute | solution.py:44
  69.8 7.4 %collective-permute-start.26 = (bf16[64,512]{1,0:T(8,128)(2,1)S(1)}, bf16[64,512]{1,0:T(8,128)(2,1)S(1)}, u32[]{:S(2)}, u32[]{:S(2)}) collective-permute-start(bf16[64,512]{1,0:T(8,128)(2,1)S(1)} %get-tuple-element.35), channel_id=1, source_target_pairs={{0,4},{1,5},{2,6},{3,7},{4,0},{5,1},{6,2},{7,3},{8,12},{9,13},{10,... | collective-permute-start | bytes 196616 | tf_op jit(solution)/shard_map/ppermute | solution.py:44
  72.2 10.8 %collective-permute-start.27 = (bf16[64,512]{1,0:T(8,128)(2,1)S(1)}, bf16[64,512]{1,0:T(8,128)(2,1)S(1)}, u32[]{:S(2)}, u32[]{:S(2)}) collective-permute-start(bf16[64,512]{1,0:T(8,128)(2,1)S(1)} %get-tuple-element.35), channel_id=1, source_target_pairs={{0,6},{1,7},{2,0},{3,1},{4,2},{5,3},{6,4},{7,5},{8,14},{9,15},{10,... | collective-permute-start | bytes 196616 | tf_op jit(solution)/shard_map/ppermute | solution.py:44
  74.3 6.4 %collective-permute-start.38 = (bf16[4,64,256]{2,1,0:T(8,128)(2,1)S(1)}, bf16[4,64,256]{2,1,0:T(8,128)(2,1)S(1)}, u32[]{:S(2)}, u32[]{:S(2)}) collective-permute-start(bf16[4,64,256]{2,1,0:T(8,128)(2,1)S(1)} %get-tuple-element.64), channel_id=1, source_target_pairs={{0,16},{1,17},{2,18},{3,19},{4,20},{5,21},{6,22},{7,23},{8,24},{9,... | collective-permute-start | bytes 393224 | tf_op jit(solution)/shard_map/ppermute | solution.py:44
  76.0 5.4 %collective-permute-start.36 = (bf16[4,64,256]{2,1,0:T(8,128)(2,1)S(1)}, bf16[4,64,256]{2,1,0:T(8,128)(2,1)S(1)}, u32[]{:S(2)}, u32[]{:S(2)}) collective-permute-start(bf16[4,64,256]{2,1,0:T(8,128)(2,1)S(1)} %get-tuple-element.66), channel_id=1, source_target_pairs={{0,1},{1,0},{2,3},{3,2},{4,5},{5,4},{6,7},{7,6},{8,9},{9,8},{10,11... | collective-permute-start | bytes 393224 | tf_op jit(solution)/shard_map/ppermute | solution.py:44
  80.8 8.4 %collective-permute-start.39 = (bf16[2,4,64,256]{3,2,1,0:T(8,128)(2,1)S(1)}, bf16[2,4,64,256]{3,2,1,0:T(8,128)(2,1)S(1)}, u32[]{:S(2)}, u32[]{:S(2)}) collective-permute-start(bf16[2,4,64,256]{3,2,1,0:T(8,128)(2,1)S(1)} %pad_maximum_fusion.5.refs_2_), channel_id=1, source_target_pairs={{0,1},{1,0},{2,3},{3,2},{4,5},{5,4},{6,7},{7,6},{8,9},{9,8},{10,11... | collective-permute-start | bytes 786440 | tf_op jit(solution)/shard_map/ppermute | solution.py:44
  81.3 8.4 %collective-permute-start.37 = (bf16[2,4,64,256]{3,2,1,0:T(8,128)(2,1)S(1)}, bf16[2,4,64,256]{3,2,1,0:T(8,128)(2,1)S(1)}, u32[]{:S(2)}, u32[]{:S(2)}) collective-permute-start(bf16[2,4,64,256]{3,2,1,0:T(8,128)(2,1)S(1)} %pad_maximum_fusion.4.refs_0_), channel_id=1, source_target_pairs={{0,16},{1,17},{2,18},{3,19},{4,20},{5,21},{6,22},{7,23},{8,24},{9,... | collective-permute-start | bytes 786440 | tf_op jit(solution)/shard_map/ppermute | solution.py:44
  83.0 6.2 %collective-permute-start.30 = (bf16[4,64,256]{2,1,0:T(8,128)(2,1)S(1)}, bf16[4,64,256]{2,1,0:T(8,128)(2,1)S(1)}, u32[]{:S(2)}, u32[]{:S(2)}) collective-permute-start(bf16[4,64,256]{2,1,0:T(8,128)(2,1)S(1)} %get-tuple-element.68), channel_id=1, source_target_pairs={{0,16},{1,17},{2,18},{3,19},{4,20},{5,21},{6,22},{7,23},{8,24},{9,... | collective-permute-start | bytes 393224 | tf_op jit(solution)/shard_map/ppermute | solution.py:44
  83.6 7.9 %collective-permute-start.42 = (bf16[2,4,64,256]{3,2,1,0:T(8,128)(2,1)S(1)}, bf16[2,4,64,256]{3,2,1,0:T(8,128)(2,1)S(1)}, u32[]{:S(2)}, u32[]{:S(2)}) collective-permute-start(bf16[2,4,64,256]{3,2,1,0:T(8,128)(2,1)S(1)} %pad_maximum_fusion.5.refs_2_), channel_id=1, source_target_pairs={{0,8},{1,9},{2,10},{3,11},{4,12},{5,13},{6,14},{7,15},{8,0},{9,1},... | collective-permute-start | bytes 786440 | tf_op jit(solution)/shard_map/ppermute | solution.py:44
  83.6 6.4 %collective-permute-start.28 = (bf16[4,64,256]{2,1,0:T(8,128)(2,1)S(1)}, bf16[4,64,256]{2,1,0:T(8,128)(2,1)S(1)}, u32[]{:S(2)}, u32[]{:S(2)}) collective-permute-start(bf16[4,64,256]{2,1,0:T(8,128)(2,1)S(1)} %get-tuple-element.70), channel_id=1, source_target_pairs={{0,1},{1,0},{2,3},{3,2},{4,5},{5,4},{6,7},{7,6},{8,9},{9,8},{10,11... | collective-permute-start | bytes 393224 | tf_op jit(solution)/shard_map/ppermute | solution.py:44
  89.2 3.9 %collective-permute-start.40 = (bf16[2,4,64,256]{3,2,1,0:T(8,128)(2,1)S(1)}, bf16[2,4,64,256]{3,2,1,0:T(8,128)(2,1)S(1)}, u32[]{:S(2)}, u32[]{:S(2)}) collective-permute-start(bf16[2,4,64,256]{3,2,1,0:T(8,128)(2,1)S(1)} %pad_maximum_fusion.4.refs_0_), channel_id=1, source_target_pairs={{0,8},{1,9},{2,10},{3,11},{4,12},{5,13},{6,14},{7,15},{8,0},{9,1},... | collective-permute-start | bytes 786440 | tf_op jit(solution)/shard_map/ppermute | solution.py:44
  89.2 3.9 %collective-permute-start.43 = (bf16[2,4,64,256]{3,2,1,0:T(8,128)(2,1)S(1)}, bf16[2,4,64,256]{3,2,1,0:T(8,128)(2,1)S(1)}, u32[]{:S(2)}, u32[]{:S(2)}) collective-permute-start(bf16[2,4,64,256]{3,2,1,0:T(8,128)(2,1)S(1)} %collective-permute-done.39.refs_3_), channel_id=1, source_target_pairs={{0,8},{1,9},{2,10},{3,11},{4,12},{5,13},{6,14},{7,15},{8,0},{9,1},... | collective-permute-start | bytes 786440 | tf_op jit(solution)/shard_map/ppermute | solution.py:44
  89.7 3.9 %collective-permute-start.41 = (bf16[2,4,64,256]{3,2,1,0:T(8,128)(2,1)S(1)}, bf16[2,4,64,256]{3,2,1,0:T(8,128)(2,1)S(1)}, u32[]{:S(2)}, u32[]{:S(2)}) collective-permute-start(bf16[2,4,64,256]{3,2,1,0:T(8,128)(2,1)S(1)} %collective-permute-done.37.refs_1_), channel_id=1, source_target_pairs={{0,8},{1,9},{2,10},{3,11},{4,12},{5,13},{6,14},{7,15},{8,0},{9,1},... | collective-permute-start | bytes 786440 | tf_op jit(solution)/shard_map/ppermute | solution.py:44
  90.0 8.5 %collective-permute-start.31 = (bf16[2,4,64,256]{3,2,1,0:T(8,128)(2,1)S(1)}, bf16[2,4,64,256]{3,2,1,0:T(8,128)(2,1)S(1)}, u32[]{:S(2)}, u32[]{:S(2)}) collective-permute-start(bf16[2,4,64,256]{3,2,1,0:T(8,128)(2,1)S(1)} %pad_maximum_fusion.3.refs_2_), channel_id=1, source_target_pairs={{0,1},{1,0},{2,3},{3,2},{4,5},{5,4},{6,7},{7,6},{8,9},{9,8},{10,11... | collective-permute-start | bytes 786440 | tf_op jit(solution)/shard_map/ppermute | solution.py:44
  91.5 8.4 %collective-permute-start.29 = (bf16[2,4,64,256]{3,2,1,0:T(8,128)(2,1)S(1)}, bf16[2,4,64,256]{3,2,1,0:T(8,128)(2,1)S(1)}, u32[]{:S(2)}, u32[]{:S(2)}) collective-permute-start(bf16[2,4,64,256]{3,2,1,0:T(8,128)(2,1)S(1)} %pad_maximum_fusion.2.refs_0_), channel_id=1, source_target_pairs={{0,16},{1,17},{2,18},{3,19},{4,20},{5,21},{6,22},{7,23},{8,24},{9,... | collective-permute-start | bytes 786440 | tf_op jit(solution)/shard_map/ppermute | solution.py:44
  93.1 8.3 %collective-permute-start.45 = (bf16[2,4,64,256]{3,2,1,0:T(8,128)(2,1)S(1)}, bf16[2,4,64,256]{3,2,1,0:T(8,128)(2,1)S(1)}, u32[]{:S(2)}, u32[]{:S(2)}) collective-permute-start(bf16[2,4,64,256]{3,2,1,0:T(8,128)(2,1)S(1)} %pad_maximum_fusion.3.refs_2_), channel_id=1, source_target_pairs={{0,8},{1,9},{2,10},{3,11},{4,12},{5,13},{6,14},{7,15},{8,0},{9,1},... | collective-permute-start | bytes 786440 | tf_op jit(solution)/shard_map/ppermute | solution.py:44
  93.1 8.2 %collective-permute-start.32 = (bf16[2,4,64,256]{3,2,1,0:T(8,128)(2,1)S(1)}, bf16[2,4,64,256]{3,2,1,0:T(8,128)(2,1)S(1)}, u32[]{:S(2)}, u32[]{:S(2)}) collective-permute-start(bf16[2,4,64,256]{3,2,1,0:T(8,128)(2,1)S(1)} %pad_maximum_fusion.2.refs_0_), channel_id=1, source_target_pairs={{0,8},{1,9},{2,10},{3,11},{4,12},{5,13},{6,14},{7,15},{8,0},{9,1},... | collective-permute-start | bytes 786440 | tf_op jit(solution)/shard_map/ppermute | solution.py:44
  99.9 1.5 %collective-permute-start.44 = (bf16[2,4,64,256]{3,2,1,0:T(8,128)(2,1)S(1)}, bf16[2,4,64,256]{3,2,1,0:T(8,128)(2,1)S(1)}, u32[]{:S(2)}, u32[]{:S(2)}) collective-permute-start(bf16[2,4,64,256]{3,2,1,0:T(8,128)(2,1)S(1)} %collective-permute-done.29.refs_1_), channel_id=1, source_target_pairs={{0,8},{1,9},{2,10},{3,11},{4,12},{5,13},{6,14},{7,15},{8,0},{9,1},... | collective-permute-start | bytes 786440 | tf_op jit(solution)/shard_map/ppermute | solution.py:44
  99.9 1.9 %collective-permute-start.46 = (bf16[2,4,64,256]{3,2,1,0:T(8,128)(2,1)S(1)}, bf16[2,4,64,256]{3,2,1,0:T(8,128)(2,1)S(1)}, u32[]{:S(2)}, u32[]{:S(2)}) collective-permute-start(bf16[2,4,64,256]{3,2,1,0:T(8,128)(2,1)S(1)} %collective-permute-done.31.refs_3_), channel_id=1, source_target_pairs={{0,8},{1,9},{2,10},{3,11},{4,12},{5,13},{6,14},{7,15},{8,0},{9,1},... | collective-permute-start | bytes 786440 | tf_op jit(solution)/shard_map/ppermute | solution.py:44
  (5 other events, 119.3 us)

commit v4 on v3

--- a/solution.py
+++ b/solution.py
@@ -13,6 +13,7 @@
 AXES = ("aa", "ba")
 BF16 = jnp.bfloat16
 F32 = jnp.float32
+LANES = 128
 LARGE = 60 * 1024 * 1024
 SMALL = 24 * 1024 * 1024
 
@@ -29,8 +30,10 @@
         a, b = lax.axis_index("aa"), lax.axis_index("ba")
         inner = self.size["c"] if axis in "xc" else self.size["y"]
         index = a if axis in "xc" else b
-        at = lax.div(index, inner) if axis in "xz" else lax.rem(index, inner)
-        return lax.rem(at + step % self.size[axis], self.size[axis]) if step else at
+        return self.partner(axis, lax.div(index, inner) if axis in "xz" else lax.rem(index, inner), step)
+
+    def partner(self, axis, at, step):
+        return at ^ step if step else at
 
     def send(self, value, **steps):
         pairs = []
@@ -39,7 +42,7 @@
                 for z in range(self.size["z"]):
                     for y in range(self.size["y"]):
                         here = {"x": x, "c": c, "z": z, "y": y}
-                        there = {k: (v + steps.get(k, 0)) % self.size[k] for k, v in here.items()}
+                        there = {k: int(self.partner(k, v, steps.get(k, 0))) for k, v in here.items()}
                         pairs.append((self.index(here), self.index(there)))
         return lax.ppermute(value, AXES, pairs)
 
@@ -192,11 +195,10 @@
     yield total
 
 
-def sum_everywhere(grid, value):
-    value = value + grid.send(value, c=1)
-    plane = [(kx, ky) for kx in range(grid.size["x"]) for ky in range(grid.size["y"]) if kx + ky]
-    value = sum([grid.send(value, x=kx, y=ky) for kx, ky in plane], value)
-    return sum([grid.send(value, z=k) for k in range(1, grid.size["z"])], value)
+def sum_everywhere(value):
+    count = lax.axis_size("aa") * lax.axis_size("ba")
+    terms = lax.all_to_all(jnp.broadcast_to(value, (count, *value.shape)), AXES, 0, 0, tiled=True)
+    return jnp.sum(terms, axis=(0, 2))
 
 
 def moments(clipped, first, second):
@@ -239,56 +241,69 @@
     return [[grid.send(next(flat), **steps) for _, steps in sends] for sends in wanted], values
 
 
-def project_kernel(grid, orders, rows, finish, tokens, *refs):
+def project_kernel(grid, orders, rows, halves, finish, *refs):
     refs = list(refs)
-    size = grid.size
-    pieces = [[[refs.pop(0) for _ in range(size[order[0]])] for order in orders] for _ in range(2)]
-    gate = refs.pop(0) if finish else None
+    nx, ny, nz = (grid.size[axis] for axis in "xyz")
+    tokens = refs.pop(0)
+    places = [(h, kc) for h, half in enumerate(halves) for kc in half]
+    pieces = [[[refs.pop(0) for _ in range(grid.size[order[0]])] for order in orders] for _ in places]
+    earlier = refs.pop(0) if finish else None
     out, held = refs
     width = out.shape[1] // len(orders)
+    block = nz * ny * rows
 
     @pl.when(pl.program_id(0) == 0)
     def _():
-        for kc in range(2):
-            for kx in range(size["x"]):
-                for ky in range(size["y"]):
-                    for kz in range(size["z"]):
-                        at = grid.here("x", -kx) * 2 + grid.here("c", kc)
-                        at = (at * size["z"] + grid.here("z", -kz)) * size["y"] + grid.here("y", -ky)
+        for i in range(len(places)):
+            for kx in range(nx):
+                for ky in range(ny):
+                    for kz in range(nz):
+                        at = (grid.here("x", kx) * nz + grid.here("z", kz)) * ny + grid.here("y", ky)
                         start = pl.multiple_of(at * rows, rows)
                         for s, order in enumerate(orders):
                             one, two = (kx, ky) if order == "xy" else (ky, kx)
-                            held[pl.ds(start, rows), s * width : (s + 1) * width] = pieces[kc][s][one][
+                            held[i, pl.ds(start, rows), s * width : (s + 1) * width] = pieces[i][s][one][
                                 two, kz
                             ].astype(held.dtype)
 
-    value = jnp.dot(tokens[...], held[...].astype(BF16), preferred_element_type=F32)
+    tile = pl.ds(pl.multiple_of(pl.program_id(0) * out.shape[0], out.shape[0]), out.shape[0])
+    totals = [earlier[tile, :], None] if finish else [None]
+    for i, (h, kc) in enumerate(places):
+        for x in range(nx):
+            weight = held[i, x * block : (x + 1) * block, :].astype(BF16)
+            term = jnp.dot(tokens[tile, column_block(grid, x, kc, block)], weight, preferred_element_type=F32)
+            totals[h] = term if totals[h] is None else totals[h] + term
+    value = totals[0]
     if finish:
-        before = gate[...]
-        value = before / (1.0 + jnp.exp(-before)) * value
+        value = value / (1.0 + jnp.exp(-value)) * totals[1]
     out[...] = value.astype(out.dtype)
 
 
-def project(grid, tokens, pieces, orders, gate=None):
+def project(grid, tokens, halves, orders, earlier=None):
     count, depth = tokens.shape
-    rows, width = pieces[0][0][0].shape[-2:]
+    nx = grid.size["x"]
+    block = depth // (nx * 2)
+    flat = [piece for half in halves for table in half.values() for part in table for piece in part]
+    rows, width = flat[0].shape[-2:]
     width *= len(orders)
-    tile = min(count, 256)
+    tile = min(count, 512)
     held = BF16 if rows % 16 == 0 else F32
-    flat = [piece for core in pieces for part in core for piece in part]
+    finish = earlier is not None
+    keys = [tuple(half) for half in halves]
+
     tiled = pl.BlockSpec((tile, width), lambda t: (t, 0))
-    finish = gate is not None
+    places = sum(len(key) for key in keys)
     return pl.pallas_call(
-        functools.partial(project_kernel, grid, orders, rows, finish),
+        functools.partial(project_kernel, grid, orders, rows, keys, finish),
         out_shape=jax.ShapeDtypeStruct((count, width), BF16 if finish else F32),
         grid=(count // tile,),
-        in_specs=[pl.BlockSpec((tile, depth), lambda t: (t, 0))]
-        + [pl.BlockSpec(memory_space=pltpu.VMEM)] * len(flat)
-        + ([tiled] if finish else []),
+        in_specs=[pl.BlockSpec(memory_space=pltpu.VMEM)] * (1 + len(flat) + finish),
         out_specs=tiled,
-        scratch_shapes=[pltpu.VMEM((depth, width), held)],
-        **kernel_params(2 * count * depth * width, count * depth * 2 + count * width * 8, SMALL),
-    )(tokens, *flat, *([gate] if finish else []))
+        scratch_shapes=[pltpu.VMEM((places, nx * block, width), held)],
+        **kernel_params(
+            2 * count * nx * block * places * width, count * depth * 2 + count * width * 8, SMALL
+        ),
+    )(tokens, *flat, *([earlier] if finish else []))
 
 
 def shards(tokens, grad_out, master_weight, first_moment, second_moment, next_tokens):
@@ -312,8 +327,8 @@
         (came_in,), values = stage(grid, [next(way)], (yield))
         yield values
         grad = way.send(came_in)
-        square = yield jnp.sum(grad * grad, axis=0).reshape(-1, 128)
-        clipped = grad * clip_factor(square)
+        factor = yield jnp.sum((grad * grad).reshape(grad.shape[0], -1, LANES), axis=(0, 1))
+        clipped = grad * factor
         state = [value[:, columns] for value in (master_weight, first_moment, second_moment)]
         low = adam(clipped, *state)
         low, clipped = lax.optimization_barrier((low, clipped))
@@ -330,10 +345,10 @@
             wanted = [way.send(got) for way, got in zip(ways, came_in)]
         own = wanted
         early = [[grid.send(part[0], c=1)] for part in own]
-        after = yield new
+        after = yield new, own
         last, _ = stage(grid, [[(piece, {"c": 1}) for piece in part[1:]] for part in own], after)
         other = [a + b for a, b in zip(early, last)]
-        yield own, other
+        yield other
 
     ways = [section(0), section(1)]
 
@@ -345,15 +360,17 @@
 
     run(3)
     squares = [next(way) for way in ways]
-    squares = sum_everywhere(grid, jnp.stack(squares))
+    factors = clip_factor(sum_everywhere(jnp.stack(squares)))
+    factors = lax.optimization_barrier(jnp.broadcast_to(factors[:, None, None], (2, 1, half)))
     for s in (0, 1):
-        ways[s].send(jnp.sum(squares[s]))
+        ways[s].send(factors[s])
     run(3)
-    news = [next(way) for way in ways]
-    gate = project(grid, next_tokens, ways[0].send([]), orders)
-    next_hidden = project(grid, next_tokens, ways[1].send([gate]), orders, gate)
-    new_first, new_second = (jnp.concatenate([news[0][k], news[1][k]], axis=1) for k in (0, 1))
-    return new_first, new_second, next_hidden
+    news, own = zip(*[next(way) for way in ways])
+    new = [jnp.concatenate([news[0][k], news[1][k]], axis=1) for k in (0, 1)]
+    gate = project(grid, next_tokens, [{0: own[0]}], orders)
+    other = [ways[0].send([]), ways[1].send([gate])]
+    halves = [{1: other[0]}, {0: own[1], 1: other[1]}]
+    return *new, project(grid, next_tokens, halves, orders, gate)
 
 
 def solution(mesh):

time: 106 us -> 101 us (0.953)
  blocking collectives: 0 us -> 11 us
  waiting for transfers between devices: 38.2 us -> 31.2 us
  starting transfers between devices: 47.6 us -> 41.4 us
  between operations: 2.39 us -> 0.97 us
    all_to_all x0 -> x1, blocking collectives: none -> 11 us  [sum_everywhere(): lax.all_to_all(jnp.broadcast_to(value, (count, *value.shape)), AXES, 0, 0...]
    ppermute x47 -> x40, waiting for transfers between devices: 38.2 us -> 31.2 us  [send(): return lax.ppermute(value, AXES, pairs)]
    ppermute x47 -> x40, starting transfers between devices: 47.6 us -> 41.4 us  [send(): return lax.ppermute(value, AXES, pairs)]
  transfers between devices with their start and end apart: 47 -> 40, of which waited for: 28 -> 19; matrix products, arithmetic and copies ran while one was open for 2% -> 2% of each run, Pallas kernels for 3% -> 1%
where the time goes in v4:
time: 101 us
  starting transfers between devices  41.4 us (41%)
  waiting for transfers between devices  31.2 us (31%)
  Pallas kernels  14.1 us (14%)
  blocking collectives  11 us (11%)
  other arithmetic  2.06 us (2%)
    ppermute x40, starting transfers between devices, send(): return lax.ppermute(value, AXES, pairs)  41.4 us
    ppermute x40, waiting for transfers between devices, send(): return lax.ppermute(value, AXES, pairs)  31.2 us
    all_to_all x1, blocking collectives, sum_everywhere(): lax.all_to_all(jnp.broadcast_to(value, (count, *value.shape)), AXES, 0, 0...  11 us
    pallas_call x2, Pallas kernels, project(): pl.pallas_call(functools.partial(project_kernel, grid, orders, rows, keys...  6.26 us
    pallas_call x1, Pallas kernels, sent_rows(): pl.pallas_call(functools.partial(sent_kernel, grid), out_shape=[jax.Shape...  4.59 us
    pallas_call x1, Pallas kernels, kept_rows(): pl.pallas_call(functools.partial(kept_kernel, grid, orders, block_rows),...  3.24 us
  transfers between devices with their start and end apart: 40, of which 19 were waited for; matrix products, arithmetic and copies ran while one was open for 2% of the time, Pallas kernels for 1%

profile of v4, /device:TPU:0, one launch (start us, length us, event | category | flops | bytes accessed | tf_op | source)
XLA Modules:
  0.0 101.1 jit_solution(1714605546331337690)
XLA Ops:
  0.6 4.6 %shard_map.85 = (bf16[1024,256]{1,0:T(8,128)(2,1)S(1)}, bf16[1024,256]{1,0:T(8,128)(2,1)S(1)}, bf16[1024,256]{1,0:T(8,128)(2,1)S(1)}, bf16[1024,256]{1,0:T(8,128)(2,1)S(1)}) custom-call(bf16[1024,2048]{1,0:T(8,128)(2,1)} %tokens.1, bf16[1024,1024]{1,0:T(8,128)(2,1)} %cot.1), custom_call_target="tpu_custom_call" | custom-call | flops 2147483648 | bytes 4194304 | tf_op jit(solution)/shard_map/pallas_call | solution.py:95
  5.2 0.5 collective-permute-start
  6.4 0.9 collective-permute-done.refs_0_
  7.3 0.7 collective-permute-done.1.refs_1_
  8.1 0.7 collective-permute-done.2.refs_2_
  8.8 0.7 collective-permute-done.3.refs_3_
  9.6 3.2 %shard_map.86 = (f32[512,256]{1,0:T(8,128)S(1)}, bf16[512,256]{1,0:T(8,128)(2,1)S(1)}, f32[2,4,64,256]{3,2,1,0:T(8,128)S(1)}, bf16[2,4,64,256]{3,2,1,0:T(8,128)(...) custom-call(bf16[1024,2048]{1,0:T(8,128)(2,1)S(1)} %copy-done.1, ...), custom_call_target="tpu_custom_call" | custom-call | flops 2147483648 | bytes 4194304 | tf_op jit(solution)/shard_map/pallas_call | solution.py:150
  12.8 2.9 %collective-permute-start.11 = (bf16[4,2,64,256]{3,2,0,1:T(8,128)(2,1)S(1)}, bf16[4,2,64,256]{3,2,0,1:T(8,128)(2,1)S(1)}, u32[]{:S(2)}, u32[]{:S(2)}) collective-permute-start(bf16[4,2,64,256]{3,2,0,1:T(8,128)(2,1)S(1)} %copy.19), channel_id=1, source_target_pairs={{0,16},{1,17},{2,18},{3,19},{4,20},{5,21},{6,22},{7,23},{8,24},{9,... | collective-permute-start | bytes 786440 | tf_op jit(solution)/shard_map/ppermute | solution.py:47
  15.8 1.5 %collective-permute-start.13 = (bf16[2,4,64,256]{3,2,1,0:T(8,128)(2,1)S(1)}, bf16[2,4,64,256]{3,2,1,0:T(8,128)(2,1)S(1)}, u32[]{:S(2)}, u32[]{:S(2)}) collective-permute-start(bf16[2,4,64,256]{3,2,1,0:T(8,128)(2,1)S(1)} %get-tuple-element.32), channel_id=1, source_target_pairs={{0,1},{1,0},{2,3},{3,2},{4,5},{5,4},{6,7},{7,6},{8,9},{9,8},{10,11... | collective-permute-start | bytes 786440 | tf_op jit(solution)/shard_map/ppermute | solution.py:47
  17.3 0.6 collective-permute-start.4
  18.0 4.9 %collective-permute-done.11 = bf16[4,2,64,256]{3,2,0,1:T(8,128)(2,1)S(1)} collective-permute-done((bf16[4,2,64,256]{3,2,0,1:T(8,128)(2,1)S(1)}, bf16[4,2,64,256]{3,2,0,1:T(8,128)(2,1)S(1)}, u32[]{:S(2)}, u32[]{:S(2)}) %collective-permute-start.11) | collective-permute-done | bytes 262176 | tf_op jit(solution)/shard_map/ppermute | solution.py:47
  22.9 2.2 %collective-permute-start.12 = (bf16[4,64,256]{2,1,0:T(8,128)(2,1)S(1)}, bf16[4,64,256]{2,1,0:T(8,128)(2,1)S(1)}, u32[]{:S(2)}, u32[]{:S(2)}) collective-permute-start(bf16[4,64,256]{2,1,0:T(8,128)(2,1)S(1)} %fusion.16), channel_id=1, source_target_pairs={{0,1},{1,0},{2,3},{3,2},{4,5},{5,4},{6,7},{7,6},{8,9},{9,8},{10,11... | collective-permute-start | bytes 393224 | tf_op jit(solution)/shard_map/ppermute | solution.py:47
  25.2 1.6 %collective-permute-start.14 = (bf16[4,64,256]{2,1,0:T(8,128)(2,1)S(1)}, bf16[4,64,256]{2,1,0:T(8,128)(2,1)S(1)}, u32[]{:S(2)}, u32[]{:S(2)}) collective-permute-start(bf16[4,64,256]{2,1,0:T(8,128)(2,1)S(1)} %fusion.17), channel_id=1, source_target_pairs={{0,16},{1,17},{2,18},{3,19},{4,20},{5,21},{6,22},{7,23},{8,24},{9,... | collective-permute-start | bytes 393224 | tf_op jit(solution)/shard_map/ppermute | solution.py:47
  26.8 1.7 %collective-permute-done.4 = bf16[4,2,64,256]{3,2,0,1:T(8,128)(2,1)S(1)} collective-permute-done((bf16[4,2,64,256]{3,2,0,1:T(8,128)(2,1)S(1)}, bf16[4,2,64,256]{3,2,0,1:T(8,128)(2,1)S(1)}, u32[]{:S(2)}, u32[]{:S(2)}) %collective-permute-start.4) | collective-permute-done | bytes 262176 | tf_op jit(solution)/shard_map/ppermute | solution.py:47
  28.6 2.2 %collective-permute-start.5 = (bf16[4,64,256]{2,1,0:T(8,128)(2,1)S(1)}, bf16[4,64,256]{2,1,0:T(8,128)(2,1)S(1)}, u32[]{:S(2)}, u32[]{:S(2)}) collective-permute-start(bf16[4,64,256]{2,1,0:T(8,128)(2,1)S(1)} %fusion.14), channel_id=1, source_target_pairs={{0,1},{1,0},{2,3},{3,2},{4,5},{5,4},{6,7},{7,6},{8,9},{9,8},{10,11... | collective-permute-start | bytes 393224 | tf_op jit(solution)/shard_map/ppermute | solution.py:47
  30.9 1.6 %collective-permute-start.7 = (bf16[4,64,256]{2,1,0:T(8,128)(2,1)S(1)}, bf16[4,64,256]{2,1,0:T(8,128)(2,1)S(1)}, u32[]{:S(2)}, u32[]{:S(2)}) collective-permute-start(bf16[4,64,256]{2,1,0:T(8,128)(2,1)S(1)} %fusion.15), channel_id=1, source_target_pairs={{0,16},{1,17},{2,18},{3,19},{4,20},{5,21},{6,22},{7,23},{8,24},{9,... | collective-permute-start | bytes 393224 | tf_op jit(solution)/shard_map/ppermute | solution.py:47
  32.4 0.9 collective-permute-done.12
  33.5 1.6 %collective-permute-start.15 = (bf16[64,512]{1,0:T(8,128)(2,1)S(1)}, bf16[64,512]{1,0:T(8,128)(2,1)S(1)}, u32[]{:S(2)}, u32[]{:S(2)}) collective-permute-start(bf16[64,512]{1,0:T(8,128)(2,1)S(1)} %get-tuple-element.52), channel_id=1, source_target_pairs={{0,2},{1,3},{2,0},{3,1},{4,6},{5,7},{6,4},{7,5},{8,10},{9,11},{10,... | collective-permute-start | bytes 196616 | tf_op jit(solution)/shard_map/ppermute | solution.py:47
  35.1 2.6 %collective-permute-start.16 = (bf16[64,512]{1,0:T(8,128)(2,1)S(1)}, bf16[64,512]{1,0:T(8,128)(2,1)S(1)}, u32[]{:S(2)}, u32[]{:S(2)}) collective-permute-start(bf16[64,512]{1,0:T(8,128)(2,1)S(1)} %get-tuple-element.53), channel_id=1, source_target_pairs={{0,4},{1,5},{2,6},{3,7},{4,0},{5,1},{6,2},{7,3},{8,12},{9,13},{10,... | collective-permute-start | bytes 196616 | tf_op jit(solution)/shard_map/ppermute | solution.py:47
  38.1 3.7 %collective-permute-start.10 = (bf16[64,512]{1,0:T(8,128)(2,1)S(1)}, bf16[64,512]{1,0:T(8,128)(2,1)S(1)}, u32[]{:S(2)}, u32[]{:S(2)}) collective-permute-start(bf16[64,512]{1,0:T(8,128)(2,1)S(1)} %get-tuple-element.51), channel_id=1, source_target_pairs={{0,6},{1,7},{2,4},{3,5},{4,2},{5,3},{6,0},{7,1},{8,14},{9,15},{10,... | collective-permute-start | bytes 196616 | tf_op jit(solution)/shard_map/ppermute | solution.py:47
  41.7 0.8 collective-permute-start.9
  42.7 1.8 %collective-permute-done.17 = bf16[64,512]{1,0:T(8,128)(2,1)S(1)} collective-permute-done((bf16[64,512]{1,0:T(8,128)(2,1)S(1)}, bf16[64,512]{1,0:T(8,128)(2,1)S(1)}, u32[]{:S(2)}, u32[]{:S(2)}) %collective-permute-start.17) | collective-permute-done | bytes 65568 | tf_op jit(solution)/shard_map/ppermute | solution.py:47
  44.6 0.7 collective-permute-done.10
  45.3 0.9 collective-permute-done.8
  46.2 1.1 %collective-permute-done.9 = bf16[64,512]{1,0:T(8,128)(2,1)S(1)} collective-permute-done((bf16[64,512]{1,0:T(8,128)(2,1)S(1)}, bf16[64,512]{1,0:T(8,128)(2,1)S(1)}, u32[]{:S(2)}, u32[]{:S(2)}) %collective-permute-start.9) | collective-permute-done | bytes 65568 | tf_op jit(solution)/shard_map/ppermute | solution.py:47
  47.4 11.0 %all_to_all.5 = f32[32,2,128]{2,1,0:T(2,128)S(1)} all-to-all(f32[32,2,128]{2,1,0:T(2,128)S(1)} %broadcast_in_dim.4), channel_id=1, replica_groups=mesh['aa'=4,'ba'=8] {'aa','ba'}, dimensions={0} | all-to-all | bytes 65536 | tf_op jit(solution)/shard_map/all_to_all | solution.py:200
  58.9 0.6 collective-permute-start.18
  59.4 0.7 collective-permute-start.19
  60.1 3.2 %collective-permute-start.20 = (bf16[64,512]{1,0:T(8,128)(2,1)S(1)}, bf16[64,512]{1,0:T(8,128)(2,1)S(1)}, u32[]{:S(2)}, u32[]{:S(2)}) collective-permute-start(bf16[64,512]{1,0:T(8,128)(2,1)S(1)} %get-tuple-element.35), channel_id=1, source_target_pairs={{0,6},{1,7},{2,4},{3,5},{4,2},{5,3},{6,0},{7,1},{8,14},{9,15},{10,... | collective-permute-start | bytes 196616 | tf_op jit(solution)/shard_map/ppermute | solution.py:47
  63.3 1.2 %collective-permute-start.30 = (bf16[64,512]{1,0:T(8,128)(2,1)S(1)}, bf16[64,512]{1,0:T(8,128)(2,1)S(1)}, u32[]{:S(2)}, u32[]{:S(2)}) collective-permute-start(bf16[64,512]{1,0:T(8,128)(2,1)S(1)} %get-tuple-element.36), channel_id=1, source_target_pairs={{0,4},{1,5},{2,6},{3,7},{4,0},{5,1},{6,2},{7,3},{8,12},{9,13},{10,... | collective-permute-start | bytes 196616 | tf_op jit(solution)/shard_map/ppermute | solution.py:47
  64.5 3.3 %collective-permute-start.31 = (bf16[64,512]{1,0:T(8,128)(2,1)S(1)}, bf16[64,512]{1,0:T(8,128)(2,1)S(1)}, u32[]{:S(2)}, u32[]{:S(2)}) collective-permute-start(bf16[64,512]{1,0:T(8,128)(2,1)S(1)} %get-tuple-element.36), channel_id=1, source_target_pairs={{0,6},{1,7},{2,4},{3,5},{4,2},{5,3},{6,0},{7,1},{8,14},{9,15},{10,... | collective-permute-start | bytes 196616 | tf_op jit(solution)/shard_map/ppermute | solution.py:47
  67.8 3.1 %collective-permute-done.19 = bf16[64,512]{1,0:T(8,128)(2,1)S(1)} collective-permute-done((bf16[64,512]{1,0:T(8,128)(2,1)S(1)}, bf16[64,512]{1,0:T(8,128)(2,1)S(1)}, u32[]{:S(2)}, u32[]{:S(2)}) %collective-permute-start.19) | collective-permute-done | bytes 65568 | tf_op jit(solution)/shard_map/ppermute | solution.py:47
  70.9 0.6 collective-permute-start.25
  71.6 0.7 collective-permute-start.21
  72.3 1.0 collective-permute-done.30
  73.3 0.7 collective-permute-start.34
  74.0 3.2 %collective-permute-done.25 = bf16[4,64,256]{2,1,0:T(8,128)(2,1)S(1)} collective-permute-done((bf16[4,64,256]{2,1,0:T(8,128)(2,1)S(1)}, bf16[4,64,256]{2,1,0:T(8,128)(2,1)S(1)}, u32[]{:S(2)}, u32[]{:S(2)}) %collective-permute-start.25) | collective-permute-done | bytes 131104 | tf_op jit(solution)/shard_map/ppermute | solution.py:47
  77.3 0.7 collective-permute-start.27
  78.1 1.5 %collective-permute-start.23 = (bf16[2,4,64,256]{3,2,1,0:T(8,128)(2,1)S(1)}, bf16[2,4,64,256]{3,2,1,0:T(8,128)(2,1)S(1)}, u32[]{:S(2)}, u32[]{:S(2)}) collective-permute-start(bf16[2,4,64,256]{3,2,1,0:T(8,128)(2,1)S(1)} %pad_maximum_fusion.2.refs_1_), channel_id=1, source_target_pairs={{0,16},{1,17},{2,18},{3,19},{4,20},{5,21},{6,22},{7,23},{8,24},{9,... | collective-permute-start | bytes 786440 | tf_op jit(solution)/shard_map/ppermute | solution.py:47
  79.6 0.7 collective-permute-start.32
  80.3 1.4 %collective-permute-start.35 = (bf16[2,4,64,256]{3,2,1,0:T(8,128)(2,1)S(1)}, bf16[2,4,64,256]{3,2,1,0:T(8,128)(2,1)S(1)}, u32[]{:S(2)}, u32[]{:S(2)}) collective-permute-start(bf16[2,4,64,256]{3,2,1,0:T(8,128)(2,1)S(1)} %pad_maximum_fusion.5.refs_7_), channel_id=1, source_target_pairs={{0,1},{1,0},{2,3},{3,2},{4,5},{5,4},{6,7},{7,6},{8,9},{9,8},{10,11... | collective-permute-start | bytes 786440 | tf_op jit(solution)/shard_map/ppermute | solution.py:47
  81.7 5.4 %collective-permute-done.32 = bf16[4,64,256]{2,1,0:T(8,128)(2,1)S(1)} collective-permute-done((bf16[4,64,256]{2,1,0:T(8,128)(2,1)S(1)}, bf16[4,64,256]{2,1,0:T(8,128)(2,1)S(1)}, u32[]{:S(2)}, u32[]{:S(2)}) %collective-permute-start.32) | collective-permute-done | bytes 131104 | tf_op jit(solution)/shard_map/ppermute | solution.py:47
  87.2 1.4 %collective-permute-start.33 = (bf16[2,4,64,256]{3,2,1,0:T(8,128)(2,1)S(1)}, bf16[2,4,64,256]{3,2,1,0:T(8,128)(2,1)S(1)}, u32[]{:S(2)}, u32[]{:S(2)}) collective-permute-start(bf16[2,4,64,256]{3,2,1,0:T(8,128)(2,1)S(1)} %pad_maximum_fusion.4.refs_5_), channel_id=1, source_target_pairs={{0,16},{1,17},{2,18},{3,19},{4,20},{5,21},{6,22},{7,23},{8,24},{9,... | collective-permute-start | bytes 786440 | tf_op jit(solution)/shard_map/ppermute | solution.py:47
  88.6 0.5 collective-permute-start.36
  89.2 1.5 %shard_map.87.refs_13_ = f32[1024,512]{1,0:T(8,128)S(1)} custom-call(bf16[1024,2048]{1,0:T(8,128)(2,1)S(1)} %copy-done, bf16[2,4,64,256]{3,2,1,0:T(8,128)(2,1)S(1)} %pad_maximum_fusion.2.refs_1_, bf16[2,4,64,256]{3,2,1,0:T(8,128)(2,1)S(1)} %collective-permute-done.23.refs_2_, bf16[2,4,64,256]{3,2,1,0:T(8,128)(2,1)S(1)} %pad_maximum_fusion.3.refs_3_, ...), custom_call_target="tpu_custom_call" | custom-call | flops 1073741824 | bytes 8388608 | tf_op jit(solution)/shard_map/pallas_call | solution.py:296
  91.2 2.4 %collective-permute-done.33.refs_6_ = bf16[2,4,64,256]{3,2,1,0:T(8,128)(2,1)S(1)} collective-permute-done((bf16[2,4,64,256]{3,2,1,0:T(8,128)(2,1)S(1)}, bf16[2,4,64,256]{3,2,1,0:T(8,128)(2,1)S(1)}, u32[]{:S(2)}, u32[]{:S(2)}) %collective-permute-start.33) | collective-permute-done | bytes 262176 | tf_op jit(solution)/shard_map/ppermute | solution.py:47
  94.8 0.8 pad_maximum_fusion
  96.3 4.7 %shard_map.88 = bf16[1024,512]{1,0:T(8,128)(2,1)} custom-call(bf16[1024,2048]{1,0:T(8,128)(2,1)S(1)} %copy-done, bf16[2,4,64,256]{3,2,1,0:T(8,128)(2,1)S(1)} %collective-permute-done.22.refs_1_, bf16[2,4,64,256]{3,2,1,0:T(8,128)(2,1)S(1)} %collective-permute-done.24.refs_2_, bf16[2,4,64,256]{3,2,1,0:T(8,128)(2,1)S(1)} %collective-permute-done.26.refs_3_, ...), custom_call_target="tpu_custom_call" | custom-call | flops 3221225472 | bytes 8388608 | tf_op jit(solution)/shard_map/pallas_call | solution.py:296
  (94 shorter events, 4.9 us)
Async XLA Ops:
  0.6 8.9 %copy-start.1 = (bf16[1024,2048]{1,0:T(8,128)(2,1)S(1)}, bf16[1024,2048]{1,0:T(8,128)(2,1)}, u32[]{:S(2)}) copy-start(bf16[1024,2048]{1,0:T(8,128)(2,1)} %tokens.1) | copy-start | bytes 12582916
  0.6 8.9 %copy-start.2 = (bf16[1024,1024]{1,0:T(8,128)(2,1)S(1)}, bf16[1024,1024]{1,0:T(8,128)(2,1)}, u32[]{:S(2)}) copy-start(bf16[1024,1024]{1,0:T(8,128)(2,1)} %cot.1) | copy-start | bytes 6291460
  5.2 2.1 %collective-permute-start = (bf16[1024,256]{1,0:T(8,128)(2,1)S(1)}, bf16[1024,256]{1,0:T(8,128)(2,1)S(1)}, u32[]{:S(2)}, u32[]{:S(2)}) collective-permute-start(bf16[1024,256]{1,0:T(8,128)(2,1)S(1)} %get-tuple-element.21), channel_id=1, source_target_pairs={{0,8},{1,9},{2,10},{3,11},{4,12},{5,13},{6,14},{7,15},{8,0},{9,1},... | collective-permute-start | bytes 1572872 | tf_op jit(solution)/shard_map/ppermute | solution.py:47
  5.8 2.3 %collective-permute-start.1 = (bf16[1024,256]{1,0:T(8,128)(2,1)S(1)}, bf16[1024,256]{1,0:T(8,128)(2,1)S(1)}, u32[]{:S(2)}, u32[]{:S(2)}) collective-permute-start(bf16[1024,256]{1,0:T(8,128)(2,1)S(1)} %get-tuple-element.22), channel_id=1, source_target_pairs={{0,8},{1,9},{2,10},{3,11},{4,12},{5,13},{6,14},{7,15},{8,0},{9,1},... | collective-permute-start | bytes 1572872 | tf_op jit(solution)/shard_map/ppermute | solution.py:47
  5.8 3.0 %collective-permute-start.2 = (bf16[1024,256]{1,0:T(8,128)(2,1)S(1)}, bf16[1024,256]{1,0:T(8,128)(2,1)S(1)}, u32[]{:S(2)}, u32[]{:S(2)}) collective-permute-start(bf16[1024,256]{1,0:T(8,128)(2,1)S(1)} %get-tuple-element.23), channel_id=1, source_target_pairs={{0,8},{1,9},{2,10},{3,11},{4,12},{5,13},{6,14},{7,15},{8,0},{9,1},... | collective-permute-start | bytes 1572872 | tf_op jit(solution)/shard_map/ppermute | solution.py:47
  6.3 3.3 %collective-permute-start.3 = (bf16[1024,256]{1,0:T(8,128)(2,1)S(1)}, bf16[1024,256]{1,0:T(8,128)(2,1)S(1)}, u32[]{:S(2)}, u32[]{:S(2)}) collective-permute-start(bf16[1024,256]{1,0:T(8,128)(2,1)S(1)} %get-tuple-element.24), channel_id=1, source_target_pairs={{0,8},{1,9},{2,10},{3,11},{4,12},{5,13},{6,14},{7,15},{8,0},{9,1},... | collective-permute-start | bytes 1572872 | tf_op jit(solution)/shard_map/ppermute | solution.py:47
  12.8 10.0 %collective-permute-start.11 = (bf16[4,2,64,256]{3,2,0,1:T(8,128)(2,1)S(1)}, bf16[4,2,64,256]{3,2,0,1:T(8,128)(2,1)S(1)}, u32[]{:S(2)}, u32[]{:S(2)}) collective-permute-start(bf16[4,2,64,256]{3,2,0,1:T(8,128)(2,1)S(1)} %copy.19), channel_id=1, source_target_pairs={{0,16},{1,17},{2,18},{3,19},{4,20},{5,21},{6,22},{7,23},{8,24},{9,... | collective-permute-start | bytes 786440 | tf_op jit(solution)/shard_map/ppermute | solution.py:47
  15.8 9.4 %collective-permute-start.13 = (bf16[2,4,64,256]{3,2,1,0:T(8,128)(2,1)S(1)}, bf16[2,4,64,256]{3,2,1,0:T(8,128)(2,1)S(1)}, u32[]{:S(2)}, u32[]{:S(2)}) collective-permute-start(bf16[2,4,64,256]{3,2,1,0:T(8,128)(2,1)S(1)} %get-tuple-element.32), channel_id=1, source_target_pairs={{0,1},{1,0},{2,3},{3,2},{4,5},{5,4},{6,7},{7,6},{8,9},{9,8},{10,11... | collective-permute-start | bytes 786440 | tf_op jit(solution)/shard_map/ppermute | solution.py:47
  17.3 11.1 %collective-permute-start.4 = (bf16[4,2,64,256]{3,2,0,1:T(8,128)(2,1)S(1)}, bf16[4,2,64,256]{3,2,0,1:T(8,128)(2,1)S(1)}, u32[]{:S(2)}, u32[]{:S(2)}) collective-permute-start(bf16[4,2,64,256]{3,2,0,1:T(8,128)(2,1)S(1)} %copy.17), channel_id=1, source_target_pairs={{0,16},{1,17},{2,18},{3,19},{4,20},{5,21},{6,22},{7,23},{8,24},{9,... | collective-permute-start | bytes 786440 | tf_op jit(solution)/shard_map/ppermute | solution.py:47
  17.9 12.9 %collective-permute-start.6 = (bf16[2,4,64,256]{3,2,1,0:T(8,128)(2,1)S(1)}, bf16[2,4,64,256]{3,2,1,0:T(8,128)(2,1)S(1)}, u32[]{:S(2)}, u32[]{:S(2)}) collective-permute-start(bf16[2,4,64,256]{3,2,1,0:T(8,128)(2,1)S(1)} %get-tuple-element.28), channel_id=1, source_target_pairs={{0,1},{1,0},{2,3},{3,2},{4,5},{5,4},{6,7},{7,6},{8,9},{9,8},{10,11... | collective-permute-start | bytes 786440 | tf_op jit(solution)/shard_map/ppermute | solution.py:47
  22.9 10.4 %collective-permute-start.12 = (bf16[4,64,256]{2,1,0:T(8,128)(2,1)S(1)}, bf16[4,64,256]{2,1,0:T(8,128)(2,1)S(1)}, u32[]{:S(2)}, u32[]{:S(2)}) collective-permute-start(bf16[4,64,256]{2,1,0:T(8,128)(2,1)S(1)} %fusion.16), channel_id=1, source_target_pairs={{0,1},{1,0},{2,3},{3,2},{4,5},{5,4},{6,7},{7,6},{8,9},{9,8},{10,11... | collective-permute-start | bytes 393224 | tf_op jit(solution)/shard_map/ppermute | solution.py:47
  25.2 8.2 %collective-permute-start.14 = (bf16[4,64,256]{2,1,0:T(8,128)(2,1)S(1)}, bf16[4,64,256]{2,1,0:T(8,128)(2,1)S(1)}, u32[]{:S(2)}, u32[]{:S(2)}) collective-permute-start(bf16[4,64,256]{2,1,0:T(8,128)(2,1)S(1)} %fusion.17), channel_id=1, source_target_pairs={{0,16},{1,17},{2,18},{3,19},{4,20},{5,21},{6,22},{7,23},{8,24},{9,... | collective-permute-start | bytes 393224 | tf_op jit(solution)/shard_map/ppermute | solution.py:47
  28.5 30.1 %copy-start.3 = (f32[64,1024]{1,0:T(8,128)S(1)}, f32[64,1024]{1,0:T(8,128)}, u32[]{:S(2)}) copy-start(f32[64,1024]{1,0:T(8,128)} %param.9) | copy-start | bytes 786436
  28.5 30.1 %copy-start.4 = (f32[64,1024]{1,0:T(8,128)S(1)}, f32[64,1024]{1,0:T(8,128)}, u32[]{:S(2)}) copy-start(f32[64,1024]{1,0:T(8,128)} %param.10) | copy-start | bytes 786436
  28.6 30.1 %copy-start.5 = (f32[64,1024]{1,0:T(8,128)S(1)}, f32[64,1024]{1,0:T(8,128)}, u32[]{:S(2)}) copy-start(f32[64,1024]{1,0:T(8,128)} %param.8) | copy-start | bytes 786436
  28.6 9.4 %collective-permute-start.5 = (bf16[4,64,256]{2,1,0:T(8,128)(2,1)S(1)}, bf16[4,64,256]{2,1,0:T(8,128)(2,1)S(1)}, u32[]{:S(2)}, u32[]{:S(2)}) collective-permute-start(bf16[4,64,256]{2,1,0:T(8,128)(2,1)S(1)} %fusion.14), channel_id=1, source_target_pairs={{0,1},{1,0},{2,3},{3,2},{4,5},{5,4},{6,7},{7,6},{8,9},{9,8},{10,11... | collective-permute-start | bytes 393224 | tf_op jit(solution)/shard_map/ppermute | solution.py:47
  30.9 7.1 %collective-permute-start.7 = (bf16[4,64,256]{2,1,0:T(8,128)(2,1)S(1)}, bf16[4,64,256]{2,1,0:T(8,128)(2,1)S(1)}, u32[]{:S(2)}, u32[]{:S(2)}) collective-permute-start(bf16[4,64,256]{2,1,0:T(8,128)(2,1)S(1)} %fusion.15), channel_id=1, source_target_pairs={{0,16},{1,17},{2,18},{3,19},{4,20},{5,21},{6,22},{7,23},{8,24},{9,... | collective-permute-start | bytes 393224 | tf_op jit(solution)/shard_map/ppermute | solution.py:47
  33.5 8.2 %collective-permute-start.15 = (bf16[64,512]{1,0:T(8,128)(2,1)S(1)}, bf16[64,512]{1,0:T(8,128)(2,1)S(1)}, u32[]{:S(2)}, u32[]{:S(2)}) collective-permute-start(bf16[64,512]{1,0:T(8,128)(2,1)S(1)} %get-tuple-element.52), channel_id=1, source_target_pairs={{0,2},{1,3},{2,0},{3,1},{4,6},{5,7},{6,4},{7,5},{8,10},{9,11},{10,... | collective-permute-start | bytes 196616 | tf_op jit(solution)/shard_map/ppermute | solution.py:47
  35.1 7.5 %collective-permute-start.16 = (bf16[64,512]{1,0:T(8,128)(2,1)S(1)}, bf16[64,512]{1,0:T(8,128)(2,1)S(1)}, u32[]{:S(2)}, u32[]{:S(2)}) collective-permute-start(bf16[64,512]{1,0:T(8,128)(2,1)S(1)} %get-tuple-element.53), channel_id=1, source_target_pairs={{0,4},{1,5},{2,6},{3,7},{4,0},{5,1},{6,2},{7,3},{8,12},{9,13},{10,... | collective-permute-start | bytes 196616 | tf_op jit(solution)/shard_map/ppermute | solution.py:47
  37.7 6.8 %collective-permute-start.17 = (bf16[64,512]{1,0:T(8,128)(2,1)S(1)}, bf16[64,512]{1,0:T(8,128)(2,1)S(1)}, u32[]{:S(2)}, u32[]{:S(2)}) collective-permute-start(bf16[64,512]{1,0:T(8,128)(2,1)S(1)} %get-tuple-element.54), channel_id=1, source_target_pairs={{0,6},{1,7},{2,4},{3,5},{4,2},{5,3},{6,0},{7,1},{8,14},{9,15},{10,... | collective-permute-start | bytes 196616 | tf_op jit(solution)/shard_map/ppermute | solution.py:47
  38.1 7.2 %collective-permute-start.10 = (bf16[64,512]{1,0:T(8,128)(2,1)S(1)}, bf16[64,512]{1,0:T(8,128)(2,1)S(1)}, u32[]{:S(2)}, u32[]{:S(2)}) collective-permute-start(bf16[64,512]{1,0:T(8,128)(2,1)S(1)} %get-tuple-element.51), channel_id=1, source_target_pairs={{0,6},{1,7},{2,4},{3,5},{4,2},{5,3},{6,0},{7,1},{8,14},{9,15},{10,... | collective-permute-start | bytes 196616 | tf_op jit(solution)/shard_map/ppermute | solution.py:47
  41.7 4.4 %collective-permute-start.8 = (bf16[64,512]{1,0:T(8,128)(2,1)S(1)}, bf16[64,512]{1,0:T(8,128)(2,1)S(1)}, u32[]{:S(2)}, u32[]{:S(2)}) collective-permute-start(bf16[64,512]{1,0:T(8,128)(2,1)S(1)} %get-tuple-element.49), channel_id=1, source_target_pairs={{0,2},{1,3},{2,0},{3,1},{4,6},{5,7},{6,4},{7,5},{8,10},{9,11},{10,... | collective-permute-start | bytes 196616 | tf_op jit(solution)/shard_map/ppermute | solution.py:47
  41.7 5.5 %collective-permute-start.9 = (bf16[64,512]{1,0:T(8,128)(2,1)S(1)}, bf16[64,512]{1,0:T(8,128)(2,1)S(1)}, u32[]{:S(2)}, u32[]{:S(2)}) collective-permute-start(bf16[64,512]{1,0:T(8,128)(2,1)S(1)} %get-tuple-element.50), channel_id=1, source_target_pairs={{0,4},{1,5},{2,6},{3,7},{4,0},{5,1},{6,2},{7,3},{8,12},{9,13},{10,... | collective-permute-start | bytes 196616 | tf_op jit(solution)/shard_map/ppermute | solution.py:47
  58.5 30.7 %copy-start = (bf16[1024,2048]{1,0:T(8,128)(2,1)S(1)}, bf16[1024,2048]{1,0:T(8,128)(2,1)}, u32[]{:S(2)}) copy-start(bf16[1024,2048]{1,0:T(8,128)(2,1)} %refs_0_.3) | copy-start | bytes 12582916
  58.9 5.7 %collective-permute-start.18 = (bf16[64,512]{1,0:T(8,128)(2,1)S(1)}, bf16[64,512]{1,0:T(8,128)(2,1)S(1)}, u32[]{:S(2)}, u32[]{:S(2)}) collective-permute-start(bf16[64,512]{1,0:T(8,128)(2,1)S(1)} %get-tuple-element.35), channel_id=1, source_target_pairs={{0,2},{1,3},{2,0},{3,1},{4,6},{5,7},{6,4},{7,5},{8,10},{9,11},{10,... | collective-permute-start | bytes 196616 | tf_op jit(solution)/shard_map/ppermute | solution.py:47
  59.4 11.4 %collective-permute-start.19 = (bf16[64,512]{1,0:T(8,128)(2,1)S(1)}, bf16[64,512]{1,0:T(8,128)(2,1)S(1)}, u32[]{:S(2)}, u32[]{:S(2)}) collective-permute-start(bf16[64,512]{1,0:T(8,128)(2,1)S(1)} %get-tuple-element.35), channel_id=1, source_target_pairs={{0,4},{1,5},{2,6},{3,7},{4,0},{5,1},{6,2},{7,3},{8,12},{9,13},{10,... | collective-permute-start | bytes 196616 | tf_op jit(solution)/shard_map/ppermute | solution.py:47
  60.1 10.7 %collective-permute-start.20 = (bf16[64,512]{1,0:T(8,128)(2,1)S(1)}, bf16[64,512]{1,0:T(8,128)(2,1)S(1)}, u32[]{:S(2)}, u32[]{:S(2)}) collective-permute-start(bf16[64,512]{1,0:T(8,128)(2,1)S(1)} %get-tuple-element.35), channel_id=1, source_target_pairs={{0,6},{1,7},{2,4},{3,5},{4,2},{5,3},{6,0},{7,1},{8,14},{9,15},{10,... | collective-permute-start | bytes 196616 | tf_op jit(solution)/shard_map/ppermute | solution.py:47
  63.3 9.0 %collective-permute-start.29 = (bf16[64,512]{1,0:T(8,128)(2,1)S(1)}, bf16[64,512]{1,0:T(8,128)(2,1)S(1)}, u32[]{:S(2)}, u32[]{:S(2)}) collective-permute-start(bf16[64,512]{1,0:T(8,128)(2,1)S(1)} %get-tuple-element.36), channel_id=1, source_target_pairs={{0,2},{1,3},{2,0},{3,1},{4,6},{5,7},{6,4},{7,5},{8,10},{9,11},{10,... | collective-permute-start | bytes 196616 | tf_op jit(solution)/shard_map/ppermute | solution.py:47
  63.3 10.0 %collective-permute-start.30 = (bf16[64,512]{1,0:T(8,128)(2,1)S(1)}, bf16[64,512]{1,0:T(8,128)(2,1)S(1)}, u32[]{:S(2)}, u32[]{:S(2)}) collective-permute-start(bf16[64,512]{1,0:T(8,128)(2,1)S(1)} %get-tuple-element.36), channel_id=1, source_target_pairs={{0,4},{1,5},{2,6},{3,7},{4,0},{5,1},{6,2},{7,3},{8,12},{9,13},{10,... | collective-permute-start | bytes 196616 | tf_op jit(solution)/shard_map/ppermute | solution.py:47
  64.5 8.8 %collective-permute-start.31 = (bf16[64,512]{1,0:T(8,128)(2,1)S(1)}, bf16[64,512]{1,0:T(8,128)(2,1)S(1)}, u32[]{:S(2)}, u32[]{:S(2)}) collective-permute-start(bf16[64,512]{1,0:T(8,128)(2,1)S(1)} %get-tuple-element.36), channel_id=1, source_target_pairs={{0,6},{1,7},{2,4},{3,5},{4,2},{5,3},{6,0},{7,1},{8,14},{9,15},{10,... | collective-permute-start | bytes 196616 | tf_op jit(solution)/shard_map/ppermute | solution.py:47
  70.9 6.4 %collective-permute-start.25 = (bf16[4,64,256]{2,1,0:T(8,128)(2,1)S(1)}, bf16[4,64,256]{2,1,0:T(8,128)(2,1)S(1)}, u32[]{:S(2)}, u32[]{:S(2)}) collective-permute-start(bf16[4,64,256]{2,1,0:T(8,128)(2,1)S(1)} %get-tuple-element.66), channel_id=1, source_target_pairs={{0,16},{1,17},{2,18},{3,19},{4,20},{5,21},{6,22},{7,23},{8,24},{9,... | collective-permute-start | bytes 393224 | tf_op jit(solution)/shard_map/ppermute | solution.py:47
  71.6 6.5 %collective-permute-start.21 = (bf16[4,64,256]{2,1,0:T(8,128)(2,1)S(1)}, bf16[4,64,256]{2,1,0:T(8,128)(2,1)S(1)}, u32[]{:S(2)}, u32[]{:S(2)}) collective-permute-start(bf16[4,64,256]{2,1,0:T(8,128)(2,1)S(1)} %get-tuple-element.68), channel_id=1, source_target_pairs={{0,1},{1,0},{2,3},{3,2},{4,5},{5,4},{6,7},{7,6},{8,9},{9,8},{10,11... | collective-permute-start | bytes 393224 | tf_op jit(solution)/shard_map/ppermute | solution.py:47
  73.3 6.9 %collective-permute-start.34 = (bf16[4,64,256]{2,1,0:T(8,128)(2,1)S(1)}, bf16[4,64,256]{2,1,0:T(8,128)(2,1)S(1)}, u32[]{:S(2)}, u32[]{:S(2)}) collective-permute-start(bf16[4,64,256]{2,1,0:T(8,128)(2,1)S(1)} %get-tuple-element.62), channel_id=1, source_target_pairs={{0,16},{1,17},{2,18},{3,19},{4,20},{5,21},{6,22},{7,23},{8,24},{9,... | collective-permute-start | bytes 393224 | tf_op jit(solution)/shard_map/ppermute | solution.py:47
  77.3 11.3 %collective-permute-start.27 = (bf16[2,4,64,256]{3,2,1,0:T(8,128)(2,1)S(1)}, bf16[2,4,64,256]{3,2,1,0:T(8,128)(2,1)S(1)}, u32[]{:S(2)}, u32[]{:S(2)}) collective-permute-start(bf16[2,4,64,256]{3,2,1,0:T(8,128)(2,1)S(1)} %pad_maximum_fusion.3.refs_3_), channel_id=1, source_target_pairs={{0,1},{1,0},{2,3},{3,2},{4,5},{5,4},{6,7},{7,6},{8,9},{9,8},{10,11... | collective-permute-start | bytes 786440 | tf_op jit(solution)/shard_map/ppermute | solution.py:47
  78.1 11.1 %collective-permute-start.23 = (bf16[2,4,64,256]{3,2,1,0:T(8,128)(2,1)S(1)}, bf16[2,4,64,256]{3,2,1,0:T(8,128)(2,1)S(1)}, u32[]{:S(2)}, u32[]{:S(2)}) collective-permute-start(bf16[2,4,64,256]{3,2,1,0:T(8,128)(2,1)S(1)} %pad_maximum_fusion.2.refs_1_), channel_id=1, source_target_pairs={{0,16},{1,17},{2,18},{3,19},{4,20},{5,21},{6,22},{7,23},{8,24},{9,... | collective-permute-start | bytes 786440 | tf_op jit(solution)/shard_map/ppermute | solution.py:47
  79.6 7.6 %collective-permute-start.32 = (bf16[4,64,256]{2,1,0:T(8,128)(2,1)S(1)}, bf16[4,64,256]{2,1,0:T(8,128)(2,1)S(1)}, u32[]{:S(2)}, u32[]{:S(2)}) collective-permute-start(bf16[4,64,256]{2,1,0:T(8,128)(2,1)S(1)} %get-tuple-element.64), channel_id=1, source_target_pairs={{0,1},{1,0},{2,3},{3,2},{4,5},{5,4},{6,7},{7,6},{8,9},{9,8},{10,11... | collective-permute-start | bytes 393224 | tf_op jit(solution)/shard_map/ppermute | solution.py:47
  80.3 10.4 %collective-permute-start.35 = (bf16[2,4,64,256]{3,2,1,0:T(8,128)(2,1)S(1)}, bf16[2,4,64,256]{3,2,1,0:T(8,128)(2,1)S(1)}, u32[]{:S(2)}, u32[]{:S(2)}) collective-permute-start(bf16[2,4,64,256]{3,2,1,0:T(8,128)(2,1)S(1)} %pad_maximum_fusion.5.refs_7_), channel_id=1, source_target_pairs={{0,1},{1,0},{2,3},{3,2},{4,5},{5,4},{6,7},{7,6},{8,9},{9,8},{10,11... | collective-permute-start | bytes 786440 | tf_op jit(solution)/shard_map/ppermute | solution.py:47
  87.2 6.4 %collective-permute-start.33 = (bf16[2,4,64,256]{3,2,1,0:T(8,128)(2,1)S(1)}, bf16[2,4,64,256]{3,2,1,0:T(8,128)(2,1)S(1)}, u32[]{:S(2)}, u32[]{:S(2)}) collective-permute-start(bf16[2,4,64,256]{3,2,1,0:T(8,128)(2,1)S(1)} %pad_maximum_fusion.4.refs_5_), channel_id=1, source_target_pairs={{0,16},{1,17},{2,18},{3,19},{4,20},{5,21},{6,22},{7,23},{8,24},{9,... | collective-permute-start | bytes 786440 | tf_op jit(solution)/shard_map/ppermute | solution.py:47
  88.6 5.0 %collective-permute-start.38 = (bf16[2,4,64,256]{3,2,1,0:T(8,128)(2,1)S(1)}, bf16[2,4,64,256]{3,2,1,0:T(8,128)(2,1)S(1)}, u32[]{:S(2)}, u32[]{:S(2)}) collective-permute-start(bf16[2,4,64,256]{3,2,1,0:T(8,128)(2,1)S(1)} %pad_maximum_fusion.5.refs_7_), channel_id=1, source_target_pairs={{0,8},{1,9},{2,10},{3,11},{4,12},{5,13},{6,14},{7,15},{8,0},{9,1},... | collective-permute-start | bytes 786440 | tf_op jit(solution)/shard_map/ppermute | solution.py:47
  88.6 5.5 %collective-permute-start.36 = (bf16[2,4,64,256]{3,2,1,0:T(8,128)(2,1)S(1)}, bf16[2,4,64,256]{3,2,1,0:T(8,128)(2,1)S(1)}, u32[]{:S(2)}, u32[]{:S(2)}) collective-permute-start(bf16[2,4,64,256]{3,2,1,0:T(8,128)(2,1)S(1)} %pad_maximum_fusion.4.refs_5_), channel_id=1, source_target_pairs={{0,8},{1,9},{2,10},{3,11},{4,12},{5,13},{6,14},{7,15},{8,0},{9,1},... | collective-permute-start | bytes 786440 | tf_op jit(solution)/shard_map/ppermute | solution.py:47
  89.1 5.1 %collective-permute-start.26 = (bf16[2,4,64,256]{3,2,1,0:T(8,128)(2,1)S(1)}, bf16[2,4,64,256]{3,2,1,0:T(8,128)(2,1)S(1)}, u32[]{:S(2)}, u32[]{:S(2)}) collective-permute-start(bf16[2,4,64,256]{3,2,1,0:T(8,128)(2,1)S(1)} %pad_maximum_fusion.3.refs_3_), channel_id=1, source_target_pairs={{0,8},{1,9},{2,10},{3,11},{4,12},{5,13},{6,14},{7,15},{8,0},{9,1},... | collective-permute-start | bytes 786440 | tf_op jit(solution)/shard_map/ppermute | solution.py:47
  90.7 4.9 %collective-permute-start.22 = (bf16[2,4,64,256]{3,2,1,0:T(8,128)(2,1)S(1)}, bf16[2,4,64,256]{3,2,1,0:T(8,128)(2,1)S(1)}, u32[]{:S(2)}, u32[]{:S(2)}) collective-permute-start(bf16[2,4,64,256]{3,2,1,0:T(8,128)(2,1)S(1)} %pad_maximum_fusion.2.refs_1_), channel_id=1, source_target_pairs={{0,8},{1,9},{2,10},{3,11},{4,12},{5,13},{6,14},{7,15},{8,0},{9,1},... | collective-permute-start | bytes 786440 | tf_op jit(solution)/shard_map/ppermute | solution.py:47
  93.7 2.0 %collective-permute-start.37 = (bf16[2,4,64,256]{3,2,1,0:T(8,128)(2,1)S(1)}, bf16[2,4,64,256]{3,2,1,0:T(8,128)(2,1)S(1)}, u32[]{:S(2)}, u32[]{:S(2)}) collective-permute-start(bf16[2,4,64,256]{3,2,1,0:T(8,128)(2,1)S(1)} %collective-permute-done.33.refs_6_), channel_id=1, source_target_pairs={{0,8},{1,9},{2,10},{3,11},{4,12},{5,13},{6,14},{7,15},{8,0},{9,1},... | collective-permute-start | bytes 786440 | tf_op jit(solution)/shard_map/ppermute | solution.py:47
  93.7 2.0 %collective-permute-start.39 = (bf16[2,4,64,256]{3,2,1,0:T(8,128)(2,1)S(1)}, bf16[2,4,64,256]{3,2,1,0:T(8,128)(2,1)S(1)}, u32[]{:S(2)}, u32[]{:S(2)}) collective-permute-start(bf16[2,4,64,256]{3,2,1,0:T(8,128)(2,1)S(1)} %collective-permute-done.35.refs_8_), channel_id=1, source_target_pairs={{0,8},{1,9},{2,10},{3,11},{4,12},{5,13},{6,14},{7,15},{8,0},{9,1},... | collective-permute-start | bytes 786440 | tf_op jit(solution)/shard_map/ppermute | solution.py:47
  94.2 1.8 %collective-permute-start.28 = (bf16[2,4,64,256]{3,2,1,0:T(8,128)(2,1)S(1)}, bf16[2,4,64,256]{3,2,1,0:T(8,128)(2,1)S(1)}, u32[]{:S(2)}, u32[]{:S(2)}) collective-permute-start(bf16[2,4,64,256]{3,2,1,0:T(8,128)(2,1)S(1)} %collective-permute-done.27.refs_4_), channel_id=1, source_target_pairs={{0,8},{1,9},{2,10},{3,11},{4,12},{5,13},{6,14},{7,15},{8,0},{9,1},... | collective-permute-start | bytes 786440 | tf_op jit(solution)/shard_map/ppermute | solution.py:47
  94.3 2.1 %collective-permute-start.24 = (bf16[2,4,64,256]{3,2,1,0:T(8,128)(2,1)S(1)}, bf16[2,4,64,256]{3,2,1,0:T(8,128)(2,1)S(1)}, u32[]{:S(2)}, u32[]{:S(2)}) collective-permute-start(bf16[2,4,64,256]{3,2,1,0:T(8,128)(2,1)S(1)} %collective-permute-done.23.refs_2_), channel_id=1, source_target_pairs={{0,8},{1,9},{2,10},{3,11},{4,12},{5,13},{6,14},{7,15},{8,0},{9,1},... | collective-permute-start | bytes 786440 | tf_op jit(solution)/shard_map/ppermute | solution.py:47

commit v5 on v4

--- a/solution.py
+++ b/solution.py
@@ -124,14 +124,13 @@
                 copies[k].wait()
             here = pl.ds(pl.multiple_of(x * rows, rows), rows)
             part = value[:, k * width : (k + 1) * width] + arrived[k, here, :].astype(F32)
-            if order == "xy":
-                outs[k][kx][...] = part.astype(outs[k][kx].dtype)
-                continue
             buffer[...] = part
-            for ky in range(ny):
+            for y in range(ny):
+                out, at = (outs[k][kx], y) if order == "xy" else (outs[k][y], x)
+                near = y if order == "xy" else grid.here("y", y)
                 for z in range(nz):
-                    start = pl.multiple_of((z * ny + grid.here("y", ky)) * block_rows, block_rows)
-                    outs[k][ky][x, z] = buffer[pl.ds(start, block_rows), :].astype(outs[k][ky].dtype)
+                    start = pl.multiple_of((z * ny + near) * block_rows, block_rows)
+                    out[at, z] = buffer[pl.ds(start, block_rows), :].astype(out.dtype)
 
 
 def kept_rows(grid, tokens, cot, came, orders):
@@ -140,7 +139,7 @@
     nx, ny, nz = (grid.size[axis] for axis in "xyz")
     rows = depth // (nx * 2)
     block_rows = rows // (nz * ny)
-    shapes = {"xy": (rows, width), "yx": (nx, nz, block_rows, width)}
+    shapes = {"xy": (ny, nz, block_rows, width), "yx": (nx, nz, block_rows, width)}
     out_shape = [
         jax.ShapeDtypeStruct(shapes[order], BF16 if k else F32)
         for order in orders
@@ -163,7 +162,7 @@
     result = []
     for order in orders:
         values = [next(outs) for _ in range(grid.size[order[0]])]
-        result.append([v.reshape(nz, ny, block_rows, width) if order == "xy" else v for v in values])
+        result.append(values)
     return result
 
 
@@ -174,11 +173,10 @@
     own = sums[0]
     for value in arriving:
         own = own + value.astype(F32)
-    dim = 1 if two_axis == "y" else 0
     arriving = yield [
-        (pick(own, dim, grid.here(two_axis, two)).astype(BF16), {two_axis: two}) for two in range(1, n_two)
+        (pick(own, 0, grid.here(two_axis, two)).astype(BF16), {two_axis: two}) for two in range(1, n_two)
     ]
-    total = pick(own, dim, grid.here(two_axis))
+    total = pick(own, 0, grid.here(two_axis))
     for value in arriving:
         total = total + value.astype(F32)
     yield total
@@ -187,7 +185,7 @@
 def scatter_z(grid, totals):
     whole = jnp.concatenate(totals, axis=2)
     arriving = yield [
-        (pick(whole, 0, grid.here("z", k)).astype(BF16), {"z": k}) for k in range(1, grid.size["z"])
+        (pick(whole, 0, grid.here("z", k)).astype(BF16), {"z": k}) for k in reversed(range(1, grid.size["z"]))
     ]
     total = pick(whole, 0, grid.here("z"))
     for value in arriving:
@@ -220,9 +218,9 @@
 
 
 def gather_z(grid, low, parts):
-    pieces = yield [(low, {"z": k}) for k in range(1, grid.size["z"])]
+    pieces = yield [(low, {"z": k}) for k in reversed(range(1, grid.size["z"]))]
     width = low.shape[1] // parts
-    yield [jnp.stack([p[:, s * width : (s + 1) * width] for p in [low] + pieces]) for s in range(parts)]
+    yield [jnp.stack([p[:, s * width : (s + 1) * width] for p in [low] + pieces[::-1]]) for s in range(parts)]
 
 
 def gather_xy(grid, value, order):
@@ -247,13 +245,21 @@
     tokens = refs.pop(0)
     places = [(h, kc) for h, half in enumerate(halves) for kc in half]
     pieces = [[[refs.pop(0) for _ in range(grid.size[order[0]])] for order in orders] for _ in places]
-    earlier = refs.pop(0) if finish else None
-    out, held = refs
+    if finish:
+        earlier, *state = [refs.pop(0) for _ in range(5)]
+        out, *new, held = refs
+    else:
+        out, held = refs
     width = out.shape[1] // len(orders)
     block = nz * ny * rows
 
     @pl.when(pl.program_id(0) == 0)
     def _():
+        if finish:
+            *clipped, first, second = state
+            for s, ref in enumerate(clipped):
+                at = slice(s * ref.shape[1], (s + 1) * ref.shape[1])
+                new[0][:, at], new[1][:, at] = moments(ref[...], first[:, at], second[:, at])
         for i in range(len(places)):
             for kx in range(nx):
                 for ky in range(ny):
@@ -279,7 +285,7 @@
     out[...] = value.astype(out.dtype)
 
 
-def project(grid, tokens, halves, orders, earlier=None):
+def project(grid, tokens, halves, orders, earlier=None, state=()):
     count, depth = tokens.shape
     nx = grid.size["x"]
     block = depth // (nx * 2)
@@ -295,15 +301,16 @@
     places = sum(len(key) for key in keys)
     return pl.pallas_call(
         functools.partial(project_kernel, grid, orders, rows, keys, finish),
-        out_shape=jax.ShapeDtypeStruct((count, width), BF16 if finish else F32),
+        out_shape=[jax.ShapeDtypeStruct((count, width), BF16 if finish else F32)]
+        + [jax.ShapeDtypeStruct(value.shape, F32) for value in state[-2:]],
         grid=(count // tile,),
-        in_specs=[pl.BlockSpec(memory_space=pltpu.VMEM)] * (1 + len(flat) + finish),
-        out_specs=tiled,
+        in_specs=[pl.BlockSpec(memory_space=pltpu.VMEM)] * (1 + len(flat) + finish + len(state)),
+        out_specs=[tiled] + [pl.BlockSpec(value.shape, lambda t: (0, 0)) for value in state[-2:]],
         scratch_shapes=[pltpu.VMEM((places, nx * block, width), held)],
         **kernel_params(
             2 * count * nx * block * places * width, count * depth * 2 + count * width * 8, SMALL
         ),
-    )(tokens, *flat, *([earlier] if finish else []))
+    )(tokens, *flat, *([earlier] if finish else []), *state)
 
 
 def shards(tokens, grad_out, master_weight, first_moment, second_moment, next_tokens):
@@ -321,6 +328,7 @@
         wanted = [next(way) for way in ways]
         for _ in range(2):
             came_in, values = stage(grid, wanted, (yield))
+            came_in = lax.optimization_barrier(came_in)
             yield values
             wanted = [way.send(got) for way, got in zip(ways, came_in)]
         way = scatter_z(grid, wanted)
@@ -332,7 +340,6 @@
         state = [value[:, columns] for value in (master_weight, first_moment, second_moment)]
         low = adam(clipped, *state)
         low, clipped = lax.optimization_barrier((low, clipped))
-        new = moments(clipped, *state[1:])
         way = gather_z(grid, low, len(orders))
         yield
         (came_in,), values = stage(grid, [next(way)], (yield))
@@ -341,11 +348,12 @@
         wanted = [next(way) for way in ways]
         for _ in range(2):
             came_in, values = stage(grid, wanted, (yield))
+            came_in = lax.optimization_barrier(came_in)
             yield values
             wanted = [way.send(got) for way, got in zip(ways, came_in)]
         own = wanted
         early = [[grid.send(part[0], c=1)] for part in own]
-        after = yield new, own
+        after = yield clipped, own
         last, _ = stage(grid, [[(piece, {"c": 1}) for piece in part[1:]] for part in own], after)
         other = [a + b for a, b in zip(early, last)]
         yield other
@@ -365,12 +373,13 @@
     for s in (0, 1):
         ways[s].send(factors[s])
     run(3)
-    news, own = zip(*[next(way) for way in ways])
-    new = [jnp.concatenate([news[0][k], news[1][k]], axis=1) for k in (0, 1)]
-    gate = project(grid, next_tokens, [{0: own[0]}], orders)
-    other = [ways[0].send([]), ways[1].send([gate])]
+    clipped, own = zip(*[next(way) for way in ways])
+    (gate,) = project(grid, next_tokens, [{0: own[0]}], orders)
+    other = [ways[0].send([]), ways[1].send([])]
     halves = [{1: other[0]}, {0: own[1], 1: other[1]}]
-    return *new, project(grid, next_tokens, halves, orders, gate)
+    state = (*clipped, first_moment, second_moment)
+    next_hidden, new_first, new_second = project(grid, next_tokens, halves, orders, gate, state)
+    return new_first, new_second, next_hidden
 
 
 def solution(mesh):

time: 101 us -> 97.3 us (0.963)
  starting transfers between devices: 41.4 us -> 36.3 us
  waiting for transfers between devices: 31.2 us -> 32.7 us
    ppermute x40, starting transfers between devices: 41.4 us -> 36.3 us  [send(): return lax.ppermute(value, AXES, pairs)]
    ppermute x40, waiting for transfers between devices: 31.2 us -> 32.7 us  [send(): return lax.ppermute(value, AXES, pairs)]
  transfers between devices with their start and end apart: 40 -> 40, of which waited for: 19 -> 21; matrix products, arithmetic and copies ran while one was open for 2% -> 2% of each run, Pallas kernels for 1% -> 2%
where the time goes in v5:
time: 97.3 us; the launch traced here: 97.1 us
  starting transfers between devices  36.3 us (37%)
  waiting for transfers between devices  32.7 us (34%)
  Pallas kernels  14.3 us (15%)
  blocking collectives  10.5 us (11%)
  other arithmetic  2.09 us (2%)
    ppermute x40, starting transfers between devices, send(): return lax.ppermute(value, AXES, pairs)  36.3 us
    ppermute x40, waiting for transfers between devices, send(): return lax.ppermute(value, AXES, pairs)  32.7 us
    all_to_all x1, blocking collectives, sum_everywhere(): lax.all_to_all(jnp.broadcast_to(value, (count, *value.shape)), AXES, 0, 0...  10.5 us
    pallas_call x2, Pallas kernels, project(): pl.pallas_call(functools.partial(project_kernel, grid, orders, rows, keys...  6.33 us
    pallas_call x1, Pallas kernels, sent_rows(): pl.pallas_call(functools.partial(sent_kernel, grid), out_shape=[jax.Shape...  4.59 us
    pallas_call x1, Pallas kernels, kept_rows(): pl.pallas_call(functools.partial(kept_kernel, grid, orders, block_rows),...  3.34 us
  transfers between devices with their start and end apart: 40, of which 21 were waited for; matrix products, arithmetic and copies ran while one was open for 2% of the time, Pallas kernels for 2%

profile of v5, /device:TPU:0, one launch (start us, length us, event | category | flops | bytes accessed | tf_op | source)
XLA Modules:
  0.0 97.1 jit_solution(5384925884441832717)
XLA Ops:
  0.6 4.6 %shard_map.85 = (bf16[1024,256]{1,0:T(8,128)(2,1)S(1)}, bf16[1024,256]{1,0:T(8,128)(2,1)S(1)}, bf16[1024,256]{1,0:T(8,128)(2,1)S(1)}, bf16[1024,256]{1,0:T(8,128)(2,1)S(1)}) custom-call(bf16[1024,2048]{1,0:T(8,128)(2,1)} %tokens.1, bf16[1024,1024]{1,0:T(8,128)(2,1)} %cot.1), custom_call_target="tpu_custom_call" | custom-call | flops 2147483648 | bytes 4194304 | tf_op jit(solution)/shard_map/pallas_call | solution.py:95
  6.4 0.9 collective-permute-done.refs_0_
  7.3 0.7 collective-permute-done.1.refs_1_
  8.1 0.7 collective-permute-done.2.refs_2_
  8.8 0.7 collective-permute-done.3.refs_3_
  9.6 3.3 %shard_map.86 = (f32[2,4,64,256]{3,2,1,0:T(8,128)S(1)}, bf16[2,4,64,256]{3,2,1,0:T(8,128)(2,1)S(1)}, f32[2,4,64,256]{3,2,1,0:T(8,128)S(1)}, bf16[2,4,64,256]{3,2...) custom-call(bf16[1024,2048]{1,0:T(8,128)(2,1)S(1)} %copy-done.1, ...), custom_call_target="tpu_custom_call" | custom-call | flops 2147483648 | bytes 4194304 | tf_op jit(solution)/shard_map/pallas_call | solution.py:149
  12.9 2.9 %collective-permute-start.4 = (bf16[2,4,64,256]{3,2,1,0:T(8,128)(2,1)S(1)}, bf16[2,4,64,256]{3,2,1,0:T(8,128)(2,1)}, u32[]{:S(2)}, u32[]{:S(2)}) collective-permute-start(bf16[2,4,64,256]{3,2,1,0:T(8,128)(2,1)S(1)} %get-tuple-element.43), channel_id=1, source_target_pairs={{0,16},{1,17},{2,18},{3,19},{4,20},{5,21},{6,22},{7,23},{8,24},{9,... | collective-permute-start | bytes 786440 | tf_op jit(solution)/shard_map/ppermute | solution.py:47
  15.8 1.5 %collective-permute-start.5 = (bf16[2,4,64,256]{3,2,1,0:T(8,128)(2,1)S(1)}, bf16[2,4,64,256]{3,2,1,0:T(8,128)(2,1)S(1)}, u32[]{:S(2)}, u32[]{:S(2)}) collective-permute-start(bf16[2,4,64,256]{3,2,1,0:T(8,128)(2,1)S(1)} %get-tuple-element.44), channel_id=1, source_target_pairs={{0,1},{1,0},{2,3},{3,2},{4,5},{5,4},{6,7},{7,6},{8,9},{9,8},{10,11... | collective-permute-start | bytes 786440 | tf_op jit(solution)/shard_map/ppermute | solution.py:47
  17.9 5.1 %collective-permute-done.4 = bf16[2,4,64,256]{3,2,1,0:T(8,128)(2,1)} collective-permute-done((bf16[2,4,64,256]{3,2,1,0:T(8,128)(2,1)S(1)}, bf16[2,4,64,256]{3,2,1,0:T(8,128)(2,1)}, u32[]{:S(2)}, u32[]{:S(2)}) %collective-permute-start.4) | collective-permute-done | bytes 262176 | tf_op jit(solution)/shard_map/ppermute | solution.py:47
  23.0 2.0 %collective-permute-done.5 = bf16[2,4,64,256]{3,2,1,0:T(8,128)(2,1)S(1)} collective-permute-done((bf16[2,4,64,256]{3,2,1,0:T(8,128)(2,1)S(1)}, bf16[2,4,64,256]{3,2,1,0:T(8,128)(2,1)S(1)}, u32[]{:S(2)}, u32[]{:S(2)}) %collective-permute-start.5) | collective-permute-done | bytes 262176 | tf_op jit(solution)/shard_map/ppermute | solution.py:47
  25.0 1.0 %convert_add_fusion.3 = f32[2,4,64,256]{3,2,1,0:T(8,128)S(1)} fusion(f32[2,4,64,256]{3,2,1,0:T(8,128)S(1)} %get-tuple-element.42, bf16[2,4,64,256]{3,2,1,0:T(8,128)(2,1)} %collective-permute-done.4), kind=kLoop, calls=%fused_computation.19 | loop fusion | flops 262144 | bytes 1310720 | tf_op jit(solution)/shard_map/add | solution.py:175
  26.1 1.6 %collective-permute-start.6 = (bf16[4,64,256]{2,1,0:T(8,128)(2,1)S(1)}, bf16[4,64,256]{2,1,0:T(8,128)(2,1)S(1)}, u32[]{:S(2)}, u32[]{:S(2)}) collective-permute-start(bf16[4,64,256]{2,1,0:T(8,128)(2,1)S(1)} %fusion.12), channel_id=1, source_target_pairs={{0,1},{1,0},{2,3},{3,2},{4,5},{5,4},{6,7},{7,6},{8,9},{9,8},{10,11... | collective-permute-start | bytes 393224 | tf_op jit(solution)/shard_map/ppermute | solution.py:47
  27.8 0.6 collective-permute-start.7
  28.4 2.3 %collective-permute-done.12 = bf16[2,4,64,256]{3,2,1,0:T(8,128)(2,1)S(1)} collective-permute-done((bf16[2,4,64,256]{3,2,1,0:T(8,128)(2,1)S(1)}, bf16[2,4,64,256]{3,2,1,0:T(8,128)(2,1)S(1)}, u32[]{:S(2)}, u32[]{:S(2)}) %collective-permute-start.12) | collective-permute-done | bytes 262176 | tf_op jit(solution)/shard_map/ppermute | solution.py:47
  30.8 1.6 %collective-permute-start.13 = (bf16[4,64,256]{2,1,0:T(8,128)(2,1)S(1)}, bf16[4,64,256]{2,1,0:T(8,128)(2,1)S(1)}, u32[]{:S(2)}, u32[]{:S(2)}) collective-permute-start(bf16[4,64,256]{2,1,0:T(8,128)(2,1)S(1)} %fusion.14), channel_id=1, source_target_pairs={{0,1},{1,0},{2,3},{3,2},{4,5},{5,4},{6,7},{7,6},{8,9},{9,8},{10,11... | collective-permute-start | bytes 393224 | tf_op jit(solution)/shard_map/ppermute | solution.py:47
  32.5 0.6 collective-permute-start.14
  33.4 3.7 %collective-permute-start.8 = (bf16[64,512]{1,0:T(8,128)(2,1)S(1)}, bf16[64,512]{1,0:T(8,128)(2,1)S(1)}, u32[]{:S(2)}, u32[]{:S(2)}) collective-permute-start(bf16[64,512]{1,0:T(8,128)(2,1)S(1)} %get-tuple-element.86), channel_id=1, source_target_pairs={{0,6},{1,7},{2,4},{3,5},{4,2},{5,3},{6,0},{7,1},{8,14},{9,15},{10,... | collective-permute-start | bytes 196616 | tf_op jit(solution)/shard_map/ppermute | solution.py:47
  37.1 0.8 collective-permute-start.10
  38.0 3.7 %collective-permute-start.15 = (bf16[64,512]{1,0:T(8,128)(2,1)S(1)}, bf16[64,512]{1,0:T(8,128)(2,1)S(1)}, u32[]{:S(2)}, u32[]{:S(2)}) collective-permute-start(bf16[64,512]{1,0:T(8,128)(2,1)S(1)} %get-tuple-element.83), channel_id=1, source_target_pairs={{0,6},{1,7},{2,4},{3,5},{4,2},{5,3},{6,0},{7,1},{8,14},{9,15},{10,... | collective-permute-start | bytes 196616 | tf_op jit(solution)/shard_map/ppermute | solution.py:47
  41.6 0.8 collective-permute-start.17
  42.4 1.5 %collective-permute-done.9 = bf16[64,512]{1,0:T(8,128)(2,1)S(1)} collective-permute-done((bf16[64,512]{1,0:T(8,128)(2,1)S(1)}, bf16[64,512]{1,0:T(8,128)(2,1)S(1)}, u32[]{:S(2)}, u32[]{:S(2)}) %collective-permute-start.9) | collective-permute-done | bytes 65568 | tf_op jit(solution)/shard_map/ppermute | solution.py:47
  44.0 1.2 %collective-permute-done.15 = bf16[64,512]{1,0:T(8,128)(2,1)S(1)} collective-permute-done((bf16[64,512]{1,0:T(8,128)(2,1)S(1)}, bf16[64,512]{1,0:T(8,128)(2,1)S(1)}, u32[]{:S(2)}, u32[]{:S(2)}) %collective-permute-start.15) | collective-permute-done | bytes 65568 | tf_op jit(solution)/shard_map/ppermute | solution.py:47
  45.2 2.0 %collective-permute-done.16 = bf16[64,512]{1,0:T(8,128)(2,1)S(1)} collective-permute-done((bf16[64,512]{1,0:T(8,128)(2,1)S(1)}, bf16[64,512]{1,0:T(8,128)(2,1)S(1)}, u32[]{:S(2)}, u32[]{:S(2)}) %collective-permute-start.16) | collective-permute-done | bytes 65568 | tf_op jit(solution)/shard_map/ppermute | solution.py:47
  47.3 10.5 %all_to_all.5 = f32[32,2,128]{2,1,0:T(2,128)S(1)} all-to-all(f32[32,2,128]{2,1,0:T(2,128)S(1)} %broadcast_in_dim.4), channel_id=1, replica_groups=mesh['aa'=4,'ba'=8] {'aa','ba'}, dimensions={0} | all-to-all | bytes 65536 | tf_op jit(solution)/shard_map/all_to_all | solution.py:198
  58.3 0.7 collective-permute-start.20
  59.0 1.3 %collective-permute-start.19 = (bf16[64,512]{1,0:T(8,128)(2,1)S(1)}, bf16[64,512]{1,0:T(8,128)(2,1)S(1)}, u32[]{:S(2)}, u32[]{:S(2)}) collective-permute-start(bf16[64,512]{1,0:T(8,128)(2,1)S(1)} %get-tuple-element.58), channel_id=1, source_target_pairs={{0,4},{1,5},{2,6},{3,7},{4,0},{5,1},{6,2},{7,3},{8,12},{9,13},{10,... | collective-permute-start | bytes 196616 | tf_op jit(solution)/shard_map/ppermute | solution.py:47
  60.3 2.4 %collective-permute-start.18 = (bf16[64,512]{1,0:T(8,128)(2,1)S(1)}, bf16[64,512]{1,0:T(8,128)(2,1)S(1)}, u32[]{:S(2)}, u32[]{:S(2)}) collective-permute-start(bf16[64,512]{1,0:T(8,128)(2,1)S(1)} %get-tuple-element.58), channel_id=1, source_target_pairs={{0,2},{1,3},{2,0},{3,1},{4,6},{5,7},{6,4},{7,5},{8,10},{9,11},{10,... | collective-permute-start | bytes 196616 | tf_op jit(solution)/shard_map/ppermute | solution.py:47
  62.7 0.6 collective-permute-start.31
  63.4 0.9 collective-permute-start.30
  64.3 0.9 collective-permute-done.20
  65.1 2.0 %collective-permute-start.29 = (bf16[64,512]{1,0:T(8,128)(2,1)S(1)}, bf16[64,512]{1,0:T(8,128)(2,1)S(1)}, u32[]{:S(2)}, u32[]{:S(2)}) collective-permute-start(bf16[64,512]{1,0:T(8,128)(2,1)S(1)} %get-tuple-element.63), channel_id=1, source_target_pairs={{0,2},{1,3},{2,0},{3,1},{4,6},{5,7},{6,4},{7,5},{8,10},{9,11},{10,... | collective-permute-start | bytes 196616 | tf_op jit(solution)/shard_map/ppermute | solution.py:47
  67.1 1.9 %collective-permute-done.19 = bf16[64,512]{1,0:T(8,128)(2,1)S(1)} collective-permute-done((bf16[64,512]{1,0:T(8,128)(2,1)S(1)}, bf16[64,512]{1,0:T(8,128)(2,1)S(1)}, u32[]{:S(2)}, u32[]{:S(2)}) %collective-permute-start.19) | collective-permute-done | bytes 65568 | tf_op jit(solution)/shard_map/ppermute | solution.py:47
  69.1 0.6 collective-permute-start.22
  69.7 0.7 collective-permute-start.21
  70.4 1.9 %collective-permute-done.30 = bf16[64,512]{1,0:T(8,128)(2,1)S(1)} collective-permute-done((bf16[64,512]{1,0:T(8,128)(2,1)S(1)}, bf16[64,512]{1,0:T(8,128)(2,1)S(1)}, u32[]{:S(2)}, u32[]{:S(2)}) %collective-permute-start.30) | collective-permute-done | bytes 65568 | tf_op jit(solution)/shard_map/ppermute | solution.py:47
  72.4 0.7 collective-permute-start.33
  73.1 0.7 collective-permute-start.32
  74.1 0.7 collective-permute-done.21
  74.8 0.7 collective-permute-start.25
  75.5 1.6 %collective-permute-start.24 = (bf16[2,4,64,256]{3,2,1,0:T(8,128)(2,1)S(1)}, bf16[2,4,64,256]{3,2,1,0:T(8,128)(2,1)S(1)}, u32[]{:S(2)}, u32[]{:S(2)}) collective-permute-start(bf16[2,4,64,256]{3,2,1,0:T(8,128)(2,1)S(1)} %pad_maximum_fusion.refs_1_), channel_id=1, source_target_pairs={{0,16},{1,17},{2,18},{3,19},{4,20},{5,21},{6,22},{7,23},{8,24},{9,... | collective-permute-start | bytes 786440 | tf_op jit(solution)/shard_map/ppermute | solution.py:47
  77.1 1.2 %collective-permute-done.33 = bf16[4,64,256]{2,1,0:T(8,128)(2,1)S(1)} collective-permute-done((bf16[4,64,256]{2,1,0:T(8,128)(2,1)S(1)}, bf16[4,64,256]{2,1,0:T(8,128)(2,1)S(1)}, u32[]{:S(2)}, u32[]{:S(2)}) %collective-permute-start.33) | collective-permute-done | bytes 131104 | tf_op jit(solution)/shard_map/ppermute | solution.py:47
  78.3 1.3 %collective-permute-done.32 = bf16[4,64,256]{2,1,0:T(8,128)(2,1)S(1)} collective-permute-done((bf16[4,64,256]{2,1,0:T(8,128)(2,1)S(1)}, bf16[4,64,256]{2,1,0:T(8,128)(2,1)S(1)}, u32[]{:S(2)}, u32[]{:S(2)}) %collective-permute-start.32) | collective-permute-done | bytes 131104 | tf_op jit(solution)/shard_map/ppermute | solution.py:47
  79.7 0.7 collective-permute-start.35
  80.4 1.5 %collective-permute-start.34 = (bf16[2,4,64,256]{3,2,1,0:T(8,128)(2,1)S(1)}, bf16[2,4,64,256]{3,2,1,0:T(8,128)(2,1)S(1)}, u32[]{:S(2)}, u32[]{:S(2)}) collective-permute-start(bf16[2,4,64,256]{3,2,1,0:T(8,128)(2,1)S(1)} %pad_maximum_fusion.2.refs_5_), channel_id=1, source_target_pairs={{0,16},{1,17},{2,18},{3,19},{4,20},{5,21},{6,22},{7,23},{8,24},{9,... | collective-permute-start | bytes 786440 | tf_op jit(solution)/shard_map/ppermute | solution.py:47
  82.0 3.3 %collective-permute-done.25.refs_4_ = bf16[2,4,64,256]{3,2,1,0:T(8,128)(2,1)S(1)} collective-permute-done((bf16[2,4,64,256]{3,2,1,0:T(8,128)(2,1)S(1)}, bf16[2,4,64,256]{3,2,1,0:T(8,128)(2,1)S(1)}, u32[]{:S(2)}, u32[]{:S(2)}) %collective-permute-start.25) | collective-permute-done | bytes 262176 | tf_op jit(solution)/shard_map/ppermute | solution.py:47
  85.8 3.5 %collective-permute-done.35.refs_8_ = bf16[2,4,64,256]{3,2,1,0:T(8,128)(2,1)S(1)} collective-permute-done((bf16[2,4,64,256]{3,2,1,0:T(8,128)(2,1)S(1)}, bf16[2,4,64,256]{3,2,1,0:T(8,128)(2,1)S(1)}, u32[]{:S(2)}, u32[]{:S(2)}) %collective-permute-start.35) | collective-permute-done | bytes 262176 | tf_op jit(solution)/shard_map/ppermute | solution.py:47
  90.4 1.5 %shard_map.87.refs_13_ = f32[1024,512]{1,0:T(8,128)S(1)} custom-call(bf16[1024,2048]{1,0:T(8,128)(2,1)S(1)} %copy-done, bf16[2,4,64,256]{3,2,1,0:T(8,128)(2,1)S(1)} %pad_maximum_fusion.refs_1_, bf16[2,4,64,256]{3,2,1,0:T(8,128)(2,1)S(1)} %collective-permute-done.24.refs_2_, bf16[2,4,64,256]{3,2,1,0:T(8,128)(2,1)S(1)} %pad_maximum_fusion.1.refs_3_, ...), custom_call_target="tpu_custom_call" | custom-call | flops 1073741824 | bytes 8388608 | tf_op jit(solution)/shard_map/pallas_call | solution.py:302
  92.3 4.8 %shard_map.88 = (bf16[1024,512]{1,0:T(8,128)(2,1)}, f32[64,1024]{1,0:T(8,128)}, f32[64,1024]{1,0:T(8,128)}) custom-call(bf16[1024,2048]{1,0:T(8,128)(2,1)S(1)} %copy-done, bf16[2,4,64,256]{3,2,1,0:T(8,128)(2,1)S(1)} %collective-permute-done.23.refs_1_, bf16[2,4,64,256]{3,2,1,0:T(8,128)(2,1)S(1)} %collective-permute-done.26.refs_2_, ...), custom_call_target="tpu_custom_call" | custom-call | flops 3221225472 | bytes 8388608 | tf_op jit(solution)/shard_map/pallas_call | solution.py:302
  (90 shorter events, 5.5 us)
Async XLA Ops:
  0.6 8.9 %copy-start.2 = (bf16[1024,1024]{1,0:T(8,128)(2,1)S(1)}, bf16[1024,1024]{1,0:T(8,128)(2,1)}, u32[]{:S(2)}) copy-start(bf16[1024,1024]{1,0:T(8,128)(2,1)} %cot.1) | copy-start | bytes 6291460
  0.6 8.9 %copy-start.1 = (bf16[1024,2048]{1,0:T(8,128)(2,1)S(1)}, bf16[1024,2048]{1,0:T(8,128)(2,1)}, u32[]{:S(2)}) copy-start(bf16[1024,2048]{1,0:T(8,128)(2,1)} %tokens.1) | copy-start | bytes 12582916
  5.2 2.1 %collective-permute-start = (bf16[1024,256]{1,0:T(8,128)(2,1)S(1)}, bf16[1024,256]{1,0:T(8,128)(2,1)S(1)}, u32[]{:S(2)}, u32[]{:S(2)}) collective-permute-start(bf16[1024,256]{1,0:T(8,128)(2,1)S(1)} %get-tuple-element.38), channel_id=1, source_target_pairs={{0,8},{1,9},{2,10},{3,11},{4,12},{5,13},{6,14},{7,15},{8,0},{9,1},... | collective-permute-start | bytes 1572872 | tf_op jit(solution)/shard_map/ppermute | solution.py:47
  5.8 2.3 %collective-permute-start.1 = (bf16[1024,256]{1,0:T(8,128)(2,1)S(1)}, bf16[1024,256]{1,0:T(8,128)(2,1)S(1)}, u32[]{:S(2)}, u32[]{:S(2)}) collective-permute-start(bf16[1024,256]{1,0:T(8,128)(2,1)S(1)} %get-tuple-element.39), channel_id=1, source_target_pairs={{0,8},{1,9},{2,10},{3,11},{4,12},{5,13},{6,14},{7,15},{8,0},{9,1},... | collective-permute-start | bytes 1572872 | tf_op jit(solution)/shard_map/ppermute | solution.py:47
  5.8 3.0 %collective-permute-start.2 = (bf16[1024,256]{1,0:T(8,128)(2,1)S(1)}, bf16[1024,256]{1,0:T(8,128)(2,1)S(1)}, u32[]{:S(2)}, u32[]{:S(2)}) collective-permute-start(bf16[1024,256]{1,0:T(8,128)(2,1)S(1)} %get-tuple-element.40), channel_id=1, source_target_pairs={{0,8},{1,9},{2,10},{3,11},{4,12},{5,13},{6,14},{7,15},{8,0},{9,1},... | collective-permute-start | bytes 1572872 | tf_op jit(solution)/shard_map/ppermute | solution.py:47
  6.3 3.3 %collective-permute-start.3 = (bf16[1024,256]{1,0:T(8,128)(2,1)S(1)}, bf16[1024,256]{1,0:T(8,128)(2,1)S(1)}, u32[]{:S(2)}, u32[]{:S(2)}) collective-permute-start(bf16[1024,256]{1,0:T(8,128)(2,1)S(1)} %get-tuple-element.41), channel_id=1, source_target_pairs={{0,8},{1,9},{2,10},{3,11},{4,12},{5,13},{6,14},{7,15},{8,0},{9,1},... | collective-permute-start | bytes 1572872 | tf_op jit(solution)/shard_map/ppermute | solution.py:47
  12.9 10.1 %collective-permute-start.4 = (bf16[2,4,64,256]{3,2,1,0:T(8,128)(2,1)S(1)}, bf16[2,4,64,256]{3,2,1,0:T(8,128)(2,1)}, u32[]{:S(2)}, u32[]{:S(2)}) collective-permute-start(bf16[2,4,64,256]{3,2,1,0:T(8,128)(2,1)S(1)} %get-tuple-element.43), channel_id=1, source_target_pairs={{0,16},{1,17},{2,18},{3,19},{4,20},{5,21},{6,22},{7,23},{8,24},{9,... | collective-permute-start | bytes 786440 | tf_op jit(solution)/shard_map/ppermute | solution.py:47
  15.8 9.2 %collective-permute-start.5 = (bf16[2,4,64,256]{3,2,1,0:T(8,128)(2,1)S(1)}, bf16[2,4,64,256]{3,2,1,0:T(8,128)(2,1)S(1)}, u32[]{:S(2)}, u32[]{:S(2)}) collective-permute-start(bf16[2,4,64,256]{3,2,1,0:T(8,128)(2,1)S(1)} %get-tuple-element.44), channel_id=1, source_target_pairs={{0,1},{1,0},{2,3},{3,2},{4,5},{5,4},{6,7},{7,6},{8,9},{9,8},{10,11... | collective-permute-start | bytes 786440 | tf_op jit(solution)/shard_map/ppermute | solution.py:47
  17.4 11.0 %collective-permute-start.11 = (bf16[2,4,64,256]{3,2,1,0:T(8,128)(2,1)S(1)}, bf16[2,4,64,256]{3,2,1,0:T(8,128)(2,1)S(1)}, u32[]{:S(2)}, u32[]{:S(2)}) collective-permute-start(bf16[2,4,64,256]{3,2,1,0:T(8,128)(2,1)S(1)} %get-tuple-element.51), channel_id=1, source_target_pairs={{0,16},{1,17},{2,18},{3,19},{4,20},{5,21},{6,22},{7,23},{8,24},{9,... | collective-permute-start | bytes 786440 | tf_op jit(solution)/shard_map/ppermute | solution.py:47
  17.9 12.7 %collective-permute-start.12 = (bf16[2,4,64,256]{3,2,1,0:T(8,128)(2,1)S(1)}, bf16[2,4,64,256]{3,2,1,0:T(8,128)(2,1)S(1)}, u32[]{:S(2)}, u32[]{:S(2)}) collective-permute-start(bf16[2,4,64,256]{3,2,1,0:T(8,128)(2,1)S(1)} %get-tuple-element.52), channel_id=1, source_target_pairs={{0,1},{1,0},{2,3},{3,2},{4,5},{5,4},{6,7},{7,6},{8,9},{9,8},{10,11... | collective-permute-start | bytes 786440 | tf_op jit(solution)/shard_map/ppermute | solution.py:47
  26.1 7.2 %collective-permute-start.6 = (bf16[4,64,256]{2,1,0:T(8,128)(2,1)S(1)}, bf16[4,64,256]{2,1,0:T(8,128)(2,1)S(1)}, u32[]{:S(2)}, u32[]{:S(2)}) collective-permute-start(bf16[4,64,256]{2,1,0:T(8,128)(2,1)S(1)} %fusion.12), channel_id=1, source_target_pairs={{0,1},{1,0},{2,3},{3,2},{4,5},{5,4},{6,7},{7,6},{8,9},{9,8},{10,11... | collective-permute-start | bytes 393224 | tf_op jit(solution)/shard_map/ppermute | solution.py:47
  27.8 5.5 %collective-permute-start.7 = (bf16[4,64,256]{2,1,0:T(8,128)(2,1)S(1)}, bf16[4,64,256]{2,1,0:T(8,128)(2,1)S(1)}, u32[]{:S(2)}, u32[]{:S(2)}) collective-permute-start(bf16[4,64,256]{2,1,0:T(8,128)(2,1)S(1)} %fusion.13), channel_id=1, source_target_pairs={{0,16},{1,17},{2,18},{3,19},{4,20},{5,21},{6,22},{7,23},{8,24},{9,... | collective-permute-start | bytes 393224 | tf_op jit(solution)/shard_map/ppermute | solution.py:47
  30.7 27.3 %copy-start.3 = (f32[64,1024]{1,0:T(8,128)S(1)}, f32[64,1024]{1,0:T(8,128)}, u32[]{:S(2)}) copy-start(f32[64,1024]{1,0:T(8,128)} %refs_17_.1) | copy-start | bytes 786436
  30.7 27.3 %copy-start.4 = (f32[64,1024]{1,0:T(8,128)S(1)}, f32[64,1024]{1,0:T(8,128)}, u32[]{:S(2)}) copy-start(f32[64,1024]{1,0:T(8,128)} %refs_16_.1) | copy-start | bytes 786436
  30.7 27.3 %copy-start.5 = (f32[64,1024]{1,0:T(8,128)S(1)}, f32[64,1024]{1,0:T(8,128)}, u32[]{:S(2)}) copy-start(f32[64,1024]{1,0:T(8,128)} %param.8) | copy-start | bytes 786436
  30.8 7.1 %collective-permute-start.13 = (bf16[4,64,256]{2,1,0:T(8,128)(2,1)S(1)}, bf16[4,64,256]{2,1,0:T(8,128)(2,1)S(1)}, u32[]{:S(2)}, u32[]{:S(2)}) collective-permute-start(bf16[4,64,256]{2,1,0:T(8,128)(2,1)S(1)} %fusion.14), channel_id=1, source_target_pairs={{0,1},{1,0},{2,3},{3,2},{4,5},{5,4},{6,7},{7,6},{8,9},{9,8},{10,11... | collective-permute-start | bytes 393224 | tf_op jit(solution)/shard_map/ppermute | solution.py:47
  32.5 5.4 %collective-permute-start.14 = (bf16[4,64,256]{2,1,0:T(8,128)(2,1)S(1)}, bf16[4,64,256]{2,1,0:T(8,128)(2,1)S(1)}, u32[]{:S(2)}, u32[]{:S(2)}) collective-permute-start(bf16[4,64,256]{2,1,0:T(8,128)(2,1)S(1)} %fusion.15), channel_id=1, source_target_pairs={{0,16},{1,17},{2,18},{3,19},{4,20},{5,21},{6,22},{7,23},{8,24},{9,... | collective-permute-start | bytes 393224 | tf_op jit(solution)/shard_map/ppermute | solution.py:47
  33.4 8.2 %collective-permute-start.8 = (bf16[64,512]{1,0:T(8,128)(2,1)S(1)}, bf16[64,512]{1,0:T(8,128)(2,1)S(1)}, u32[]{:S(2)}, u32[]{:S(2)}) collective-permute-start(bf16[64,512]{1,0:T(8,128)(2,1)S(1)} %get-tuple-element.86), channel_id=1, source_target_pairs={{0,6},{1,7},{2,4},{3,5},{4,2},{5,3},{6,0},{7,1},{8,14},{9,15},{10,... | collective-permute-start | bytes 196616 | tf_op jit(solution)/shard_map/ppermute | solution.py:47
  37.1 6.8 %collective-permute-start.9 = (bf16[64,512]{1,0:T(8,128)(2,1)S(1)}, bf16[64,512]{1,0:T(8,128)(2,1)S(1)}, u32[]{:S(2)}, u32[]{:S(2)}) collective-permute-start(bf16[64,512]{1,0:T(8,128)(2,1)S(1)} %get-tuple-element.87), channel_id=1, source_target_pairs={{0,4},{1,5},{2,6},{3,7},{4,0},{5,1},{6,2},{7,3},{8,12},{9,13},{10,... | collective-permute-start | bytes 196616 | tf_op jit(solution)/shard_map/ppermute | solution.py:47
  37.1 6.8 %collective-permute-start.10 = (bf16[64,512]{1,0:T(8,128)(2,1)S(1)}, bf16[64,512]{1,0:T(8,128)(2,1)S(1)}, u32[]{:S(2)}, u32[]{:S(2)}) collective-permute-start(bf16[64,512]{1,0:T(8,128)(2,1)S(1)} %get-tuple-element.88), channel_id=1, source_target_pairs={{0,2},{1,3},{2,0},{3,1},{4,6},{5,7},{6,4},{7,5},{8,10},{9,11},{10,... | collective-permute-start | bytes 196616 | tf_op jit(solution)/shard_map/ppermute | solution.py:47
  38.0 7.2 %collective-permute-start.15 = (bf16[64,512]{1,0:T(8,128)(2,1)S(1)}, bf16[64,512]{1,0:T(8,128)(2,1)S(1)}, u32[]{:S(2)}, u32[]{:S(2)}) collective-permute-start(bf16[64,512]{1,0:T(8,128)(2,1)S(1)} %get-tuple-element.83), channel_id=1, source_target_pairs={{0,6},{1,7},{2,4},{3,5},{4,2},{5,3},{6,0},{7,1},{8,14},{9,15},{10,... | collective-permute-start | bytes 196616 | tf_op jit(solution)/shard_map/ppermute | solution.py:47
  41.6 5.5 %collective-permute-start.16 = (bf16[64,512]{1,0:T(8,128)(2,1)S(1)}, bf16[64,512]{1,0:T(8,128)(2,1)S(1)}, u32[]{:S(2)}, u32[]{:S(2)}) collective-permute-start(bf16[64,512]{1,0:T(8,128)(2,1)S(1)} %get-tuple-element.84), channel_id=1, source_target_pairs={{0,4},{1,5},{2,6},{3,7},{4,0},{5,1},{6,2},{7,3},{8,12},{9,13},{10,... | collective-permute-start | bytes 196616 | tf_op jit(solution)/shard_map/ppermute | solution.py:47
  41.6 5.5 %collective-permute-start.17 = (bf16[64,512]{1,0:T(8,128)(2,1)S(1)}, bf16[64,512]{1,0:T(8,128)(2,1)S(1)}, u32[]{:S(2)}, u32[]{:S(2)}) collective-permute-start(bf16[64,512]{1,0:T(8,128)(2,1)S(1)} %get-tuple-element.85), channel_id=1, source_target_pairs={{0,2},{1,3},{2,0},{3,1},{4,6},{5,7},{6,4},{7,5},{8,10},{9,11},{10,... | collective-permute-start | bytes 196616 | tf_op jit(solution)/shard_map/ppermute | solution.py:47
  57.9 32.4 %copy-start = (bf16[1024,2048]{1,0:T(8,128)(2,1)S(1)}, bf16[1024,2048]{1,0:T(8,128)(2,1)}, u32[]{:S(2)}) copy-start(bf16[1024,2048]{1,0:T(8,128)(2,1)} %refs_0_.3) | copy-start | bytes 12582916
  58.3 6.9 %collective-permute-start.20 = (bf16[64,512]{1,0:T(8,128)(2,1)S(1)}, bf16[64,512]{1,0:T(8,128)(2,1)S(1)}, u32[]{:S(2)}, u32[]{:S(2)}) collective-permute-start(bf16[64,512]{1,0:T(8,128)(2,1)S(1)} %get-tuple-element.58), channel_id=1, source_target_pairs={{0,6},{1,7},{2,4},{3,5},{4,2},{5,3},{6,0},{7,1},{8,14},{9,15},{10,... | collective-permute-start | bytes 196616 | tf_op jit(solution)/shard_map/ppermute | solution.py:47
  59.0 10.0 %collective-permute-start.19 = (bf16[64,512]{1,0:T(8,128)(2,1)S(1)}, bf16[64,512]{1,0:T(8,128)(2,1)S(1)}, u32[]{:S(2)}, u32[]{:S(2)}) collective-permute-start(bf16[64,512]{1,0:T(8,128)(2,1)S(1)} %get-tuple-element.58), channel_id=1, source_target_pairs={{0,4},{1,5},{2,6},{3,7},{4,0},{5,1},{6,2},{7,3},{8,12},{9,13},{10,... | collective-permute-start | bytes 196616 | tf_op jit(solution)/shard_map/ppermute | solution.py:47
  60.3 8.7 %collective-permute-start.18 = (bf16[64,512]{1,0:T(8,128)(2,1)S(1)}, bf16[64,512]{1,0:T(8,128)(2,1)S(1)}, u32[]{:S(2)}, u32[]{:S(2)}) collective-permute-start(bf16[64,512]{1,0:T(8,128)(2,1)S(1)} %get-tuple-element.58), channel_id=1, source_target_pairs={{0,2},{1,3},{2,0},{3,1},{4,6},{5,7},{6,4},{7,5},{8,10},{9,11},{10,... | collective-permute-start | bytes 196616 | tf_op jit(solution)/shard_map/ppermute | solution.py:47
  62.7 7.7 %collective-permute-start.31 = (bf16[64,512]{1,0:T(8,128)(2,1)S(1)}, bf16[64,512]{1,0:T(8,128)(2,1)S(1)}, u32[]{:S(2)}, u32[]{:S(2)}) collective-permute-start(bf16[64,512]{1,0:T(8,128)(2,1)S(1)} %get-tuple-element.63), channel_id=1, source_target_pairs={{0,6},{1,7},{2,4},{3,5},{4,2},{5,3},{6,0},{7,1},{8,14},{9,15},{10,... | collective-permute-start | bytes 196616 | tf_op jit(solution)/shard_map/ppermute | solution.py:47
  63.4 9.0 %collective-permute-start.30 = (bf16[64,512]{1,0:T(8,128)(2,1)S(1)}, bf16[64,512]{1,0:T(8,128)(2,1)S(1)}, u32[]{:S(2)}, u32[]{:S(2)}) collective-permute-start(bf16[64,512]{1,0:T(8,128)(2,1)S(1)} %get-tuple-element.63), channel_id=1, source_target_pairs={{0,4},{1,5},{2,6},{3,7},{4,0},{5,1},{6,2},{7,3},{8,12},{9,13},{10,... | collective-permute-start | bytes 196616 | tf_op jit(solution)/shard_map/ppermute | solution.py:47
  65.1 7.2 %collective-permute-start.29 = (bf16[64,512]{1,0:T(8,128)(2,1)S(1)}, bf16[64,512]{1,0:T(8,128)(2,1)S(1)}, u32[]{:S(2)}, u32[]{:S(2)}) collective-permute-start(bf16[64,512]{1,0:T(8,128)(2,1)S(1)} %get-tuple-element.63), channel_id=1, source_target_pairs={{0,2},{1,3},{2,0},{3,1},{4,6},{5,7},{6,4},{7,5},{8,10},{9,11},{10,... | collective-permute-start | bytes 196616 | tf_op jit(solution)/shard_map/ppermute | solution.py:47
  69.1 5.0 %collective-permute-start.22 = (bf16[4,64,256]{2,1,0:T(8,128)(2,1)S(1)}, bf16[4,64,256]{2,1,0:T(8,128)(2,1)S(1)}, u32[]{:S(2)}, u32[]{:S(2)}) collective-permute-start(bf16[4,64,256]{2,1,0:T(8,128)(2,1)S(1)} %get-tuple-element.94), channel_id=1, source_target_pairs={{0,16},{1,17},{2,18},{3,19},{4,20},{5,21},{6,22},{7,23},{8,24},{9,... | collective-permute-start | bytes 393224 | tf_op jit(solution)/shard_map/ppermute | solution.py:47
  69.7 5.0 %collective-permute-start.21 = (bf16[4,64,256]{2,1,0:T(8,128)(2,1)S(1)}, bf16[4,64,256]{2,1,0:T(8,128)(2,1)S(1)}, u32[]{:S(2)}, u32[]{:S(2)}) collective-permute-start(bf16[4,64,256]{2,1,0:T(8,128)(2,1)S(1)} %get-tuple-element.96), channel_id=1, source_target_pairs={{0,1},{1,0},{2,3},{3,2},{4,5},{5,4},{6,7},{7,6},{8,9},{9,8},{10,11... | collective-permute-start | bytes 393224 | tf_op jit(solution)/shard_map/ppermute | solution.py:47
  72.4 5.9 %collective-permute-start.33 = (bf16[4,64,256]{2,1,0:T(8,128)(2,1)S(1)}, bf16[4,64,256]{2,1,0:T(8,128)(2,1)S(1)}, u32[]{:S(2)}, u32[]{:S(2)}) collective-permute-start(bf16[4,64,256]{2,1,0:T(8,128)(2,1)S(1)} %get-tuple-element.90), channel_id=1, source_target_pairs={{0,16},{1,17},{2,18},{3,19},{4,20},{5,21},{6,22},{7,23},{8,24},{9,... | collective-permute-start | bytes 393224 | tf_op jit(solution)/shard_map/ppermute | solution.py:47
  73.1 6.5 %collective-permute-start.32 = (bf16[4,64,256]{2,1,0:T(8,128)(2,1)S(1)}, bf16[4,64,256]{2,1,0:T(8,128)(2,1)S(1)}, u32[]{:S(2)}, u32[]{:S(2)}) collective-permute-start(bf16[4,64,256]{2,1,0:T(8,128)(2,1)S(1)} %get-tuple-element.92), channel_id=1, source_target_pairs={{0,1},{1,0},{2,3},{3,2},{4,5},{5,4},{6,7},{7,6},{8,9},{9,8},{10,11... | collective-permute-start | bytes 393224 | tf_op jit(solution)/shard_map/ppermute | solution.py:47
  74.8 10.5 %collective-permute-start.25 = (bf16[2,4,64,256]{3,2,1,0:T(8,128)(2,1)S(1)}, bf16[2,4,64,256]{3,2,1,0:T(8,128)(2,1)S(1)}, u32[]{:S(2)}, u32[]{:S(2)}) collective-permute-start(bf16[2,4,64,256]{3,2,1,0:T(8,128)(2,1)S(1)} %pad_maximum_fusion.1.refs_3_), channel_id=1, source_target_pairs={{0,1},{1,0},{2,3},{3,2},{4,5},{5,4},{6,7},{7,6},{8,9},{9,8},{10,11... | collective-permute-start | bytes 786440 | tf_op jit(solution)/shard_map/ppermute | solution.py:47
  75.5 9.8 %collective-permute-start.24 = (bf16[2,4,64,256]{3,2,1,0:T(8,128)(2,1)S(1)}, bf16[2,4,64,256]{3,2,1,0:T(8,128)(2,1)S(1)}, u32[]{:S(2)}, u32[]{:S(2)}) collective-permute-start(bf16[2,4,64,256]{3,2,1,0:T(8,128)(2,1)S(1)} %pad_maximum_fusion.refs_1_), channel_id=1, source_target_pairs={{0,16},{1,17},{2,18},{3,19},{4,20},{5,21},{6,22},{7,23},{8,24},{9,... | collective-permute-start | bytes 786440 | tf_op jit(solution)/shard_map/ppermute | solution.py:47
  79.7 9.6 %collective-permute-start.35 = (bf16[2,4,64,256]{3,2,1,0:T(8,128)(2,1)S(1)}, bf16[2,4,64,256]{3,2,1,0:T(8,128)(2,1)S(1)}, u32[]{:S(2)}, u32[]{:S(2)}) collective-permute-start(bf16[2,4,64,256]{3,2,1,0:T(8,128)(2,1)S(1)} %pad_maximum_fusion.3.refs_7_), channel_id=1, source_target_pairs={{0,1},{1,0},{2,3},{3,2},{4,5},{5,4},{6,7},{7,6},{8,9},{9,8},{10,11... | collective-permute-start | bytes 786440 | tf_op jit(solution)/shard_map/ppermute | solution.py:47
  80.4 8.8 %collective-permute-start.34 = (bf16[2,4,64,256]{3,2,1,0:T(8,128)(2,1)S(1)}, bf16[2,4,64,256]{3,2,1,0:T(8,128)(2,1)S(1)}, u32[]{:S(2)}, u32[]{:S(2)}) collective-permute-start(bf16[2,4,64,256]{3,2,1,0:T(8,128)(2,1)S(1)} %pad_maximum_fusion.2.refs_5_), channel_id=1, source_target_pairs={{0,16},{1,17},{2,18},{3,19},{4,20},{5,21},{6,22},{7,23},{8,24},{9,... | collective-permute-start | bytes 786440 | tf_op jit(solution)/shard_map/ppermute | solution.py:47
  82.0 7.8 %collective-permute-start.27 = (bf16[2,4,64,256]{3,2,1,0:T(8,128)(2,1)S(1)}, bf16[2,4,64,256]{3,2,1,0:T(8,128)(2,1)S(1)}, u32[]{:S(2)}, u32[]{:S(2)}) collective-permute-start(bf16[2,4,64,256]{3,2,1,0:T(8,128)(2,1)S(1)} %pad_maximum_fusion.1.refs_3_), channel_id=1, source_target_pairs={{0,8},{1,9},{2,10},{3,11},{4,12},{5,13},{6,14},{7,15},{8,0},{9,1},... | collective-permute-start | bytes 786440 | tf_op jit(solution)/shard_map/ppermute | solution.py:47
  85.3 4.6 %collective-permute-start.23 = (bf16[2,4,64,256]{3,2,1,0:T(8,128)(2,1)S(1)}, bf16[2,4,64,256]{3,2,1,0:T(8,128)(2,1)S(1)}, u32[]{:S(2)}, u32[]{:S(2)}) collective-permute-start(bf16[2,4,64,256]{3,2,1,0:T(8,128)(2,1)S(1)} %pad_maximum_fusion.refs_1_), channel_id=1, source_target_pairs={{0,8},{1,9},{2,10},{3,11},{4,12},{5,13},{6,14},{7,15},{8,0},{9,1},... | collective-permute-start | bytes 786440 | tf_op jit(solution)/shard_map/ppermute | solution.py:47
  85.3 5.0 %collective-permute-start.38 = (bf16[2,4,64,256]{3,2,1,0:T(8,128)(2,1)S(1)}, bf16[2,4,64,256]{3,2,1,0:T(8,128)(2,1)S(1)}, u32[]{:S(2)}, u32[]{:S(2)}) collective-permute-start(bf16[2,4,64,256]{3,2,1,0:T(8,128)(2,1)S(1)} %pad_maximum_fusion.3.refs_7_), channel_id=1, source_target_pairs={{0,8},{1,9},{2,10},{3,11},{4,12},{5,13},{6,14},{7,15},{8,0},{9,1},... | collective-permute-start | bytes 786440 | tf_op jit(solution)/shard_map/ppermute | solution.py:47
  89.3 2.6 %collective-permute-start.36 = (bf16[2,4,64,256]{3,2,1,0:T(8,128)(2,1)S(1)}, bf16[2,4,64,256]{3,2,1,0:T(8,128)(2,1)S(1)}, u32[]{:S(2)}, u32[]{:S(2)}) collective-permute-start(bf16[2,4,64,256]{3,2,1,0:T(8,128)(2,1)S(1)} %pad_maximum_fusion.2.refs_5_), channel_id=1, source_target_pairs={{0,8},{1,9},{2,10},{3,11},{4,12},{5,13},{6,14},{7,15},{8,0},{9,1},... | collective-permute-start | bytes 786440 | tf_op jit(solution)/shard_map/ppermute | solution.py:47
  89.3 2.6 %collective-permute-start.26 = (bf16[2,4,64,256]{3,2,1,0:T(8,128)(2,1)S(1)}, bf16[2,4,64,256]{3,2,1,0:T(8,128)(2,1)S(1)}, u32[]{:S(2)}, u32[]{:S(2)}) collective-permute-start(bf16[2,4,64,256]{3,2,1,0:T(8,128)(2,1)S(1)} %collective-permute-done.24.refs_2_), channel_id=1, source_target_pairs={{0,8},{1,9},{2,10},{3,11},{4,12},{5,13},{6,14},{7,15},{8,0},{9,1},... | collective-permute-start | bytes 786440 | tf_op jit(solution)/shard_map/ppermute | solution.py:47
  89.8 2.1 %collective-permute-start.28 = (bf16[2,4,64,256]{3,2,1,0:T(8,128)(2,1)S(1)}, bf16[2,4,64,256]{3,2,1,0:T(8,128)(2,1)S(1)}, u32[]{:S(2)}, u32[]{:S(2)}) collective-permute-start(bf16[2,4,64,256]{3,2,1,0:T(8,128)(2,1)S(1)} %collective-permute-done.25.refs_4_), channel_id=1, source_target_pairs={{0,8},{1,9},{2,10},{3,11},{4,12},{5,13},{6,14},{7,15},{8,0},{9,1},... | collective-permute-start | bytes 786440 | tf_op jit(solution)/shard_map/ppermute | solution.py:47
  89.9 2.1 %collective-permute-start.37 = (bf16[2,4,64,256]{3,2,1,0:T(8,128)(2,1)S(1)}, bf16[2,4,64,256]{3,2,1,0:T(8,128)(2,1)S(1)}, u32[]{:S(2)}, u32[]{:S(2)}) collective-permute-start(bf16[2,4,64,256]{3,2,1,0:T(8,128)(2,1)S(1)} %collective-permute-done.34.refs_6_), channel_id=1, source_target_pairs={{0,8},{1,9},{2,10},{3,11},{4,12},{5,13},{6,14},{7,15},{8,0},{9,1},... | collective-permute-start | bytes 786440 | tf_op jit(solution)/shard_map/ppermute | solution.py:47
  90.3 2.0 %collective-permute-start.39 = (bf16[2,4,64,256]{3,2,1,0:T(8,128)(2,1)S(1)}, bf16[2,4,64,256]{3,2,1,0:T(8,128)(2,1)S(1)}, u32[]{:S(2)}, u32[]{:S(2)}) collective-permute-start(bf16[2,4,64,256]{3,2,1,0:T(8,128)(2,1)S(1)} %collective-permute-done.35.refs_8_), channel_id=1, source_target_pairs={{0,8},{1,9},{2,10},{3,11},{4,12},{5,13},{6,14},{7,15},{8,0},{9,1},... | collective-permute-start | bytes 786440 | tf_op jit(solution)/shard_map/ppermute | solution.py:47

commit v6 on v5

v6 whole, which is shorter than its diff:
```python
import functools
import math

import jax
import jax.numpy as jnp
from jax import lax
from jax.experimental import pallas as pl
from jax.experimental.pallas import tpu as pltpu
from jax.sharding import PartitionSpec as P

D = 2048
FF = 512
AXES = ("aa", "ba")
BF16 = jnp.bfloat16
F32 = jnp.float32
LANES = 128
LARGE = 60 * 1024 * 1024
SMALL = 14 * 1024 * 1024


class Grid:
    def __init__(self):
        outer, inner = lax.axis_size("aa"), lax.axis_size("ba")
        y = 1
        while y * y * 4 <= inner:
            y *= 2
        self.size = {"x": outer // 2, "c": 2, "z": inner // y, "y": y}

    def here(self, axis, step=0):
        a, b = lax.axis_index("aa"), lax.axis_index("ba")
        inner = self.size["c"] if axis in "xc" else self.size["y"]
        index = a if axis in "xc" else b
        return self.partner(axis, lax.div(index, inner) if axis in "xz" else lax.rem(index, inner), step)

    def partner(self, axis, at, step):
        return at ^ step if step else at

    def send(self, value, **steps):
        pairs = []
        for x in range(self.size["x"]):
            for c in range(self.size["c"]):
                for z in range(self.size["z"]):
                    for y in range(self.size["y"]):
                        here = {"x": x, "c": c, "z": z, "y": y}
                        there = {k: int(self.partner(k, v, steps.get(k, 0))) for k, v in here.items()}
                        pairs.append((self.index(here), self.index(there)))
        return lax.ppermute(value, AXES, pairs)

    def index(self, at):
        return ((at["x"] * self.size["c"] + at["c"]) * self.size["z"] + at["z"]) * self.size["y"] + at["y"]


def pick(value, axis, index):
    return lax.dynamic_index_in_dim(value, index, axis, keepdims=False)


def kernel_params(flops, moved, limit=LARGE):
    return dict(
        compiler_params=pltpu.CompilerParams(vmem_limit_bytes=limit),
        cost_estimate=pl.CostEstimate(flops=flops, bytes_accessed=moved, transcendentals=0),
    )


def column_block(grid, x, step, rows):
    return pl.ds(pl.multiple_of((x * 2 + grid.here("c", step)) * rows, rows), rows)


def product(block, cot):
    return lax.dot_general(block, cot, (((0,), (0,)), ((), ())), preferred_element_type=F32)


def cut_columns(total, cuts):
    bounds = [total * cut // 8 for cut in (0, *cuts, 8)]
    orders = ("xy", "yx") * (len(bounds) // 2)
    return [(order, slice(a, b)) for order, a, b in zip(orders, bounds, bounds[1:])]


def width_of(part):
    return part[1].stop - part[1].start


def sent_kernel(grid, parts, tokens_ref, cot_ref, *refs):
    outs, (tokens, cot, sems) = refs[:-3], refs[-3:]
    n, _, rows = tokens.shape
    half = cot.shape[1] // 2
    halves = [slice(0, half), slice(half, 2 * half)]
    cot_copies = [pltpu.make_async_copy(cot_ref.at[:, h], cot.at[:, h], sems.at[n + i]) for i, h in enumerate(halves)]
    copies = []
    for x in range(n):
        block = tokens_ref.at[:, column_block(grid, x, 1, rows)]
        copies.append(pltpu.make_async_copy(block, tokens.at[x], sems.at[x]))
    for copy in (cot_copies[0], copies[0], cot_copies[1], *copies[1:]):
        copy.start()
    for x in range(n):
        copies[x].wait()
        for h, copy in zip(halves, cot_copies):
            if x == 0:
                copy.wait()
            value = product(tokens[x], cot[:, h])
            for ref, (_, columns) in zip(outs, parts):
                if h.start <= columns.start < h.stop:
                    inner = slice(columns.start - h.start, columns.stop - h.start)
                    ref[pl.ds(x * rows, rows), :] = value[:, inner].astype(ref.dtype)


def sent_rows(grid, tokens, cot, parts):
    count, depth = tokens.shape
    n = grid.size["x"]
    rows = depth // (n * 2)
    return pl.pallas_call(
        functools.partial(sent_kernel, grid, parts),
        out_shape=[jax.ShapeDtypeStruct((n * rows, width_of(part)), BF16) for part in parts],
        in_specs=[pl.BlockSpec(memory_space=pltpu.HBM)] * 2,
        out_specs=[pl.BlockSpec(memory_space=pltpu.VMEM)] * len(parts),
        scratch_shapes=[
            pltpu.VMEM((n, count, rows), BF16),
            pltpu.VMEM(cot.shape, BF16),
            pltpu.SemaphoreType.DMA((n + 2,)),
        ],
        **kernel_params(2 * count * n * rows * cot.shape[1], count * n * rows * 2 + cot.size * 2, SMALL),
    )(*(pltpu.with_memory_space_constraint(v, pltpu.HBM) for v in (tokens, cot)))


def kept_product_kernel(grid, tokens, cot, out):
    rows = out.shape[0] // grid.size["x"]
    for x in range(grid.size["x"]):
        out[x * rows : (x + 1) * rows, :] = product(tokens[:, column_block(grid, x, 0, rows)], cot[...])


def kept_product(grid, tokens, cot):
    count, depth = tokens.shape
    whole = pl.BlockSpec(memory_space=pltpu.VMEM)
    return pl.pallas_call(
        functools.partial(kept_product_kernel, grid),
        out_shape=jax.ShapeDtypeStruct((depth // 2, cot.shape[1]), F32),
        in_specs=[whole] * 2,
        out_specs=whole,
        **kernel_params(count * depth * cot.shape[1], count * depth + cot.size * 2, SMALL),
    )(tokens, cot)


def kept_kernel(grid, parts, block_rows, value_ref, *refs):
    refs = list(refs)
    came = [refs.pop(0) for _ in parts]
    outs = [[refs.pop(0) for _ in range(1, grid.size[order[0]])] for order, _ in parts]
    outs = [[refs.pop(0), *others] for others in outs]
    *arrived, buffer, sems = refs
    nx, ny, nz = (grid.size[axis] for axis in "xyz")
    rows = buffer.shape[0]
    copies = [pltpu.make_async_copy(ref, arrived[k], sems.at[k]) for k, ref in enumerate(came)]
    for copy in copies:
        copy.start()
    for kx in range(nx):
        x = grid.here("x", kx)
        here = pl.ds(pl.multiple_of(x * rows, rows), rows)
        for k, (order, columns) in enumerate(parts):
            if kx == 0:
                copies[k].wait()
            wide = slice(0, columns.stop - columns.start)
            buffer[:, wide] = value_ref[here, columns] + arrived[k][here, :].astype(F32)
            for y in range(ny):
                out, at = (outs[k][kx], y) if order == "xy" else (outs[k][y], x)
                near = y if order == "xy" else grid.here("y", y)
                for z in range(nz):
                    start = pl.multiple_of((z * ny + near) * block_rows, block_rows)
                    out[at, z] = buffer[pl.ds(start, block_rows), wide].astype(out.dtype)


def kept_rows(grid, value, came, parts):
    nx, ny, nz = (grid.size[axis] for axis in "xyz")
    rows = value.shape[0] // nx
    block_rows = rows // (nz * ny)
    lead = {"xy": (ny, nz, block_rows), "yx": (nx, nz, block_rows)}
    shapes = [(*lead[part[0]], width_of(part)) for part in parts]
    counts = [grid.size[part[0][0]] - 1 for part in parts]
    out_shape = [jax.ShapeDtypeStruct(shape, BF16) for shape, n in zip(shapes, counts) for _ in range(n)]
    out_shape += [jax.ShapeDtypeStruct(shape, F32) for shape in shapes]
    whole = pl.BlockSpec(memory_space=pltpu.VMEM)
    outs = pl.pallas_call(
        functools.partial(kept_kernel, grid, parts, block_rows),
        out_shape=out_shape,
        in_specs=[whole] + [pl.BlockSpec(memory_space=pl.ANY)] * len(came),
        out_specs=[whole] * len(out_shape),
        scratch_shapes=[pltpu.VMEM(value.shape, BF16) for value in came]
        + [
            pltpu.VMEM((rows, max(width_of(part) for part in parts)), F32),
            pltpu.SemaphoreType.DMA((len(parts),)),
        ],
        **kernel_params(0, value.size * 12, SMALL),
    )(value, *came)
    outs = iter(outs)
    others = [[next(outs) for _ in range(n)] for n in counts]
    return [[next(outs), *values] for values in others]


def scatter_xy(grid, sums, order):
    one_axis, two_axis = order
    n_one, n_two = grid.size[one_axis], grid.size[two_axis]
    arriving = yield [(sums[one], {one_axis: one}) for one in range(1, n_one)]
    own = sums[0]
    for value in arriving:
        own = own + value.astype(F32)
    arriving = yield [
        (pick(own, 0, grid.here(two_axis, two)).astype(BF16), {two_axis: two}) for two in range(1, n_two)
    ]
    total = pick(own, 0, grid.here(two_axis))
    for value in arriving:
        total = total + value.astype(F32)
    yield total


def scatter_z(grid, totals):
    whole = jnp.concatenate(totals, axis=2)
    arriving = yield [
        (pick(whole, 0, grid.here("z", k)).astype(BF16), {"z": k}) for k in reversed(range(1, grid.size["z"]))
    ]
    total = pick(whole, 0, grid.here("z"))
    for value in arriving:
        total = total + value.astype(F32)
    yield total


def sum_everywhere(value):
    count = lax.axis_size("aa") * lax.axis_size("ba")
    terms = lax.all_to_all(jnp.broadcast_to(value, (count, *value.shape)), AXES, 0, 0, tiled=True)
    return jnp.sum(terms, axis=(0, 2))


def moments(clipped, first, second):
    return 0.9 * first + 0.1 * clipped, 0.95 * second + 0.05 * clipped * clipped


def clip_factor(square):
    return jnp.minimum(1.0, math.sqrt(D * FF) / jnp.sqrt(square + 1e-06))


def adam(clipped, weight, first, second):
    new_first, new_second = moments(clipped, first, second)
    corr_first = 1.0 - 0.9**10
    corr_second = 1.0 - 0.95**10
    updated = weight * (1.0 - 0.003 * 0.1) - 0.003 * (new_first / corr_first) / (
        jnp.sqrt(new_second / corr_second) + 1e-08
    )
    return updated.astype(BF16)


def gather_z(grid, low, widths):
    steps = range(1, grid.size["z"])
    pieces = yield [(low, {"z": k}) for k in reversed(steps)]
    pieces = [low] + pieces[::-1]
    starts = [sum(widths[:k]) for k in range(len(widths))]
    yield [jnp.stack([p[:, a : a + width] for p in pieces]) for a, width in zip(starts, widths)]


def gather_xy(grid, value, order):
    one_axis, two_axis = order
    pieces = yield [(value, {two_axis: two}) for two in range(1, grid.size[two_axis])]
    value = jnp.stack([value] + pieces)
    pieces = yield [(value, {one_axis: one}) for one in range(1, grid.size[one_axis])]
    yield [value] + pieces


def stage(grid, wanted):
    return [[grid.send(value, **steps) for value, steps in sends] for sends in wanted]


def overlaps(parts, half, which):
    found = []
    for p, (order, columns) in enumerate(parts):
        a, b = max(columns.start, which * half), min(columns.stop, (which + 1) * half)
        if a < b:
            inner = slice(a - columns.start, b - columns.start)
            found.append((p, order, inner, slice(a - which * half, b - which * half)))
    return found


def project_kernel(grid, plan, rows, finish, *refs):
    refs = list(refs)
    nx, ny, nz = (grid.size[axis] for axis in "xyz")
    tokens = refs.pop(0)
    pieces = [[[refs.pop(0) for _ in range(grid.size[order[0]])] for _, order, _, _ in cut] for _, _, cut in plan]
    if finish:
        earlier, *state = [refs.pop(0) for _ in range(5)]
        out, *new, held = refs
    else:
        out, held = refs
    block = nz * ny * rows

    @pl.when(pl.program_id(0) == 0)
    def _():
        if finish:
            *clipped, first, second = state
            start = 0
            for ref in clipped:
                at = slice(start, start + ref.shape[1])
                new[0][:, at], new[1][:, at] = moments(ref[...], first[:, at], second[:, at])
                start = at.stop
        for i, (_, _, cut) in enumerate(plan):
            for kx in range(nx):
                for ky in range(ny):
                    for kz in range(nz):
                        at = (grid.here("x", kx) * nz + grid.here("z", kz)) * ny + grid.here("y", ky)
                        at = pl.ds(pl.multiple_of(at * rows, rows), rows)
                        for piece, (_, order, inner, columns) in zip(pieces[i], cut):
                            one, two = (kx, ky) if order == "xy" else (ky, kx)
                            held[i, at, columns] = piece[one][two, kz, :, inner].astype(held.dtype)

    tile = pl.ds(pl.multiple_of(pl.program_id(0) * out.shape[0], out.shape[0]), out.shape[0])
    totals = [earlier[tile, :], None] if finish else [None]
    for i, (h, kc, _) in enumerate(plan):
        for x in range(nx):
            weight = held[i, x * block : (x + 1) * block, :].astype(BF16)
            term = jnp.dot(tokens[tile, column_block(grid, x, kc, block)], weight, preferred_element_type=F32)
            totals[h] = term if totals[h] is None else totals[h] + term
    value = totals[0]
    if finish:
        value = value / (1.0 + jnp.exp(-value)) * totals[1]
    out[...] = value.astype(out.dtype)


def project(grid, tokens, places, parts, half, earlier=None, state=()):
    count, depth = tokens.shape
    nx = grid.size["x"]
    block = depth // (nx * 2)
    plan = [(which, kc, overlaps(parts, half, which)) for which, kc, _ in places]
    flat = [piece for (_, _, cut), (_, _, table) in zip(plan, places) for p, *_ in cut for piece in table[p]]
    rows = flat[0].shape[2]
    tile = min(count, 512)
    held = BF16 if rows % 16 == 0 else F32
    finish = earlier is not None
    tiled = pl.BlockSpec((tile, half), lambda t: (t, 0))
    return pl.pallas_call(
        functools.partial(project_kernel, grid, plan, rows, finish),
        out_shape=[jax.ShapeDtypeStruct((count, half), BF16 if finish else F32)]
        + [jax.ShapeDtypeStruct(value.shape, F32) for value in state[-2:]],
        grid=(count // tile,),
        in_specs=[pl.BlockSpec(memory_space=pltpu.VMEM)] * (1 + len(flat) + finish + len(state)),
        out_specs=[tiled] + [pl.BlockSpec(value.shape, lambda t: (0, 0)) for value in state[-2:]],
        scratch_shapes=[pltpu.VMEM((len(plan), nx * block, half), held)],
        **kernel_params(
            2 * count * nx * block * len(plan) * half, count * depth * 2 + count * half * 8, SMALL
        ),
    )(tokens, *flat, *([earlier] if finish else []), *state)


def shards(tokens, grad_out, master_weight, first_moment, second_moment, next_tokens):
    grid = Grid()
    total = grad_out.shape[1]
    half = total // 2
    inward, outward = cut_columns(total, (2, 4, 6)), cut_columns(total, (2, 4, 6))

    came = [grid.send(value, c=1) for value in sent_rows(grid, tokens, grad_out, inward)]
    sums = kept_rows(grid, kept_product(grid, tokens, grad_out), came, inward)

    def scatter(first):
        ways = [scatter_xy(grid, sums[k], inward[k][0]) for k in (first, first + 1)]
        wanted = [next(way) for way in ways]
        for _ in range(2):
            came_in = lax.optimization_barrier(stage(grid, wanted))
            yield
            wanted = [way.send(got) for way, got in zip(ways, came_in)]
        way = scatter_z(grid, wanted)
        (came_in,) = stage(grid, [next(way)])
        yield
        yield way.send(came_in)

    def gather(first, grad, factor):
        parts = outward[first : first + 2]
        columns = slice(parts[0][1].start, parts[1][1].stop)
        clipped = grad[:, columns] * factor[:, columns]
        low = adam(clipped, *[value[:, columns] for value in (master_weight, first_moment, second_moment)])
        low, clipped = lax.optimization_barrier((low, clipped))
        way = gather_z(grid, low, [width_of(part) for part in parts])
        (came_in,) = stage(grid, [next(way)])
        yield
        ways = [gather_xy(grid, value, part[0]) for value, part in zip(way.send(came_in), parts)]
        wanted = [next(way) for way in ways]
        for _ in range(2):
            came_in = lax.optimization_barrier(stage(grid, wanted))
            yield
            wanted = [way.send(got) for way, got in zip(ways, came_in)]
        yield clipped, wanted, [[grid.send(piece, c=1) for piece in table] for table in wanted]

    def run(ways):
        for _ in range(3):
            for way in ways:
                next(way)
        return [next(way) for way in ways]

    grad = jnp.concatenate(run([scatter(0), scatter(2)]), axis=1)
    squares = jnp.sum((grad * grad).reshape(grad.shape[0], 2, -1, LANES), axis=(0, 2))
    factors = clip_factor(sum_everywhere(squares))
    factors = lax.optimization_barrier(jnp.broadcast_to(factors[:, None], (2, half)).reshape(1, total))
    (clipped_a, own_a, other_a), (clipped_b, own_b, other_b) = run([gather(0, grad, factors), gather(2, grad, factors)])
    own, other = own_a + own_b, other_a + other_b
    (gate,) = project(grid, next_tokens, [(0, 0, own)], outward, half)
    places = [(0, 1, other), (1, 0, own), (1, 1, other)]
    state = (clipped_a, clipped_b, first_moment, second_moment)
    next_hidden, new_first, new_second = project(grid, next_tokens, places, outward, half, gate, state)
    return new_first, new_second, next_hidden


def solution(mesh):
    spec = P(AXES, None)
    return jax.shard_map(shards, mesh=mesh, in_specs=(spec,) * 6, out_specs=(spec,) * 3, check_vma=False)
```

time: 97.3 us -> 96 us (0.987)
  waiting for transfers between devices: 32.7 us -> 30.3 us
  starting transfers between devices: 36.3 us -> 37.6 us
    ppermute x40, waiting for transfers between devices: 32.7 us -> 30.3 us  [send(): return lax.ppermute(value, AXES, pairs)]
    ppermute x40, starting transfers between devices: 36.3 us -> 37.6 us  [send(): return lax.ppermute(value, AXES, pairs)]
    pallas_call x4 -> x5, Pallas kernels: 14.3 us -> 14.2 us  [the longest x2 6.33 us: project(): pl.pallas_call(functools.partial(project_kernel, grid, plan, rows, finish...]
  transfers between devices with their start and end apart: 40 -> 40, of which waited for: 21 -> 15; matrix products, arithmetic and copies ran while one was open for 2% -> 2% of each run, Pallas kernels for 2% -> 4%
where the time goes in v6:
time: 96 us; the launch traced here: 95.8 us
  starting transfers between devices  37.6 us (39%)
  waiting for transfers between devices  30.3 us (32%)
  Pallas kernels  14.2 us (15%)
  blocking collectives  10.2 us (11%)
  other arithmetic  2.07 us (2%)
  between operations  1.01 us (1%)
    ppermute x40, starting transfers between devices, send(): return lax.ppermute(value, AXES, pairs)  37.6 us
    ppermute x40, waiting for transfers between devices, send(): return lax.ppermute(value, AXES, pairs)  30.3 us
    all_to_all x1, blocking collectives, sum_everywhere(): lax.all_to_all(jnp.broadcast_to(value, (count, *value.shape)), AXES, 0, 0...  10.2 us
    pallas_call x2, Pallas kernels, project(): pl.pallas_call(functools.partial(project_kernel, grid, plan, rows, finish...  6.33 us
    pallas_call x1, Pallas kernels, sent_rows(): pl.pallas_call(functools.partial(sent_kernel, grid, parts), out_shape=[ja...  4.49 us
    pallas_call x1, Pallas kernels, kept_product(): pl.pallas_call(functools.partial(kept_product_kernel, grid), out_shape=ja...  2.38 us
  transfers between devices with their start and end apart: 40, of which 15 were waited for; matrix products, arithmetic and copies ran while one was open for 2% of the time, Pallas kernels for 4%

profile of v6, /device:TPU:0, one launch (start us, length us, event | category | flops | bytes accessed | tf_op | source)
XLA Modules:
  0.0 95.8 jit_solution(9155424692086674141)
XLA Ops:
  0.6 4.5 %shard_map.86 = (bf16[1024,256]{1,0:T(8,128)(2,1)S(1)}, bf16[1024,256]{1,0:T(8,128)(2,1)S(1)}, bf16[1024,256]{1,0:T(8,128)(2,1)S(1)}, bf16[1024,256]{1,0:T(8,128)(2,1)S(1)}) custom-call(bf16[1024,2048]{1,0:T(8,128)(2,1)} %tokens_ref.1, bf16[1024,1024]{1,0:T(8,128)(2,1)} %cot_ref.1), custom_call_target="tpu_custom_call" | custom-call | flops 2147483648 | bytes 4194304 | tf_op jit(solution)/shard_map/pallas_call | solution.py:110
  5.1 0.5 collective-permute-start
  6.3 2.4 %shard_map.85.value_ref = f32[1024,1024]{1,0:T(8,128)S(1)} custom-call(bf16[1024,2048]{1,0:T(8,128)(2,1)S(1)} %copy-done.1, bf16[1024,1024]{1,0:T(8,128)(2,1)S(1)} %copy-done.2), custom_call_target="tpu_custom_call" | custom-call | flops 2147483648 | bytes 4194304 | tf_op jit(solution)/shard_map/pallas_call | solution.py:133
  8.7 0.7 collective-permute-done.3.refs_3_
  9.5 1.0 %shard_map.87 = (bf16[2,4,64,256]{3,2,1,0:T(8,128)(2,1)S(1)}, bf16[2,4,64,256]{3,2,1,0:T(8,128)(2,1)S(1)}, bf16[2,4,64,256]{3,2,1,0:T(8,128)(2,1)S(1)}, bf16[2,4...) custom-call(f32[1024,1024]{1,0:T(8,128)S(1)} %shard_map.85.value_ref, ...), custom_call_target="tpu_custom_call" | custom-call | bytes 12582912 | tf_op jit(solution)/shard_map/pallas_call | solution.py:179
  10.5 2.9 %collective-permute-start.4 = (bf16[2,4,64,256]{3,2,1,0:T(8,128)(2,1)S(1)}, bf16[2,4,64,256]{3,2,1,0:T(8,128)(2,1)}, u32[]{:S(2)}, u32[]{:S(2)}) collective-permute-start(bf16[2,4,64,256]{3,2,1,0:T(8,128)(2,1)S(1)} %get-tuple-element.43), channel_id=1, source_target_pairs={{0,16},{1,17},{2,18},{3,19},{4,20},{5,21},{6,22},{7,23},{8,24},{9,... | collective-permute-start | bytes 786440 | tf_op jit(solution)/shard_map/ppermute | solution.py:47
  13.4 1.5 %collective-permute-start.5 = (bf16[2,4,64,256]{3,2,1,0:T(8,128)(2,1)S(1)}, bf16[2,4,64,256]{3,2,1,0:T(8,128)(2,1)S(1)}, u32[]{:S(2)}, u32[]{:S(2)}) collective-permute-start(bf16[2,4,64,256]{3,2,1,0:T(8,128)(2,1)S(1)} %get-tuple-element.44), channel_id=1, source_target_pairs={{0,1},{1,0},{2,3},{3,2},{4,5},{5,4},{6,7},{7,6},{8,9},{9,8},{10,11... | collective-permute-start | bytes 786440 | tf_op jit(solution)/shard_map/ppermute | solution.py:47
  14.9 0.5 collective-permute-start.11
  15.5 5.1 %collective-permute-done.4 = bf16[2,4,64,256]{3,2,1,0:T(8,128)(2,1)} collective-permute-done((bf16[2,4,64,256]{3,2,1,0:T(8,128)(2,1)S(1)}, bf16[2,4,64,256]{3,2,1,0:T(8,128)(2,1)}, u32[]{:S(2)}, u32[]{:S(2)}) %collective-permute-start.4) | collective-permute-done | bytes 262176 | tf_op jit(solution)/shard_map/ppermute | solution.py:47
  20.6 2.0 %collective-permute-done.5 = bf16[2,4,64,256]{3,2,1,0:T(8,128)(2,1)S(1)} collective-permute-done((bf16[2,4,64,256]{3,2,1,0:T(8,128)(2,1)S(1)}, bf16[2,4,64,256]{3,2,1,0:T(8,128)(2,1)S(1)}, u32[]{:S(2)}, u32[]{:S(2)}) %collective-permute-start.5) | collective-permute-done | bytes 262176 | tf_op jit(solution)/shard_map/ppermute | solution.py:47
  22.6 1.0 %convert_add_fusion.3 = f32[2,4,64,256]{3,2,1,0:T(8,128)S(1)} fusion(f32[2,4,64,256]{3,2,1,0:T(8,128)S(1)} %get-tuple-element.42, bf16[2,4,64,256]{3,2,1,0:T(8,128)(2,1)} %collective-permute-done.4), kind=kLoop, calls=%fused_computation.19 | loop fusion | flops 262144 | bytes 1310720 | tf_op jit(solution)/shard_map/add | solution.py:202
  23.7 1.6 %collective-permute-start.6 = (bf16[4,64,256]{2,1,0:T(8,128)(2,1)S(1)}, bf16[4,64,256]{2,1,0:T(8,128)(2,1)S(1)}, u32[]{:S(2)}, u32[]{:S(2)}) collective-permute-start(bf16[4,64,256]{2,1,0:T(8,128)(2,1)S(1)} %fusion.13), channel_id=1, source_target_pairs={{0,1},{1,0},{2,3},{3,2},{4,5},{5,4},{6,7},{7,6},{8,9},{9,8},{10,11... | collective-permute-start | bytes 393224 | tf_op jit(solution)/shard_map/ppermute | solution.py:47
  25.3 0.6 collective-permute-start.7
  25.9 2.3 %collective-permute-done.12 = bf16[2,4,64,256]{3,2,1,0:T(8,128)(2,1)S(1)} collective-permute-done((bf16[2,4,64,256]{3,2,1,0:T(8,128)(2,1)S(1)}, bf16[2,4,64,256]{3,2,1,0:T(8,128)(2,1)S(1)}, u32[]{:S(2)}, u32[]{:S(2)}) %collective-permute-start.12) | collective-permute-done | bytes 262176 | tf_op jit(solution)/shard_map/ppermute | solution.py:47
  28.4 1.6 %collective-permute-start.13 = (bf16[4,64,256]{2,1,0:T(8,128)(2,1)S(1)}, bf16[4,64,256]{2,1,0:T(8,128)(2,1)S(1)}, u32[]{:S(2)}, u32[]{:S(2)}) collective-permute-start(bf16[4,64,256]{2,1,0:T(8,128)(2,1)S(1)} %fusion.15), channel_id=1, source_target_pairs={{0,1},{1,0},{2,3},{3,2},{4,5},{5,4},{6,7},{7,6},{8,9},{9,8},{10,11... | collective-permute-start | bytes 393224 | tf_op jit(solution)/shard_map/ppermute | solution.py:47
  30.1 0.6 collective-permute-start.14
  31.0 1.6 %collective-permute-start.10 = (bf16[64,512]{1,0:T(8,128)(2,1)S(1)}, bf16[64,512]{1,0:T(8,128)(2,1)S(1)}, u32[]{:S(2)}, u32[]{:S(2)}) collective-permute-start(bf16[64,512]{1,0:T(8,128)(2,1)S(1)} %get-tuple-element.84), channel_id=1, source_target_pairs={{0,2},{1,3},{2,0},{3,1},{4,6},{5,7},{6,4},{7,5},{8,10},{9,11},{10,... | collective-permute-start | bytes 196616 | tf_op jit(solution)/shard_map/ppermute | solution.py:47
  32.6 2.5 %collective-permute-start.8 = (bf16[64,512]{1,0:T(8,128)(2,1)S(1)}, bf16[64,512]{1,0:T(8,128)(2,1)S(1)}, u32[]{:S(2)}, u32[]{:S(2)}) collective-permute-start(bf16[64,512]{1,0:T(8,128)(2,1)S(1)} %get-tuple-element.82), channel_id=1, source_target_pairs={{0,6},{1,7},{2,4},{3,5},{4,2},{5,3},{6,0},{7,1},{8,14},{9,15},{10,... | collective-permute-start | bytes 196616 | tf_op jit(solution)/shard_map/ppermute | solution.py:47
  35.4 3.5 %collective-permute-start.15 = (bf16[64,512]{1,0:T(8,128)(2,1)S(1)}, bf16[64,512]{1,0:T(8,128)(2,1)S(1)}, u32[]{:S(2)}, u32[]{:S(2)}) collective-permute-start(bf16[64,512]{1,0:T(8,128)(2,1)S(1)} %get-tuple-element.79), channel_id=1, source_target_pairs={{0,6},{1,7},{2,4},{3,5},{4,2},{5,3},{6,0},{7,1},{8,14},{9,15},{10,... | collective-permute-start | bytes 196616 | tf_op jit(solution)/shard_map/ppermute | solution.py:47
  38.9 0.9 collective-permute-start.17
  39.8 4.2 %collective-permute-done.9 = bf16[64,512]{1,0:T(8,128)(2,1)S(1)} collective-permute-done((bf16[64,512]{1,0:T(8,128)(2,1)S(1)}, bf16[64,512]{1,0:T(8,128)(2,1)S(1)}, u32[]{:S(2)}, u32[]{:S(2)}) %collective-permute-start.9) | collective-permute-done | bytes 65568 | tf_op jit(solution)/shard_map/ppermute | solution.py:47
  44.1 1.8 %collective-permute-done.16 = bf16[64,512]{1,0:T(8,128)(2,1)S(1)} collective-permute-done((bf16[64,512]{1,0:T(8,128)(2,1)S(1)}, bf16[64,512]{1,0:T(8,128)(2,1)S(1)}, u32[]{:S(2)}, u32[]{:S(2)}) %collective-permute-start.16) | collective-permute-done | bytes 65568 | tf_op jit(solution)/shard_map/ppermute | solution.py:47
  46.1 10.2 %all_to_all.5 = f32[32,2,128]{2,1,0:T(2,128)S(1)} all-to-all(f32[32,2,128]{2,1,0:T(2,128)S(1)} %broadcast_in_dim.4), channel_id=1, replica_groups=mesh['aa'=4,'ba'=8] {'aa','ba'}, dimensions={0} | all-to-all | bytes 65536 | tf_op jit(solution)/shard_map/all_to_all | solution.py:225
  56.8 0.6 collective-permute-start.18
  57.4 0.7 collective-permute-start.19
  58.1 3.2 %collective-permute-start.20 = (bf16[64,512]{1,0:T(8,128)(2,1)S(1)}, bf16[64,512]{1,0:T(8,128)(2,1)S(1)}, u32[]{:S(2)}, u32[]{:S(2)}) collective-permute-start(bf16[64,512]{1,0:T(8,128)(2,1)S(1)} %get-tuple-element.58), channel_id=1, source_target_pairs={{0,6},{1,7},{2,4},{3,5},{4,2},{5,3},{6,0},{7,1},{8,14},{9,15},{10,... | collective-permute-start | bytes 196616 | tf_op jit(solution)/shard_map/ppermute | solution.py:47
  61.3 1.2 %collective-permute-start.30 = (bf16[64,512]{1,0:T(8,128)(2,1)S(1)}, bf16[64,512]{1,0:T(8,128)(2,1)S(1)}, u32[]{:S(2)}, u32[]{:S(2)}) collective-permute-start(bf16[64,512]{1,0:T(8,128)(2,1)S(1)} %get-tuple-element.63), channel_id=1, source_target_pairs={{0,4},{1,5},{2,6},{3,7},{4,0},{5,1},{6,2},{7,3},{8,12},{9,13},{10,... | collective-permute-start | bytes 196616 | tf_op jit(solution)/shard_map/ppermute | solution.py:47
  62.5 3.3 %collective-permute-start.31 = (bf16[64,512]{1,0:T(8,128)(2,1)S(1)}, bf16[64,512]{1,0:T(8,128)(2,1)S(1)}, u32[]{:S(2)}, u32[]{:S(2)}) collective-permute-start(bf16[64,512]{1,0:T(8,128)(2,1)S(1)} %get-tuple-element.63), channel_id=1, source_target_pairs={{0,6},{1,7},{2,4},{3,5},{4,2},{5,3},{6,0},{7,1},{8,14},{9,15},{10,... | collective-permute-start | bytes 196616 | tf_op jit(solution)/shard_map/ppermute | solution.py:47
  65.8 3.1 %collective-permute-done.19 = bf16[64,512]{1,0:T(8,128)(2,1)S(1)} collective-permute-done((bf16[64,512]{1,0:T(8,128)(2,1)S(1)}, bf16[64,512]{1,0:T(8,128)(2,1)S(1)}, u32[]{:S(2)}, u32[]{:S(2)}) %collective-permute-start.19) | collective-permute-done | bytes 65568 | tf_op jit(solution)/shard_map/ppermute | solution.py:47
  68.9 0.6 collective-permute-start.22
  69.5 0.7 collective-permute-start.21
  70.3 1.0 %collective-permute-done.30 = bf16[64,512]{1,0:T(8,128)(2,1)S(1)} collective-permute-done((bf16[64,512]{1,0:T(8,128)(2,1)S(1)}, bf16[64,512]{1,0:T(8,128)(2,1)S(1)}, u32[]{:S(2)}, u32[]{:S(2)}) %collective-permute-start.30) | collective-permute-done | bytes 65568 | tf_op jit(solution)/shard_map/ppermute | solution.py:47
  71.3 0.7 collective-permute-start.33
  72.0 1.3 %collective-permute-start.32 = (bf16[4,64,256]{2,1,0:T(8,128)(2,1)S(1)}, bf16[4,64,256]{2,1,0:T(8,128)(2,1)S(1)}, u32[]{:S(2)}, u32[]{:S(2)}) collective-permute-start(bf16[4,64,256]{2,1,0:T(8,128)(2,1)S(1)} %get-tuple-element.88), channel_id=1, source_target_pairs={{0,1},{1,0},{2,3},{3,2},{4,5},{5,4},{6,7},{7,6},{8,9},{9,8},{10,11... | collective-permute-start | bytes 393224 | tf_op jit(solution)/shard_map/ppermute | solution.py:47
  73.3 1.9 %collective-permute-done.22 = bf16[4,64,256]{2,1,0:T(8,128)(2,1)S(1)} collective-permute-done((bf16[4,64,256]{2,1,0:T(8,128)(2,1)S(1)}, bf16[4,64,256]{2,1,0:T(8,128)(2,1)S(1)}, u32[]{:S(2)}, u32[]{:S(2)}) %collective-permute-start.22) | collective-permute-done | bytes 131104 | tf_op jit(solution)/shard_map/ppermute | solution.py:47
  75.2 0.7 collective-permute-done.21
  75.9 0.7 collective-permute-start.25
  76.7 1.5 %collective-permute-start.24 = (bf16[2,4,64,256]{3,2,1,0:T(8,128)(2,1)S(1)}, bf16[2,4,64,256]{3,2,1,0:T(8,128)(2,1)S(1)}, u32[]{:S(2)}, u32[]{:S(2)}) collective-permute-start(bf16[2,4,64,256]{3,2,1,0:T(8,128)(2,1)S(1)} %pad_maximum_fusion.refs_1_), channel_id=1, source_target_pairs={{0,16},{1,17},{2,18},{3,19},{4,20},{5,21},{6,22},{7,23},{8,24},{9,... | collective-permute-start | bytes 786440 | tf_op jit(solution)/shard_map/ppermute | solution.py:47
  78.2 0.5 collective-permute-done.32
  78.7 1.1 %collective-permute-start.35 = (bf16[2,4,64,256]{3,2,1,0:T(8,128)(2,1)S(1)}, bf16[2,4,64,256]{3,2,1,0:T(8,128)(2,1)S(1)}, u32[]{:S(2)}, u32[]{:S(2)}) collective-permute-start(bf16[2,4,64,256]{3,2,1,0:T(8,128)(2,1)S(1)} %pad_maximum_fusion.3.refs_7_), channel_id=1, source_target_pairs={{0,1},{1,0},{2,3},{3,2},{4,5},{5,4},{6,7},{7,6},{8,9},{9,8},{10,11... | collective-permute-start | bytes 786440 | tf_op jit(solution)/shard_map/ppermute | solution.py:47
  79.9 1.1 %collective-permute-start.34 = (bf16[2,4,64,256]{3,2,1,0:T(8,128)(2,1)S(1)}, bf16[2,4,64,256]{3,2,1,0:T(8,128)(2,1)S(1)}, u32[]{:S(2)}, u32[]{:S(2)}) collective-permute-start(bf16[2,4,64,256]{3,2,1,0:T(8,128)(2,1)S(1)} %pad_maximum_fusion.2.refs_5_), channel_id=1, source_target_pairs={{0,16},{1,17},{2,18},{3,19},{4,20},{5,21},{6,22},{7,23},{8,24},{9,... | collective-permute-start | bytes 786440 | tf_op jit(solution)/shard_map/ppermute | solution.py:47
  81.1 4.1 %collective-permute-done.25.refs_4_ = bf16[2,4,64,256]{3,2,1,0:T(8,128)(2,1)S(1)} collective-permute-done((bf16[2,4,64,256]{3,2,1,0:T(8,128)(2,1)S(1)}, bf16[2,4,64,256]{3,2,1,0:T(8,128)(2,1)S(1)}, u32[]{:S(2)}, u32[]{:S(2)}) %collective-permute-start.25) | collective-permute-done | bytes 262176 | tf_op jit(solution)/shard_map/ppermute | solution.py:47
  85.2 0.5 collective-permute-start.27
  85.7 2.3 %collective-permute-done.35.refs_8_ = bf16[2,4,64,256]{3,2,1,0:T(8,128)(2,1)S(1)} collective-permute-done((bf16[2,4,64,256]{3,2,1,0:T(8,128)(2,1)S(1)}, bf16[2,4,64,256]{3,2,1,0:T(8,128)(2,1)S(1)}, u32[]{:S(2)}, u32[]{:S(2)}) %collective-permute-start.35) | collective-permute-done | bytes 262176 | tf_op jit(solution)/shard_map/ppermute | solution.py:47
  88.0 0.5 collective-permute-start.37
  88.5 0.4 collective-permute-start.26
  89.1 1.5 %shard_map.88.refs_13_ = f32[1024,512]{1,0:T(8,128)S(1)} custom-call(bf16[1024,2048]{1,0:T(8,128)(2,1)S(1)} %copy-done, bf16[2,4,64,256]{3,2,1,0:T(8,128)(2,1)S(1)} %pad_maximum_fusion.refs_1_, bf16[2,4,64,256]{3,2,1,0:T(8,128)(2,1)S(1)} %collective-permute-done.24.refs_2_, bf16[2,4,64,256]{3,2,1,0:T(8,128)(2,1)S(1)} %pad_maximum_fusion.1.refs_3_, ...), custom_call_target="tpu_custom_call" | custom-call | flops 1073741824 | bytes 8388608 | tf_op jit(solution)/shard_map/pallas_call | solution.py:332
  91.0 4.8 %shard_map.89 = (bf16[1024,512]{1,0:T(8,128)(2,1)}, f32[64,1024]{1,0:T(8,128)}, f32[64,1024]{1,0:T(8,128)}) custom-call(bf16[1024,2048]{1,0:T(8,128)(2,1)S(1)} %copy-done, bf16[2,4,64,256]{3,2,1,0:T(8,128)(2,1)S(1)} %collective-permute-done.23.refs_1_, bf16[2,4,64,256]{3,2,1,0:T(8,128)(2,1)S(1)} %collective-permute-done.26.refs_2_, ...), custom_call_target="tpu_custom_call" | custom-call | flops 3221225472 | bytes 8388608 | tf_op jit(solution)/shard_map/pallas_call | solution.py:332
  (92 shorter events, 3.0 us)
Async XLA Ops:
  0.6 5.6 %copy-start.1 = (bf16[1024,2048]{1,0:T(8,128)(2,1)S(1)}, bf16[1024,2048]{1,0:T(8,128)(2,1)}, u32[]{:S(2)}) copy-start(bf16[1024,2048]{1,0:T(8,128)(2,1)} %tokens_ref.1) | copy-start | bytes 12582916
  0.6 5.6 %copy-start.2 = (bf16[1024,1024]{1,0:T(8,128)(2,1)S(1)}, bf16[1024,1024]{1,0:T(8,128)(2,1)}, u32[]{:S(2)}) copy-start(bf16[1024,1024]{1,0:T(8,128)(2,1)} %cot_ref.1) | copy-start | bytes 6291460
  5.1 3.5 %collective-permute-start = (bf16[1024,256]{1,0:T(8,128)(2,1)S(1)}, bf16[1024,256]{1,0:T(8,128)(2,1)S(1)}, u32[]{:S(2)}, u32[]{:S(2)}) collective-permute-start(bf16[1024,256]{1,0:T(8,128)(2,1)S(1)} %get-tuple-element.38), channel_id=1, source_target_pairs={{0,8},{1,9},{2,10},{3,11},{4,12},{5,13},{6,14},{7,15},{8,0},{9,1},... | collective-permute-start | bytes 1572872 | tf_op jit(solution)/shard_map/ppermute | solution.py:47
  5.7 3.0 %collective-permute-start.1 = (bf16[1024,256]{1,0:T(8,128)(2,1)S(1)}, bf16[1024,256]{1,0:T(8,128)(2,1)S(1)}, u32[]{:S(2)}, u32[]{:S(2)}) collective-permute-start(bf16[1024,256]{1,0:T(8,128)(2,1)S(1)} %get-tuple-element.39), channel_id=1, source_target_pairs={{0,8},{1,9},{2,10},{3,11},{4,12},{5,13},{6,14},{7,15},{8,0},{9,1},... | collective-permute-start | bytes 1572872 | tf_op jit(solution)/shard_map/ppermute | solution.py:47
  5.7 3.0 %collective-permute-start.2 = (bf16[1024,256]{1,0:T(8,128)(2,1)S(1)}, bf16[1024,256]{1,0:T(8,128)(2,1)S(1)}, u32[]{:S(2)}, u32[]{:S(2)}) collective-permute-start(bf16[1024,256]{1,0:T(8,128)(2,1)S(1)} %get-tuple-element.40), channel_id=1, source_target_pairs={{0,8},{1,9},{2,10},{3,11},{4,12},{5,13},{6,14},{7,15},{8,0},{9,1},... | collective-permute-start | bytes 1572872 | tf_op jit(solution)/shard_map/ppermute | solution.py:47
  6.2 3.3 %collective-permute-start.3 = (bf16[1024,256]{1,0:T(8,128)(2,1)S(1)}, bf16[1024,256]{1,0:T(8,128)(2,1)S(1)}, u32[]{:S(2)}, u32[]{:S(2)}) collective-permute-start(bf16[1024,256]{1,0:T(8,128)(2,1)S(1)} %get-tuple-element.41), channel_id=1, source_target_pairs={{0,8},{1,9},{2,10},{3,11},{4,12},{5,13},{6,14},{7,15},{8,0},{9,1},... | collective-permute-start | bytes 1572872 | tf_op jit(solution)/shard_map/ppermute | solution.py:47
  10.5 10.1 %collective-permute-start.4 = (bf16[2,4,64,256]{3,2,1,0:T(8,128)(2,1)S(1)}, bf16[2,4,64,256]{3,2,1,0:T(8,128)(2,1)}, u32[]{:S(2)}, u32[]{:S(2)}) collective-permute-start(bf16[2,4,64,256]{3,2,1,0:T(8,128)(2,1)S(1)} %get-tuple-element.43), channel_id=1, source_target_pairs={{0,16},{1,17},{2,18},{3,19},{4,20},{5,21},{6,22},{7,23},{8,24},{9,... | collective-permute-start | bytes 786440 | tf_op jit(solution)/shard_map/ppermute | solution.py:47
  13.4 9.2 %collective-permute-start.5 = (bf16[2,4,64,256]{3,2,1,0:T(8,128)(2,1)S(1)}, bf16[2,4,64,256]{3,2,1,0:T(8,128)(2,1)S(1)}, u32[]{:S(2)}, u32[]{:S(2)}) collective-permute-start(bf16[2,4,64,256]{3,2,1,0:T(8,128)(2,1)S(1)} %get-tuple-element.44), channel_id=1, source_target_pairs={{0,1},{1,0},{2,3},{3,2},{4,5},{5,4},{6,7},{7,6},{8,9},{9,8},{10,11... | collective-permute-start | bytes 786440 | tf_op jit(solution)/shard_map/ppermute | solution.py:47
  14.9 11.0 %collective-permute-start.11 = (bf16[2,4,64,256]{3,2,1,0:T(8,128)(2,1)S(1)}, bf16[2,4,64,256]{3,2,1,0:T(8,128)(2,1)S(1)}, u32[]{:S(2)}, u32[]{:S(2)}) collective-permute-start(bf16[2,4,64,256]{3,2,1,0:T(8,128)(2,1)S(1)} %get-tuple-element.51), channel_id=1, source_target_pairs={{0,16},{1,17},{2,18},{3,19},{4,20},{5,21},{6,22},{7,23},{8,24},{9,... | collective-permute-start | bytes 786440 | tf_op jit(solution)/shard_map/ppermute | solution.py:47
  15.5 12.8 %collective-permute-start.12 = (bf16[2,4,64,256]{3,2,1,0:T(8,128)(2,1)S(1)}, bf16[2,4,64,256]{3,2,1,0:T(8,128)(2,1)S(1)}, u32[]{:S(2)}, u32[]{:S(2)}) collective-permute-start(bf16[2,4,64,256]{3,2,1,0:T(8,128)(2,1)S(1)} %get-tuple-element.52), channel_id=1, source_target_pairs={{0,1},{1,0},{2,3},{3,2},{4,5},{5,4},{6,7},{7,6},{8,9},{9,8},{10,11... | collective-permute-start | bytes 786440 | tf_op jit(solution)/shard_map/ppermute | solution.py:47
  23.7 7.2 %collective-permute-start.6 = (bf16[4,64,256]{2,1,0:T(8,128)(2,1)S(1)}, bf16[4,64,256]{2,1,0:T(8,128)(2,1)S(1)}, u32[]{:S(2)}, u32[]{:S(2)}) collective-permute-start(bf16[4,64,256]{2,1,0:T(8,128)(2,1)S(1)} %fusion.13), channel_id=1, source_target_pairs={{0,1},{1,0},{2,3},{3,2},{4,5},{5,4},{6,7},{7,6},{8,9},{9,8},{10,11... | collective-permute-start | bytes 393224 | tf_op jit(solution)/shard_map/ppermute | solution.py:47
  25.3 5.6 %collective-permute-start.7 = (bf16[4,64,256]{2,1,0:T(8,128)(2,1)S(1)}, bf16[4,64,256]{2,1,0:T(8,128)(2,1)S(1)}, u32[]{:S(2)}, u32[]{:S(2)}) collective-permute-start(bf16[4,64,256]{2,1,0:T(8,128)(2,1)S(1)} %fusion.14), channel_id=1, source_target_pairs={{0,16},{1,17},{2,18},{3,19},{4,20},{5,21},{6,22},{7,23},{8,24},{9,... | collective-permute-start | bytes 393224 | tf_op jit(solution)/shard_map/ppermute | solution.py:47
  28.3 28.3 %copy-start.3 = (f32[64,1024]{1,0:T(8,128)S(1)}, f32[64,1024]{1,0:T(8,128)}, u32[]{:S(2)}) copy-start(f32[64,1024]{1,0:T(8,128)} %refs_17_.1) | copy-start | bytes 786436
  28.3 28.2 %copy-start.4 = (f32[64,1024]{1,0:T(8,128)S(1)}, f32[64,1024]{1,0:T(8,128)}, u32[]{:S(2)}) copy-start(f32[64,1024]{1,0:T(8,128)} %refs_16_.1) | copy-start | bytes 786436
  28.4 28.2 %copy-start.5 = (f32[64,1024]{1,0:T(8,128)S(1)}, f32[64,1024]{1,0:T(8,128)}, u32[]{:S(2)}) copy-start(f32[64,1024]{1,0:T(8,128)} %param.8) | copy-start | bytes 786436
  28.4 6.9 %collective-permute-start.13 = (bf16[4,64,256]{2,1,0:T(8,128)(2,1)S(1)}, bf16[4,64,256]{2,1,0:T(8,128)(2,1)S(1)}, u32[]{:S(2)}, u32[]{:S(2)}) collective-permute-start(bf16[4,64,256]{2,1,0:T(8,128)(2,1)S(1)} %fusion.15), channel_id=1, source_target_pairs={{0,1},{1,0},{2,3},{3,2},{4,5},{5,4},{6,7},{7,6},{8,9},{9,8},{10,11... | collective-permute-start | bytes 393224 | tf_op jit(solution)/shard_map/ppermute | solution.py:47
  30.1 5.2 %collective-permute-start.14 = (bf16[4,64,256]{2,1,0:T(8,128)(2,1)S(1)}, bf16[4,64,256]{2,1,0:T(8,128)(2,1)S(1)}, u32[]{:S(2)}, u32[]{:S(2)}) collective-permute-start(bf16[4,64,256]{2,1,0:T(8,128)(2,1)S(1)} %fusion.16), channel_id=1, source_target_pairs={{0,16},{1,17},{2,18},{3,19},{4,20},{5,21},{6,22},{7,23},{8,24},{9,... | collective-permute-start | bytes 393224 | tf_op jit(solution)/shard_map/ppermute | solution.py:47
  31.0 7.9 %collective-permute-start.10 = (bf16[64,512]{1,0:T(8,128)(2,1)S(1)}, bf16[64,512]{1,0:T(8,128)(2,1)S(1)}, u32[]{:S(2)}, u32[]{:S(2)}) collective-permute-start(bf16[64,512]{1,0:T(8,128)(2,1)S(1)} %get-tuple-element.84), channel_id=1, source_target_pairs={{0,2},{1,3},{2,0},{3,1},{4,6},{5,7},{6,4},{7,5},{8,10},{9,11},{10,... | collective-permute-start | bytes 196616 | tf_op jit(solution)/shard_map/ppermute | solution.py:47
  32.6 7.2 %collective-permute-start.8 = (bf16[64,512]{1,0:T(8,128)(2,1)S(1)}, bf16[64,512]{1,0:T(8,128)(2,1)S(1)}, u32[]{:S(2)}, u32[]{:S(2)}) collective-permute-start(bf16[64,512]{1,0:T(8,128)(2,1)S(1)} %get-tuple-element.82), channel_id=1, source_target_pairs={{0,6},{1,7},{2,4},{3,5},{4,2},{5,3},{6,0},{7,1},{8,14},{9,15},{10,... | collective-permute-start | bytes 196616 | tf_op jit(solution)/shard_map/ppermute | solution.py:47
  35.1 8.9 %collective-permute-start.9 = (bf16[64,512]{1,0:T(8,128)(2,1)S(1)}, bf16[64,512]{1,0:T(8,128)(2,1)S(1)}, u32[]{:S(2)}, u32[]{:S(2)}) collective-permute-start(bf16[64,512]{1,0:T(8,128)(2,1)S(1)} %get-tuple-element.83), channel_id=1, source_target_pairs={{0,4},{1,5},{2,6},{3,7},{4,0},{5,1},{6,2},{7,3},{8,12},{9,13},{10,... | collective-permute-start | bytes 196616 | tf_op jit(solution)/shard_map/ppermute | solution.py:47
  35.4 8.7 %collective-permute-start.15 = (bf16[64,512]{1,0:T(8,128)(2,1)S(1)}, bf16[64,512]{1,0:T(8,128)(2,1)S(1)}, u32[]{:S(2)}, u32[]{:S(2)}) collective-permute-start(bf16[64,512]{1,0:T(8,128)(2,1)S(1)} %get-tuple-element.79), channel_id=1, source_target_pairs={{0,6},{1,7},{2,4},{3,5},{4,2},{5,3},{6,0},{7,1},{8,14},{9,15},{10,... | collective-permute-start | bytes 196616 | tf_op jit(solution)/shard_map/ppermute | solution.py:47
  38.9 7.0 %collective-permute-start.16 = (bf16[64,512]{1,0:T(8,128)(2,1)S(1)}, bf16[64,512]{1,0:T(8,128)(2,1)S(1)}, u32[]{:S(2)}, u32[]{:S(2)}) collective-permute-start(bf16[64,512]{1,0:T(8,128)(2,1)S(1)} %get-tuple-element.80), channel_id=1, source_target_pairs={{0,4},{1,5},{2,6},{3,7},{4,0},{5,1},{6,2},{7,3},{8,12},{9,13},{10,... | collective-permute-start | bytes 196616 | tf_op jit(solution)/shard_map/ppermute | solution.py:47
  38.9 7.0 %collective-permute-start.17 = (bf16[64,512]{1,0:T(8,128)(2,1)S(1)}, bf16[64,512]{1,0:T(8,128)(2,1)S(1)}, u32[]{:S(2)}, u32[]{:S(2)}) collective-permute-start(bf16[64,512]{1,0:T(8,128)(2,1)S(1)} %get-tuple-element.81), channel_id=1, source_target_pairs={{0,2},{1,3},{2,0},{3,1},{4,6},{5,7},{6,4},{7,5},{8,10},{9,11},{10,... | collective-permute-start | bytes 196616 | tf_op jit(solution)/shard_map/ppermute | solution.py:47
  56.5 32.6 %copy-start = (bf16[1024,2048]{1,0:T(8,128)(2,1)S(1)}, bf16[1024,2048]{1,0:T(8,128)(2,1)}, u32[]{:S(2)}) copy-start(bf16[1024,2048]{1,0:T(8,128)(2,1)} %refs_0_.3) | copy-start | bytes 12582916
  56.8 5.7 %collective-permute-start.18 = (bf16[64,512]{1,0:T(8,128)(2,1)S(1)}, bf16[64,512]{1,0:T(8,128)(2,1)S(1)}, u32[]{:S(2)}, u32[]{:S(2)}) collective-permute-start(bf16[64,512]{1,0:T(8,128)(2,1)S(1)} %get-tuple-element.58), channel_id=1, source_target_pairs={{0,2},{1,3},{2,0},{3,1},{4,6},{5,7},{6,4},{7,5},{8,10},{9,11},{10,... | collective-permute-start | bytes 196616 | tf_op jit(solution)/shard_map/ppermute | solution.py:47
  57.4 11.4 %collective-permute-start.19 = (bf16[64,512]{1,0:T(8,128)(2,1)S(1)}, bf16[64,512]{1,0:T(8,128)(2,1)S(1)}, u32[]{:S(2)}, u32[]{:S(2)}) collective-permute-start(bf16[64,512]{1,0:T(8,128)(2,1)S(1)} %get-tuple-element.58), channel_id=1, source_target_pairs={{0,4},{1,5},{2,6},{3,7},{4,0},{5,1},{6,2},{7,3},{8,12},{9,13},{10,... | collective-permute-start | bytes 196616 | tf_op jit(solution)/shard_map/ppermute | solution.py:47
  58.1 10.7 %collective-permute-start.20 = (bf16[64,512]{1,0:T(8,128)(2,1)S(1)}, bf16[64,512]{1,0:T(8,128)(2,1)S(1)}, u32[]{:S(2)}, u32[]{:S(2)}) collective-permute-start(bf16[64,512]{1,0:T(8,128)(2,1)S(1)} %get-tuple-element.58), channel_id=1, source_target_pairs={{0,6},{1,7},{2,4},{3,5},{4,2},{5,3},{6,0},{7,1},{8,14},{9,15},{10,... | collective-permute-start | bytes 196616 | tf_op jit(solution)/shard_map/ppermute | solution.py:47
  61.3 9.0 %collective-permute-start.29 = (bf16[64,512]{1,0:T(8,128)(2,1)S(1)}, bf16[64,512]{1,0:T(8,128)(2,1)S(1)}, u32[]{:S(2)}, u32[]{:S(2)}) collective-permute-start(bf16[64,512]{1,0:T(8,128)(2,1)S(1)} %get-tuple-element.63), channel_id=1, source_target_pairs={{0,2},{1,3},{2,0},{3,1},{4,6},{5,7},{6,4},{7,5},{8,10},{9,11},{10,... | collective-permute-start | bytes 196616 | tf_op jit(solution)/shard_map/ppermute | solution.py:47
  61.3 10.0 %collective-permute-start.30 = (bf16[64,512]{1,0:T(8,128)(2,1)S(1)}, bf16[64,512]{1,0:T(8,128)(2,1)S(1)}, u32[]{:S(2)}, u32[]{:S(2)}) collective-permute-start(bf16[64,512]{1,0:T(8,128)(2,1)S(1)} %get-tuple-element.63), channel_id=1, source_target_pairs={{0,4},{1,5},{2,6},{3,7},{4,0},{5,1},{6,2},{7,3},{8,12},{9,13},{10,... | collective-permute-start | bytes 196616 | tf_op jit(solution)/shard_map/ppermute | solution.py:47
  62.5 8.8 %collective-permute-start.31 = (bf16[64,512]{1,0:T(8,128)(2,1)S(1)}, bf16[64,512]{1,0:T(8,128)(2,1)S(1)}, u32[]{:S(2)}, u32[]{:S(2)}) collective-permute-start(bf16[64,512]{1,0:T(8,128)(2,1)S(1)} %get-tuple-element.63), channel_id=1, source_target_pairs={{0,6},{1,7},{2,4},{3,5},{4,2},{5,3},{6,0},{7,1},{8,14},{9,15},{10,... | collective-permute-start | bytes 196616 | tf_op jit(solution)/shard_map/ppermute | solution.py:47
  68.9 6.4 %collective-permute-start.22 = (bf16[4,64,256]{2,1,0:T(8,128)(2,1)S(1)}, bf16[4,64,256]{2,1,0:T(8,128)(2,1)S(1)}, u32[]{:S(2)}, u32[]{:S(2)}) collective-permute-start(bf16[4,64,256]{2,1,0:T(8,128)(2,1)S(1)} %get-tuple-element.90), channel_id=1, source_target_pairs={{0,16},{1,17},{2,18},{3,19},{4,20},{5,21},{6,22},{7,23},{8,24},{9,... | collective-permute-start | bytes 393224 | tf_op jit(solution)/shard_map/ppermute | solution.py:47
  69.5 6.4 %collective-permute-start.21 = (bf16[4,64,256]{2,1,0:T(8,128)(2,1)S(1)}, bf16[4,64,256]{2,1,0:T(8,128)(2,1)S(1)}, u32[]{:S(2)}, u32[]{:S(2)}) collective-permute-start(bf16[4,64,256]{2,1,0:T(8,128)(2,1)S(1)} %get-tuple-element.92), channel_id=1, source_target_pairs={{0,1},{1,0},{2,3},{3,2},{4,5},{5,4},{6,7},{7,6},{8,9},{9,8},{10,11... | collective-permute-start | bytes 393224 | tf_op jit(solution)/shard_map/ppermute | solution.py:47
  71.3 6.9 %collective-permute-start.33 = (bf16[4,64,256]{2,1,0:T(8,128)(2,1)S(1)}, bf16[4,64,256]{2,1,0:T(8,128)(2,1)S(1)}, u32[]{:S(2)}, u32[]{:S(2)}) collective-permute-start(bf16[4,64,256]{2,1,0:T(8,128)(2,1)S(1)} %get-tuple-element.86), channel_id=1, source_target_pairs={{0,16},{1,17},{2,18},{3,19},{4,20},{5,21},{6,22},{7,23},{8,24},{9,... | collective-permute-start | bytes 393224 | tf_op jit(solution)/shard_map/ppermute | solution.py:47
  72.0 6.7 %collective-permute-start.32 = (bf16[4,64,256]{2,1,0:T(8,128)(2,1)S(1)}, bf16[4,64,256]{2,1,0:T(8,128)(2,1)S(1)}, u32[]{:S(2)}, u32[]{:S(2)}) collective-permute-start(bf16[4,64,256]{2,1,0:T(8,128)(2,1)S(1)} %get-tuple-element.88), channel_id=1, source_target_pairs={{0,1},{1,0},{2,3},{3,2},{4,5},{5,4},{6,7},{7,6},{8,9},{9,8},{10,11... | collective-permute-start | bytes 393224 | tf_op jit(solution)/shard_map/ppermute | solution.py:47
  75.9 9.2 %collective-permute-start.25 = (bf16[2,4,64,256]{3,2,1,0:T(8,128)(2,1)S(1)}, bf16[2,4,64,256]{3,2,1,0:T(8,128)(2,1)S(1)}, u32[]{:S(2)}, u32[]{:S(2)}) collective-permute-start(bf16[2,4,64,256]{3,2,1,0:T(8,128)(2,1)S(1)} %pad_maximum_fusion.1.refs_3_), channel_id=1, source_target_pairs={{0,1},{1,0},{2,3},{3,2},{4,5},{5,4},{6,7},{7,6},{8,9},{9,8},{10,11... | collective-permute-start | bytes 786440 | tf_op jit(solution)/shard_map/ppermute | solution.py:47
  76.7 8.5 %collective-permute-start.24 = (bf16[2,4,64,256]{3,2,1,0:T(8,128)(2,1)S(1)}, bf16[2,4,64,256]{3,2,1,0:T(8,128)(2,1)S(1)}, u32[]{:S(2)}, u32[]{:S(2)}) collective-permute-start(bf16[2,4,64,256]{3,2,1,0:T(8,128)(2,1)S(1)} %pad_maximum_fusion.refs_1_), channel_id=1, source_target_pairs={{0,16},{1,17},{2,18},{3,19},{4,20},{5,21},{6,22},{7,23},{8,24},{9,... | collective-permute-start | bytes 786440 | tf_op jit(solution)/shard_map/ppermute | solution.py:47
  78.7 9.2 %collective-permute-start.35 = (bf16[2,4,64,256]{3,2,1,0:T(8,128)(2,1)S(1)}, bf16[2,4,64,256]{3,2,1,0:T(8,128)(2,1)S(1)}, u32[]{:S(2)}, u32[]{:S(2)}) collective-permute-start(bf16[2,4,64,256]{3,2,1,0:T(8,128)(2,1)S(1)} %pad_maximum_fusion.3.refs_7_), channel_id=1, source_target_pairs={{0,1},{1,0},{2,3},{3,2},{4,5},{5,4},{6,7},{7,6},{8,9},{9,8},{10,11... | collective-permute-start | bytes 786440 | tf_op jit(solution)/shard_map/ppermute | solution.py:47
  79.9 8.1 %collective-permute-start.34 = (bf16[2,4,64,256]{3,2,1,0:T(8,128)(2,1)S(1)}, bf16[2,4,64,256]{3,2,1,0:T(8,128)(2,1)S(1)}, u32[]{:S(2)}, u32[]{:S(2)}) collective-permute-start(bf16[2,4,64,256]{3,2,1,0:T(8,128)(2,1)S(1)} %pad_maximum_fusion.2.refs_5_), channel_id=1, source_target_pairs={{0,16},{1,17},{2,18},{3,19},{4,20},{5,21},{6,22},{7,23},{8,24},{9,... | collective-permute-start | bytes 786440 | tf_op jit(solution)/shard_map/ppermute | solution.py:47
  81.1 7.4 %collective-permute-start.38 = (bf16[2,4,64,256]{3,2,1,0:T(8,128)(2,1)S(1)}, bf16[2,4,64,256]{3,2,1,0:T(8,128)(2,1)S(1)}, u32[]{:S(2)}, u32[]{:S(2)}) collective-permute-start(bf16[2,4,64,256]{3,2,1,0:T(8,128)(2,1)S(1)} %pad_maximum_fusion.3.refs_7_), channel_id=1, source_target_pairs={{0,8},{1,9},{2,10},{3,11},{4,12},{5,13},{6,14},{7,15},{8,0},{9,1},... | collective-permute-start | bytes 786440 | tf_op jit(solution)/shard_map/ppermute | solution.py:47
  85.1 3.4 %collective-permute-start.36 = (bf16[2,4,64,256]{3,2,1,0:T(8,128)(2,1)S(1)}, bf16[2,4,64,256]{3,2,1,0:T(8,128)(2,1)S(1)}, u32[]{:S(2)}, u32[]{:S(2)}) collective-permute-start(bf16[2,4,64,256]{3,2,1,0:T(8,128)(2,1)S(1)} %pad_maximum_fusion.2.refs_5_), channel_id=1, source_target_pairs={{0,8},{1,9},{2,10},{3,11},{4,12},{5,13},{6,14},{7,15},{8,0},{9,1},... | collective-permute-start | bytes 786440 | tf_op jit(solution)/shard_map/ppermute | solution.py:47
  85.2 3.8 %collective-permute-start.27 = (bf16[2,4,64,256]{3,2,1,0:T(8,128)(2,1)S(1)}, bf16[2,4,64,256]{3,2,1,0:T(8,128)(2,1)S(1)}, u32[]{:S(2)}, u32[]{:S(2)}) collective-permute-start(bf16[2,4,64,256]{3,2,1,0:T(8,128)(2,1)S(1)} %pad_maximum_fusion.1.refs_3_), channel_id=1, source_target_pairs={{0,8},{1,9},{2,10},{3,11},{4,12},{5,13},{6,14},{7,15},{8,0},{9,1},... | collective-permute-start | bytes 786440 | tf_op jit(solution)/shard_map/ppermute | solution.py:47
  88.0 2.6 %collective-permute-start.23 = (bf16[2,4,64,256]{3,2,1,0:T(8,128)(2,1)S(1)}, bf16[2,4,64,256]{3,2,1,0:T(8,128)(2,1)S(1)}, u32[]{:S(2)}, u32[]{:S(2)}) collective-permute-start(bf16[2,4,64,256]{3,2,1,0:T(8,128)(2,1)S(1)} %pad_maximum_fusion.refs_1_), channel_id=1, source_target_pairs={{0,8},{1,9},{2,10},{3,11},{4,12},{5,13},{6,14},{7,15},{8,0},{9,1},... | collective-permute-start | bytes 786440 | tf_op jit(solution)/shard_map/ppermute | solution.py:47
  88.0 2.6 %collective-permute-start.37 = (bf16[2,4,64,256]{3,2,1,0:T(8,128)(2,1)S(1)}, bf16[2,4,64,256]{3,2,1,0:T(8,128)(2,1)S(1)}, u32[]{:S(2)}, u32[]{:S(2)}) collective-permute-start(bf16[2,4,64,256]{3,2,1,0:T(8,128)(2,1)S(1)} %collective-permute-done.34.refs_6_), channel_id=1, source_target_pairs={{0,8},{1,9},{2,10},{3,11},{4,12},{5,13},{6,14},{7,15},{8,0},{9,1},... | collective-permute-start | bytes 786440 | tf_op jit(solution)/shard_map/ppermute | solution.py:47
  88.5 2.1 %collective-permute-start.39 = (bf16[2,4,64,256]{3,2,1,0:T(8,128)(2,1)S(1)}, bf16[2,4,64,256]{3,2,1,0:T(8,128)(2,1)S(1)}, u32[]{:S(2)}, u32[]{:S(2)}) collective-permute-start(bf16[2,4,64,256]{3,2,1,0:T(8,128)(2,1)S(1)} %collective-permute-done.35.refs_8_), channel_id=1, source_target_pairs={{0,8},{1,9},{2,10},{3,11},{4,12},{5,13},{6,14},{7,15},{8,0},{9,1},... | collective-permute-start | bytes 786440 | tf_op jit(solution)/shard_map/ppermute | solution.py:47
  88.5 2.1 %collective-permute-start.26 = (bf16[2,4,64,256]{3,2,1,0:T(8,128)(2,1)S(1)}, bf16[2,4,64,256]{3,2,1,0:T(8,128)(2,1)S(1)}, u32[]{:S(2)}, u32[]{:S(2)}) collective-permute-start(bf16[2,4,64,256]{3,2,1,0:T(8,128)(2,1)S(1)} %collective-permute-done.24.refs_2_), channel_id=1, source_target_pairs={{0,8},{1,9},{2,10},{3,11},{4,12},{5,13},{6,14},{7,15},{8,0},{9,1},... | collective-permute-start | bytes 786440 | tf_op jit(solution)/shard_map/ppermute | solution.py:47
  89.0 2.0 %collective-permute-start.28 = (bf16[2,4,64,256]{3,2,1,0:T(8,128)(2,1)S(1)}, bf16[2,4,64,256]{3,2,1,0:T(8,128)(2,1)S(1)}, u32[]{:S(2)}, u32[]{:S(2)}) collective-permute-start(bf16[2,4,64,256]{3,2,1,0:T(8,128)(2,1)S(1)} %collective-permute-done.25.refs_4_), channel_id=1, source_target_pairs={{0,8},{1,9},{2,10},{3,11},{4,12},{5,13},{6,14},{7,15},{8,0},{9,1},... | collective-permute-start | bytes 786440 | tf_op jit(solution)/shard_map/ppermute | solution.py:47

commit v7 on v6

--- a/solution.py
+++ b/solution.py
@@ -212,7 +212,7 @@
 def scatter_z(grid, totals):
     whole = jnp.concatenate(totals, axis=2)
     arriving = yield [
-        (pick(whole, 0, grid.here("z", k)).astype(BF16), {"z": k}) for k in reversed(range(1, grid.size["z"]))
+        (pick(whole, 0, grid.here("z", k)).astype(BF16), {"z": k}) for k in list(range(1, grid.size["z"]))
     ]
     total = pick(whole, 0, grid.here("z"))
     for value in arriving:
@@ -246,8 +246,9 @@
 
 def gather_z(grid, low, widths):
     steps = range(1, grid.size["z"])
-    pieces = yield [(low, {"z": k}) for k in reversed(steps)]
-    pieces = [low] + pieces[::-1]
+    way = [grid.size["z"] - 1, *range(1, grid.size["z"] - 1)]
+    pieces = yield [(low, {"z": k}) for k in way]
+    pieces = [low] + [pieces[way.index(k)] for k in steps]
     starts = [sum(widths[:k]) for k in range(len(widths))]
     yield [jnp.stack([p[:, a : a + width] for p in pieces]) for a, width in zip(starts, widths)]
 
@@ -274,16 +275,14 @@
     return found
 
 
-def project_kernel(grid, plan, rows, finish, *refs):
+def project_kernel(grid, plan, rows, before, finish, *refs):
     refs = list(refs)
     nx, ny, nz = (grid.size[axis] for axis in "xyz")
     tokens = refs.pop(0)
     pieces = [[[refs.pop(0) for _ in range(grid.size[order[0]])] for _, order, _, _ in cut] for _, _, cut in plan]
-    if finish:
-        earlier, *state = [refs.pop(0) for _ in range(5)]
-        out, *new, held = refs
-    else:
-        out, held = refs
+    earlier = refs.pop(0) if before else None
+    state = [refs.pop(0) for _ in range(4)] if finish else []
+    out, *new, held = refs
     block = nz * ny * rows
 
     @pl.when(pl.program_id(0) == 0)
@@ -306,7 +305,7 @@
                             held[i, at, columns] = piece[one][two, kz, :, inner].astype(held.dtype)
 
     tile = pl.ds(pl.multiple_of(pl.program_id(0) * out.shape[0], out.shape[0]), out.shape[0])
-    totals = [earlier[tile, :], None] if finish else [None]
+    totals = [earlier[tile, :] if before else None, None]
     for i, (h, kc, _) in enumerate(plan):
         for x in range(nx):
             weight = held[i, x * block : (x + 1) * block, :].astype(BF16)
@@ -327,20 +326,20 @@
     rows = flat[0].shape[2]
     tile = min(count, 512)
     held = BF16 if rows % 16 == 0 else F32
-    finish = earlier is not None
+    before, finish = earlier is not None, bool(state)
     tiled = pl.BlockSpec((tile, half), lambda t: (t, 0))
     return pl.pallas_call(
-        functools.partial(project_kernel, grid, plan, rows, finish),
+        functools.partial(project_kernel, grid, plan, rows, before, finish),
         out_shape=[jax.ShapeDtypeStruct((count, half), BF16 if finish else F32)]
         + [jax.ShapeDtypeStruct(value.shape, F32) for value in state[-2:]],
         grid=(count // tile,),
-        in_specs=[pl.BlockSpec(memory_space=pltpu.VMEM)] * (1 + len(flat) + finish + len(state)),
+        in_specs=[pl.BlockSpec(memory_space=pltpu.VMEM)] * (1 + len(flat) + before + len(state)),
         out_specs=[tiled] + [pl.BlockSpec(value.shape, lambda t: (0, 0)) for value in state[-2:]],
         scratch_shapes=[pltpu.VMEM((len(plan), nx * block, half), held)],
         **kernel_params(
             2 * count * nx * block * len(plan) * half, count * depth * 2 + count * half * 8, SMALL
         ),
-    )(tokens, *flat, *([earlier] if finish else []), *state)
+    )(tokens, *flat, *([earlier] if before else []), *state)
 
 
 def shards(tokens, grad_out, master_weight, first_moment, second_moment, next_tokens):
@@ -379,7 +378,12 @@
             came_in = lax.optimization_barrier(stage(grid, wanted))
             yield
             wanted = [way.send(got) for way, got in zip(ways, came_in)]
-        yield clipped, wanted, [[grid.send(piece, c=1) for piece in table] for table in wanted]
+        early = [[grid.send(table[0], c=1)] for table in wanted]
+        after = yield clipped, wanted
+        last = [table[1:] for table in wanted]
+        if after is not None:
+            last, _ = lax.optimization_barrier((last, after))
+        yield [first + [grid.send(piece, c=1) for piece in rest] for first, rest in zip(early, last)]
 
     def run(ways):
         for _ in range(3):
@@ -391,11 +395,14 @@
     squares = jnp.sum((grad * grad).reshape(grad.shape[0], 2, -1, LANES), axis=(0, 2))
     factors = clip_factor(sum_everywhere(squares))
     factors = lax.optimization_barrier(jnp.broadcast_to(factors[:, None], (2, half)).reshape(1, total))
-    (clipped_a, own_a, other_a), (clipped_b, own_b, other_b) = run([gather(0, grad, factors), gather(2, grad, factors)])
-    own, other = own_a + own_b, other_a + other_b
+    ways = [gather(0, grad, factors), gather(2, grad, factors)]
+    (clipped_a, own_a), (clipped_b, own_b) = run(ways)
+    own = own_a + own_b
     (gate,) = project(grid, next_tokens, [(0, 0, own)], outward, half)
-    places = [(0, 1, other), (1, 0, own), (1, 1, other)]
+    other = ways[0].send(gate) + ways[1].send(None)
+    (gate,) = project(grid, next_tokens, [(0, 1, other)], outward, half, gate)
     state = (clipped_a, clipped_b, first_moment, second_moment)
+    places = [(1, 0, own), (1, 1, other)]
     next_hidden, new_first, new_second = project(grid, next_tokens, places, outward, half, gate, state)
     return new_first, new_second, next_hidden
 

time: 96 us -> 94.6 us (0.985)
  starting transfers between devices: 37.6 us -> 36.4 us
    ppermute x40, starting transfers between devices: 37.6 us -> 36.4 us  [send(): return lax.ppermute(value, AXES, pairs)]
    pallas_call x2 -> x3, Pallas kernels: 6.33 us -> 6.74 us  [project(): pl.pallas_call(functools.partial(project_kernel, grid, plan, rows, before...]
  transfers between devices with their start and end apart: 40 -> 40, of which waited for: 15 -> 18; matrix products, arithmetic and copies ran while one was open for 2% -> 2% of each run, Pallas kernels for 4% -> 6%
where the time goes in v7:
time: 94.6 us; the launch traced here: 94.4 us
  starting transfers between devices  36.4 us (38%)
  waiting for transfers between devices  30.5 us (32%)
  Pallas kernels  14.7 us (16%)
  blocking collectives  9.47 us (10%)
  other arithmetic  2.07 us (2%)
  between operations  1 us (1%)
    ppermute x40, starting transfers between devices, send(): return lax.ppermute(value, AXES, pairs)  36.4 us
    ppermute x40, waiting for transfers between devices, send(): return lax.ppermute(value, AXES, pairs)  30.5 us
    all_to_all x1, blocking collectives, sum_everywhere(): lax.all_to_all(jnp.broadcast_to(value, (count, *value.shape)), AXES, 0, 0...  9.47 us
    pallas_call x3, Pallas kernels, project(): pl.pallas_call(functools.partial(project_kernel, grid, plan, rows, before...  6.74 us
    pallas_call x1, Pallas kernels, sent_rows(): pl.pallas_call(functools.partial(sent_kernel, grid, parts), out_shape=[ja...  4.49 us
    pallas_call x1, Pallas kernels, kept_product(): pl.pallas_call(functools.partial(kept_product_kernel, grid), out_shape=ja...  2.38 us
  transfers between devices with their start and end apart: 40, of which 18 were waited for; matrix products, arithmetic and copies ran while one was open for 2% of the time, Pallas kernels for 6%

profile of v7, /device:TPU:0, one launch (start us, length us, event | category | flops | bytes accessed | tf_op | source)
XLA Modules:
  0.0 94.4 jit_solution(167263144205554282)
XLA Ops:
  0.6 4.5 %shard_map.86 = (bf16[1024,256]{1,0:T(8,128)(2,1)S(1)}, bf16[1024,256]{1,0:T(8,128)(2,1)S(1)}, bf16[1024,256]{1,0:T(8,128)(2,1)S(1)}, bf16[1024,256]{1,0:T(8,128)(2,1)S(1)}) custom-call(bf16[1024,2048]{1,0:T(8,128)(2,1)} %tokens_ref.1, bf16[1024,1024]{1,0:T(8,128)(2,1)} %cot_ref.1), custom_call_target="tpu_custom_call" | custom-call | flops 2147483648 | bytes 4194304 | tf_op jit(solution)/shard_map/pallas_call | solution.py:110
  6.3 2.4 %shard_map.85.value_ref = f32[1024,1024]{1,0:T(8,128)S(1)} custom-call(bf16[1024,2048]{1,0:T(8,128)(2,1)S(1)} %copy-done.1, bf16[1024,1024]{1,0:T(8,128)(2,1)S(1)} %copy-done.2), custom_call_target="tpu_custom_call" | custom-call | flops 2147483648 | bytes 4194304 | tf_op jit(solution)/shard_map/pallas_call | solution.py:133
  8.7 0.7 collective-permute-done.3.refs_3_
  9.5 1.0 %shard_map.87 = (bf16[2,4,64,256]{3,2,1,0:T(8,128)(2,1)S(1)}, bf16[2,4,64,256]{3,2,1,0:T(8,128)(2,1)S(1)}, bf16[2,4,64,256]{3,2,1,0:T(8,128)(2,1)S(1)}, bf16[2,4...) custom-call(f32[1024,1024]{1,0:T(8,128)S(1)} %shard_map.85.value_ref, ...), custom_call_target="tpu_custom_call" | custom-call | bytes 12582912 | tf_op jit(solution)/shard_map/pallas_call | solution.py:179
  10.5 2.9 %collective-permute-start.4 = (bf16[2,4,64,256]{3,2,1,0:T(8,128)(2,1)S(1)}, bf16[2,4,64,256]{3,2,1,0:T(8,128)(2,1)}, u32[]{:S(2)}, u32[]{:S(2)}) collective-permute-start(bf16[2,4,64,256]{3,2,1,0:T(8,128)(2,1)S(1)} %get-tuple-element.45), channel_id=1, source_target_pairs={{0,16},{1,17},{2,18},{3,19},{4,20},{5,21},{6,22},{7,23},{8,24},{9,... | collective-permute-start | bytes 786440 | tf_op jit(solution)/shard_map/ppermute | solution.py:47
  13.4 1.5 %collective-permute-start.5 = (bf16[2,4,64,256]{3,2,1,0:T(8,128)(2,1)S(1)}, bf16[2,4,64,256]{3,2,1,0:T(8,128)(2,1)S(1)}, u32[]{:S(2)}, u32[]{:S(2)}) collective-permute-start(bf16[2,4,64,256]{3,2,1,0:T(8,128)(2,1)S(1)} %get-tuple-element.46), channel_id=1, source_target_pairs={{0,1},{1,0},{2,3},{3,2},{4,5},{5,4},{6,7},{7,6},{8,9},{9,8},{10,11... | collective-permute-start | bytes 786440 | tf_op jit(solution)/shard_map/ppermute | solution.py:47
  14.9 0.5 collective-permute-start.11
  15.5 5.1 %collective-permute-done.4 = bf16[2,4,64,256]{3,2,1,0:T(8,128)(2,1)} collective-permute-done((bf16[2,4,64,256]{3,2,1,0:T(8,128)(2,1)S(1)}, bf16[2,4,64,256]{3,2,1,0:T(8,128)(2,1)}, u32[]{:S(2)}, u32[]{:S(2)}) %collective-permute-start.4) | collective-permute-done | bytes 262176 | tf_op jit(solution)/shard_map/ppermute | solution.py:47
  20.6 2.0 %collective-permute-done.5 = bf16[2,4,64,256]{3,2,1,0:T(8,128)(2,1)S(1)} collective-permute-done((bf16[2,4,64,256]{3,2,1,0:T(8,128)(2,1)S(1)}, bf16[2,4,64,256]{3,2,1,0:T(8,128)(2,1)S(1)}, u32[]{:S(2)}, u32[]{:S(2)}) %collective-permute-start.5) | collective-permute-done | bytes 262176 | tf_op jit(solution)/shard_map/ppermute | solution.py:47
  22.6 1.0 %convert_add_fusion.3 = f32[2,4,64,256]{3,2,1,0:T(8,128)S(1)} fusion(f32[2,4,64,256]{3,2,1,0:T(8,128)S(1)} %get-tuple-element.44, bf16[2,4,64,256]{3,2,1,0:T(8,128)(2,1)} %collective-permute-done.4), kind=kLoop, calls=%fused_computation.19 | loop fusion | flops 262144 | bytes 1310720 | tf_op jit(solution)/shard_map/add | solution.py:202
  23.7 1.6 %collective-permute-start.6 = (bf16[4,64,256]{2,1,0:T(8,128)(2,1)S(1)}, bf16[4,64,256]{2,1,0:T(8,128)(2,1)S(1)}, u32[]{:S(2)}, u32[]{:S(2)}) collective-permute-start(bf16[4,64,256]{2,1,0:T(8,128)(2,1)S(1)} %fusion.13), channel_id=1, source_target_pairs={{0,1},{1,0},{2,3},{3,2},{4,5},{5,4},{6,7},{7,6},{8,9},{9,8},{10,11... | collective-permute-start | bytes 393224 | tf_op jit(solution)/shard_map/ppermute | solution.py:47
  25.3 0.6 collective-permute-start.7
  25.9 2.3 %collective-permute-done.12 = bf16[2,4,64,256]{3,2,1,0:T(8,128)(2,1)S(1)} collective-permute-done((bf16[2,4,64,256]{3,2,1,0:T(8,128)(2,1)S(1)}, bf16[2,4,64,256]{3,2,1,0:T(8,128)(2,1)S(1)}, u32[]{:S(2)}, u32[]{:S(2)}) %collective-permute-start.12) | collective-permute-done | bytes 262176 | tf_op jit(solution)/shard_map/ppermute | solution.py:47
  28.4 1.6 %collective-permute-start.13 = (bf16[4,64,256]{2,1,0:T(8,128)(2,1)S(1)}, bf16[4,64,256]{2,1,0:T(8,128)(2,1)S(1)}, u32[]{:S(2)}, u32[]{:S(2)}) collective-permute-start(bf16[4,64,256]{2,1,0:T(8,128)(2,1)S(1)} %fusion.15), channel_id=1, source_target_pairs={{0,1},{1,0},{2,3},{3,2},{4,5},{5,4},{6,7},{7,6},{8,9},{9,8},{10,11... | collective-permute-start | bytes 393224 | tf_op jit(solution)/shard_map/ppermute | solution.py:47
  30.1 0.6 collective-permute-start.14
  31.0 3.7 %collective-permute-start.10 = (bf16[64,512]{1,0:T(8,128)(2,1)S(1)}, bf16[64,512]{1,0:T(8,128)(2,1)S(1)}, u32[]{:S(2)}, u32[]{:S(2)}) collective-permute-start(bf16[64,512]{1,0:T(8,128)(2,1)S(1)} %get-tuple-element.88), channel_id=1, source_target_pairs={{0,6},{1,7},{2,4},{3,5},{4,2},{5,3},{6,0},{7,1},{8,14},{9,15},{10,... | collective-permute-start | bytes 196616 | tf_op jit(solution)/shard_map/ppermute | solution.py:47
  34.7 0.8 collective-permute-start.9
  35.6 1.3 %collective-permute-start.15 = (bf16[64,512]{1,0:T(8,128)(2,1)S(1)}, bf16[64,512]{1,0:T(8,128)(2,1)S(1)}, u32[]{:S(2)}, u32[]{:S(2)}) collective-permute-start(bf16[64,512]{1,0:T(8,128)(2,1)S(1)} %get-tuple-element.83), channel_id=1, source_target_pairs={{0,2},{1,3},{2,0},{3,1},{4,6},{5,7},{6,4},{7,5},{8,10},{9,11},{10,... | collective-permute-start | bytes 196616 | tf_op jit(solution)/shard_map/ppermute | solution.py:47
  36.9 2.9 %collective-permute-start.16 = (bf16[64,512]{1,0:T(8,128)(2,1)S(1)}, bf16[64,512]{1,0:T(8,128)(2,1)S(1)}, u32[]{:S(2)}, u32[]{:S(2)}) collective-permute-start(bf16[64,512]{1,0:T(8,128)(2,1)S(1)} %get-tuple-element.84), channel_id=1, source_target_pairs={{0,4},{1,5},{2,6},{3,7},{4,0},{5,1},{6,2},{7,3},{8,12},{9,13},{10,... | collective-permute-start | bytes 196616 | tf_op jit(solution)/shard_map/ppermute | solution.py:47
  39.8 1.1 %collective-permute-start.17 = (bf16[64,512]{1,0:T(8,128)(2,1)S(1)}, bf16[64,512]{1,0:T(8,128)(2,1)S(1)}, u32[]{:S(2)}, u32[]{:S(2)}) collective-permute-start(bf16[64,512]{1,0:T(8,128)(2,1)S(1)} %get-tuple-element.85), channel_id=1, source_target_pairs={{0,6},{1,7},{2,4},{3,5},{4,2},{5,3},{6,0},{7,1},{8,14},{9,15},{10,... | collective-permute-start | bytes 196616 | tf_op jit(solution)/shard_map/ppermute | solution.py:47
  40.9 1.8 %collective-permute-done.9 = bf16[64,512]{1,0:T(8,128)(2,1)S(1)} collective-permute-done((bf16[64,512]{1,0:T(8,128)(2,1)S(1)}, bf16[64,512]{1,0:T(8,128)(2,1)S(1)}, u32[]{:S(2)}, u32[]{:S(2)}) %collective-permute-start.9) | collective-permute-done | bytes 65568 | tf_op jit(solution)/shard_map/ppermute | solution.py:47
  42.8 1.3 %collective-permute-done.16 = bf16[64,512]{1,0:T(8,128)(2,1)S(1)} collective-permute-done((bf16[64,512]{1,0:T(8,128)(2,1)S(1)}, bf16[64,512]{1,0:T(8,128)(2,1)S(1)}, u32[]{:S(2)}, u32[]{:S(2)}) %collective-permute-start.16) | collective-permute-done | bytes 65568 | tf_op jit(solution)/shard_map/ppermute | solution.py:47
  44.1 1.8 %collective-permute-done.17 = bf16[64,512]{1,0:T(8,128)(2,1)S(1)} collective-permute-done((bf16[64,512]{1,0:T(8,128)(2,1)S(1)}, bf16[64,512]{1,0:T(8,128)(2,1)S(1)}, u32[]{:S(2)}, u32[]{:S(2)}) %collective-permute-start.17) | collective-permute-done | bytes 65568 | tf_op jit(solution)/shard_map/ppermute | solution.py:47
  46.1 9.5 %all_to_all.5 = f32[32,2,128]{2,1,0:T(2,128)S(1)} all-to-all(f32[32,2,128]{2,1,0:T(2,128)S(1)} %broadcast_in_dim.4), channel_id=1, replica_groups=mesh['aa'=4,'ba'=8] {'aa','ba'}, dimensions={0} | all-to-all | bytes 65536 | tf_op jit(solution)/shard_map/all_to_all | solution.py:225
  56.0 0.8 collective-permute-start.30
  56.8 2.2 %collective-permute-start.31 = (bf16[64,512]{1,0:T(8,128)(2,1)S(1)}, bf16[64,512]{1,0:T(8,128)(2,1)S(1)}, u32[]{:S(2)}, u32[]{:S(2)}) collective-permute-start(bf16[64,512]{1,0:T(8,128)(2,1)S(1)} %get-tuple-element.65), channel_id=1, source_target_pairs={{0,6},{1,7},{2,4},{3,5},{4,2},{5,3},{6,0},{7,1},{8,14},{9,15},{10,... | collective-permute-start | bytes 196616 | tf_op jit(solution)/shard_map/ppermute | solution.py:47
  58.9 0.6 collective-permute-start.29
  59.6 1.4 %collective-permute-start.18 = (bf16[64,512]{1,0:T(8,128)(2,1)S(1)}, bf16[64,512]{1,0:T(8,128)(2,1)S(1)}, u32[]{:S(2)}, u32[]{:S(2)}) collective-permute-start(bf16[64,512]{1,0:T(8,128)(2,1)S(1)} %get-tuple-element.60), channel_id=1, source_target_pairs={{0,2},{1,3},{2,0},{3,1},{4,6},{5,7},{6,4},{7,5},{8,10},{9,11},{10,... | collective-permute-start | bytes 196616 | tf_op jit(solution)/shard_map/ppermute | solution.py:47
  61.3 2.8 %collective-permute-done.30 = bf16[64,512]{1,0:T(8,128)(2,1)S(1)} collective-permute-done((bf16[64,512]{1,0:T(8,128)(2,1)S(1)}, bf16[64,512]{1,0:T(8,128)(2,1)S(1)}, u32[]{:S(2)}, u32[]{:S(2)}) %collective-permute-start.30) | collective-permute-done | bytes 65568 | tf_op jit(solution)/shard_map/ppermute | solution.py:47
  64.5 0.8 collective-permute-done.29
  65.4 0.7 collective-permute-start.33
  66.1 0.8 collective-permute-start.32
  66.9 1.4 %collective-permute-done.19 = bf16[64,512]{1,0:T(8,128)(2,1)S(1)} collective-permute-done((bf16[64,512]{1,0:T(8,128)(2,1)S(1)}, bf16[64,512]{1,0:T(8,128)(2,1)S(1)}, u32[]{:S(2)}, u32[]{:S(2)}) %collective-permute-start.19) | collective-permute-done | bytes 65568 | tf_op jit(solution)/shard_map/ppermute | solution.py:47
  68.3 1.9 %collective-permute-done.20 = bf16[64,512]{1,0:T(8,128)(2,1)S(1)} collective-permute-done((bf16[64,512]{1,0:T(8,128)(2,1)S(1)}, bf16[64,512]{1,0:T(8,128)(2,1)S(1)}, u32[]{:S(2)}, u32[]{:S(2)}) %collective-permute-start.20) | collective-permute-done | bytes 65568 | tf_op jit(solution)/shard_map/ppermute | solution.py:47
  70.2 0.7 collective-permute-start.22
  70.9 0.7 collective-permute-start.21
  71.7 1.4 %collective-permute-start.36 = (bf16[2,4,64,256]{3,2,1,0:T(8,128)(2,1)S(1)}, bf16[2,4,64,256]{3,2,1,0:T(8,128)(2,1)S(1)}, u32[]{:S(2)}, u32[]{:S(2)}) collective-permute-start(bf16[2,4,64,256]{3,2,1,0:T(8,128)(2,1)S(1)} %pad_maximum_fusion.3.refs_3_), channel_id=1, source_target_pairs={{0,1},{1,0},{2,3},{3,2},{4,5},{5,4},{6,7},{7,6},{8,9},{9,8},{10,11... | collective-permute-start | bytes 786440 | tf_op jit(solution)/shard_map/ppermute | solution.py:47
  73.1 1.5 %collective-permute-start.35 = (bf16[2,4,64,256]{3,2,1,0:T(8,128)(2,1)S(1)}, bf16[2,4,64,256]{3,2,1,0:T(8,128)(2,1)S(1)}, u32[]{:S(2)}, u32[]{:S(2)}) collective-permute-start(bf16[2,4,64,256]{3,2,1,0:T(8,128)(2,1)S(1)} %pad_maximum_fusion.2.refs_1_), channel_id=1, source_target_pairs={{0,16},{1,17},{2,18},{3,19},{4,20},{5,21},{6,22},{7,23},{8,24},{9,... | collective-permute-start | bytes 786440 | tf_op jit(solution)/shard_map/ppermute | solution.py:47
  74.6 2.0 %collective-permute-done.22 = bf16[4,64,256]{2,1,0:T(8,128)(2,1)S(1)} collective-permute-done((bf16[4,64,256]{2,1,0:T(8,128)(2,1)S(1)}, bf16[4,64,256]{2,1,0:T(8,128)(2,1)S(1)}, u32[]{:S(2)}, u32[]{:S(2)}) %collective-permute-start.22) | collective-permute-done | bytes 131104 | tf_op jit(solution)/shard_map/ppermute | solution.py:47
  76.6 0.8 collective-permute-done.21
  77.4 0.7 collective-permute-start.24
  78.2 2.7 %collective-permute-done.36.refs_4_ = bf16[2,4,64,256]{3,2,1,0:T(8,128)(2,1)S(1)} collective-permute-done((bf16[2,4,64,256]{3,2,1,0:T(8,128)(2,1)S(1)}, bf16[2,4,64,256]{3,2,1,0:T(8,128)(2,1)S(1)}, u32[]{:S(2)}, u32[]{:S(2)}) %collective-permute-start.36) | collective-permute-done | bytes 262176 | tf_op jit(solution)/shard_map/ppermute | solution.py:47
  80.9 2.8 %collective-permute-start.23 = (bf16[2,4,64,256]{3,2,1,0:T(8,128)(2,1)S(1)}, bf16[2,4,64,256]{3,2,1,0:T(8,128)(2,1)S(1)}, u32[]{:S(2)}, u32[]{:S(2)}) collective-permute-start(bf16[2,4,64,256]{3,2,1,0:T(8,128)(2,1)S(1)} %pad_maximum_fusion.refs_1_), channel_id=1, source_target_pairs={{0,16},{1,17},{2,18},{3,19},{4,20},{5,21},{6,22},{7,23},{8,24},{9,... | collective-permute-start | bytes 786440 | tf_op jit(solution)/shard_map/ppermute | solution.py:47
  83.7 1.5 %shard_map.88.refs_5_ = f32[1024,512]{1,0:T(8,128)S(1)} custom-call(bf16[1024,2048]{1,0:T(8,128)(2,1)S(1)} %copy-done, bf16[2,4,64,256]{3,2,1,0:T(8,128)(2,1)S(1)} %pad_maximum_fusion.2.refs_1_, bf16[2,4,64,256]{3,2,1,0:T(8,128)(2,1)S(1)} %collective-permute-done.35.refs_2_, bf16[2,4,64,256]{3,2,1,0:T(8,128)(2,1)S(1)} %pad_maximum_fusion.3.refs_3_, ...), custom_call_target="tpu_custom_call" | custom-call | flops 1073741824 | bytes 8388608 | tf_op jit(solution)/shard_map/pallas_call | solution.py:331
  85.3 0.7 collective-permute-done.24.refs_4_
  86.0 2.0 %collective-permute-done.23.refs_2_ = bf16[2,4,64,256]{3,2,1,0:T(8,128)(2,1)S(1)} collective-permute-done((bf16[2,4,64,256]{3,2,1,0:T(8,128)(2,1)S(1)}, bf16[2,4,64,256]{3,2,1,0:T(8,128)(2,1)S(1)}, u32[]{:S(2)}, u32[]{:S(2)}) %collective-permute-start.23) | collective-permute-done | bytes 262176 | tf_op jit(solution)/shard_map/ppermute | solution.py:47
  89.1 1.5 %shard_map.89.refs_9_ = f32[1024,512]{1,0:T(8,128)S(1)} custom-call(bf16[1024,2048]{1,0:T(8,128)(2,1)S(1)} %copy-done, bf16[2,4,64,256]{3,2,1,0:T(8,128)(2,1)S(1)} %collective-permute-done.34.refs_1_, bf16[2,4,64,256]{3,2,1,0:T(8,128)(2,1)S(1)} %collective-permute-done.37.refs_2_, bf16[2,4,64,256]{3,2,1,0:T(8,128)(2,1)S(1)} %collective-permute-done.38.refs_3_, ...), custom_call_target="tpu_custom_call" | custom-call | flops 1073741824 | bytes 8388608 | tf_op jit(solution)/shard_map/pallas_call | solution.py:331
  90.7 3.7 %shard_map.90 = (bf16[1024,512]{1,0:T(8,128)(2,1)}, f32[64,1024]{1,0:T(8,128)}, f32[64,1024]{1,0:T(8,128)}) custom-call(bf16[1024,2048]{1,0:T(8,128)(2,1)S(1)} %copy-done, bf16[2,4,64,256]{3,2,1,0:T(8,128)(2,1)S(1)} %pad_maximum_fusion.refs_1_, bf16[2,4,64,256]{3,2,1,0:T(8,128)(2,1)S(1)} %collective-permute-done.23.refs_2_, ...), custom_call_target="tpu_custom_call" | custom-call | flops 2147483648 | bytes 8388608 | tf_op jit(solution)/shard_map/pallas_call | solution.py:331
  (93 shorter events, 4.8 us)
Async XLA Ops:
  0.6 5.6 %copy-start.1 = (bf16[1024,2048]{1,0:T(8,128)(2,1)S(1)}, bf16[1024,2048]{1,0:T(8,128)(2,1)}, u32[]{:S(2)}) copy-start(bf16[1024,2048]{1,0:T(8,128)(2,1)} %tokens_ref.1) | copy-start | bytes 12582916
  0.6 5.6 %copy-start.2 = (bf16[1024,1024]{1,0:T(8,128)(2,1)S(1)}, bf16[1024,1024]{1,0:T(8,128)(2,1)}, u32[]{:S(2)}) copy-start(bf16[1024,1024]{1,0:T(8,128)(2,1)} %cot_ref.1) | copy-start | bytes 6291460
  5.1 3.5 %collective-permute-start = (bf16[1024,256]{1,0:T(8,128)(2,1)S(1)}, bf16[1024,256]{1,0:T(8,128)(2,1)S(1)}, u32[]{:S(2)}, u32[]{:S(2)}) collective-permute-start(bf16[1024,256]{1,0:T(8,128)(2,1)S(1)} %get-tuple-element.40), channel_id=1, source_target_pairs={{0,8},{1,9},{2,10},{3,11},{4,12},{5,13},{6,14},{7,15},{8,0},{9,1},... | collective-permute-start | bytes 1572872 | tf_op jit(solution)/shard_map/ppermute | solution.py:47
  5.7 3.0 %collective-permute-start.1 = (bf16[1024,256]{1,0:T(8,128)(2,1)S(1)}, bf16[1024,256]{1,0:T(8,128)(2,1)S(1)}, u32[]{:S(2)}, u32[]{:S(2)}) collective-permute-start(bf16[1024,256]{1,0:T(8,128)(2,1)S(1)} %get-tuple-element.41), channel_id=1, source_target_pairs={{0,8},{1,9},{2,10},{3,11},{4,12},{5,13},{6,14},{7,15},{8,0},{9,1},... | collective-permute-start | bytes 1572872 | tf_op jit(solution)/shard_map/ppermute | solution.py:47
  5.7 3.0 %collective-permute-start.2 = (bf16[1024,256]{1,0:T(8,128)(2,1)S(1)}, bf16[1024,256]{1,0:T(8,128)(2,1)S(1)}, u32[]{:S(2)}, u32[]{:S(2)}) collective-permute-start(bf16[1024,256]{1,0:T(8,128)(2,1)S(1)} %get-tuple-element.42), channel_id=1, source_target_pairs={{0,8},{1,9},{2,10},{3,11},{4,12},{5,13},{6,14},{7,15},{8,0},{9,1},... | collective-permute-start | bytes 1572872 | tf_op jit(solution)/shard_map/ppermute | solution.py:47
  6.2 3.3 %collective-permute-start.3 = (bf16[1024,256]{1,0:T(8,128)(2,1)S(1)}, bf16[1024,256]{1,0:T(8,128)(2,1)S(1)}, u32[]{:S(2)}, u32[]{:S(2)}) collective-permute-start(bf16[1024,256]{1,0:T(8,128)(2,1)S(1)} %get-tuple-element.43), channel_id=1, source_target_pairs={{0,8},{1,9},{2,10},{3,11},{4,12},{5,13},{6,14},{7,15},{8,0},{9,1},... | collective-permute-start | bytes 1572872 | tf_op jit(solution)/shard_map/ppermute | solution.py:47
  10.5 10.1 %collective-permute-start.4 = (bf16[2,4,64,256]{3,2,1,0:T(8,128)(2,1)S(1)}, bf16[2,4,64,256]{3,2,1,0:T(8,128)(2,1)}, u32[]{:S(2)}, u32[]{:S(2)}) collective-permute-start(bf16[2,4,64,256]{3,2,1,0:T(8,128)(2,1)S(1)} %get-tuple-element.45), channel_id=1, source_target_pairs={{0,16},{1,17},{2,18},{3,19},{4,20},{5,21},{6,22},{7,23},{8,24},{9,... | collective-permute-start | bytes 786440 | tf_op jit(solution)/shard_map/ppermute | solution.py:47
  13.4 9.2 %collective-permute-start.5 = (bf16[2,4,64,256]{3,2,1,0:T(8,128)(2,1)S(1)}, bf16[2,4,64,256]{3,2,1,0:T(8,128)(2,1)S(1)}, u32[]{:S(2)}, u32[]{:S(2)}) collective-permute-start(bf16[2,4,64,256]{3,2,1,0:T(8,128)(2,1)S(1)} %get-tuple-element.46), channel_id=1, source_target_pairs={{0,1},{1,0},{2,3},{3,2},{4,5},{5,4},{6,7},{7,6},{8,9},{9,8},{10,11... | collective-permute-start | bytes 786440 | tf_op jit(solution)/shard_map/ppermute | solution.py:47
  14.9 11.0 %collective-permute-start.11 = (bf16[2,4,64,256]{3,2,1,0:T(8,128)(2,1)S(1)}, bf16[2,4,64,256]{3,2,1,0:T(8,128)(2,1)S(1)}, u32[]{:S(2)}, u32[]{:S(2)}) collective-permute-start(bf16[2,4,64,256]{3,2,1,0:T(8,128)(2,1)S(1)} %get-tuple-element.53), channel_id=1, source_target_pairs={{0,16},{1,17},{2,18},{3,19},{4,20},{5,21},{6,22},{7,23},{8,24},{9,... | collective-permute-start | bytes 786440 | tf_op jit(solution)/shard_map/ppermute | solution.py:47
  15.5 12.8 %collective-permute-start.12 = (bf16[2,4,64,256]{3,2,1,0:T(8,128)(2,1)S(1)}, bf16[2,4,64,256]{3,2,1,0:T(8,128)(2,1)S(1)}, u32[]{:S(2)}, u32[]{:S(2)}) collective-permute-start(bf16[2,4,64,256]{3,2,1,0:T(8,128)(2,1)S(1)} %get-tuple-element.54), channel_id=1, source_target_pairs={{0,1},{1,0},{2,3},{3,2},{4,5},{5,4},{6,7},{7,6},{8,9},{9,8},{10,11... | collective-permute-start | bytes 786440 | tf_op jit(solution)/shard_map/ppermute | solution.py:47
  23.7 7.2 %collective-permute-start.6 = (bf16[4,64,256]{2,1,0:T(8,128)(2,1)S(1)}, bf16[4,64,256]{2,1,0:T(8,128)(2,1)S(1)}, u32[]{:S(2)}, u32[]{:S(2)}) collective-permute-start(bf16[4,64,256]{2,1,0:T(8,128)(2,1)S(1)} %fusion.13), channel_id=1, source_target_pairs={{0,1},{1,0},{2,3},{3,2},{4,5},{5,4},{6,7},{7,6},{8,9},{9,8},{10,11... | collective-permute-start | bytes 393224 | tf_op jit(solution)/shard_map/ppermute | solution.py:47
  25.3 5.6 %collective-permute-start.7 = (bf16[4,64,256]{2,1,0:T(8,128)(2,1)S(1)}, bf16[4,64,256]{2,1,0:T(8,128)(2,1)S(1)}, u32[]{:S(2)}, u32[]{:S(2)}) collective-permute-start(bf16[4,64,256]{2,1,0:T(8,128)(2,1)S(1)} %fusion.14), channel_id=1, source_target_pairs={{0,16},{1,17},{2,18},{3,19},{4,20},{5,21},{6,22},{7,23},{8,24},{9,... | collective-permute-start | bytes 393224 | tf_op jit(solution)/shard_map/ppermute | solution.py:47
  28.3 27.5 %copy-start.3 = (f32[64,1024]{1,0:T(8,128)S(1)}, f32[64,1024]{1,0:T(8,128)}, u32[]{:S(2)}) copy-start(f32[64,1024]{1,0:T(8,128)} %refs_13_.1) | copy-start | bytes 786436
  28.3 27.4 %copy-start.4 = (f32[64,1024]{1,0:T(8,128)S(1)}, f32[64,1024]{1,0:T(8,128)}, u32[]{:S(2)}) copy-start(f32[64,1024]{1,0:T(8,128)} %refs_12_.1) | copy-start | bytes 786436
  28.4 27.4 %copy-start.5 = (f32[64,1024]{1,0:T(8,128)S(1)}, f32[64,1024]{1,0:T(8,128)}, u32[]{:S(2)}) copy-start(f32[64,1024]{1,0:T(8,128)} %param.8) | copy-start | bytes 786436
  28.4 7.1 %collective-permute-start.13 = (bf16[4,64,256]{2,1,0:T(8,128)(2,1)S(1)}, bf16[4,64,256]{2,1,0:T(8,128)(2,1)S(1)}, u32[]{:S(2)}, u32[]{:S(2)}) collective-permute-start(bf16[4,64,256]{2,1,0:T(8,128)(2,1)S(1)} %fusion.15), channel_id=1, source_target_pairs={{0,1},{1,0},{2,3},{3,2},{4,5},{5,4},{6,7},{7,6},{8,9},{9,8},{10,11... | collective-permute-start | bytes 393224 | tf_op jit(solution)/shard_map/ppermute | solution.py:47
  30.1 5.4 %collective-permute-start.14 = (bf16[4,64,256]{2,1,0:T(8,128)(2,1)S(1)}, bf16[4,64,256]{2,1,0:T(8,128)(2,1)S(1)}, u32[]{:S(2)}, u32[]{:S(2)}) collective-permute-start(bf16[4,64,256]{2,1,0:T(8,128)(2,1)S(1)} %fusion.16), channel_id=1, source_target_pairs={{0,16},{1,17},{2,18},{3,19},{4,20},{5,21},{6,22},{7,23},{8,24},{9,... | collective-permute-start | bytes 393224 | tf_op jit(solution)/shard_map/ppermute | solution.py:47
  31.0 8.8 %collective-permute-start.10 = (bf16[64,512]{1,0:T(8,128)(2,1)S(1)}, bf16[64,512]{1,0:T(8,128)(2,1)S(1)}, u32[]{:S(2)}, u32[]{:S(2)}) collective-permute-start(bf16[64,512]{1,0:T(8,128)(2,1)S(1)} %get-tuple-element.88), channel_id=1, source_target_pairs={{0,6},{1,7},{2,4},{3,5},{4,2},{5,3},{6,0},{7,1},{8,14},{9,15},{10,... | collective-permute-start | bytes 196616 | tf_op jit(solution)/shard_map/ppermute | solution.py:47
  34.7 6.2 %collective-permute-start.8 = (bf16[64,512]{1,0:T(8,128)(2,1)S(1)}, bf16[64,512]{1,0:T(8,128)(2,1)S(1)}, u32[]{:S(2)}, u32[]{:S(2)}) collective-permute-start(bf16[64,512]{1,0:T(8,128)(2,1)S(1)} %get-tuple-element.86), channel_id=1, source_target_pairs={{0,2},{1,3},{2,0},{3,1},{4,6},{5,7},{6,4},{7,5},{8,10},{9,11},{10,... | collective-permute-start | bytes 196616 | tf_op jit(solution)/shard_map/ppermute | solution.py:47
  34.7 8.0 %collective-permute-start.9 = (bf16[64,512]{1,0:T(8,128)(2,1)S(1)}, bf16[64,512]{1,0:T(8,128)(2,1)S(1)}, u32[]{:S(2)}, u32[]{:S(2)}) collective-permute-start(bf16[64,512]{1,0:T(8,128)(2,1)S(1)} %get-tuple-element.87), channel_id=1, source_target_pairs={{0,4},{1,5},{2,6},{3,7},{4,0},{5,1},{6,2},{7,3},{8,12},{9,13},{10,... | collective-permute-start | bytes 196616 | tf_op jit(solution)/shard_map/ppermute | solution.py:47
  35.6 7.2 %collective-permute-start.15 = (bf16[64,512]{1,0:T(8,128)(2,1)S(1)}, bf16[64,512]{1,0:T(8,128)(2,1)S(1)}, u32[]{:S(2)}, u32[]{:S(2)}) collective-permute-start(bf16[64,512]{1,0:T(8,128)(2,1)S(1)} %get-tuple-element.83), channel_id=1, source_target_pairs={{0,2},{1,3},{2,0},{3,1},{4,6},{5,7},{6,4},{7,5},{8,10},{9,11},{10,... | collective-permute-start | bytes 196616 | tf_op jit(solution)/shard_map/ppermute | solution.py:47
  36.9 7.2 %collective-permute-start.16 = (bf16[64,512]{1,0:T(8,128)(2,1)S(1)}, bf16[64,512]{1,0:T(8,128)(2,1)S(1)}, u32[]{:S(2)}, u32[]{:S(2)}) collective-permute-start(bf16[64,512]{1,0:T(8,128)(2,1)S(1)} %get-tuple-element.84), channel_id=1, source_target_pairs={{0,4},{1,5},{2,6},{3,7},{4,0},{5,1},{6,2},{7,3},{8,12},{9,13},{10,... | collective-permute-start | bytes 196616 | tf_op jit(solution)/shard_map/ppermute | solution.py:47
  39.8 6.1 %collective-permute-start.17 = (bf16[64,512]{1,0:T(8,128)(2,1)S(1)}, bf16[64,512]{1,0:T(8,128)(2,1)S(1)}, u32[]{:S(2)}, u32[]{:S(2)}) collective-permute-start(bf16[64,512]{1,0:T(8,128)(2,1)S(1)} %get-tuple-element.85), channel_id=1, source_target_pairs={{0,6},{1,7},{2,4},{3,5},{4,2},{5,3},{6,0},{7,1},{8,14},{9,15},{10,... | collective-permute-start | bytes 196616 | tf_op jit(solution)/shard_map/ppermute | solution.py:47
  55.7 28.0 %copy-start = (bf16[1024,2048]{1,0:T(8,128)(2,1)S(1)}, bf16[1024,2048]{1,0:T(8,128)(2,1)}, u32[]{:S(2)}) copy-start(bf16[1024,2048]{1,0:T(8,128)(2,1)} %refs_0_.5) | copy-start | bytes 12582916
  56.0 8.0 %collective-permute-start.30 = (bf16[64,512]{1,0:T(8,128)(2,1)S(1)}, bf16[64,512]{1,0:T(8,128)(2,1)S(1)}, u32[]{:S(2)}, u32[]{:S(2)}) collective-permute-start(bf16[64,512]{1,0:T(8,128)(2,1)S(1)} %get-tuple-element.65), channel_id=1, source_target_pairs={{0,4},{1,5},{2,6},{3,7},{4,0},{5,1},{6,2},{7,3},{8,12},{9,13},{10,... | collective-permute-start | bytes 196616 | tf_op jit(solution)/shard_map/ppermute | solution.py:47
  56.8 7.7 %collective-permute-start.31 = (bf16[64,512]{1,0:T(8,128)(2,1)S(1)}, bf16[64,512]{1,0:T(8,128)(2,1)S(1)}, u32[]{:S(2)}, u32[]{:S(2)}) collective-permute-start(bf16[64,512]{1,0:T(8,128)(2,1)S(1)} %get-tuple-element.65), channel_id=1, source_target_pairs={{0,6},{1,7},{2,4},{3,5},{4,2},{5,3},{6,0},{7,1},{8,14},{9,15},{10,... | collective-permute-start | bytes 196616 | tf_op jit(solution)/shard_map/ppermute | solution.py:47
  58.9 6.4 %collective-permute-start.29 = (bf16[64,512]{1,0:T(8,128)(2,1)S(1)}, bf16[64,512]{1,0:T(8,128)(2,1)S(1)}, u32[]{:S(2)}, u32[]{:S(2)}) collective-permute-start(bf16[64,512]{1,0:T(8,128)(2,1)S(1)} %get-tuple-element.65), channel_id=1, source_target_pairs={{0,2},{1,3},{2,0},{3,1},{4,6},{5,7},{6,4},{7,5},{8,10},{9,11},{10,... | collective-permute-start | bytes 196616 | tf_op jit(solution)/shard_map/ppermute | solution.py:47
  59.6 7.3 %collective-permute-start.18 = (bf16[64,512]{1,0:T(8,128)(2,1)S(1)}, bf16[64,512]{1,0:T(8,128)(2,1)S(1)}, u32[]{:S(2)}, u32[]{:S(2)}) collective-permute-start(bf16[64,512]{1,0:T(8,128)(2,1)S(1)} %get-tuple-element.60), channel_id=1, source_target_pairs={{0,2},{1,3},{2,0},{3,1},{4,6},{5,7},{6,4},{7,5},{8,10},{9,11},{10,... | collective-permute-start | bytes 196616 | tf_op jit(solution)/shard_map/ppermute | solution.py:47
  61.0 7.3 %collective-permute-start.19 = (bf16[64,512]{1,0:T(8,128)(2,1)S(1)}, bf16[64,512]{1,0:T(8,128)(2,1)S(1)}, u32[]{:S(2)}, u32[]{:S(2)}) collective-permute-start(bf16[64,512]{1,0:T(8,128)(2,1)S(1)} %get-tuple-element.60), channel_id=1, source_target_pairs={{0,4},{1,5},{2,6},{3,7},{4,0},{5,1},{6,2},{7,3},{8,12},{9,13},{10,... | collective-permute-start | bytes 196616 | tf_op jit(solution)/shard_map/ppermute | solution.py:47
  64.0 6.1 %collective-permute-start.20 = (bf16[64,512]{1,0:T(8,128)(2,1)S(1)}, bf16[64,512]{1,0:T(8,128)(2,1)S(1)}, u32[]{:S(2)}, u32[]{:S(2)}) collective-permute-start(bf16[64,512]{1,0:T(8,128)(2,1)S(1)} %get-tuple-element.60), channel_id=1, source_target_pairs={{0,6},{1,7},{2,4},{3,5},{4,2},{5,3},{6,0},{7,1},{8,14},{9,15},{10,... | collective-permute-start | bytes 196616 | tf_op jit(solution)/shard_map/ppermute | solution.py:47
  65.4 6.3 %collective-permute-start.33 = (bf16[4,64,256]{2,1,0:T(8,128)(2,1)S(1)}, bf16[4,64,256]{2,1,0:T(8,128)(2,1)S(1)}, u32[]{:S(2)}, u32[]{:S(2)}) collective-permute-start(bf16[4,64,256]{2,1,0:T(8,128)(2,1)S(1)} %get-tuple-element.90), channel_id=1, source_target_pairs={{0,16},{1,17},{2,18},{3,19},{4,20},{5,21},{6,22},{7,23},{8,24},{9,... | collective-permute-start | bytes 393224 | tf_op jit(solution)/shard_map/ppermute | solution.py:47
  66.1 5.6 %collective-permute-start.32 = (bf16[4,64,256]{2,1,0:T(8,128)(2,1)S(1)}, bf16[4,64,256]{2,1,0:T(8,128)(2,1)S(1)}, u32[]{:S(2)}, u32[]{:S(2)}) collective-permute-start(bf16[4,64,256]{2,1,0:T(8,128)(2,1)S(1)} %get-tuple-element.92), channel_id=1, source_target_pairs={{0,1},{1,0},{2,3},{3,2},{4,5},{5,4},{6,7},{7,6},{8,9},{9,8},{10,11... | collective-permute-start | bytes 393224 | tf_op jit(solution)/shard_map/ppermute | solution.py:47
  70.2 6.4 %collective-permute-start.22 = (bf16[4,64,256]{2,1,0:T(8,128)(2,1)S(1)}, bf16[4,64,256]{2,1,0:T(8,128)(2,1)S(1)}, u32[]{:S(2)}, u32[]{:S(2)}) collective-permute-start(bf16[4,64,256]{2,1,0:T(8,128)(2,1)S(1)} %get-tuple-element.94), channel_id=1, source_target_pairs={{0,16},{1,17},{2,18},{3,19},{4,20},{5,21},{6,22},{7,23},{8,24},{9,... | collective-permute-start | bytes 393224 | tf_op jit(solution)/shard_map/ppermute | solution.py:47
  70.9 6.5 %collective-permute-start.21 = (bf16[4,64,256]{2,1,0:T(8,128)(2,1)S(1)}, bf16[4,64,256]{2,1,0:T(8,128)(2,1)S(1)}, u32[]{:S(2)}, u32[]{:S(2)}) collective-permute-start(bf16[4,64,256]{2,1,0:T(8,128)(2,1)S(1)} %get-tuple-element.96), channel_id=1, source_target_pairs={{0,1},{1,0},{2,3},{3,2},{4,5},{5,4},{6,7},{7,6},{8,9},{9,8},{10,11... | collective-permute-start | bytes 393224 | tf_op jit(solution)/shard_map/ppermute | solution.py:47
  71.7 9.2 %collective-permute-start.36 = (bf16[2,4,64,256]{3,2,1,0:T(8,128)(2,1)S(1)}, bf16[2,4,64,256]{3,2,1,0:T(8,128)(2,1)S(1)}, u32[]{:S(2)}, u32[]{:S(2)}) collective-permute-start(bf16[2,4,64,256]{3,2,1,0:T(8,128)(2,1)S(1)} %pad_maximum_fusion.3.refs_3_), channel_id=1, source_target_pairs={{0,1},{1,0},{2,3},{3,2},{4,5},{5,4},{6,7},{7,6},{8,9},{9,8},{10,11... | collective-permute-start | bytes 786440 | tf_op jit(solution)/shard_map/ppermute | solution.py:47
  73.1 10.6 %collective-permute-start.35 = (bf16[2,4,64,256]{3,2,1,0:T(8,128)(2,1)S(1)}, bf16[2,4,64,256]{3,2,1,0:T(8,128)(2,1)S(1)}, u32[]{:S(2)}, u32[]{:S(2)}) collective-permute-start(bf16[2,4,64,256]{3,2,1,0:T(8,128)(2,1)S(1)} %pad_maximum_fusion.2.refs_1_), channel_id=1, source_target_pairs={{0,16},{1,17},{2,18},{3,19},{4,20},{5,21},{6,22},{7,23},{8,24},{9,... | collective-permute-start | bytes 786440 | tf_op jit(solution)/shard_map/ppermute | solution.py:47
  74.6 13.5 %collective-permute-start.38 = (bf16[2,4,64,256]{3,2,1,0:T(8,128)(2,1)S(1)}, bf16[2,4,64,256]{3,2,1,0:T(8,128)(2,1)S(1)}, u32[]{:S(2)}, u32[]{:S(2)}) collective-permute-start(bf16[2,4,64,256]{3,2,1,0:T(8,128)(2,1)S(1)} %pad_maximum_fusion.3.refs_3_), channel_id=1, source_target_pairs={{0,8},{1,9},{2,10},{3,11},{4,12},{5,13},{6,14},{7,15},{8,0},{9,1},... | collective-permute-start | bytes 786440 | tf_op jit(solution)/shard_map/ppermute | solution.py:47
  76.6 12.0 %collective-permute-start.34 = (bf16[2,4,64,256]{3,2,1,0:T(8,128)(2,1)S(1)}, bf16[2,4,64,256]{3,2,1,0:T(8,128)(2,1)S(1)}, u32[]{:S(2)}, u32[]{:S(2)}) collective-permute-start(bf16[2,4,64,256]{3,2,1,0:T(8,128)(2,1)S(1)} %pad_maximum_fusion.2.refs_1_), channel_id=1, source_target_pairs={{0,8},{1,9},{2,10},{3,11},{4,12},{5,13},{6,14},{7,15},{8,0},{9,1},... | collective-permute-start | bytes 786440 | tf_op jit(solution)/shard_map/ppermute | solution.py:47
  77.4 8.6 %collective-permute-start.24 = (bf16[2,4,64,256]{3,2,1,0:T(8,128)(2,1)S(1)}, bf16[2,4,64,256]{3,2,1,0:T(8,128)(2,1)S(1)}, u32[]{:S(2)}, u32[]{:S(2)}) collective-permute-start(bf16[2,4,64,256]{3,2,1,0:T(8,128)(2,1)S(1)} %pad_maximum_fusion.1.refs_3_), channel_id=1, source_target_pairs={{0,1},{1,0},{2,3},{3,2},{4,5},{5,4},{6,7},{7,6},{8,9},{9,8},{10,11... | collective-permute-start | bytes 786440 | tf_op jit(solution)/shard_map/ppermute | solution.py:47
  80.9 7.1 %collective-permute-start.23 = (bf16[2,4,64,256]{3,2,1,0:T(8,128)(2,1)S(1)}, bf16[2,4,64,256]{3,2,1,0:T(8,128)(2,1)S(1)}, u32[]{:S(2)}, u32[]{:S(2)}) collective-permute-start(bf16[2,4,64,256]{3,2,1,0:T(8,128)(2,1)S(1)} %pad_maximum_fusion.refs_1_), channel_id=1, source_target_pairs={{0,16},{1,17},{2,18},{3,19},{4,20},{5,21},{6,22},{7,23},{8,24},{9,... | collective-permute-start | bytes 786440 | tf_op jit(solution)/shard_map/ppermute | solution.py:47
  85.2 3.4 %collective-permute-start.37 = (bf16[2,4,64,256]{3,2,1,0:T(8,128)(2,1)S(1)}, bf16[2,4,64,256]{3,2,1,0:T(8,128)(2,1)S(1)}, u32[]{:S(2)}, u32[]{:S(2)}) collective-permute-start(bf16[2,4,64,256]{3,2,1,0:T(8,128)(2,1)S(1)} %collective-permute-done.35.refs_2_), channel_id=1, source_target_pairs={{0,8},{1,9},{2,10},{3,11},{4,12},{5,13},{6,14},{7,15},{8,0},{9,1},... | collective-permute-start | bytes 786440 | tf_op jit(solution)/shard_map/ppermute | solution.py:47
  86.0 3.1 %collective-permute-start.39 = (bf16[2,4,64,256]{3,2,1,0:T(8,128)(2,1)S(1)}, bf16[2,4,64,256]{3,2,1,0:T(8,128)(2,1)S(1)}, u32[]{:S(2)}, u32[]{:S(2)}) collective-permute-start(bf16[2,4,64,256]{3,2,1,0:T(8,128)(2,1)S(1)} %collective-permute-done.36.refs_4_), channel_id=1, source_target_pairs={{0,8},{1,9},{2,10},{3,11},{4,12},{5,13},{6,14},{7,15},{8,0},{9,1},... | collective-permute-start | bytes 786440 | tf_op jit(solution)/shard_map/ppermute | solution.py:47
  88.1 2.6 %collective-permute-start.27 = (bf16[2,4,64,256]{3,2,1,0:T(8,128)(2,1)S(1)}, bf16[2,4,64,256]{3,2,1,0:T(8,128)(2,1)S(1)}, u32[]{:S(2)}, u32[]{:S(2)}) collective-permute-start(bf16[2,4,64,256]{3,2,1,0:T(8,128)(2,1)S(1)} %pad_maximum_fusion.1.refs_3_), channel_id=1, source_target_pairs={{0,8},{1,9},{2,10},{3,11},{4,12},{5,13},{6,14},{7,15},{8,0},{9,1},... | collective-permute-start | bytes 786440 | tf_op jit(solution)/shard_map/ppermute | solution.py:47
  88.1 2.6 %collective-permute-start.25 = (bf16[2,4,64,256]{3,2,1,0:T(8,128)(2,1)S(1)}, bf16[2,4,64,256]{3,2,1,0:T(8,128)(2,1)S(1)}, u32[]{:S(2)}, u32[]{:S(2)}) collective-permute-start(bf16[2,4,64,256]{3,2,1,0:T(8,128)(2,1)S(1)} %pad_maximum_fusion.refs_1_), channel_id=1, source_target_pairs={{0,8},{1,9},{2,10},{3,11},{4,12},{5,13},{6,14},{7,15},{8,0},{9,1},... | collective-permute-start | bytes 786440 | tf_op jit(solution)/shard_map/ppermute | solution.py:47
  88.6 2.1 %collective-permute-start.26 = (bf16[2,4,64,256]{3,2,1,0:T(8,128)(2,1)S(1)}, bf16[2,4,64,256]{3,2,1,0:T(8,128)(2,1)S(1)}, u32[]{:S(2)}, u32[]{:S(2)}) collective-permute-start(bf16[2,4,64,256]{3,2,1,0:T(8,128)(2,1)S(1)} %collective-permute-done.23.refs_2_), channel_id=1, source_target_pairs={{0,8},{1,9},{2,10},{3,11},{4,12},{5,13},{6,14},{7,15},{8,0},{9,1},... | collective-permute-start | bytes 786440 | tf_op jit(solution)/shard_map/ppermute | solution.py:47
  88.7 2.1 %collective-permute-start.28 = (bf16[2,4,64,256]{3,2,1,0:T(8,128)(2,1)S(1)}, bf16[2,4,64,256]{3,2,1,0:T(8,128)(2,1)S(1)}, u32[]{:S(2)}, u32[]{:S(2)}) collective-permute-start(bf16[2,4,64,256]{3,2,1,0:T(8,128)(2,1)S(1)} %collective-permute-done.24.refs_4_), channel_id=1, source_target_pairs={{0,8},{1,9},{2,10},{3,11},{4,12},{5,13},{6,14},{7,15},{8,0},{9,1},... | collective-permute-start | bytes 786440 | tf_op jit(solution)/shard_map/ppermute | solution.py:47

commit v8 on v7

--- a/solution.py
+++ b/solution.py
@@ -382,7 +382,7 @@
         after = yield clipped, wanted
         last = [table[1:] for table in wanted]
         if after is not None:
-            last, _ = lax.optimization_barrier((last, after))
+            last[-1], _ = lax.optimization_barrier((last[-1], after))
         yield [first + [grid.send(piece, c=1) for piece in rest] for first, rest in zip(early, last)]
 
     def run(ways):

time: 94.6 us -> 94 us (level)
  waiting for transfers between devices: 30.5 us -> 26.9 us
  starting transfers between devices: 36.4 us -> 38.4 us
    ppermute x40, waiting for transfers between devices: 30.5 us -> 26.9 us  [send(): return lax.ppermute(value, AXES, pairs)]
    ppermute x40, starting transfers between devices: 36.4 us -> 38.4 us  [send(): return lax.ppermute(value, AXES, pairs)]
  transfers between devices with their start and end apart: 40 -> 40, of which waited for: 18 -> 16; matrix products, arithmetic and copies ran while one was open for 2% -> 2% of each run, Pallas kernels for 6% -> 6%
where the time goes in v8:
time: 94 us; the launch traced here: 92.9 us
  starting transfers between devices  38.4 us (41%)
  waiting for transfers between devices  26.9 us (29%)
  Pallas kernels  14.7 us (16%)
  blocking collectives  9.47 us (10%)
  other arithmetic  2.07 us (2%)
  between operations  1.03 us (1%)
    ppermute x40, starting transfers between devices, send(): return lax.ppermute(value, AXES, pairs)  38.4 us
    ppermute x40, waiting for transfers between devices, send(): return lax.ppermute(value, AXES, pairs)  26.9 us
    all_to_all x1, blocking collectives, sum_everywhere(): lax.all_to_all(jnp.broadcast_to(value, (count, *value.shape)), AXES, 0, 0...  9.47 us
    pallas_call x3, Pallas kernels, project(): pl.pallas_call(functools.partial(project_kernel, grid, plan, rows, before...  6.74 us
    pallas_call x1, Pallas kernels, sent_rows(): pl.pallas_call(functools.partial(sent_kernel, grid, parts), out_shape=[ja...  4.49 us
    pallas_call x1, Pallas kernels, kept_product(): pl.pallas_call(functools.partial(kept_product_kernel, grid), out_shape=ja...  2.38 us
  transfers between devices with their start and end apart: 40, of which 16 were waited for; matrix products, arithmetic and copies ran while one was open for 2% of the time, Pallas kernels for 6%

profile of v8, /device:TPU:0, one launch (start us, length us, event | category | flops | bytes accessed | tf_op | source)
XLA Modules:
  0.0 92.9 jit_solution(16685343771655881341)
XLA Ops:
  0.6 4.5 %shard_map.86 = (bf16[1024,256]{1,0:T(8,128)(2,1)S(1)}, bf16[1024,256]{1,0:T(8,128)(2,1)S(1)}, bf16[1024,256]{1,0:T(8,128)(2,1)S(1)}, bf16[1024,256]{1,0:T(8,128)(2,1)S(1)}) custom-call(bf16[1024,2048]{1,0:T(8,128)(2,1)} %tokens_ref.1, bf16[1024,1024]{1,0:T(8,128)(2,1)} %cot_ref.1), custom_call_target="tpu_custom_call" | custom-call | flops 2147483648 | bytes 4194304 | tf_op jit(solution)/shard_map/pallas_call | solution.py:110
  5.1 0.5 collective-permute-start
  6.3 2.4 %shard_map.85.value_ref = f32[1024,1024]{1,0:T(8,128)S(1)} custom-call(bf16[1024,2048]{1,0:T(8,128)(2,1)S(1)} %copy-done.1, bf16[1024,1024]{1,0:T(8,128)(2,1)S(1)} %copy-done.2), custom_call_target="tpu_custom_call" | custom-call | flops 2147483648 | bytes 4194304 | tf_op jit(solution)/shard_map/pallas_call | solution.py:133
  8.7 0.7 collective-permute-done.3.refs_3_
  9.5 1.0 %shard_map.87 = (bf16[2,4,64,256]{3,2,1,0:T(8,128)(2,1)S(1)}, bf16[2,4,64,256]{3,2,1,0:T(8,128)(2,1)S(1)}, bf16[2,4,64,256]{3,2,1,0:T(8,128)(2,1)S(1)}, bf16[2,4...) custom-call(f32[1024,1024]{1,0:T(8,128)S(1)} %shard_map.85.value_ref, ...), custom_call_target="tpu_custom_call" | custom-call | bytes 12582912 | tf_op jit(solution)/shard_map/pallas_call | solution.py:179
  10.5 2.9 %collective-permute-start.4 = (bf16[2,4,64,256]{3,2,1,0:T(8,128)(2,1)S(1)}, bf16[2,4,64,256]{3,2,1,0:T(8,128)(2,1)}, u32[]{:S(2)}, u32[]{:S(2)}) collective-permute-start(bf16[2,4,64,256]{3,2,1,0:T(8,128)(2,1)S(1)} %get-tuple-element.44), channel_id=1, source_target_pairs={{0,16},{1,17},{2,18},{3,19},{4,20},{5,21},{6,22},{7,23},{8,24},{9,... | collective-permute-start | bytes 786440 | tf_op jit(solution)/shard_map/ppermute | solution.py:47
  13.4 1.5 %collective-permute-start.5 = (bf16[2,4,64,256]{3,2,1,0:T(8,128)(2,1)S(1)}, bf16[2,4,64,256]{3,2,1,0:T(8,128)(2,1)S(1)}, u32[]{:S(2)}, u32[]{:S(2)}) collective-permute-start(bf16[2,4,64,256]{3,2,1,0:T(8,128)(2,1)S(1)} %get-tuple-element.45), channel_id=1, source_target_pairs={{0,1},{1,0},{2,3},{3,2},{4,5},{5,4},{6,7},{7,6},{8,9},{9,8},{10,11... | collective-permute-start | bytes 786440 | tf_op jit(solution)/shard_map/ppermute | solution.py:47
  14.9 0.5 collective-permute-start.11
  15.5 5.1 %collective-permute-done.4 = bf16[2,4,64,256]{3,2,1,0:T(8,128)(2,1)} collective-permute-done((bf16[2,4,64,256]{3,2,1,0:T(8,128)(2,1)S(1)}, bf16[2,4,64,256]{3,2,1,0:T(8,128)(2,1)}, u32[]{:S(2)}, u32[]{:S(2)}) %collective-permute-start.4) | collective-permute-done | bytes 262176 | tf_op jit(solution)/shard_map/ppermute | solution.py:47
  20.6 2.0 %collective-permute-done.5 = bf16[2,4,64,256]{3,2,1,0:T(8,128)(2,1)S(1)} collective-permute-done((bf16[2,4,64,256]{3,2,1,0:T(8,128)(2,1)S(1)}, bf16[2,4,64,256]{3,2,1,0:T(8,128)(2,1)S(1)}, u32[]{:S(2)}, u32[]{:S(2)}) %collective-permute-start.5) | collective-permute-done | bytes 262176 | tf_op jit(solution)/shard_map/ppermute | solution.py:47
  22.6 1.0 %convert_add_fusion.3 = f32[2,4,64,256]{3,2,1,0:T(8,128)S(1)} fusion(f32[2,4,64,256]{3,2,1,0:T(8,128)S(1)} %get-tuple-element.43, bf16[2,4,64,256]{3,2,1,0:T(8,128)(2,1)} %collective-permute-done.4), kind=kLoop, calls=%fused_computation.19 | loop fusion | flops 262144 | bytes 1310720 | tf_op jit(solution)/shard_map/add | solution.py:202
  23.7 1.6 %collective-permute-start.6 = (bf16[4,64,256]{2,1,0:T(8,128)(2,1)S(1)}, bf16[4,64,256]{2,1,0:T(8,128)(2,1)S(1)}, u32[]{:S(2)}, u32[]{:S(2)}) collective-permute-start(bf16[4,64,256]{2,1,0:T(8,128)(2,1)S(1)} %fusion.13), channel_id=1, source_target_pairs={{0,1},{1,0},{2,3},{3,2},{4,5},{5,4},{6,7},{7,6},{8,9},{9,8},{10,11... | collective-permute-start | bytes 393224 | tf_op jit(solution)/shard_map/ppermute | solution.py:47
  25.3 0.6 collective-permute-start.7
  25.9 2.3 %collective-permute-done.12 = bf16[2,4,64,256]{3,2,1,0:T(8,128)(2,1)S(1)} collective-permute-done((bf16[2,4,64,256]{3,2,1,0:T(8,128)(2,1)S(1)}, bf16[2,4,64,256]{3,2,1,0:T(8,128)(2,1)S(1)}, u32[]{:S(2)}, u32[]{:S(2)}) %collective-permute-start.12) | collective-permute-done | bytes 262176 | tf_op jit(solution)/shard_map/ppermute | solution.py:47
  28.4 1.6 %collective-permute-start.13 = (bf16[4,64,256]{2,1,0:T(8,128)(2,1)S(1)}, bf16[4,64,256]{2,1,0:T(8,128)(2,1)S(1)}, u32[]{:S(2)}, u32[]{:S(2)}) collective-permute-start(bf16[4,64,256]{2,1,0:T(8,128)(2,1)S(1)} %fusion.15), channel_id=1, source_target_pairs={{0,1},{1,0},{2,3},{3,2},{4,5},{5,4},{6,7},{7,6},{8,9},{9,8},{10,11... | collective-permute-start | bytes 393224 | tf_op jit(solution)/shard_map/ppermute | solution.py:47
  30.1 0.6 collective-permute-start.14
  31.0 3.7 %collective-permute-start.10 = (bf16[64,512]{1,0:T(8,128)(2,1)S(1)}, bf16[64,512]{1,0:T(8,128)(2,1)S(1)}, u32[]{:S(2)}, u32[]{:S(2)}) collective-permute-start(bf16[64,512]{1,0:T(8,128)(2,1)S(1)} %get-tuple-element.86), channel_id=1, source_target_pairs={{0,6},{1,7},{2,4},{3,5},{4,2},{5,3},{6,0},{7,1},{8,14},{9,15},{10,... | collective-permute-start | bytes 196616 | tf_op jit(solution)/shard_map/ppermute | solution.py:47
  34.7 0.8 collective-permute-start.9
  35.6 1.3 %collective-permute-start.15 = (bf16[64,512]{1,0:T(8,128)(2,1)S(1)}, bf16[64,512]{1,0:T(8,128)(2,1)S(1)}, u32[]{:S(2)}, u32[]{:S(2)}) collective-permute-start(bf16[64,512]{1,0:T(8,128)(2,1)S(1)} %get-tuple-element.81), channel_id=1, source_target_pairs={{0,2},{1,3},{2,0},{3,1},{4,6},{5,7},{6,4},{7,5},{8,10},{9,11},{10,... | collective-permute-start | bytes 196616 | tf_op jit(solution)/shard_map/ppermute | solution.py:47
  36.9 2.9 %collective-permute-start.16 = (bf16[64,512]{1,0:T(8,128)(2,1)S(1)}, bf16[64,512]{1,0:T(8,128)(2,1)S(1)}, u32[]{:S(2)}, u32[]{:S(2)}) collective-permute-start(bf16[64,512]{1,0:T(8,128)(2,1)S(1)} %get-tuple-element.82), channel_id=1, source_target_pairs={{0,4},{1,5},{2,6},{3,7},{4,0},{5,1},{6,2},{7,3},{8,12},{9,13},{10,... | collective-permute-start | bytes 196616 | tf_op jit(solution)/shard_map/ppermute | solution.py:47
  39.8 1.1 %collective-permute-start.17 = (bf16[64,512]{1,0:T(8,128)(2,1)S(1)}, bf16[64,512]{1,0:T(8,128)(2,1)S(1)}, u32[]{:S(2)}, u32[]{:S(2)}) collective-permute-start(bf16[64,512]{1,0:T(8,128)(2,1)S(1)} %get-tuple-element.83), channel_id=1, source_target_pairs={{0,6},{1,7},{2,4},{3,5},{4,2},{5,3},{6,0},{7,1},{8,14},{9,15},{10,... | collective-permute-start | bytes 196616 | tf_op jit(solution)/shard_map/ppermute | solution.py:47
  40.9 1.8 %collective-permute-done.9 = bf16[64,512]{1,0:T(8,128)(2,1)S(1)} collective-permute-done((bf16[64,512]{1,0:T(8,128)(2,1)S(1)}, bf16[64,512]{1,0:T(8,128)(2,1)S(1)}, u32[]{:S(2)}, u32[]{:S(2)}) %collective-permute-start.9) | collective-permute-done | bytes 65568 | tf_op jit(solution)/shard_map/ppermute | solution.py:47
  42.8 1.3 %collective-permute-done.16 = bf16[64,512]{1,0:T(8,128)(2,1)S(1)} collective-permute-done((bf16[64,512]{1,0:T(8,128)(2,1)S(1)}, bf16[64,512]{1,0:T(8,128)(2,1)S(1)}, u32[]{:S(2)}, u32[]{:S(2)}) %collective-permute-start.16) | collective-permute-done | bytes 65568 | tf_op jit(solution)/shard_map/ppermute | solution.py:47
  44.1 1.8 %collective-permute-done.17 = bf16[64,512]{1,0:T(8,128)(2,1)S(1)} collective-permute-done((bf16[64,512]{1,0:T(8,128)(2,1)S(1)}, bf16[64,512]{1,0:T(8,128)(2,1)S(1)}, u32[]{:S(2)}, u32[]{:S(2)}) %collective-permute-start.17) | collective-permute-done | bytes 65568 | tf_op jit(solution)/shard_map/ppermute | solution.py:47
  46.1 9.5 %all_to_all.5 = f32[32,2,128]{2,1,0:T(2,128)S(1)} all-to-all(f32[32,2,128]{2,1,0:T(2,128)S(1)} %broadcast_in_dim.4), channel_id=1, replica_groups=mesh['aa'=4,'ba'=8] {'aa','ba'}, dimensions={0} | all-to-all | bytes 65536 | tf_op jit(solution)/shard_map/all_to_all | solution.py:225
  56.0 0.7 collective-permute-start.31
  56.7 0.6 collective-permute-start.29
  57.4 3.1 %collective-permute-start.30 = (bf16[64,512]{1,0:T(8,128)(2,1)S(1)}, bf16[64,512]{1,0:T(8,128)(2,1)S(1)}, u32[]{:S(2)}, u32[]{:S(2)}) collective-permute-start(bf16[64,512]{1,0:T(8,128)(2,1)S(1)} %get-tuple-element.64), channel_id=1, source_target_pairs={{0,4},{1,5},{2,6},{3,7},{4,0},{5,1},{6,2},{7,3},{8,12},{9,13},{10,... | collective-permute-start | bytes 196616 | tf_op jit(solution)/shard_map/ppermute | solution.py:47
  60.5 1.2 %collective-permute-start.19 = (bf16[64,512]{1,0:T(8,128)(2,1)S(1)}, bf16[64,512]{1,0:T(8,128)(2,1)S(1)}, u32[]{:S(2)}, u32[]{:S(2)}) collective-permute-start(bf16[64,512]{1,0:T(8,128)(2,1)S(1)} %get-tuple-element.59), channel_id=1, source_target_pairs={{0,4},{1,5},{2,6},{3,7},{4,0},{5,1},{6,2},{7,3},{8,12},{9,13},{10,... | collective-permute-start | bytes 196616 | tf_op jit(solution)/shard_map/ppermute | solution.py:47
  61.7 1.1 %collective-permute-done.31 = bf16[64,512]{1,0:T(8,128)(2,1)S(1)} collective-permute-done((bf16[64,512]{1,0:T(8,128)(2,1)S(1)}, bf16[64,512]{1,0:T(8,128)(2,1)S(1)}, u32[]{:S(2)}, u32[]{:S(2)}) %collective-permute-start.31) | collective-permute-done | bytes 65568 | tf_op jit(solution)/shard_map/ppermute | solution.py:47
  62.8 2.1 %collective-permute-start.20 = (bf16[64,512]{1,0:T(8,128)(2,1)S(1)}, bf16[64,512]{1,0:T(8,128)(2,1)S(1)}, u32[]{:S(2)}, u32[]{:S(2)}) collective-permute-start(bf16[64,512]{1,0:T(8,128)(2,1)S(1)} %get-tuple-element.59), channel_id=1, source_target_pairs={{0,6},{1,7},{2,4},{3,5},{4,2},{5,3},{6,0},{7,1},{8,14},{9,15},{10,... | collective-permute-start | bytes 196616 | tf_op jit(solution)/shard_map/ppermute | solution.py:47
  65.0 0.7 collective-permute-start.33
  65.8 0.7 collective-permute-start.32
  66.5 3.1 %collective-permute-done.19 = bf16[64,512]{1,0:T(8,128)(2,1)S(1)} collective-permute-done((bf16[64,512]{1,0:T(8,128)(2,1)S(1)}, bf16[64,512]{1,0:T(8,128)(2,1)S(1)}, u32[]{:S(2)}, u32[]{:S(2)}) %collective-permute-start.19) | collective-permute-done | bytes 65568 | tf_op jit(solution)/shard_map/ppermute | solution.py:47
  69.7 0.7 collective-permute-start.22
  70.4 0.7 collective-permute-start.21
  71.2 1.4 %collective-permute-start.36 = (bf16[2,4,64,256]{3,2,1,0:T(8,128)(2,1)S(1)}, bf16[2,4,64,256]{3,2,1,0:T(8,128)(2,1)S(1)}, u32[]{:S(2)}, u32[]{:S(2)}) collective-permute-start(bf16[2,4,64,256]{3,2,1,0:T(8,128)(2,1)S(1)} %pad_maximum_fusion.3.refs_3_), channel_id=1, source_target_pairs={{0,1},{1,0},{2,3},{3,2},{4,5},{5,4},{6,7},{7,6},{8,9},{9,8},{10,11... | collective-permute-start | bytes 786440 | tf_op jit(solution)/shard_map/ppermute | solution.py:47
  72.6 1.4 %collective-permute-start.35 = (bf16[2,4,64,256]{3,2,1,0:T(8,128)(2,1)S(1)}, bf16[2,4,64,256]{3,2,1,0:T(8,128)(2,1)S(1)}, u32[]{:S(2)}, u32[]{:S(2)}) collective-permute-start(bf16[2,4,64,256]{3,2,1,0:T(8,128)(2,1)S(1)} %pad_maximum_fusion.2.refs_1_), channel_id=1, source_target_pairs={{0,16},{1,17},{2,18},{3,19},{4,20},{5,21},{6,22},{7,23},{8,24},{9,... | collective-permute-start | bytes 786440 | tf_op jit(solution)/shard_map/ppermute | solution.py:47
  74.1 2.0 %collective-permute-done.22 = bf16[4,64,256]{2,1,0:T(8,128)(2,1)S(1)} collective-permute-done((bf16[4,64,256]{2,1,0:T(8,128)(2,1)S(1)}, bf16[4,64,256]{2,1,0:T(8,128)(2,1)S(1)}, u32[]{:S(2)}, u32[]{:S(2)}) %collective-permute-start.22) | collective-permute-done | bytes 131104 | tf_op jit(solution)/shard_map/ppermute | solution.py:47
  76.1 0.5 collective-permute-done.21
  76.6 0.8 collective-permute-start.24
  77.4 2.1 %collective-permute-done.36.refs_4_ = bf16[2,4,64,256]{3,2,1,0:T(8,128)(2,1)S(1)} collective-permute-done((bf16[2,4,64,256]{3,2,1,0:T(8,128)(2,1)S(1)}, bf16[2,4,64,256]{3,2,1,0:T(8,128)(2,1)S(1)}, u32[]{:S(2)}, u32[]{:S(2)}) %collective-permute-start.36) | collective-permute-done | bytes 262176 | tf_op jit(solution)/shard_map/ppermute | solution.py:47
  79.5 2.7 %collective-permute-start.23 = (bf16[2,4,64,256]{3,2,1,0:T(8,128)(2,1)S(1)}, bf16[2,4,64,256]{3,2,1,0:T(8,128)(2,1)S(1)}, u32[]{:S(2)}, u32[]{:S(2)}) collective-permute-start(bf16[2,4,64,256]{3,2,1,0:T(8,128)(2,1)S(1)} %pad_maximum_fusion.refs_1_), channel_id=1, source_target_pairs={{0,16},{1,17},{2,18},{3,19},{4,20},{5,21},{6,22},{7,23},{8,24},{9,... | collective-permute-start | bytes 786440 | tf_op jit(solution)/shard_map/ppermute | solution.py:47
  82.2 1.5 %shard_map.88.refs_5_ = f32[1024,512]{1,0:T(8,128)S(1)} custom-call(bf16[1024,2048]{1,0:T(8,128)(2,1)S(1)} %copy-done, bf16[2,4,64,256]{3,2,1,0:T(8,128)(2,1)S(1)} %pad_maximum_fusion.2.refs_1_, bf16[2,4,64,256]{3,2,1,0:T(8,128)(2,1)S(1)} %collective-permute-done.35.refs_2_, bf16[2,4,64,256]{3,2,1,0:T(8,128)(2,1)S(1)} %pad_maximum_fusion.3.refs_3_, ...), custom_call_target="tpu_custom_call" | custom-call | flops 1073741824 | bytes 8388608 | tf_op jit(solution)/shard_map/pallas_call | solution.py:331
  83.8 1.2 %collective-permute-done.24.refs_4_ = bf16[2,4,64,256]{3,2,1,0:T(8,128)(2,1)S(1)} collective-permute-done((bf16[2,4,64,256]{3,2,1,0:T(8,128)(2,1)S(1)}, bf16[2,4,64,256]{3,2,1,0:T(8,128)(2,1)S(1)}, u32[]{:S(2)}, u32[]{:S(2)}) %collective-permute-start.24) | collective-permute-done | bytes 262176 | tf_op jit(solution)/shard_map/ppermute | solution.py:47
  85.0 1.5 %collective-permute-done.23.refs_2_ = bf16[2,4,64,256]{3,2,1,0:T(8,128)(2,1)S(1)} collective-permute-done((bf16[2,4,64,256]{3,2,1,0:T(8,128)(2,1)S(1)}, bf16[2,4,64,256]{3,2,1,0:T(8,128)(2,1)S(1)}, u32[]{:S(2)}, u32[]{:S(2)}) %collective-permute-start.23) | collective-permute-done | bytes 262176 | tf_op jit(solution)/shard_map/ppermute | solution.py:47
  87.6 1.5 %shard_map.89.refs_9_ = f32[1024,512]{1,0:T(8,128)S(1)} custom-call(bf16[1024,2048]{1,0:T(8,128)(2,1)S(1)} %copy-done, bf16[2,4,64,256]{3,2,1,0:T(8,128)(2,1)S(1)} %collective-permute-done.34.refs_1_, bf16[2,4,64,256]{3,2,1,0:T(8,128)(2,1)S(1)} %collective-permute-done.37.refs_2_, bf16[2,4,64,256]{3,2,1,0:T(8,128)(2,1)S(1)} %collective-permute-done.38.refs_3_, ...), custom_call_target="tpu_custom_call" | custom-call | flops 1073741824 | bytes 8388608 | tf_op jit(solution)/shard_map/pallas_call | solution.py:331
  89.2 3.7 %shard_map.90 = (bf16[1024,512]{1,0:T(8,128)(2,1)}, f32[64,1024]{1,0:T(8,128)}, f32[64,1024]{1,0:T(8,128)}) custom-call(bf16[1024,2048]{1,0:T(8,128)(2,1)S(1)} %copy-done, bf16[2,4,64,256]{3,2,1,0:T(8,128)(2,1)S(1)} %pad_maximum_fusion.refs_1_, bf16[2,4,64,256]{3,2,1,0:T(8,128)(2,1)S(1)} %collective-permute-done.23.refs_2_, ...), custom_call_target="tpu_custom_call" | custom-call | flops 2147483648 | bytes 8388608 | tf_op jit(solution)/shard_map/pallas_call | solution.py:331
  (93 shorter events, 3.6 us)
Async XLA Ops:
  0.6 5.6 %copy-start.1 = (bf16[1024,2048]{1,0:T(8,128)(2,1)S(1)}, bf16[1024,2048]{1,0:T(8,128)(2,1)}, u32[]{:S(2)}) copy-start(bf16[1024,2048]{1,0:T(8,128)(2,1)} %tokens_ref.1) | copy-start | bytes 12582916
  0.6 5.6 %copy-start.2 = (bf16[1024,1024]{1,0:T(8,128)(2,1)S(1)}, bf16[1024,1024]{1,0:T(8,128)(2,1)}, u32[]{:S(2)}) copy-start(bf16[1024,1024]{1,0:T(8,128)(2,1)} %cot_ref.1) | copy-start | bytes 6291460
  5.1 3.5 %collective-permute-start = (bf16[1024,256]{1,0:T(8,128)(2,1)S(1)}, bf16[1024,256]{1,0:T(8,128)(2,1)S(1)}, u32[]{:S(2)}, u32[]{:S(2)}) collective-permute-start(bf16[1024,256]{1,0:T(8,128)(2,1)S(1)} %get-tuple-element.39), channel_id=1, source_target_pairs={{0,8},{1,9},{2,10},{3,11},{4,12},{5,13},{6,14},{7,15},{8,0},{9,1},... | collective-permute-start | bytes 1572872 | tf_op jit(solution)/shard_map/ppermute | solution.py:47
  5.7 3.0 %collective-permute-start.1 = (bf16[1024,256]{1,0:T(8,128)(2,1)S(1)}, bf16[1024,256]{1,0:T(8,128)(2,1)S(1)}, u32[]{:S(2)}, u32[]{:S(2)}) collective-permute-start(bf16[1024,256]{1,0:T(8,128)(2,1)S(1)} %get-tuple-element.40), channel_id=1, source_target_pairs={{0,8},{1,9},{2,10},{3,11},{4,12},{5,13},{6,14},{7,15},{8,0},{9,1},... | collective-permute-start | bytes 1572872 | tf_op jit(solution)/shard_map/ppermute | solution.py:47
  5.7 3.0 %collective-permute-start.2 = (bf16[1024,256]{1,0:T(8,128)(2,1)S(1)}, bf16[1024,256]{1,0:T(8,128)(2,1)S(1)}, u32[]{:S(2)}, u32[]{:S(2)}) collective-permute-start(bf16[1024,256]{1,0:T(8,128)(2,1)S(1)} %get-tuple-element.41), channel_id=1, source_target_pairs={{0,8},{1,9},{2,10},{3,11},{4,12},{5,13},{6,14},{7,15},{8,0},{9,1},... | collective-permute-start | bytes 1572872 | tf_op jit(solution)/shard_map/ppermute | solution.py:47
  6.2 3.3 %collective-permute-start.3 = (bf16[1024,256]{1,0:T(8,128)(2,1)S(1)}, bf16[1024,256]{1,0:T(8,128)(2,1)S(1)}, u32[]{:S(2)}, u32[]{:S(2)}) collective-permute-start(bf16[1024,256]{1,0:T(8,128)(2,1)S(1)} %get-tuple-element.42), channel_id=1, source_target_pairs={{0,8},{1,9},{2,10},{3,11},{4,12},{5,13},{6,14},{7,15},{8,0},{9,1},... | collective-permute-start | bytes 1572872 | tf_op jit(solution)/shard_map/ppermute | solution.py:47
  10.5 10.1 %collective-permute-start.4 = (bf16[2,4,64,256]{3,2,1,0:T(8,128)(2,1)S(1)}, bf16[2,4,64,256]{3,2,1,0:T(8,128)(2,1)}, u32[]{:S(2)}, u32[]{:S(2)}) collective-permute-start(bf16[2,4,64,256]{3,2,1,0:T(8,128)(2,1)S(1)} %get-tuple-element.44), channel_id=1, source_target_pairs={{0,16},{1,17},{2,18},{3,19},{4,20},{5,21},{6,22},{7,23},{8,24},{9,... | collective-permute-start | bytes 786440 | tf_op jit(solution)/shard_map/ppermute | solution.py:47
  13.4 9.2 %collective-permute-start.5 = (bf16[2,4,64,256]{3,2,1,0:T(8,128)(2,1)S(1)}, bf16[2,4,64,256]{3,2,1,0:T(8,128)(2,1)S(1)}, u32[]{:S(2)}, u32[]{:S(2)}) collective-permute-start(bf16[2,4,64,256]{3,2,1,0:T(8,128)(2,1)S(1)} %get-tuple-element.45), channel_id=1, source_target_pairs={{0,1},{1,0},{2,3},{3,2},{4,5},{5,4},{6,7},{7,6},{8,9},{9,8},{10,11... | collective-permute-start | bytes 786440 | tf_op jit(solution)/shard_map/ppermute | solution.py:47
  14.9 11.0 %collective-permute-start.11 = (bf16[2,4,64,256]{3,2,1,0:T(8,128)(2,1)S(1)}, bf16[2,4,64,256]{3,2,1,0:T(8,128)(2,1)S(1)}, u32[]{:S(2)}, u32[]{:S(2)}) collective-permute-start(bf16[2,4,64,256]{3,2,1,0:T(8,128)(2,1)S(1)} %get-tuple-element.52), channel_id=1, source_target_pairs={{0,16},{1,17},{2,18},{3,19},{4,20},{5,21},{6,22},{7,23},{8,24},{9,... | collective-permute-start | bytes 786440 | tf_op jit(solution)/shard_map/ppermute | solution.py:47
  15.5 12.8 %collective-permute-start.12 = (bf16[2,4,64,256]{3,2,1,0:T(8,128)(2,1)S(1)}, bf16[2,4,64,256]{3,2,1,0:T(8,128)(2,1)S(1)}, u32[]{:S(2)}, u32[]{:S(2)}) collective-permute-start(bf16[2,4,64,256]{3,2,1,0:T(8,128)(2,1)S(1)} %get-tuple-element.53), channel_id=1, source_target_pairs={{0,1},{1,0},{2,3},{3,2},{4,5},{5,4},{6,7},{7,6},{8,9},{9,8},{10,11... | collective-permute-start | bytes 786440 | tf_op jit(solution)/shard_map/ppermute | solution.py:47
  23.7 7.2 %collective-permute-start.6 = (bf16[4,64,256]{2,1,0:T(8,128)(2,1)S(1)}, bf16[4,64,256]{2,1,0:T(8,128)(2,1)S(1)}, u32[]{:S(2)}, u32[]{:S(2)}) collective-permute-start(bf16[4,64,256]{2,1,0:T(8,128)(2,1)S(1)} %fusion.13), channel_id=1, source_target_pairs={{0,1},{1,0},{2,3},{3,2},{4,5},{5,4},{6,7},{7,6},{8,9},{9,8},{10,11... | collective-permute-start | bytes 393224 | tf_op jit(solution)/shard_map/ppermute | solution.py:47
  25.3 5.6 %collective-permute-start.7 = (bf16[4,64,256]{2,1,0:T(8,128)(2,1)S(1)}, bf16[4,64,256]{2,1,0:T(8,128)(2,1)S(1)}, u32[]{:S(2)}, u32[]{:S(2)}) collective-permute-start(bf16[4,64,256]{2,1,0:T(8,128)(2,1)S(1)} %fusion.14), channel_id=1, source_target_pairs={{0,16},{1,17},{2,18},{3,19},{4,20},{5,21},{6,22},{7,23},{8,24},{9,... | collective-permute-start | bytes 393224 | tf_op jit(solution)/shard_map/ppermute | solution.py:47
  28.3 27.5 %copy-start.3 = (f32[64,1024]{1,0:T(8,128)S(1)}, f32[64,1024]{1,0:T(8,128)}, u32[]{:S(2)}) copy-start(f32[64,1024]{1,0:T(8,128)} %refs_13_.1) | copy-start | bytes 786436
  28.3 27.4 %copy-start.4 = (f32[64,1024]{1,0:T(8,128)S(1)}, f32[64,1024]{1,0:T(8,128)}, u32[]{:S(2)}) copy-start(f32[64,1024]{1,0:T(8,128)} %refs_12_.1) | copy-start | bytes 786436
  28.4 27.4 %copy-start.5 = (f32[64,1024]{1,0:T(8,128)S(1)}, f32[64,1024]{1,0:T(8,128)}, u32[]{:S(2)}) copy-start(f32[64,1024]{1,0:T(8,128)} %param.8) | copy-start | bytes 786436
  28.4 7.1 %collective-permute-start.13 = (bf16[4,64,256]{2,1,0:T(8,128)(2,1)S(1)}, bf16[4,64,256]{2,1,0:T(8,128)(2,1)S(1)}, u32[]{:S(2)}, u32[]{:S(2)}) collective-permute-start(bf16[4,64,256]{2,1,0:T(8,128)(2,1)S(1)} %fusion.15), channel_id=1, source_target_pairs={{0,1},{1,0},{2,3},{3,2},{4,5},{5,4},{6,7},{7,6},{8,9},{9,8},{10,11... | collective-permute-start | bytes 393224 | tf_op jit(solution)/shard_map/ppermute | solution.py:47
  30.1 5.4 %collective-permute-start.14 = (bf16[4,64,256]{2,1,0:T(8,128)(2,1)S(1)}, bf16[4,64,256]{2,1,0:T(8,128)(2,1)S(1)}, u32[]{:S(2)}, u32[]{:S(2)}) collective-permute-start(bf16[4,64,256]{2,1,0:T(8,128)(2,1)S(1)} %fusion.16), channel_id=1, source_target_pairs={{0,16},{1,17},{2,18},{3,19},{4,20},{5,21},{6,22},{7,23},{8,24},{9,... | collective-permute-start | bytes 393224 | tf_op jit(solution)/shard_map/ppermute | solution.py:47
  31.0 8.8 %collective-permute-start.10 = (bf16[64,512]{1,0:T(8,128)(2,1)S(1)}, bf16[64,512]{1,0:T(8,128)(2,1)S(1)}, u32[]{:S(2)}, u32[]{:S(2)}) collective-permute-start(bf16[64,512]{1,0:T(8,128)(2,1)S(1)} %get-tuple-element.86), channel_id=1, source_target_pairs={{0,6},{1,7},{2,4},{3,5},{4,2},{5,3},{6,0},{7,1},{8,14},{9,15},{10,... | collective-permute-start | bytes 196616 | tf_op jit(solution)/shard_map/ppermute | solution.py:47
  34.7 6.2 %collective-permute-start.8 = (bf16[64,512]{1,0:T(8,128)(2,1)S(1)}, bf16[64,512]{1,0:T(8,128)(2,1)S(1)}, u32[]{:S(2)}, u32[]{:S(2)}) collective-permute-start(bf16[64,512]{1,0:T(8,128)(2,1)S(1)} %get-tuple-element.84), channel_id=1, source_target_pairs={{0,2},{1,3},{2,0},{3,1},{4,6},{5,7},{6,4},{7,5},{8,10},{9,11},{10,... | collective-permute-start | bytes 196616 | tf_op jit(solution)/shard_map/ppermute | solution.py:47
  34.7 8.0 %collective-permute-start.9 = (bf16[64,512]{1,0:T(8,128)(2,1)S(1)}, bf16[64,512]{1,0:T(8,128)(2,1)S(1)}, u32[]{:S(2)}, u32[]{:S(2)}) collective-permute-start(bf16[64,512]{1,0:T(8,128)(2,1)S(1)} %get-tuple-element.85), channel_id=1, source_target_pairs={{0,4},{1,5},{2,6},{3,7},{4,0},{5,1},{6,2},{7,3},{8,12},{9,13},{10,... | collective-permute-start | bytes 196616 | tf_op jit(solution)/shard_map/ppermute | solution.py:47
  35.6 7.2 %collective-permute-start.15 = (bf16[64,512]{1,0:T(8,128)(2,1)S(1)}, bf16[64,512]{1,0:T(8,128)(2,1)S(1)}, u32[]{:S(2)}, u32[]{:S(2)}) collective-permute-start(bf16[64,512]{1,0:T(8,128)(2,1)S(1)} %get-tuple-element.81), channel_id=1, source_target_pairs={{0,2},{1,3},{2,0},{3,1},{4,6},{5,7},{6,4},{7,5},{8,10},{9,11},{10,... | collective-permute-start | bytes 196616 | tf_op jit(solution)/shard_map/ppermute | solution.py:47
  36.9 7.2 %collective-permute-start.16 = (bf16[64,512]{1,0:T(8,128)(2,1)S(1)}, bf16[64,512]{1,0:T(8,128)(2,1)S(1)}, u32[]{:S(2)}, u32[]{:S(2)}) collective-permute-start(bf16[64,512]{1,0:T(8,128)(2,1)S(1)} %get-tuple-element.82), channel_id=1, source_target_pairs={{0,4},{1,5},{2,6},{3,7},{4,0},{5,1},{6,2},{7,3},{8,12},{9,13},{10,... | collective-permute-start | bytes 196616 | tf_op jit(solution)/shard_map/ppermute | solution.py:47
  39.8 6.1 %collective-permute-start.17 = (bf16[64,512]{1,0:T(8,128)(2,1)S(1)}, bf16[64,512]{1,0:T(8,128)(2,1)S(1)}, u32[]{:S(2)}, u32[]{:S(2)}) collective-permute-start(bf16[64,512]{1,0:T(8,128)(2,1)S(1)} %get-tuple-element.83), channel_id=1, source_target_pairs={{0,6},{1,7},{2,4},{3,5},{4,2},{5,3},{6,0},{7,1},{8,14},{9,15},{10,... | collective-permute-start | bytes 196616 | tf_op jit(solution)/shard_map/ppermute | solution.py:47
  55.7 26.5 %copy-start = (bf16[1024,2048]{1,0:T(8,128)(2,1)S(1)}, bf16[1024,2048]{1,0:T(8,128)(2,1)}, u32[]{:S(2)}) copy-start(bf16[1024,2048]{1,0:T(8,128)(2,1)} %refs_0_.5) | copy-start | bytes 12582916
  56.0 6.8 %collective-permute-start.31 = (bf16[64,512]{1,0:T(8,128)(2,1)S(1)}, bf16[64,512]{1,0:T(8,128)(2,1)S(1)}, u32[]{:S(2)}, u32[]{:S(2)}) collective-permute-start(bf16[64,512]{1,0:T(8,128)(2,1)S(1)} %get-tuple-element.64), channel_id=1, source_target_pairs={{0,6},{1,7},{2,4},{3,5},{4,2},{5,3},{6,0},{7,1},{8,14},{9,15},{10,... | collective-permute-start | bytes 196616 | tf_op jit(solution)/shard_map/ppermute | solution.py:47
  56.7 8.2 %collective-permute-start.29 = (bf16[64,512]{1,0:T(8,128)(2,1)S(1)}, bf16[64,512]{1,0:T(8,128)(2,1)S(1)}, u32[]{:S(2)}, u32[]{:S(2)}) collective-permute-start(bf16[64,512]{1,0:T(8,128)(2,1)S(1)} %get-tuple-element.64), channel_id=1, source_target_pairs={{0,2},{1,3},{2,0},{3,1},{4,6},{5,7},{6,4},{7,5},{8,10},{9,11},{10,... | collective-permute-start | bytes 196616 | tf_op jit(solution)/shard_map/ppermute | solution.py:47
  57.4 7.6 %collective-permute-start.30 = (bf16[64,512]{1,0:T(8,128)(2,1)S(1)}, bf16[64,512]{1,0:T(8,128)(2,1)S(1)}, u32[]{:S(2)}, u32[]{:S(2)}) collective-permute-start(bf16[64,512]{1,0:T(8,128)(2,1)S(1)} %get-tuple-element.64), channel_id=1, source_target_pairs={{0,4},{1,5},{2,6},{3,7},{4,0},{5,1},{6,2},{7,3},{8,12},{9,13},{10,... | collective-permute-start | bytes 196616 | tf_op jit(solution)/shard_map/ppermute | solution.py:47
  60.5 6.0 %collective-permute-start.18 = (bf16[64,512]{1,0:T(8,128)(2,1)S(1)}, bf16[64,512]{1,0:T(8,128)(2,1)S(1)}, u32[]{:S(2)}, u32[]{:S(2)}) collective-permute-start(bf16[64,512]{1,0:T(8,128)(2,1)S(1)} %get-tuple-element.59), channel_id=1, source_target_pairs={{0,2},{1,3},{2,0},{3,1},{4,6},{5,7},{6,4},{7,5},{8,10},{9,11},{10,... | collective-permute-start | bytes 196616 | tf_op jit(solution)/shard_map/ppermute | solution.py:47
  60.5 9.1 %collective-permute-start.19 = (bf16[64,512]{1,0:T(8,128)(2,1)S(1)}, bf16[64,512]{1,0:T(8,128)(2,1)S(1)}, u32[]{:S(2)}, u32[]{:S(2)}) collective-permute-start(bf16[64,512]{1,0:T(8,128)(2,1)S(1)} %get-tuple-element.59), channel_id=1, source_target_pairs={{0,4},{1,5},{2,6},{3,7},{4,0},{5,1},{6,2},{7,3},{8,12},{9,13},{10,... | collective-permute-start | bytes 196616 | tf_op jit(solution)/shard_map/ppermute | solution.py:47
  62.8 6.8 %collective-permute-start.20 = (bf16[64,512]{1,0:T(8,128)(2,1)S(1)}, bf16[64,512]{1,0:T(8,128)(2,1)S(1)}, u32[]{:S(2)}, u32[]{:S(2)}) collective-permute-start(bf16[64,512]{1,0:T(8,128)(2,1)S(1)} %get-tuple-element.59), channel_id=1, source_target_pairs={{0,6},{1,7},{2,4},{3,5},{4,2},{5,3},{6,0},{7,1},{8,14},{9,15},{10,... | collective-permute-start | bytes 196616 | tf_op jit(solution)/shard_map/ppermute | solution.py:47
  65.0 6.1 %collective-permute-start.33 = (bf16[4,64,256]{2,1,0:T(8,128)(2,1)S(1)}, bf16[4,64,256]{2,1,0:T(8,128)(2,1)S(1)}, u32[]{:S(2)}, u32[]{:S(2)}) collective-permute-start(bf16[4,64,256]{2,1,0:T(8,128)(2,1)S(1)} %get-tuple-element.88), channel_id=1, source_target_pairs={{0,16},{1,17},{2,18},{3,19},{4,20},{5,21},{6,22},{7,23},{8,24},{9,... | collective-permute-start | bytes 393224 | tf_op jit(solution)/shard_map/ppermute | solution.py:47
  65.8 5.3 %collective-permute-start.32 = (bf16[4,64,256]{2,1,0:T(8,128)(2,1)S(1)}, bf16[4,64,256]{2,1,0:T(8,128)(2,1)S(1)}, u32[]{:S(2)}, u32[]{:S(2)}) collective-permute-start(bf16[4,64,256]{2,1,0:T(8,128)(2,1)S(1)} %get-tuple-element.90), channel_id=1, source_target_pairs={{0,1},{1,0},{2,3},{3,2},{4,5},{5,4},{6,7},{7,6},{8,9},{9,8},{10,11... | collective-permute-start | bytes 393224 | tf_op jit(solution)/shard_map/ppermute | solution.py:47
  69.7 6.4 %collective-permute-start.22 = (bf16[4,64,256]{2,1,0:T(8,128)(2,1)S(1)}, bf16[4,64,256]{2,1,0:T(8,128)(2,1)S(1)}, u32[]{:S(2)}, u32[]{:S(2)}) collective-permute-start(bf16[4,64,256]{2,1,0:T(8,128)(2,1)S(1)} %get-tuple-element.92), channel_id=1, source_target_pairs={{0,16},{1,17},{2,18},{3,19},{4,20},{5,21},{6,22},{7,23},{8,24},{9,... | collective-permute-start | bytes 393224 | tf_op jit(solution)/shard_map/ppermute | solution.py:47
  70.4 6.2 %collective-permute-start.21 = (bf16[4,64,256]{2,1,0:T(8,128)(2,1)S(1)}, bf16[4,64,256]{2,1,0:T(8,128)(2,1)S(1)}, u32[]{:S(2)}, u32[]{:S(2)}) collective-permute-start(bf16[4,64,256]{2,1,0:T(8,128)(2,1)S(1)} %get-tuple-element.94), channel_id=1, source_target_pairs={{0,1},{1,0},{2,3},{3,2},{4,5},{5,4},{6,7},{7,6},{8,9},{9,8},{10,11... | collective-permute-start | bytes 393224 | tf_op jit(solution)/shard_map/ppermute | solution.py:47
  71.2 8.3 %collective-permute-start.36 = (bf16[2,4,64,256]{3,2,1,0:T(8,128)(2,1)S(1)}, bf16[2,4,64,256]{3,2,1,0:T(8,128)(2,1)S(1)}, u32[]{:S(2)}, u32[]{:S(2)}) collective-permute-start(bf16[2,4,64,256]{3,2,1,0:T(8,128)(2,1)S(1)} %pad_maximum_fusion.3.refs_3_), channel_id=1, source_target_pairs={{0,1},{1,0},{2,3},{3,2},{4,5},{5,4},{6,7},{7,6},{8,9},{9,8},{10,11... | collective-permute-start | bytes 786440 | tf_op jit(solution)/shard_map/ppermute | solution.py:47
  72.6 9.6 %collective-permute-start.35 = (bf16[2,4,64,256]{3,2,1,0:T(8,128)(2,1)S(1)}, bf16[2,4,64,256]{3,2,1,0:T(8,128)(2,1)S(1)}, u32[]{:S(2)}, u32[]{:S(2)}) collective-permute-start(bf16[2,4,64,256]{3,2,1,0:T(8,128)(2,1)S(1)} %pad_maximum_fusion.2.refs_1_), channel_id=1, source_target_pairs={{0,16},{1,17},{2,18},{3,19},{4,20},{5,21},{6,22},{7,23},{8,24},{9,... | collective-permute-start | bytes 786440 | tf_op jit(solution)/shard_map/ppermute | solution.py:47
  74.1 12.5 %collective-permute-start.38 = (bf16[2,4,64,256]{3,2,1,0:T(8,128)(2,1)S(1)}, bf16[2,4,64,256]{3,2,1,0:T(8,128)(2,1)S(1)}, u32[]{:S(2)}, u32[]{:S(2)}) collective-permute-start(bf16[2,4,64,256]{3,2,1,0:T(8,128)(2,1)S(1)} %pad_maximum_fusion.3.refs_3_), channel_id=1, source_target_pairs={{0,8},{1,9},{2,10},{3,11},{4,12},{5,13},{6,14},{7,15},{8,0},{9,1},... | collective-permute-start | bytes 786440 | tf_op jit(solution)/shard_map/ppermute | solution.py:47
  76.1 11.0 %collective-permute-start.34 = (bf16[2,4,64,256]{3,2,1,0:T(8,128)(2,1)S(1)}, bf16[2,4,64,256]{3,2,1,0:T(8,128)(2,1)S(1)}, u32[]{:S(2)}, u32[]{:S(2)}) collective-permute-start(bf16[2,4,64,256]{3,2,1,0:T(8,128)(2,1)S(1)} %pad_maximum_fusion.2.refs_1_), channel_id=1, source_target_pairs={{0,8},{1,9},{2,10},{3,11},{4,12},{5,13},{6,14},{7,15},{8,0},{9,1},... | collective-permute-start | bytes 786440 | tf_op jit(solution)/shard_map/ppermute | solution.py:47
  76.6 8.4 %collective-permute-start.24 = (bf16[2,4,64,256]{3,2,1,0:T(8,128)(2,1)S(1)}, bf16[2,4,64,256]{3,2,1,0:T(8,128)(2,1)S(1)}, u32[]{:S(2)}, u32[]{:S(2)}) collective-permute-start(bf16[2,4,64,256]{3,2,1,0:T(8,128)(2,1)S(1)} %pad_maximum_fusion.1.refs_3_), channel_id=1, source_target_pairs={{0,1},{1,0},{2,3},{3,2},{4,5},{5,4},{6,7},{7,6},{8,9},{9,8},{10,11... | collective-permute-start | bytes 786440 | tf_op jit(solution)/shard_map/ppermute | solution.py:47
  79.5 7.1 %collective-permute-start.23 = (bf16[2,4,64,256]{3,2,1,0:T(8,128)(2,1)S(1)}, bf16[2,4,64,256]{3,2,1,0:T(8,128)(2,1)S(1)}, u32[]{:S(2)}, u32[]{:S(2)}) collective-permute-start(bf16[2,4,64,256]{3,2,1,0:T(8,128)(2,1)S(1)} %pad_maximum_fusion.refs_1_), channel_id=1, source_target_pairs={{0,16},{1,17},{2,18},{3,19},{4,20},{5,21},{6,22},{7,23},{8,24},{9,... | collective-permute-start | bytes 786440 | tf_op jit(solution)/shard_map/ppermute | solution.py:47
  83.7 3.4 %collective-permute-start.39 = (bf16[2,4,64,256]{3,2,1,0:T(8,128)(2,1)S(1)}, bf16[2,4,64,256]{3,2,1,0:T(8,128)(2,1)S(1)}, u32[]{:S(2)}, u32[]{:S(2)}) collective-permute-start(bf16[2,4,64,256]{3,2,1,0:T(8,128)(2,1)S(1)} %collective-permute-done.36.refs_4_), channel_id=1, source_target_pairs={{0,8},{1,9},{2,10},{3,11},{4,12},{5,13},{6,14},{7,15},{8,0},{9,1},... | collective-permute-start | bytes 786440 | tf_op jit(solution)/shard_map/ppermute | solution.py:47
  85.0 2.6 %collective-permute-start.37 = (bf16[2,4,64,256]{3,2,1,0:T(8,128)(2,1)S(1)}, bf16[2,4,64,256]{3,2,1,0:T(8,128)(2,1)S(1)}, u32[]{:S(2)}, u32[]{:S(2)}) collective-permute-start(bf16[2,4,64,256]{3,2,1,0:T(8,128)(2,1)S(1)} %collective-permute-done.35.refs_2_), channel_id=1, source_target_pairs={{0,8},{1,9},{2,10},{3,11},{4,12},{5,13},{6,14},{7,15},{8,0},{9,1},... | collective-permute-start | bytes 786440 | tf_op jit(solution)/shard_map/ppermute | solution.py:47
  86.5 2.6 %collective-permute-start.27 = (bf16[2,4,64,256]{3,2,1,0:T(8,128)(2,1)S(1)}, bf16[2,4,64,256]{3,2,1,0:T(8,128)(2,1)S(1)}, u32[]{:S(2)}, u32[]{:S(2)}) collective-permute-start(bf16[2,4,64,256]{3,2,1,0:T(8,128)(2,1)S(1)} %pad_maximum_fusion.1.refs_3_), channel_id=1, source_target_pairs={{0,8},{1,9},{2,10},{3,11},{4,12},{5,13},{6,14},{7,15},{8,0},{9,1},... | collective-permute-start | bytes 786440 | tf_op jit(solution)/shard_map/ppermute | solution.py:47
  86.5 2.6 %collective-permute-start.25 = (bf16[2,4,64,256]{3,2,1,0:T(8,128)(2,1)S(1)}, bf16[2,4,64,256]{3,2,1,0:T(8,128)(2,1)S(1)}, u32[]{:S(2)}, u32[]{:S(2)}) collective-permute-start(bf16[2,4,64,256]{3,2,1,0:T(8,128)(2,1)S(1)} %pad_maximum_fusion.refs_1_), channel_id=1, source_target_pairs={{0,8},{1,9},{2,10},{3,11},{4,12},{5,13},{6,14},{7,15},{8,0},{9,1},... | collective-permute-start | bytes 786440 | tf_op jit(solution)/shard_map/ppermute | solution.py:47
  87.1 2.1 %collective-permute-start.26 = (bf16[2,4,64,256]{3,2,1,0:T(8,128)(2,1)S(1)}, bf16[2,4,64,256]{3,2,1,0:T(8,128)(2,1)S(1)}, u32[]{:S(2)}, u32[]{:S(2)}) collective-permute-start(bf16[2,4,64,256]{3,2,1,0:T(8,128)(2,1)S(1)} %collective-permute-done.23.refs_2_), channel_id=1, source_target_pairs={{0,8},{1,9},{2,10},{3,11},{4,12},{5,13},{6,14},{7,15},{8,0},{9,1},... | collective-permute-start | bytes 786440 | tf_op jit(solution)/shard_map/ppermute | solution.py:47
  87.1 2.1 %collective-permute-start.28 = (bf16[2,4,64,256]{3,2,1,0:T(8,128)(2,1)S(1)}, bf16[2,4,64,256]{3,2,1,0:T(8,128)(2,1)S(1)}, u32[]{:S(2)}, u32[]{:S(2)}) collective-permute-start(bf16[2,4,64,256]{3,2,1,0:T(8,128)(2,1)S(1)} %collective-permute-done.24.refs_4_), channel_id=1, source_target_pairs={{0,8},{1,9},{2,10},{3,11},{4,12},{5,13},{6,14},{7,15},{8,0},{9,1},... | collective-permute-start | bytes 786440 | tf_op jit(solution)/shard_map/ppermute | solution.py:47

commit v9 on v8

--- a/solution.py
+++ b/solution.py
@@ -382,7 +382,7 @@
         after = yield clipped, wanted
         last = [table[1:] for table in wanted]
         if after is not None:
-            last[-1], _ = lax.optimization_barrier((last[-1], after))
+            last[0], _ = lax.optimization_barrier((last[0], after))
         yield [first + [grid.send(piece, c=1) for piece in rest] for first, rest in zip(early, last)]
 
     def run(ways):

time: 94 us -> 94 us (level)
  no operation moved by 1% of the time
where the time goes in v9:
time: 94 us; the launch traced here: 92.9 us
  starting transfers between devices  38.4 us (41%)
  waiting for transfers between devices  26.9 us (29%)
  Pallas kernels  14.7 us (16%)
  blocking collectives  9.47 us (10%)
  other arithmetic  2.07 us (2%)
  between operations  1.03 us (1%)
    ppermute x40, starting transfers between devices, send(): return lax.ppermute(value, AXES, pairs)  38.4 us
    ppermute x40, waiting for transfers between devices, send(): return lax.ppermute(value, AXES, pairs)  26.9 us
    all_to_all x1, blocking collectives, sum_everywhere(): lax.all_to_all(jnp.broadcast_to(value, (count, *value.shape)), AXES, 0, 0...  9.47 us
    pallas_call x3, Pallas kernels, project(): pl.pallas_call(functools.partial(project_kernel, grid, plan, rows, before...  6.74 us
    pallas_call x1, Pallas kernels, sent_rows(): pl.pallas_call(functools.partial(sent_kernel, grid, parts), out_shape=[ja...  4.49 us
    pallas_call x1, Pallas kernels, kept_product(): pl.pallas_call(functools.partial(kept_product_kernel, grid), out_shape=ja...  2.38 us
  transfers between devices with their start and end apart: 40, of which 16 were waited for; matrix products, arithmetic and copies ran while one was open for 2% of the time, Pallas kernels for 6%

profile of v9, /device:TPU:0, one launch (start us, length us, event | category | flops | bytes accessed | tf_op | source)
XLA Modules:
  0.0 92.9 jit_solution(9478823117705432887)
XLA Ops:
  0.6 4.5 %shard_map.86 = (bf16[1024,256]{1,0:T(8,128)(2,1)S(1)}, bf16[1024,256]{1,0:T(8,128)(2,1)S(1)}, bf16[1024,256]{1,0:T(8,128)(2,1)S(1)}, bf16[1024,256]{1,0:T(8,128)(2,1)S(1)}) custom-call(bf16[1024,2048]{1,0:T(8,128)(2,1)} %tokens_ref.1, bf16[1024,1024]{1,0:T(8,128)(2,1)} %cot_ref.1), custom_call_target="tpu_custom_call" | custom-call | flops 2147483648 | bytes 4194304 | tf_op jit(solution)/shard_map/pallas_call | solution.py:110
  5.1 0.5 collective-permute-start
  6.3 2.4 %shard_map.85.value_ref = f32[1024,1024]{1,0:T(8,128)S(1)} custom-call(bf16[1024,2048]{1,0:T(8,128)(2,1)S(1)} %copy-done.1, bf16[1024,1024]{1,0:T(8,128)(2,1)S(1)} %copy-done.2), custom_call_target="tpu_custom_call" | custom-call | flops 2147483648 | bytes 4194304 | tf_op jit(solution)/shard_map/pallas_call | solution.py:133
  8.7 0.7 collective-permute-done.3.refs_3_
  9.5 1.0 %shard_map.87 = (bf16[2,4,64,256]{3,2,1,0:T(8,128)(2,1)S(1)}, bf16[2,4,64,256]{3,2,1,0:T(8,128)(2,1)S(1)}, bf16[2,4,64,256]{3,2,1,0:T(8,128)(2,1)S(1)}, bf16[2,4...) custom-call(f32[1024,1024]{1,0:T(8,128)S(1)} %shard_map.85.value_ref, ...), custom_call_target="tpu_custom_call" | custom-call | bytes 12582912 | tf_op jit(solution)/shard_map/pallas_call | solution.py:179
  10.5 2.9 %collective-permute-start.4 = (bf16[2,4,64,256]{3,2,1,0:T(8,128)(2,1)S(1)}, bf16[2,4,64,256]{3,2,1,0:T(8,128)(2,1)}, u32[]{:S(2)}, u32[]{:S(2)}) collective-permute-start(bf16[2,4,64,256]{3,2,1,0:T(8,128)(2,1)S(1)} %get-tuple-element.44), channel_id=1, source_target_pairs={{0,16},{1,17},{2,18},{3,19},{4,20},{5,21},{6,22},{7,23},{8,24},{9,... | collective-permute-start | bytes 786440 | tf_op jit(solution)/shard_map/ppermute | solution.py:47
  13.4 1.5 %collective-permute-start.5 = (bf16[2,4,64,256]{3,2,1,0:T(8,128)(2,1)S(1)}, bf16[2,4,64,256]{3,2,1,0:T(8,128)(2,1)S(1)}, u32[]{:S(2)}, u32[]{:S(2)}) collective-permute-start(bf16[2,4,64,256]{3,2,1,0:T(8,128)(2,1)S(1)} %get-tuple-element.45), channel_id=1, source_target_pairs={{0,1},{1,0},{2,3},{3,2},{4,5},{5,4},{6,7},{7,6},{8,9},{9,8},{10,11... | collective-permute-start | bytes 786440 | tf_op jit(solution)/shard_map/ppermute | solution.py:47
  14.9 0.5 collective-permute-start.11
  15.5 5.1 %collective-permute-done.4 = bf16[2,4,64,256]{3,2,1,0:T(8,128)(2,1)} collective-permute-done((bf16[2,4,64,256]{3,2,1,0:T(8,128)(2,1)S(1)}, bf16[2,4,64,256]{3,2,1,0:T(8,128)(2,1)}, u32[]{:S(2)}, u32[]{:S(2)}) %collective-permute-start.4) | collective-permute-done | bytes 262176 | tf_op jit(solution)/shard_map/ppermute | solution.py:47
  20.6 2.0 %collective-permute-done.5 = bf16[2,4,64,256]{3,2,1,0:T(8,128)(2,1)S(1)} collective-permute-done((bf16[2,4,64,256]{3,2,1,0:T(8,128)(2,1)S(1)}, bf16[2,4,64,256]{3,2,1,0:T(8,128)(2,1)S(1)}, u32[]{:S(2)}, u32[]{:S(2)}) %collective-permute-start.5) | collective-permute-done | bytes 262176 | tf_op jit(solution)/shard_map/ppermute | solution.py:47
  22.6 1.0 %convert_add_fusion.3 = f32[2,4,64,256]{3,2,1,0:T(8,128)S(1)} fusion(f32[2,4,64,256]{3,2,1,0:T(8,128)S(1)} %get-tuple-element.43, bf16[2,4,64,256]{3,2,1,0:T(8,128)(2,1)} %collective-permute-done.4), kind=kLoop, calls=%fused_computation.19 | loop fusion | flops 262144 | bytes 1310720 | tf_op jit(solution)/shard_map/add | solution.py:202
  23.7 1.6 %collective-permute-start.6 = (bf16[4,64,256]{2,1,0:T(8,128)(2,1)S(1)}, bf16[4,64,256]{2,1,0:T(8,128)(2,1)S(1)}, u32[]{:S(2)}, u32[]{:S(2)}) collective-permute-start(bf16[4,64,256]{2,1,0:T(8,128)(2,1)S(1)} %fusion.13), channel_id=1, source_target_pairs={{0,1},{1,0},{2,3},{3,2},{4,5},{5,4},{6,7},{7,6},{8,9},{9,8},{10,11... | collective-permute-start | bytes 393224 | tf_op jit(solution)/shard_map/ppermute | solution.py:47
  25.3 0.6 collective-permute-start.7
  25.9 2.3 %collective-permute-done.12 = bf16[2,4,64,256]{3,2,1,0:T(8,128)(2,1)S(1)} collective-permute-done((bf16[2,4,64,256]{3,2,1,0:T(8,128)(2,1)S(1)}, bf16[2,4,64,256]{3,2,1,0:T(8,128)(2,1)S(1)}, u32[]{:S(2)}, u32[]{:S(2)}) %collective-permute-start.12) | collective-permute-done | bytes 262176 | tf_op jit(solution)/shard_map/ppermute | solution.py:47
  28.4 1.6 %collective-permute-start.13 = (bf16[4,64,256]{2,1,0:T(8,128)(2,1)S(1)}, bf16[4,64,256]{2,1,0:T(8,128)(2,1)S(1)}, u32[]{:S(2)}, u32[]{:S(2)}) collective-permute-start(bf16[4,64,256]{2,1,0:T(8,128)(2,1)S(1)} %fusion.15), channel_id=1, source_target_pairs={{0,1},{1,0},{2,3},{3,2},{4,5},{5,4},{6,7},{7,6},{8,9},{9,8},{10,11... | collective-permute-start | bytes 393224 | tf_op jit(solution)/shard_map/ppermute | solution.py:47
  30.1 0.6 collective-permute-start.14
  31.0 3.7 %collective-permute-start.10 = (bf16[64,512]{1,0:T(8,128)(2,1)S(1)}, bf16[64,512]{1,0:T(8,128)(2,1)S(1)}, u32[]{:S(2)}, u32[]{:S(2)}) collective-permute-start(bf16[64,512]{1,0:T(8,128)(2,1)S(1)} %get-tuple-element.86), channel_id=1, source_target_pairs={{0,6},{1,7},{2,4},{3,5},{4,2},{5,3},{6,0},{7,1},{8,14},{9,15},{10,... | collective-permute-start | bytes 196616 | tf_op jit(solution)/shard_map/ppermute | solution.py:47
  34.7 0.8 collective-permute-start.9
  35.6 1.3 %collective-permute-start.15 = (bf16[64,512]{1,0:T(8,128)(2,1)S(1)}, bf16[64,512]{1,0:T(8,128)(2,1)S(1)}, u32[]{:S(2)}, u32[]{:S(2)}) collective-permute-start(bf16[64,512]{1,0:T(8,128)(2,1)S(1)} %get-tuple-element.81), channel_id=1, source_target_pairs={{0,2},{1,3},{2,0},{3,1},{4,6},{5,7},{6,4},{7,5},{8,10},{9,11},{10,... | collective-permute-start | bytes 196616 | tf_op jit(solution)/shard_map/ppermute | solution.py:47
  36.9 2.9 %collective-permute-start.16 = (bf16[64,512]{1,0:T(8,128)(2,1)S(1)}, bf16[64,512]{1,0:T(8,128)(2,1)S(1)}, u32[]{:S(2)}, u32[]{:S(2)}) collective-permute-start(bf16[64,512]{1,0:T(8,128)(2,1)S(1)} %get-tuple-element.82), channel_id=1, source_target_pairs={{0,4},{1,5},{2,6},{3,7},{4,0},{5,1},{6,2},{7,3},{8,12},{9,13},{10,... | collective-permute-start | bytes 196616 | tf_op jit(solution)/shard_map/ppermute | solution.py:47
  39.8 1.1 %collective-permute-start.17 = (bf16[64,512]{1,0:T(8,128)(2,1)S(1)}, bf16[64,512]{1,0:T(8,128)(2,1)S(1)}, u32[]{:S(2)}, u32[]{:S(2)}) collective-permute-start(bf16[64,512]{1,0:T(8,128)(2,1)S(1)} %get-tuple-element.83), channel_id=1, source_target_pairs={{0,6},{1,7},{2,4},{3,5},{4,2},{5,3},{6,0},{7,1},{8,14},{9,15},{10,... | collective-permute-start | bytes 196616 | tf_op jit(solution)/shard_map/ppermute | solution.py:47
  40.9 1.8 %collective-permute-done.9 = bf16[64,512]{1,0:T(8,128)(2,1)S(1)} collective-permute-done((bf16[64,512]{1,0:T(8,128)(2,1)S(1)}, bf16[64,512]{1,0:T(8,128)(2,1)S(1)}, u32[]{:S(2)}, u32[]{:S(2)}) %collective-permute-start.9) | collective-permute-done | bytes 65568 | tf_op jit(solution)/shard_map/ppermute | solution.py:47
  42.8 1.3 %collective-permute-done.16 = bf16[64,512]{1,0:T(8,128)(2,1)S(1)} collective-permute-done((bf16[64,512]{1,0:T(8,128)(2,1)S(1)}, bf16[64,512]{1,0:T(8,128)(2,1)S(1)}, u32[]{:S(2)}, u32[]{:S(2)}) %collective-permute-start.16) | collective-permute-done | bytes 65568 | tf_op jit(solution)/shard_map/ppermute | solution.py:47
  44.1 1.8 %collective-permute-done.17 = bf16[64,512]{1,0:T(8,128)(2,1)S(1)} collective-permute-done((bf16[64,512]{1,0:T(8,128)(2,1)S(1)}, bf16[64,512]{1,0:T(8,128)(2,1)S(1)}, u32[]{:S(2)}, u32[]{:S(2)}) %collective-permute-start.17) | collective-permute-done | bytes 65568 | tf_op jit(solution)/shard_map/ppermute | solution.py:47
  46.1 9.5 %all_to_all.5 = f32[32,2,128]{2,1,0:T(2,128)S(1)} all-to-all(f32[32,2,128]{2,1,0:T(2,128)S(1)} %broadcast_in_dim.4), channel_id=1, replica_groups=mesh['aa'=4,'ba'=8] {'aa','ba'}, dimensions={0} | all-to-all | bytes 65536 | tf_op jit(solution)/shard_map/all_to_all | solution.py:225
  56.0 0.7 collective-permute-start.31
  56.7 0.6 collective-permute-start.29
  57.4 3.1 %collective-permute-start.30 = (bf16[64,512]{1,0:T(8,128)(2,1)S(1)}, bf16[64,512]{1,0:T(8,128)(2,1)S(1)}, u32[]{:S(2)}, u32[]{:S(2)}) collective-permute-start(bf16[64,512]{1,0:T(8,128)(2,1)S(1)} %get-tuple-element.64), channel_id=1, source_target_pairs={{0,4},{1,5},{2,6},{3,7},{4,0},{5,1},{6,2},{7,3},{8,12},{9,13},{10,... | collective-permute-start | bytes 196616 | tf_op jit(solution)/shard_map/ppermute | solution.py:47
  60.5 1.2 %collective-permute-start.19 = (bf16[64,512]{1,0:T(8,128)(2,1)S(1)}, bf16[64,512]{1,0:T(8,128)(2,1)S(1)}, u32[]{:S(2)}, u32[]{:S(2)}) collective-permute-start(bf16[64,512]{1,0:T(8,128)(2,1)S(1)} %get-tuple-element.59), channel_id=1, source_target_pairs={{0,4},{1,5},{2,6},{3,7},{4,0},{5,1},{6,2},{7,3},{8,12},{9,13},{10,... | collective-permute-start | bytes 196616 | tf_op jit(solution)/shard_map/ppermute | solution.py:47
  61.7 1.1 %collective-permute-done.31 = bf16[64,512]{1,0:T(8,128)(2,1)S(1)} collective-permute-done((bf16[64,512]{1,0:T(8,128)(2,1)S(1)}, bf16[64,512]{1,0:T(8,128)(2,1)S(1)}, u32[]{:S(2)}, u32[]{:S(2)}) %collective-permute-start.31) | collective-permute-done | bytes 65568 | tf_op jit(solution)/shard_map/ppermute | solution.py:47
  62.8 2.1 %collective-permute-start.20 = (bf16[64,512]{1,0:T(8,128)(2,1)S(1)}, bf16[64,512]{1,0:T(8,128)(2,1)S(1)}, u32[]{:S(2)}, u32[]{:S(2)}) collective-permute-start(bf16[64,512]{1,0:T(8,128)(2,1)S(1)} %get-tuple-element.59), channel_id=1, source_target_pairs={{0,6},{1,7},{2,4},{3,5},{4,2},{5,3},{6,0},{7,1},{8,14},{9,15},{10,... | collective-permute-start | bytes 196616 | tf_op jit(solution)/shard_map/ppermute | solution.py:47
  65.0 0.7 collective-permute-start.33
  65.8 0.7 collective-permute-start.32
  66.5 3.1 %collective-permute-done.19 = bf16[64,512]{1,0:T(8,128)(2,1)S(1)} collective-permute-done((bf16[64,512]{1,0:T(8,128)(2,1)S(1)}, bf16[64,512]{1,0:T(8,128)(2,1)S(1)}, u32[]{:S(2)}, u32[]{:S(2)}) %collective-permute-start.19) | collective-permute-done | bytes 65568 | tf_op jit(solution)/shard_map/ppermute | solution.py:47
  69.7 0.7 collective-permute-start.22
  70.4 0.7 collective-permute-start.21
  71.2 1.4 %collective-permute-start.36 = (bf16[2,4,64,256]{3,2,1,0:T(8,128)(2,1)S(1)}, bf16[2,4,64,256]{3,2,1,0:T(8,128)(2,1)S(1)}, u32[]{:S(2)}, u32[]{:S(2)}) collective-permute-start(bf16[2,4,64,256]{3,2,1,0:T(8,128)(2,1)S(1)} %pad_maximum_fusion.3.refs_3_), channel_id=1, source_target_pairs={{0,1},{1,0},{2,3},{3,2},{4,5},{5,4},{6,7},{7,6},{8,9},{9,8},{10,11... | collective-permute-start | bytes 786440 | tf_op jit(solution)/shard_map/ppermute | solution.py:47
  72.6 1.4 %collective-permute-start.35 = (bf16[2,4,64,256]{3,2,1,0:T(8,128)(2,1)S(1)}, bf16[2,4,64,256]{3,2,1,0:T(8,128)(2,1)S(1)}, u32[]{:S(2)}, u32[]{:S(2)}) collective-permute-start(bf16[2,4,64,256]{3,2,1,0:T(8,128)(2,1)S(1)} %pad_maximum_fusion.2.refs_1_), channel_id=1, source_target_pairs={{0,16},{1,17},{2,18},{3,19},{4,20},{5,21},{6,22},{7,23},{8,24},{9,... | collective-permute-start | bytes 786440 | tf_op jit(solution)/shard_map/ppermute | solution.py:47
  74.1 2.0 %collective-permute-done.22 = bf16[4,64,256]{2,1,0:T(8,128)(2,1)S(1)} collective-permute-done((bf16[4,64,256]{2,1,0:T(8,128)(2,1)S(1)}, bf16[4,64,256]{2,1,0:T(8,128)(2,1)S(1)}, u32[]{:S(2)}, u32[]{:S(2)}) %collective-permute-start.22) | collective-permute-done | bytes 131104 | tf_op jit(solution)/shard_map/ppermute | solution.py:47
  76.1 0.5 collective-permute-done.21
  76.6 0.8 collective-permute-start.24
  77.4 2.1 %collective-permute-done.36.refs_4_ = bf16[2,4,64,256]{3,2,1,0:T(8,128)(2,1)S(1)} collective-permute-done((bf16[2,4,64,256]{3,2,1,0:T(8,128)(2,1)S(1)}, bf16[2,4,64,256]{3,2,1,0:T(8,128)(2,1)S(1)}, u32[]{:S(2)}, u32[]{:S(2)}) %collective-permute-start.36) | collective-permute-done | bytes 262176 | tf_op jit(solution)/shard_map/ppermute | solution.py:47
  79.5 2.7 %collective-permute-start.23 = (bf16[2,4,64,256]{3,2,1,0:T(8,128)(2,1)S(1)}, bf16[2,4,64,256]{3,2,1,0:T(8,128)(2,1)S(1)}, u32[]{:S(2)}, u32[]{:S(2)}) collective-permute-start(bf16[2,4,64,256]{3,2,1,0:T(8,128)(2,1)S(1)} %pad_maximum_fusion.refs_1_), channel_id=1, source_target_pairs={{0,16},{1,17},{2,18},{3,19},{4,20},{5,21},{6,22},{7,23},{8,24},{9,... | collective-permute-start | bytes 786440 | tf_op jit(solution)/shard_map/ppermute | solution.py:47
  82.2 1.5 %shard_map.88.refs_5_ = f32[1024,512]{1,0:T(8,128)S(1)} custom-call(bf16[1024,2048]{1,0:T(8,128)(2,1)S(1)} %copy-done, bf16[2,4,64,256]{3,2,1,0:T(8,128)(2,1)S(1)} %pad_maximum_fusion.2.refs_1_, bf16[2,4,64,256]{3,2,1,0:T(8,128)(2,1)S(1)} %collective-permute-done.35.refs_2_, bf16[2,4,64,256]{3,2,1,0:T(8,128)(2,1)S(1)} %pad_maximum_fusion.3.refs_3_, ...), custom_call_target="tpu_custom_call" | custom-call | flops 1073741824 | bytes 8388608 | tf_op jit(solution)/shard_map/pallas_call | solution.py:331
  83.8 1.2 %collective-permute-done.24.refs_4_ = bf16[2,4,64,256]{3,2,1,0:T(8,128)(2,1)S(1)} collective-permute-done((bf16[2,4,64,256]{3,2,1,0:T(8,128)(2,1)S(1)}, bf16[2,4,64,256]{3,2,1,0:T(8,128)(2,1)S(1)}, u32[]{:S(2)}, u32[]{:S(2)}) %collective-permute-start.24) | collective-permute-done | bytes 262176 | tf_op jit(solution)/shard_map/ppermute | solution.py:47
  85.0 1.5 %collective-permute-done.23.refs_2_ = bf16[2,4,64,256]{3,2,1,0:T(8,128)(2,1)S(1)} collective-permute-done((bf16[2,4,64,256]{3,2,1,0:T(8,128)(2,1)S(1)}, bf16[2,4,64,256]{3,2,1,0:T(8,128)(2,1)S(1)}, u32[]{:S(2)}, u32[]{:S(2)}) %collective-permute-start.23) | collective-permute-done | bytes 262176 | tf_op jit(solution)/shard_map/ppermute | solution.py:47
  87.6 1.5 %shard_map.89.refs_9_ = f32[1024,512]{1,0:T(8,128)S(1)} custom-call(bf16[1024,2048]{1,0:T(8,128)(2,1)S(1)} %copy-done, bf16[2,4,64,256]{3,2,1,0:T(8,128)(2,1)S(1)} %collective-permute-done.34.refs_1_, bf16[2,4,64,256]{3,2,1,0:T(8,128)(2,1)S(1)} %collective-permute-done.37.refs_2_, bf16[2,4,64,256]{3,2,1,0:T(8,128)(2,1)S(1)} %collective-permute-done.38.refs_3_, ...), custom_call_target="tpu_custom_call" | custom-call | flops 1073741824 | bytes 8388608 | tf_op jit(solution)/shard_map/pallas_call | solution.py:331
  89.2 3.7 %shard_map.90 = (bf16[1024,512]{1,0:T(8,128)(2,1)}, f32[64,1024]{1,0:T(8,128)}, f32[64,1024]{1,0:T(8,128)}) custom-call(bf16[1024,2048]{1,0:T(8,128)(2,1)S(1)} %copy-done, bf16[2,4,64,256]{3,2,1,0:T(8,128)(2,1)S(1)} %pad_maximum_fusion.refs_1_, bf16[2,4,64,256]{3,2,1,0:T(8,128)(2,1)S(1)} %collective-permute-done.23.refs_2_, ...), custom_call_target="tpu_custom_call" | custom-call | flops 2147483648 | bytes 8388608 | tf_op jit(solution)/shard_map/pallas_call | solution.py:331
  (93 shorter events, 3.6 us)
Async XLA Ops:
  0.6 5.6 %copy-start.1 = (bf16[1024,2048]{1,0:T(8,128)(2,1)S(1)}, bf16[1024,2048]{1,0:T(8,128)(2,1)}, u32[]{:S(2)}) copy-start(bf16[1024,2048]{1,0:T(8,128)(2,1)} %tokens_ref.1) | copy-start | bytes 12582916
  0.6 5.6 %copy-start.2 = (bf16[1024,1024]{1,0:T(8,128)(2,1)S(1)}, bf16[1024,1024]{1,0:T(8,128)(2,1)}, u32[]{:S(2)}) copy-start(bf16[1024,1024]{1,0:T(8,128)(2,1)} %cot_ref.1) | copy-start | bytes 6291460
  5.1 3.5 %collective-permute-start = (bf16[1024,256]{1,0:T(8,128)(2,1)S(1)}, bf16[1024,256]{1,0:T(8,128)(2,1)S(1)}, u32[]{:S(2)}, u32[]{:S(2)}) collective-permute-start(bf16[1024,256]{1,0:T(8,128)(2,1)S(1)} %get-tuple-element.39), channel_id=1, source_target_pairs={{0,8},{1,9},{2,10},{3,11},{4,12},{5,13},{6,14},{7,15},{8,0},{9,1},... | collective-permute-start | bytes 1572872 | tf_op jit(solution)/shard_map/ppermute | solution.py:47
  5.7 3.0 %collective-permute-start.1 = (bf16[1024,256]{1,0:T(8,128)(2,1)S(1)}, bf16[1024,256]{1,0:T(8,128)(2,1)S(1)}, u32[]{:S(2)}, u32[]{:S(2)}) collective-permute-start(bf16[1024,256]{1,0:T(8,128)(2,1)S(1)} %get-tuple-element.40), channel_id=1, source_target_pairs={{0,8},{1,9},{2,10},{3,11},{4,12},{5,13},{6,14},{7,15},{8,0},{9,1},... | collective-permute-start | bytes 1572872 | tf_op jit(solution)/shard_map/ppermute | solution.py:47
  5.7 3.0 %collective-permute-start.2 = (bf16[1024,256]{1,0:T(8,128)(2,1)S(1)}, bf16[1024,256]{1,0:T(8,128)(2,1)S(1)}, u32[]{:S(2)}, u32[]{:S(2)}) collective-permute-start(bf16[1024,256]{1,0:T(8,128)(2,1)S(1)} %get-tuple-element.41), channel_id=1, source_target_pairs={{0,8},{1,9},{2,10},{3,11},{4,12},{5,13},{6,14},{7,15},{8,0},{9,1},... | collective-permute-start | bytes 1572872 | tf_op jit(solution)/shard_map/ppermute | solution.py:47
  6.2 3.3 %collective-permute-start.3 = (bf16[1024,256]{1,0:T(8,128)(2,1)S(1)}, bf16[1024,256]{1,0:T(8,128)(2,1)S(1)}, u32[]{:S(2)}, u32[]{:S(2)}) collective-permute-start(bf16[1024,256]{1,0:T(8,128)(2,1)S(1)} %get-tuple-element.42), channel_id=1, source_target_pairs={{0,8},{1,9},{2,10},{3,11},{4,12},{5,13},{6,14},{7,15},{8,0},{9,1},... | collective-permute-start | bytes 1572872 | tf_op jit(solution)/shard_map/ppermute | solution.py:47
  10.5 10.1 %collective-permute-start.4 = (bf16[2,4,64,256]{3,2,1,0:T(8,128)(2,1)S(1)}, bf16[2,4,64,256]{3,2,1,0:T(8,128)(2,1)}, u32[]{:S(2)}, u32[]{:S(2)}) collective-permute-start(bf16[2,4,64,256]{3,2,1,0:T(8,128)(2,1)S(1)} %get-tuple-element.44), channel_id=1, source_target_pairs={{0,16},{1,17},{2,18},{3,19},{4,20},{5,21},{6,22},{7,23},{8,24},{9,... | collective-permute-start | bytes 786440 | tf_op jit(solution)/shard_map/ppermute | solution.py:47
  13.4 9.2 %collective-permute-start.5 = (bf16[2,4,64,256]{3,2,1,0:T(8,128)(2,1)S(1)}, bf16[2,4,64,256]{3,2,1,0:T(8,128)(2,1)S(1)}, u32[]{:S(2)}, u32[]{:S(2)}) collective-permute-start(bf16[2,4,64,256]{3,2,1,0:T(8,128)(2,1)S(1)} %get-tuple-element.45), channel_id=1, source_target_pairs={{0,1},{1,0},{2,3},{3,2},{4,5},{5,4},{6,7},{7,6},{8,9},{9,8},{10,11... | collective-permute-start | bytes 786440 | tf_op jit(solution)/shard_map/ppermute | solution.py:47
  14.9 11.0 %collective-permute-start.11 = (bf16[2,4,64,256]{3,2,1,0:T(8,128)(2,1)S(1)}, bf16[2,4,64,256]{3,2,1,0:T(8,128)(2,1)S(1)}, u32[]{:S(2)}, u32[]{:S(2)}) collective-permute-start(bf16[2,4,64,256]{3,2,1,0:T(8,128)(2,1)S(1)} %get-tuple-element.52), channel_id=1, source_target_pairs={{0,16},{1,17},{2,18},{3,19},{4,20},{5,21},{6,22},{7,23},{8,24},{9,... | collective-permute-start | bytes 786440 | tf_op jit(solution)/shard_map/ppermute | solution.py:47
  15.5 12.8 %collective-permute-start.12 = (bf16[2,4,64,256]{3,2,1,0:T(8,128)(2,1)S(1)}, bf16[2,4,64,256]{3,2,1,0:T(8,128)(2,1)S(1)}, u32[]{:S(2)}, u32[]{:S(2)}) collective-permute-start(bf16[2,4,64,256]{3,2,1,0:T(8,128)(2,1)S(1)} %get-tuple-element.53), channel_id=1, source_target_pairs={{0,1},{1,0},{2,3},{3,2},{4,5},{5,4},{6,7},{7,6},{8,9},{9,8},{10,11... | collective-permute-start | bytes 786440 | tf_op jit(solution)/shard_map/ppermute | solution.py:47
  23.7 7.2 %collective-permute-start.6 = (bf16[4,64,256]{2,1,0:T(8,128)(2,1)S(1)}, bf16[4,64,256]{2,1,0:T(8,128)(2,1)S(1)}, u32[]{:S(2)}, u32[]{:S(2)}) collective-permute-start(bf16[4,64,256]{2,1,0:T(8,128)(2,1)S(1)} %fusion.13), channel_id=1, source_target_pairs={{0,1},{1,0},{2,3},{3,2},{4,5},{5,4},{6,7},{7,6},{8,9},{9,8},{10,11... | collective-permute-start | bytes 393224 | tf_op jit(solution)/shard_map/ppermute | solution.py:47
  25.3 5.6 %collective-permute-start.7 = (bf16[4,64,256]{2,1,0:T(8,128)(2,1)S(1)}, bf16[4,64,256]{2,1,0:T(8,128)(2,1)S(1)}, u32[]{:S(2)}, u32[]{:S(2)}) collective-permute-start(bf16[4,64,256]{2,1,0:T(8,128)(2,1)S(1)} %fusion.14), channel_id=1, source_target_pairs={{0,16},{1,17},{2,18},{3,19},{4,20},{5,21},{6,22},{7,23},{8,24},{9,... | collective-permute-start | bytes 393224 | tf_op jit(solution)/shard_map/ppermute | solution.py:47
  28.3 27.5 %copy-start.3 = (f32[64,1024]{1,0:T(8,128)S(1)}, f32[64,1024]{1,0:T(8,128)}, u32[]{:S(2)}) copy-start(f32[64,1024]{1,0:T(8,128)} %refs_13_.1) | copy-start | bytes 786436
  28.3 27.4 %copy-start.4 = (f32[64,1024]{1,0:T(8,128)S(1)}, f32[64,1024]{1,0:T(8,128)}, u32[]{:S(2)}) copy-start(f32[64,1024]{1,0:T(8,128)} %refs_12_.1) | copy-start | bytes 786436
  28.4 27.4 %copy-start.5 = (f32[64,1024]{1,0:T(8,128)S(1)}, f32[64,1024]{1,0:T(8,128)}, u32[]{:S(2)}) copy-start(f32[64,1024]{1,0:T(8,128)} %param.8) | copy-start | bytes 786436
  28.4 7.1 %collective-permute-start.13 = (bf16[4,64,256]{2,1,0:T(8,128)(2,1)S(1)}, bf16[4,64,256]{2,1,0:T(8,128)(2,1)S(1)}, u32[]{:S(2)}, u32[]{:S(2)}) collective-permute-start(bf16[4,64,256]{2,1,0:T(8,128)(2,1)S(1)} %fusion.15), channel_id=1, source_target_pairs={{0,1},{1,0},{2,3},{3,2},{4,5},{5,4},{6,7},{7,6},{8,9},{9,8},{10,11... | collective-permute-start | bytes 393224 | tf_op jit(solution)/shard_map/ppermute | solution.py:47
  30.1 5.4 %collective-permute-start.14 = (bf16[4,64,256]{2,1,0:T(8,128)(2,1)S(1)}, bf16[4,64,256]{2,1,0:T(8,128)(2,1)S(1)}, u32[]{:S(2)}, u32[]{:S(2)}) collective-permute-start(bf16[4,64,256]{2,1,0:T(8,128)(2,1)S(1)} %fusion.16), channel_id=1, source_target_pairs={{0,16},{1,17},{2,18},{3,19},{4,20},{5,21},{6,22},{7,23},{8,24},{9,... | collective-permute-start | bytes 393224 | tf_op jit(solution)/shard_map/ppermute | solution.py:47
  31.0 8.8 %collective-permute-start.10 = (bf16[64,512]{1,0:T(8,128)(2,1)S(1)}, bf16[64,512]{1,0:T(8,128)(2,1)S(1)}, u32[]{:S(2)}, u32[]{:S(2)}) collective-permute-start(bf16[64,512]{1,0:T(8,128)(2,1)S(1)} %get-tuple-element.86), channel_id=1, source_target_pairs={{0,6},{1,7},{2,4},{3,5},{4,2},{5,3},{6,0},{7,1},{8,14},{9,15},{10,... | collective-permute-start | bytes 196616 | tf_op jit(solution)/shard_map/ppermute | solution.py:47
  34.7 6.2 %collective-permute-start.8 = (bf16[64,512]{1,0:T(8,128)(2,1)S(1)}, bf16[64,512]{1,0:T(8,128)(2,1)S(1)}, u32[]{:S(2)}, u32[]{:S(2)}) collective-permute-start(bf16[64,512]{1,0:T(8,128)(2,1)S(1)} %get-tuple-element.84), channel_id=1, source_target_pairs={{0,2},{1,3},{2,0},{3,1},{4,6},{5,7},{6,4},{7,5},{8,10},{9,11},{10,... | collective-permute-start | bytes 196616 | tf_op jit(solution)/shard_map/ppermute | solution.py:47
  34.7 8.0 %collective-permute-start.9 = (bf16[64,512]{1,0:T(8,128)(2,1)S(1)}, bf16[64,512]{1,0:T(8,128)(2,1)S(1)}, u32[]{:S(2)}, u32[]{:S(2)}) collective-permute-start(bf16[64,512]{1,0:T(8,128)(2,1)S(1)} %get-tuple-element.85), channel_id=1, source_target_pairs={{0,4},{1,5},{2,6},{3,7},{4,0},{5,1},{6,2},{7,3},{8,12},{9,13},{10,... | collective-permute-start | bytes 196616 | tf_op jit(solution)/shard_map/ppermute | solution.py:47
  35.6 7.2 %collective-permute-start.15 = (bf16[64,512]{1,0:T(8,128)(2,1)S(1)}, bf16[64,512]{1,0:T(8,128)(2,1)S(1)}, u32[]{:S(2)}, u32[]{:S(2)}) collective-permute-start(bf16[64,512]{1,0:T(8,128)(2,1)S(1)} %get-tuple-element.81), channel_id=1, source_target_pairs={{0,2},{1,3},{2,0},{3,1},{4,6},{5,7},{6,4},{7,5},{8,10},{9,11},{10,... | collective-permute-start | bytes 196616 | tf_op jit(solution)/shard_map/ppermute | solution.py:47
  36.9 7.2 %collective-permute-start.16 = (bf16[64,512]{1,0:T(8,128)(2,1)S(1)}, bf16[64,512]{1,0:T(8,128)(2,1)S(1)}, u32[]{:S(2)}, u32[]{:S(2)}) collective-permute-start(bf16[64,512]{1,0:T(8,128)(2,1)S(1)} %get-tuple-element.82), channel_id=1, source_target_pairs={{0,4},{1,5},{2,6},{3,7},{4,0},{5,1},{6,2},{7,3},{8,12},{9,13},{10,... | collective-permute-start | bytes 196616 | tf_op jit(solution)/shard_map/ppermute | solution.py:47
  39.8 6.1 %collective-permute-start.17 = (bf16[64,512]{1,0:T(8,128)(2,1)S(1)}, bf16[64,512]{1,0:T(8,128)(2,1)S(1)}, u32[]{:S(2)}, u32[]{:S(2)}) collective-permute-start(bf16[64,512]{1,0:T(8,128)(2,1)S(1)} %get-tuple-element.83), channel_id=1, source_target_pairs={{0,6},{1,7},{2,4},{3,5},{4,2},{5,3},{6,0},{7,1},{8,14},{9,15},{10,... | collective-permute-start | bytes 196616 | tf_op jit(solution)/shard_map/ppermute | solution.py:47
  55.7 26.5 %copy-start = (bf16[1024,2048]{1,0:T(8,128)(2,1)S(1)}, bf16[1024,2048]{1,0:T(8,128)(2,1)}, u32[]{:S(2)}) copy-start(bf16[1024,2048]{1,0:T(8,128)(2,1)} %refs_0_.5) | copy-start | bytes 12582916
  56.0 6.8 %collective-permute-start.31 = (bf16[64,512]{1,0:T(8,128)(2,1)S(1)}, bf16[64,512]{1,0:T(8,128)(2,1)S(1)}, u32[]{:S(2)}, u32[]{:S(2)}) collective-permute-start(bf16[64,512]{1,0:T(8,128)(2,1)S(1)} %get-tuple-element.64), channel_id=1, source_target_pairs={{0,6},{1,7},{2,4},{3,5},{4,2},{5,3},{6,0},{7,1},{8,14},{9,15},{10,... | collective-permute-start | bytes 196616 | tf_op jit(solution)/shard_map/ppermute | solution.py:47
  56.7 8.2 %collective-permute-start.29 = (bf16[64,512]{1,0:T(8,128)(2,1)S(1)}, bf16[64,512]{1,0:T(8,128)(2,1)S(1)}, u32[]{:S(2)}, u32[]{:S(2)}) collective-permute-start(bf16[64,512]{1,0:T(8,128)(2,1)S(1)} %get-tuple-element.64), channel_id=1, source_target_pairs={{0,2},{1,3},{2,0},{3,1},{4,6},{5,7},{6,4},{7,5},{8,10},{9,11},{10,... | collective-permute-start | bytes 196616 | tf_op jit(solution)/shard_map/ppermute | solution.py:47
  57.4 7.6 %collective-permute-start.30 = (bf16[64,512]{1,0:T(8,128)(2,1)S(1)}, bf16[64,512]{1,0:T(8,128)(2,1)S(1)}, u32[]{:S(2)}, u32[]{:S(2)}) collective-permute-start(bf16[64,512]{1,0:T(8,128)(2,1)S(1)} %get-tuple-element.64), channel_id=1, source_target_pairs={{0,4},{1,5},{2,6},{3,7},{4,0},{5,1},{6,2},{7,3},{8,12},{9,13},{10,... | collective-permute-start | bytes 196616 | tf_op jit(solution)/shard_map/ppermute | solution.py:47
  60.5 6.0 %collective-permute-start.18 = (bf16[64,512]{1,0:T(8,128)(2,1)S(1)}, bf16[64,512]{1,0:T(8,128)(2,1)S(1)}, u32[]{:S(2)}, u32[]{:S(2)}) collective-permute-start(bf16[64,512]{1,0:T(8,128)(2,1)S(1)} %get-tuple-element.59), channel_id=1, source_target_pairs={{0,2},{1,3},{2,0},{3,1},{4,6},{5,7},{6,4},{7,5},{8,10},{9,11},{10,... | collective-permute-start | bytes 196616 | tf_op jit(solution)/shard_map/ppermute | solution.py:47
  60.5 9.1 %collective-permute-start.19 = (bf16[64,512]{1,0:T(8,128)(2,1)S(1)}, bf16[64,512]{1,0:T(8,128)(2,1)S(1)}, u32[]{:S(2)}, u32[]{:S(2)}) collective-permute-start(bf16[64,512]{1,0:T(8,128)(2,1)S(1)} %get-tuple-element.59), channel_id=1, source_target_pairs={{0,4},{1,5},{2,6},{3,7},{4,0},{5,1},{6,2},{7,3},{8,12},{9,13},{10,... | collective-permute-start | bytes 196616 | tf_op jit(solution)/shard_map/ppermute | solution.py:47
  62.8 6.8 %collective-permute-start.20 = (bf16[64,512]{1,0:T(8,128)(2,1)S(1)}, bf16[64,512]{1,0:T(8,128)(2,1)S(1)}, u32[]{:S(2)}, u32[]{:S(2)}) collective-permute-start(bf16[64,512]{1,0:T(8,128)(2,1)S(1)} %get-tuple-element.59), channel_id=1, source_target_pairs={{0,6},{1,7},{2,4},{3,5},{4,2},{5,3},{6,0},{7,1},{8,14},{9,15},{10,... | collective-permute-start | bytes 196616 | tf_op jit(solution)/shard_map/ppermute | solution.py:47
  65.0 6.1 %collective-permute-start.33 = (bf16[4,64,256]{2,1,0:T(8,128)(2,1)S(1)}, bf16[4,64,256]{2,1,0:T(8,128)(2,1)S(1)}, u32[]{:S(2)}, u32[]{:S(2)}) collective-permute-start(bf16[4,64,256]{2,1,0:T(8,128)(2,1)S(1)} %get-tuple-element.88), channel_id=1, source_target_pairs={{0,16},{1,17},{2,18},{3,19},{4,20},{5,21},{6,22},{7,23},{8,24},{9,... | collective-permute-start | bytes 393224 | tf_op jit(solution)/shard_map/ppermute | solution.py:47
  65.8 5.3 %collective-permute-start.32 = (bf16[4,64,256]{2,1,0:T(8,128)(2,1)S(1)}, bf16[4,64,256]{2,1,0:T(8,128)(2,1)S(1)}, u32[]{:S(2)}, u32[]{:S(2)}) collective-permute-start(bf16[4,64,256]{2,1,0:T(8,128)(2,1)S(1)} %get-tuple-element.90), channel_id=1, source_target_pairs={{0,1},{1,0},{2,3},{3,2},{4,5},{5,4},{6,7},{7,6},{8,9},{9,8},{10,11... | collective-permute-start | bytes 393224 | tf_op jit(solution)/shard_map/ppermute | solution.py:47
  69.7 6.4 %collective-permute-start.22 = (bf16[4,64,256]{2,1,0:T(8,128)(2,1)S(1)}, bf16[4,64,256]{2,1,0:T(8,128)(2,1)S(1)}, u32[]{:S(2)}, u32[]{:S(2)}) collective-permute-start(bf16[4,64,256]{2,1,0:T(8,128)(2,1)S(1)} %get-tuple-element.92), channel_id=1, source_target_pairs={{0,16},{1,17},{2,18},{3,19},{4,20},{5,21},{6,22},{7,23},{8,24},{9,... | collective-permute-start | bytes 393224 | tf_op jit(solution)/shard_map/ppermute | solution.py:47
  70.4 6.2 %collective-permute-start.21 = (bf16[4,64,256]{2,1,0:T(8,128)(2,1)S(1)}, bf16[4,64,256]{2,1,0:T(8,128)(2,1)S(1)}, u32[]{:S(2)}, u32[]{:S(2)}) collective-permute-start(bf16[4,64,256]{2,1,0:T(8,128)(2,1)S(1)} %get-tuple-element.94), channel_id=1, source_target_pairs={{0,1},{1,0},{2,3},{3,2},{4,5},{5,4},{6,7},{7,6},{8,9},{9,8},{10,11... | collective-permute-start | bytes 393224 | tf_op jit(solution)/shard_map/ppermute | solution.py:47
  71.2 8.3 %collective-permute-start.36 = (bf16[2,4,64,256]{3,2,1,0:T(8,128)(2,1)S(1)}, bf16[2,4,64,256]{3,2,1,0:T(8,128)(2,1)S(1)}, u32[]{:S(2)}, u32[]{:S(2)}) collective-permute-start(bf16[2,4,64,256]{3,2,1,0:T(8,128)(2,1)S(1)} %pad_maximum_fusion.3.refs_3_), channel_id=1, source_target_pairs={{0,1},{1,0},{2,3},{3,2},{4,5},{5,4},{6,7},{7,6},{8,9},{9,8},{10,11... | collective-permute-start | bytes 786440 | tf_op jit(solution)/shard_map/ppermute | solution.py:47
  72.6 9.6 %collective-permute-start.35 = (bf16[2,4,64,256]{3,2,1,0:T(8,128)(2,1)S(1)}, bf16[2,4,64,256]{3,2,1,0:T(8,128)(2,1)S(1)}, u32[]{:S(2)}, u32[]{:S(2)}) collective-permute-start(bf16[2,4,64,256]{3,2,1,0:T(8,128)(2,1)S(1)} %pad_maximum_fusion.2.refs_1_), channel_id=1, source_target_pairs={{0,16},{1,17},{2,18},{3,19},{4,20},{5,21},{6,22},{7,23},{8,24},{9,... | collective-permute-start | bytes 786440 | tf_op jit(solution)/shard_map/ppermute | solution.py:47
  74.1 12.5 %collective-permute-start.38 = (bf16[2,4,64,256]{3,2,1,0:T(8,128)(2,1)S(1)}, bf16[2,4,64,256]{3,2,1,0:T(8,128)(2,1)S(1)}, u32[]{:S(2)}, u32[]{:S(2)}) collective-permute-start(bf16[2,4,64,256]{3,2,1,0:T(8,128)(2,1)S(1)} %pad_maximum_fusion.3.refs_3_), channel_id=1, source_target_pairs={{0,8},{1,9},{2,10},{3,11},{4,12},{5,13},{6,14},{7,15},{8,0},{9,1},... | collective-permute-start | bytes 786440 | tf_op jit(solution)/shard_map/ppermute | solution.py:47
  76.1 11.0 %collective-permute-start.34 = (bf16[2,4,64,256]{3,2,1,0:T(8,128)(2,1)S(1)}, bf16[2,4,64,256]{3,2,1,0:T(8,128)(2,1)S(1)}, u32[]{:S(2)}, u32[]{:S(2)}) collective-permute-start(bf16[2,4,64,256]{3,2,1,0:T(8,128)(2,1)S(1)} %pad_maximum_fusion.2.refs_1_), channel_id=1, source_target_pairs={{0,8},{1,9},{2,10},{3,11},{4,12},{5,13},{6,14},{7,15},{8,0},{9,1},... | collective-permute-start | bytes 786440 | tf_op jit(solution)/shard_map/ppermute | solution.py:47
  76.6 8.4 %collective-permute-start.24 = (bf16[2,4,64,256]{3,2,1,0:T(8,128)(2,1)S(1)}, bf16[2,4,64,256]{3,2,1,0:T(8,128)(2,1)S(1)}, u32[]{:S(2)}, u32[]{:S(2)}) collective-permute-start(bf16[2,4,64,256]{3,2,1,0:T(8,128)(2,1)S(1)} %pad_maximum_fusion.1.refs_3_), channel_id=1, source_target_pairs={{0,1},{1,0},{2,3},{3,2},{4,5},{5,4},{6,7},{7,6},{8,9},{9,8},{10,11... | collective-permute-start | bytes 786440 | tf_op jit(solution)/shard_map/ppermute | solution.py:47
  79.5 7.1 %collective-permute-start.23 = (bf16[2,4,64,256]{3,2,1,0:T(8,128)(2,1)S(1)}, bf16[2,4,64,256]{3,2,1,0:T(8,128)(2,1)S(1)}, u32[]{:S(2)}, u32[]{:S(2)}) collective-permute-start(bf16[2,4,64,256]{3,2,1,0:T(8,128)(2,1)S(1)} %pad_maximum_fusion.refs_1_), channel_id=1, source_target_pairs={{0,16},{1,17},{2,18},{3,19},{4,20},{5,21},{6,22},{7,23},{8,24},{9,... | collective-permute-start | bytes 786440 | tf_op jit(solution)/shard_map/ppermute | solution.py:47
  83.7 3.4 %collective-permute-start.37 = (bf16[2,4,64,256]{3,2,1,0:T(8,128)(2,1)S(1)}, bf16[2,4,64,256]{3,2,1,0:T(8,128)(2,1)S(1)}, u32[]{:S(2)}, u32[]{:S(2)}) collective-permute-start(bf16[2,4,64,256]{3,2,1,0:T(8,128)(2,1)S(1)} %collective-permute-done.35.refs_2_), channel_id=1, source_target_pairs={{0,8},{1,9},{2,10},{3,11},{4,12},{5,13},{6,14},{7,15},{8,0},{9,1},... | collective-permute-start | bytes 786440 | tf_op jit(solution)/shard_map/ppermute | solution.py:47
  85.0 2.6 %collective-permute-start.39 = (bf16[2,4,64,256]{3,2,1,0:T(8,128)(2,1)S(1)}, bf16[2,4,64,256]{3,2,1,0:T(8,128)(2,1)S(1)}, u32[]{:S(2)}, u32[]{:S(2)}) collective-permute-start(bf16[2,4,64,256]{3,2,1,0:T(8,128)(2,1)S(1)} %collective-permute-done.36.refs_4_), channel_id=1, source_target_pairs={{0,8},{1,9},{2,10},{3,11},{4,12},{5,13},{6,14},{7,15},{8,0},{9,1},... | collective-permute-start | bytes 786440 | tf_op jit(solution)/shard_map/ppermute | solution.py:47
  86.5 2.6 %collective-permute-start.27 = (bf16[2,4,64,256]{3,2,1,0:T(8,128)(2,1)S(1)}, bf16[2,4,64,256]{3,2,1,0:T(8,128)(2,1)S(1)}, u32[]{:S(2)}, u32[]{:S(2)}) collective-permute-start(bf16[2,4,64,256]{3,2,1,0:T(8,128)(2,1)S(1)} %pad_maximum_fusion.1.refs_3_), channel_id=1, source_target_pairs={{0,8},{1,9},{2,10},{3,11},{4,12},{5,13},{6,14},{7,15},{8,0},{9,1},... | collective-permute-start | bytes 786440 | tf_op jit(solution)/shard_map/ppermute | solution.py:47
  86.5 2.6 %collective-permute-start.25 = (bf16[2,4,64,256]{3,2,1,0:T(8,128)(2,1)S(1)}, bf16[2,4,64,256]{3,2,1,0:T(8,128)(2,1)S(1)}, u32[]{:S(2)}, u32[]{:S(2)}) collective-permute-start(bf16[2,4,64,256]{3,2,1,0:T(8,128)(2,1)S(1)} %pad_maximum_fusion.refs_1_), channel_id=1, source_target_pairs={{0,8},{1,9},{2,10},{3,11},{4,12},{5,13},{6,14},{7,15},{8,0},{9,1},... | collective-permute-start | bytes 786440 | tf_op jit(solution)/shard_map/ppermute | solution.py:47
  87.1 2.1 %collective-permute-start.26 = (bf16[2,4,64,256]{3,2,1,0:T(8,128)(2,1)S(1)}, bf16[2,4,64,256]{3,2,1,0:T(8,128)(2,1)S(1)}, u32[]{:S(2)}, u32[]{:S(2)}) collective-permute-start(bf16[2,4,64,256]{3,2,1,0:T(8,128)(2,1)S(1)} %collective-permute-done.23.refs_2_), channel_id=1, source_target_pairs={{0,8},{1,9},{2,10},{3,11},{4,12},{5,13},{6,14},{7,15},{8,0},{9,1},... | collective-permute-start | bytes 786440 | tf_op jit(solution)/shard_map/ppermute | solution.py:47
  87.1 2.1 %collective-permute-start.28 = (bf16[2,4,64,256]{3,2,1,0:T(8,128)(2,1)S(1)}, bf16[2,4,64,256]{3,2,1,0:T(8,128)(2,1)S(1)}, u32[]{:S(2)}, u32[]{:S(2)}) collective-permute-start(bf16[2,4,64,256]{3,2,1,0:T(8,128)(2,1)S(1)} %collective-permute-done.24.refs_4_), channel_id=1, source_target_pairs={{0,8},{1,9},{2,10},{3,11},{4,12},{5,13},{6,14},{7,15},{8,0},{9,1},... | collective-permute-start | bytes 786440 | tf_op jit(solution)/shard_map/ppermute | solution.py:47
